TPU v7x, 512 devices: a whole 4x8x8 slice. The times are simulated.
512 devices in a mesh: rep: 8 (over z_hi, core), row: 8 (over z_lo, x), col: 8 (over y).
Axes of the slice: x: 4, y: 8, z: 8 (z_hi: 4, z_lo: 2; z = z_hi * 2 + z_lo), core: 2. Of those that a mesh axis runs over, the one named last changes fastest.
Arguments:
- inputs: bfloat16 [8, 128, 6144], P('rep', 'col', 'row'), may hold values from -6 to 6
- w_in: bfloat16 [6144, 24576], P('row', ('rep', 'col')), may hold values from -0.078125 to 0.078125
- w_out: bfloat16 [24576, 6144], P(('rep', 'col'), 'row'), may hold values from -0.0390625 to 0.0390625
- cotangent: bfloat16 [8, 128, 6144], P('rep', 'col', 'row'), may hold values from -3072 to 3072
- counts: int32 [8], replicated, may hold values from 0 to 4, as said below
Outputs:
- block_output: bfloat16 [8, 128, 6144], P('rep', 'col', 'row')
- input_grad: bfloat16 [8, 128, 6144], P('rep', 'col', 'row')
- w_in_grad: float32 [6144, 24576], P('row', ('rep', 'col'))
- w_out_grad: float32 [24576, 6144], P(('rep', 'col'), 'row')
Inputs may be any that keep to these rules, and one draw needn't show every extreme that they name: Replica r completed its first counts[r] micro-batches; at least one replica completed all 4.
All inputs are finite; a program needn't handle non-finite values.
Results may differ from a plain program's by a relative error of at most 0.015.
Values may be sent and summed in bfloat16 or wider, within the bound.
No kernel may reach another device: no remote copies, remote signals or barrier semaphores. Data moves between devices by JAX's collectives and lax.ppermute only.
A program may use at most 64 MiB of HBM per device.

v0:
```python
import jax
import jax.numpy as jnp
from jax import lax
from jax.sharding import PartitionSpec as P

MBT = 32


root_coef = 0.7978845608028654
cubic_coef = 0.044715


def in_one_piece(arrays, axis, dim, along):
    both = jnp.concatenate(arrays, axis=along)
    result, at, finished = (lax.all_gather(both, axis, axis=dim, tiled=True), 0, [])
    for a in arrays:
        finished.append(lax.slice_in_dim(result, at, at + a.shape[along], axis=along))
        at += a.shape[along]
    return tuple(finished)


def split_up(value, dim, size):
    dims = value.shape
    pieces = value.reshape(*dims[:dim], size, dims[dim] // size, *dims[dim + 1 :])
    return jnp.moveaxis(pieces, dim, 0)


def summed_on_arrival(value, axis, dim):
    size = lax.axis_size(axis)
    pieces = lax.all_to_all(split_up(value, dim, size), axis, 0, 0, tiled=True)
    return jnp.sum(pieces.astype(jnp.float32), axis=0)


def sent_to_all(value, axis):
    size = lax.axis_size(axis)
    return lax.all_to_all(
        jnp.broadcast_to(value[None], (size, *value.shape)), axis, 0, 0, tiled=True
    )


def joined_along(pieces, dim):
    pieces = jnp.moveaxis(pieces, 0, dim)
    dims = pieces.shape
    return pieces.reshape(*dims[:dim], dims[dim] * dims[dim + 1], *dims[dim + 2 :])


def gathered_copies(value, axis, dim):
    pieces = sent_to_all(value, axis)
    return joined_along(pieces, dim)


def gelu_tanh(values):
    inner = root_coef * (values + cubic_coef * values * values * values)
    return 0.5 * values * (1.0 + jnp.tanh(inner))


def gelu_slope(values):
    inner = root_coef * (values + cubic_coef * values * values * values)
    tangent = jnp.tanh(inner)
    return 0.5 * (1.0 + tangent) + 0.5 * values * (1.0 - tangent * tangent) * root_coef * (
        1.0 + 3.0 * cubic_coef * values * values
    )


def right_product(left, right):
    return lax.dot_general(
        left, right, (((1,), (1,)), ((), ())), preferred_element_type=jnp.float32
    )


def first_product(left, right):
    return lax.dot_general(
        left, right, (((0,), (0,)), ((), ())), preferred_element_type=jnp.float32
    )


def body(inputs, w_in, w_out, cotangent, counts):
    rows_local = inputs.shape[1]
    width_local = inputs.shape[2]
    tokens_local = inputs.reshape(rows_local, width_local)
    replicas = lax.axis_size("rep")
    replica_index = lax.axis_index("rep")
    column_index = lax.axis_index("col")
    own_count = jnp.sum(jnp.where(jnp.arange(replicas) == replica_index, counts, 0))
    token_total = (MBT * jnp.sum(counts)).astype(jnp.float32)
    positions = column_index * rows_local + jnp.arange(rows_local, dtype=jnp.int32)
    kept_mask = (positions // MBT < own_count).astype(jnp.float32)
    scaled = (
        cotangent.reshape(rows_local, width_local).astype(jnp.float32)
        * kept_mask[:, None]
        / token_total
    ).astype(jnp.bfloat16)
    tokens_all, scaled_all = in_one_piece((tokens_local, scaled), "col", 0, 1)
    inner_cols = lax.all_gather(w_in, "rep", axis=1, tiled=True)
    outer_rows = lax.all_gather(w_out, "rep", axis=0, tiled=True)
    partial_hidden = jnp.dot(tokens_all, inner_cols, preferred_element_type=jnp.float32)
    hidden = summed_on_arrival(partial_hidden.astype(jnp.bfloat16), "row", 0)
    active_share = gelu_tanh(hidden).astype(jnp.bfloat16)
    activated = gathered_copies(active_share, "row", 0)
    output_terms = jnp.dot(activated, outer_rows, preferred_element_type=jnp.float32)
    output_local = summed_on_arrival(output_terms.astype(jnp.bfloat16), "col", 0)
    block_output = (tokens_local.astype(jnp.float32) + output_local).astype(jnp.bfloat16)
    slope_terms = right_product(scaled_all, outer_rows)
    slope_sum = summed_on_arrival(slope_terms.astype(jnp.bfloat16), "row", 0)
    grad_share = (slope_sum * gelu_slope(hidden)).astype(jnp.bfloat16)
    hidden_grad = gathered_copies(grad_share, "row", 0)
    back_terms = right_product(hidden_grad, inner_cols)
    back_local = summed_on_arrival(back_terms.astype(jnp.bfloat16), "col", 0)
    input_grad = (scaled.astype(jnp.float32) + back_local).astype(jnp.bfloat16)
    token_reps, scaled_reps = in_one_piece((tokens_all, scaled_all), "rep", 0, 1)
    hidden_reps, active_reps = (
        lax.all_to_all(hidden_grad, "rep", split_axis=1, concat_axis=0, tiled=True),
        lax.all_to_all(activated, "rep", split_axis=1, concat_axis=0, tiled=True),
    )
    w_in_grad = first_product(token_reps, hidden_reps)
    w_out_grad = first_product(active_reps, scaled_reps)
    return (
        block_output.reshape(1, rows_local, width_local),
        input_grad.reshape(1, rows_local, width_local),
        w_in_grad,
        w_out_grad,
    )


def solution(mesh):
    placed = (
        P("rep", "col", "row"),
        P("row", ("rep", "col")),
        P(("rep", "col"), "row"),
        P("rep", "col", "row"),
        P(),
    )
    return jax.shard_map(
        body,
        mesh=mesh,
        in_specs=placed,
        out_specs=(
            P("rep", "col", "row"),
            P("rep", "col", "row"),
            P("row", ("rep", "col")),
            P(("rep", "col"), "row"),
        ),
        check_vma=False,
    )
```

profile of v0, /device:TPU:6, one launch (start us, length us, event | category | flops | bytes accessed | tf_op | source)
XLA Modules:
  0.0 305.8 jit_solution(1008410382800476033)
XLA Ops:
  7.2 0.0 all-gather.6.cloned.1.call-start
  7.2 0.7 all-gather.6.cloned.1.call-update
  7.9 0.0 all-gather.4.cloned.1.call-start
  7.9 0.7 all-gather.4.cloned.1.call-update
  8.7 1.3 fusion.20
  10.6 0.7 compare_convert_fusion
  11.3 0.8 fusion.15
  12.1 0.7 pad_maximum_fusion
  12.8 26.6 %all_gather.12 = bf16[128,1536]{1,0:T(8,128)(2,1)S(1)} all-gather(bf16[16,1536]{1,0:T(8,128)(2,1)S(1)} %pad_maximum_fusion), channel_id=1, replica_groups=mesh['rep'=8,'row'=8,'col'=8] {'col'}, dimensions={0}, use_global_device_ids=true | all-gather | bytes 442368 | tf_op jit(solution)/shard_map/all_gather | solution.py:15
  39.4 35.8 %all-gather.6.cloned.1.call-done = bf16[3072,768]{1,0:T(8,128)(2,1)} async-done(((bf16[384,768]{1,0:T(8,128)(2,1)}), bf16[3072,768]{1,0:T(8,128)(2,1)}) %all-gather.6.cloned.1.call-update) | async-done | bytes 4718608 | tf_op jit(solution)/shard_map/all_gather | solution.py:95
  75.3 4.8 %convolution_convert_fusion = bf16[128,3072]{1,0:T(8,128)(2,1)} fusion(bf16[3072,768]{1,0:T(8,128)(2,1)} %all-gather.6.cloned.1.call-done, bf16[128,1536]{1,0:T(8,128)(2,1)S(1)} %all_gather.12), kind=kOutput, calls=%fused_computation | convolution fusion | flops 604372992 | bytes 5701632 | tf_op jit(solution)/shard_map/dot_general | solution.py:66
  80.1 4.8 %all-to-all-start.3 = ((bf16[8,16,3072]{2,1,0:T(8,128)(2,1)}), bf16[8,16,3072]{2,1,0:T(8,128)(2,1)S(1)}, u32[]{:S(2)}, u32[]{:S(2)}) async-start(bf16[8,16,3072]{2,1,0:T(8,128)(2,1)} %bitcast.6), calls=%async_computation.3 | async-start | bytes 1572864 | tf_op jit(solution)/shard_map/all_to_all | solution.py:30
  85.0 53.2 %all-gather.4.cloned.1.call-done = bf16[768,3072]{1,0:T(8,128)(2,1)} async-done(((bf16[768,384]{1,0:T(8,128)(2,1)}), bf16[768,3072]{1,0:T(8,128)(2,1)}) %all-gather.4.cloned.1.call-update) | async-done | bytes 4718608 | tf_op jit(solution)/shard_map/all_gather | solution.py:94
  138.2 0.0 copy-done
  138.2 4.1 %convolution_convert_fusion.1 = bf16[128,3072]{1,0:T(8,128)(2,1)} fusion(bf16[768,3072]{1,0:T(8,128)(2,1)} %all-gather.4.cloned.1.call-done, bf16[128,1536]{1,0:T(8,128)(2,1)S(1)} %all_gather.12), kind=kOutput, calls=%fused_computation.1 | convolution fusion | flops 604372992 | bytes 5701632 | tf_op jit(solution)/shard_map/dot_general | solution.py:96
  142.3 0.0 all-to-all-done.3
  142.3 4.8 %all-to-all-start = ((bf16[8,16,3072]{2,1,0:T(8,128)(2,1)}), bf16[8,16,3072]{2,1,0:T(8,128)(2,1)S(1)}, u32[]{:S(2)}, u32[]{:S(2)}) async-start(bf16[8,16,3072]{2,1,0:T(8,128)(2,1)} %bitcast.2), calls=%async_computation | async-start | bytes 1572864 | tf_op jit(solution)/shard_map/all_to_all | solution.py:30
  147.1 0.1 convert_reduce_fusion
  147.2 10.6 %all-to-all-done = bf16[8,16,3072]{2,1,0:T(8,128)(2,1)S(1)} async-done(((bf16[8,16,3072]{2,1,0:T(8,128)(2,1)}), bf16[8,16,3072]{2,1,0:T(8,128)(2,1)S(1)}, u32[]{:S(2)}, u32[]{:S(2)}) %all-to-all-start) | async-done | bytes 786464 | tf_op jit(solution)/shard_map/all_to_all | solution.py:30
  157.7 0.1 convert_reduce_fusion.1
  157.9 0.1 fusion.10
  158.0 1.0 broadcast_in_dim.9
  159.0 5.4 %all-to-all-start.1 = ((bf16[8,16,3072]{2,1,0:T(8,128)(2,1)}), bf16[8,16,3072]{2,1,0:T(8,128)(2,1)S(1)}, u32[]{:S(2)}, u32[]{:S(2)}) async-start(bf16[8,16,3072]{2,1,0:T(8,128)(2,1)} %broadcast_in_dim.9), calls=%async_computation.1 | async-start | bytes 1572864 | tf_op jit(solution)/shard_map/all_to_all | solution.py:36
  164.3 0.0 all-gather.8.cloned.1.call-start
  164.3 0.7 all-gather.8.cloned.1.call-update
  165.1 9.7 %all-to-all-done.1 = bf16[8,16,3072]{2,1,0:T(8,128)(2,1)S(1)} async-done(((bf16[8,16,3072]{2,1,0:T(8,128)(2,1)}), bf16[8,16,3072]{2,1,0:T(8,128)(2,1)S(1)}, u32[]{:S(2)}, u32[]{:S(2)}) %all-to-all-start.1) | async-done | bytes 786464 | tf_op jit(solution)/shard_map/all_to_all | solution.py:36
  174.8 1.0 broadcast_in_dim.10
  175.7 5.4 %all-to-all-start.4 = ((bf16[8,16,3072]{2,1,0:T(8,128)(2,1)}), bf16[8,16,3072]{2,1,0:T(8,128)(2,1)S(1)}, u32[]{:S(2)}, u32[]{:S(2)}) async-start(bf16[8,16,3072]{2,1,0:T(8,128)(2,1)} %broadcast_in_dim.10), calls=%async_computation.4 | async-start | bytes 1572864 | tf_op jit(solution)/shard_map/all_to_all | solution.py:36
  181.1 3.8 %convolution_convert_fusion.3 = bf16[128,768]{1,0:T(8,128)(2,1)} fusion(bf16[128,3072]{1,0:T(8,128)(2,1)S(1)} %bitcast.43, bf16[3072,768]{1,0:T(8,128)(2,1)} %all-gather.6.cloned.1.call-done), kind=kOutput, calls=%fused_computation.9 | convolution fusion | flops 604078080 | bytes 5701632 | tf_op jit(solution)/shard_map/dot_general | solution.py:100
  184.9 26.9 %all-to-all-done.4 = bf16[8,16,3072]{2,1,0:T(8,128)(2,1)S(1)} async-done(((bf16[8,16,3072]{2,1,0:T(8,128)(2,1)}), bf16[8,16,3072]{2,1,0:T(8,128)(2,1)S(1)}, u32[]{:S(2)}, u32[]{:S(2)}) %all-to-all-start.4) | async-done | bytes 786464 | tf_op jit(solution)/shard_map/all_to_all | solution.py:36
  211.8 6.9 %all-to-all-start.2 = ((bf16[8,16,768]{2,1,0:T(8,128)(2,1)}), bf16[8,16,768]{2,1,0:T(8,128)(2,1)S(1)}, u32[]{:S(2)}, u32[]{:S(2)}) async-start(bf16[8,16,768]{2,1,0:T(8,128)(2,1)} %bitcast.4), calls=%async_computation.2 | async-start | bytes 393216 | tf_op jit(solution)/shard_map/all_to_all | solution.py:30
  218.7 4.7 %convolution_convert_fusion.2 = bf16[128,768]{1,0:T(8,128)(2,1)} fusion(bf16[128,3072]{1,0:T(8,128)(2,1)S(1)} %bitcast.45, bf16[768,3072]{1,0:T(8,128)(2,1)} %all-gather.4.cloned.1.call-done), kind=kOutput, calls=%fused_computation.8 | convolution fusion | flops 604078080 | bytes 5701632 | tf_op jit(solution)/shard_map/dot_general | solution.py:66
  223.4 5.3 %all-to-all-done.2 = bf16[8,16,768]{2,1,0:T(8,128)(2,1)S(1)} async-done(((bf16[8,16,768]{2,1,0:T(8,128)(2,1)}), bf16[8,16,768]{2,1,0:T(8,128)(2,1)S(1)}, u32[]{:S(2)}, u32[]{:S(2)}) %all-to-all-start.2) | async-done | bytes 196640 | tf_op jit(solution)/shard_map/all_to_all | solution.py:30
  228.7 3.4 %all-to-all-start.5 = ((bf16[8,16,768]{2,1,0:T(8,128)(2,1)}), bf16[8,16,768]{2,1,0:T(8,128)(2,1)S(1)}, u32[]{:S(2)}, u32[]{:S(2)}) async-start(bf16[8,16,768]{2,1,0:T(8,128)(2,1)} %bitcast.8), calls=%async_computation.5 | async-start | bytes 393216 | tf_op jit(solution)/shard_map/all_to_all | solution.py:30
  232.1 0.1 copy.13
  232.2 1.0 copy.11
  233.2 8.6 %all-to-all-done.5 = bf16[8,16,768]{2,1,0:T(8,128)(2,1)S(1)} async-done(((bf16[8,16,768]{2,1,0:T(8,128)(2,1)}), bf16[8,16,768]{2,1,0:T(8,128)(2,1)S(1)}, u32[]{:S(2)}, u32[]{:S(2)}) %all-to-all-start.5) | async-done | bytes 196640 | tf_op jit(solution)/shard_map/all_to_all | solution.py:30
  241.8 3.5 %all-to-all-start.6 = ((bf16[128,8,384]{2,0,1:T(8,128)(2,1)}), bf16[128,8,384]{2,0,1:T(8,128)(2,1)S(1)}, u32[]{:S(2)}, u32[]{:S(2)}) async-start(bf16[128,8,384]{2,0,1:T(8,128)(2,1)} %copy.11), calls=%async_computation.6 | async-start | bytes 1572864 | tf_op jit(solution)/shard_map/all_to_all | solution.py:112
  245.3 0.1 copy.14
  245.5 1.0 copy.12
  246.5 22.3 %all-to-all-done.6 = bf16[128,8,384]{2,0,1:T(8,128)(2,1)S(1)} async-done(((bf16[128,8,384]{2,0,1:T(8,128)(2,1)}), bf16[128,8,384]{2,0,1:T(8,128)(2,1)S(1)}, u32[]{:S(2)}, u32[]{:S(2)}) %all-to-all-start.6) | async-done | bytes 786464 | tf_op jit(solution)/shard_map/all_to_all | solution.py:112
  268.8 3.5 %all-to-all-start.7 = ((bf16[128,8,384]{2,0,1:T(8,128)(2,1)}), bf16[128,8,384]{2,0,1:T(8,128)(2,1)S(1)}, u32[]{:S(2)}, u32[]{:S(2)}) async-start(bf16[128,8,384]{2,0,1:T(8,128)(2,1)} %copy.12), calls=%async_computation.7 | async-start | bytes 1572864 | tf_op jit(solution)/shard_map/all_to_all | solution.py:113
  272.4 0.6 fusion.19
  273.0 0.0 copy-done.1
  273.0 0.7 fusion.18
  273.7 3.4 %fusion.2 = f32[768,384]{1,0:T(8,128)} fusion(bf16[1024,384]{1,0:T(8,128)(2,1)S(1)} %bitcast.49, bf16[1024,1536]{1,0:T(8,128)(2,1)} %all-gather.8.cloned.1.call-done), kind=kOutput, calls=%fused_computation.4 | convolution fusion | flops 603979776 | bytes 3538944 | tf_op jit(solution)/shard_map/dot_general | solution.py:72
  277.1 18.9 %all-to-all-done.7 = bf16[128,8,384]{2,0,1:T(8,128)(2,1)S(1)} async-done(((bf16[128,8,384]{2,0,1:T(8,128)(2,1)}), bf16[128,8,384]{2,0,1:T(8,128)(2,1)S(1)}, u32[]{:S(2)}, u32[]{:S(2)}) %all-to-all-start.7) | async-done | bytes 786464 | tf_op jit(solution)/shard_map/all_to_all | solution.py:113
  296.0 3.2 %fusion = f32[384,768]{1,0:T(8,128)} fusion(bf16[1024,384]{1,0:T(8,128)(2,1)S(1)} %bitcast.50, bf16[1024,1536]{1,0:T(8,128)(2,1)} %all-gather.8.cloned.1.call-done), kind=kOutput, calls=%fused_computation.2 | convolution fusion | flops 603979776 | bytes 3538944 | tf_op jit(solution)/shard_map/dot_general | solution.py:72
  (7 shorter events, 0.1 us)
Async XLA Ops:
  7.2 68.1 %all-gather.6.cloned.1.call-start = ((), (), s32[]{:S(2)}) async-start(), calls=%async_computation.9 | async-start | bytes 5308416 | tf_op jit(solution)/shard_map/all_gather | solution.py:95
  7.9 130.3 %all-gather.4.cloned.1.call-start = ((), (), s32[]{:S(2)}) async-start(), calls=%async_computation.8 | async-start | bytes 5308416 | tf_op jit(solution)/shard_map/all_gather | solution.py:94
  39.4 98.8 %copy-start = (bf16[128,1536]{1,0:T(8,128)(2,1)}, bf16[128,1536]{1,0:T(8,128)(2,1)S(1)}, u32[]{:S(2)}) copy-start(bf16[128,1536]{1,0:T(8,128)(2,1)S(1)} %all_gather.12) | copy-start | bytes 1179652
  80.1 62.1 %all-to-all-start.3 = ((bf16[8,16,3072]{2,1,0:T(8,128)(2,1)}), bf16[8,16,3072]{2,1,0:T(8,128)(2,1)S(1)}, u32[]{:S(2)}, u32[]{:S(2)}) async-start(bf16[8,16,3072]{2,1,0:T(8,128)(2,1)} %bitcast.6), calls=%async_computation.3 | async-start | bytes 1572864 | tf_op jit(solution)/shard_map/all_to_all | solution.py:30
  142.3 15.5 %all-to-all-start = ((bf16[8,16,3072]{2,1,0:T(8,128)(2,1)}), bf16[8,16,3072]{2,1,0:T(8,128)(2,1)S(1)}, u32[]{:S(2)}, u32[]{:S(2)}) async-start(bf16[8,16,3072]{2,1,0:T(8,128)(2,1)} %bitcast.2), calls=%async_computation | async-start | bytes 1572864 | tf_op jit(solution)/shard_map/all_to_all | solution.py:30
  159.0 15.8 %all-to-all-start.1 = ((bf16[8,16,3072]{2,1,0:T(8,128)(2,1)}), bf16[8,16,3072]{2,1,0:T(8,128)(2,1)S(1)}, u32[]{:S(2)}, u32[]{:S(2)}) async-start(bf16[8,16,3072]{2,1,0:T(8,128)(2,1)} %broadcast_in_dim.9), calls=%async_computation.1 | async-start | bytes 1572864 | tf_op jit(solution)/shard_map/all_to_all | solution.py:36
  164.3 109.4 %all-gather.8.cloned.1.call-start = ((), (), s32[]{:S(2)}) async-start(), calls=%async_computation.10 | async-start | bytes 3538944 | tf_op jit(solution)/shard_map/all_gather | solution.py:15
  175.7 36.1 %all-to-all-start.4 = ((bf16[8,16,3072]{2,1,0:T(8,128)(2,1)}), bf16[8,16,3072]{2,1,0:T(8,128)(2,1)S(1)}, u32[]{:S(2)}, u32[]{:S(2)}) async-start(bf16[8,16,3072]{2,1,0:T(8,128)(2,1)} %broadcast_in_dim.10), calls=%async_computation.4 | async-start | bytes 1572864 | tf_op jit(solution)/shard_map/all_to_all | solution.py:36
  211.8 16.8 %all-to-all-start.2 = ((bf16[8,16,768]{2,1,0:T(8,128)(2,1)}), bf16[8,16,768]{2,1,0:T(8,128)(2,1)S(1)}, u32[]{:S(2)}, u32[]{:S(2)}) async-start(bf16[8,16,768]{2,1,0:T(8,128)(2,1)} %bitcast.4), calls=%async_computation.2 | async-start | bytes 393216 | tf_op jit(solution)/shard_map/all_to_all | solution.py:30
  228.7 13.1 %all-to-all-start.5 = ((bf16[8,16,768]{2,1,0:T(8,128)(2,1)}), bf16[8,16,768]{2,1,0:T(8,128)(2,1)S(1)}, u32[]{:S(2)}, u32[]{:S(2)}) async-start(bf16[8,16,768]{2,1,0:T(8,128)(2,1)} %bitcast.8), calls=%async_computation.5 | async-start | bytes 393216 | tf_op jit(solution)/shard_map/all_to_all | solution.py:30
  233.2 39.2 %copy-start.2 = (bf16[1,16,768]{2,1,0:T(8,128)(2,1)S(1)}, bf16[1,16,768]{2,1,0:T(8,128)(2,1)}, u32[]{:S(2)}) copy-start(bf16[1,16,768]{2,1,0:T(8,128)(2,1)} %param.5) | copy-start | bytes 73732
  233.2 39.8 %copy-start.1 = (bf16[1,16,768]{2,1,0:T(8,128)(2,1)S(1)}, bf16[1,16,768]{2,1,0:T(8,128)(2,1)}, u32[]{:S(2)}) copy-start(bf16[1,16,768]{2,1,0:T(8,128)(2,1)} %param.8) | copy-start | bytes 73732
  241.8 27.0 %all-to-all-start.6 = ((bf16[128,8,384]{2,0,1:T(8,128)(2,1)}), bf16[128,8,384]{2,0,1:T(8,128)(2,1)S(1)}, u32[]{:S(2)}, u32[]{:S(2)}) async-start(bf16[128,8,384]{2,0,1:T(8,128)(2,1)} %copy.11), calls=%async_computation.6 | async-start | bytes 1572864 | tf_op jit(solution)/shard_map/all_to_all | solution.py:112
  268.8 27.3 %all-to-all-start.7 = ((bf16[128,8,384]{2,0,1:T(8,128)(2,1)}), bf16[128,8,384]{2,0,1:T(8,128)(2,1)S(1)}, u32[]{:S(2)}, u32[]{:S(2)}) async-start(bf16[128,8,384]{2,0,1:T(8,128)(2,1)} %copy.12), calls=%async_computation.7 | async-start | bytes 1572864 | tf_op jit(solution)/shard_map/all_to_all | solution.py:113
Sparse Core Ops, SparseCore 0:
  10.1 65.1 all-gather.5
  77.4 60.7 all-gather.3
  167.3 52.0 all-gather.7
where the time goes:
time: 307 us; the launch traced here: 306 us
  waiting for transfers between devices  193 us (63%)
  starting transfers between devices  37.8 us (12%)
  blocking collectives  26.6 us (9%)
  matrix products  24.1 us (8%)
  between operations  14.5 us (5%)
  other arithmetic  5.26 us (2%)
  local copies, waits for them, and re-layouts  4.15 us (1%)
    all_gather x1, waiting for transfers between devices, body(): inner_cols = lax.all_gather(w_in, 'rep', axis=1, tiled=True)  53.2 us
    all_to_all x2, waiting for transfers between devices, sent_to_all(): lax.all_to_all(jnp.broadcast_to(value[None], (size, *value.shape)), axis,...  36.7 us
    all_gather x1, waiting for transfers between devices, body(): outer_rows = lax.all_gather(w_out, 'rep', axis=0, tiled=True)  35.8 us
    all_gather x1, blocking collectives, in_one_piece(): lax.all_gather(both, axis, axis=dim, tiled=True)  26.6 us
    all_to_all x4, waiting for transfers between devices, summed_on_arrival(): pieces = lax.all_to_all(split_up(value, dim, size), axis, 0, 0, tiled=True)  24.4 us
    all_to_all x1, waiting for transfers between devices, body(): lax.all_to_all(hidden_grad, 'rep', split_axis=1, concat_axis=0, tiled=True)  22.3 us
    all_to_all x4, starting transfers between devices, summed_on_arrival(): pieces = lax.all_to_all(split_up(value, dim, size), axis, 0, 0, tiled=True)  19.9 us
    all_to_all x1, waiting for transfers between devices, body(): lax.all_to_all(activated, 'rep', split_axis=1, concat_axis=0, tiled=True)  18.9 us
  transfers between devices with their start and end apart: 11, of which 9 were waited for; matrix products, arithmetic and copies ran while one was open for 9% of the time, Pallas kernels for 0%

commit v1 on v0

v1 whole, which is shorter than its diff:
```python
import jax
import jax.numpy as jnp
from jax import lax
from jax.sharding import PartitionSpec as P

MBT = 32


root_coef = 0.7978845608028654
cubic_coef = 0.044715


def gelu_both(values):
    inner = root_coef * (values + cubic_coef * values * values * values)
    tangent = jnp.tanh(inner)
    slope = 0.5 * (1.0 + tangent) + 0.5 * values * (1.0 - tangent * tangent) * root_coef * (
        1.0 + 3.0 * cubic_coef * values * values
    )
    return 0.5 * values * (1.0 + tangent), slope


def product(left, right, left_dim, right_dim):
    return lax.dot_general(
        left, right, (((left_dim,), (right_dim,)), ((), ())), preferred_element_type=jnp.float32
    )


def summed_on_arrival(value, axis):
    size = lax.axis_size(axis)
    rows, width = value.shape
    pieces = lax.all_to_all(value.reshape(size, rows // size, width), axis, 0, 0, tiled=True)
    return jnp.sum(pieces.astype(jnp.float32), axis=0)


def body(inputs, w_in, w_out, cotangent, counts):
    rows_local = inputs.shape[1]
    width = inputs.shape[2]
    units = w_in.shape[1]
    tokens_local = inputs.reshape(rows_local, width)
    replicas = lax.axis_size("rep")
    columns = lax.axis_size("col")
    replica_index = lax.axis_index("rep")
    column_index = lax.axis_index("col")
    own_count = jnp.sum(jnp.where(jnp.arange(replicas) == replica_index, counts, 0))
    token_total = (MBT * jnp.sum(counts)).astype(jnp.float32)
    positions = column_index * rows_local + jnp.arange(rows_local, dtype=jnp.int32)
    kept_mask = (positions // MBT < own_count).astype(jnp.float32)
    scaled = (
        cotangent.reshape(rows_local, width).astype(jnp.float32)
        * kept_mask[:, None]
        / token_total
    ).astype(jnp.bfloat16)
    both = jnp.concatenate([tokens_local, scaled], axis=1)
    everyone = lax.all_gather(both, ("rep", "col"), axis=0, tiled=True)
    tokens_all, scaled_all = everyone[:, :width], everyone[:, width:]
    hidden_terms = product(tokens_all, w_in, 1, 0).astype(jnp.bfloat16)
    slope_terms = product(scaled_all, w_out, 1, 1).astype(jnp.bfloat16)
    sums = summed_on_arrival(jnp.concatenate([hidden_terms, slope_terms], axis=1), "row")
    active, slope = gelu_both(sums[:, :units])
    active_share = active.astype(jnp.bfloat16)
    grad_share = (sums[:, units:] * slope).astype(jnp.bfloat16)
    shares = lax.all_gather(
        jnp.concatenate([active_share, grad_share], axis=1), "row", axis=0, tiled=True
    )
    activated, hidden_grad = shares[:, :units], shares[:, units:]
    output_terms = product(activated, w_out, 1, 0).astype(jnp.bfloat16)
    back_terms = product(hidden_grad, w_in, 1, 1).astype(jnp.bfloat16)
    terms = jnp.concatenate([output_terms, back_terms], axis=1)
    by_rep = summed_on_arrival(terms, "rep").astype(jnp.bfloat16)
    finished = summed_on_arrival(by_rep, "col")
    block_output = (tokens_local.astype(jnp.float32) + finished[:, :width]).astype(jnp.bfloat16)
    input_grad = (scaled.astype(jnp.float32) + finished[:, width:]).astype(jnp.bfloat16)
    w_in_grad = product(tokens_all, hidden_grad, 0, 0)
    w_out_grad = product(activated, scaled_all, 0, 0)
    return (
        block_output.reshape(1, rows_local, width),
        input_grad.reshape(1, rows_local, width),
        w_in_grad,
        w_out_grad,
    )


def solution(mesh):
    placed = (
        P("rep", "col", "row"),
        P("row", ("rep", "col")),
        P(("rep", "col"), "row"),
        P("rep", "col", "row"),
        P(),
    )
    return jax.shard_map(
        body,
        mesh=mesh,
        in_specs=placed,
        out_specs=(
            P("rep", "col", "row"),
            P("rep", "col", "row"),
            P("row", ("rep", "col")),
            P(("rep", "col"), "row"),
        ),
        check_vma=False,
    )
```

time: 307 us -> 294 us (0.958)
  blocking collectives: 26.6 us -> 106 us
  waiting for transfers between devices: 193 us -> 140 us
  starting transfers between devices: 37.8 us -> 6.82 us
  matrix products: 24.1 us -> 12 us
  other arithmetic: 5.26 us -> 9.35 us
  local copies, waits for them, and re-layouts: 4.15 us -> 1 us
    all_to_all x0 -> x2, blocking collectives: none -> 106 us  [summed_on_arrival(): lax.all_to_all(value.reshape(size, rows // size, width), axis, 0, 0, tile...]
    all_to_all x8 -> x1, waiting for transfers between devices: 102 us -> 6.48 us  [summed_on_arrival(): lax.all_to_all(value.reshape(size, rows // size, width), axis, 0, 0, tile...]
    all_gather x3 -> x2, waiting for transfers between devices: 89.1 us -> 134 us  [the longest x1 90.7 us: body(): everyone = lax.all_gather(both, ('rep', 'col'), axis=0, tiled=True)]
    all_to_all x8 -> x1, starting transfers between devices: 37.7 us -> 6.74 us  [summed_on_arrival(): lax.all_to_all(value.reshape(size, rows // size, width), axis, 0, 0, tile...]
    all_gather x1 -> x0, blocking collectives: 26.6 us -> none  [in_one_piece(): lax.all_gather(both, axis, axis=dim, tiled=True)]
    dot_general x6, matrix products: 24.1 us -> 12 us  [product(): lax.dot_general(left, right, (((left_dim,), (right_dim,)), ((), ())), pre...]
  transfers between devices with their start and end apart: 11 -> 3, of which waited for: 9 -> 3; matrix products, arithmetic and copies ran while one was open for 9% -> 2% of each run, Pallas kernels for 0% -> 0%
where the time goes in v1:
time: 294 us; the launch traced here: 290 us
  waiting for transfers between devices  140 us (48%)
  blocking collectives  106 us (36%)
  between operations  14.8 us (5%)
  matrix products  12 us (4%)
  other arithmetic  9.35 us (3%)
  starting transfers between devices  6.82 us (2%)
    all_to_all x2, blocking collectives, summed_on_arrival(): lax.all_to_all(value.reshape(size, rows // size, width), axis, 0, 0, tile...  106 us
    all_gather x1, waiting for transfers between devices, body(): everyone = lax.all_gather(both, ('rep', 'col'), axis=0, tiled=True)  90.7 us
    all_gather x1, waiting for transfers between devices, body(): lax.all_gather(jnp.concatenate([active_share, grad_share], axis=1), 'row'...  42.9 us
    dot_general x6, matrix products, product(): lax.dot_general(left, right, (((left_dim,), (right_dim,)), ((), ())), pre...  12 us
    all_to_all x1, starting transfers between devices, summed_on_arrival(): lax.all_to_all(value.reshape(size, rows // size, width), axis, 0, 0, tile...  6.74 us
    all_to_all x1, waiting for transfers between devices, summed_on_arrival(): lax.all_to_all(value.reshape(size, rows // size, width), axis, 0, 0, tile...  6.48 us
  transfers between devices with their start and end apart: 3, of which 3 were waited for; matrix products, arithmetic and copies ran while one was open for 2% of the time, Pallas kernels for 0%

profile of v1, /device:TPU:6, one launch (start us, length us, event | category | flops | bytes accessed | tf_op | source)
XLA Modules:
  0.0 290.4 jit_solution(16606115941424367019)
XLA Ops:
  7.2 0.0 copy-start
  7.2 0.0 all-gather.3.cloned.1.call-start
  7.2 1.3 fusion.23
  9.2 0.7 compare_convert_fusion
  9.9 0.8 fusion.20
  10.7 1.4 pad_maximum_fusion.1
  12.1 0.0 all-gather.3.cloned.1.call-update
  12.1 0.0 all-gather.5.cloned.1.call-start
  12.2 90.7 %all-gather.3.cloned.1.call-done = bf16[1024,1536]{1,0:T(8,128)(2,1)} async-done(((bf16[16,1536]{1,0:T(8,128)(2,1)}), bf16[1024,1536]{1,0:T(8,128)(2,1)}) %all-gather.3.cloned.1.call-update) | async-done | bytes 3145744 | tf_op jit(solution)/shard_map/all_gather | solution.py:54
  102.9 0.0 copy-start.3
  102.9 2.5 convolution_convert_fusion.2
  105.4 0.0 copy-done
  105.4 0.0 copy-done.3
  105.4 0.8 convolution_convert_fusion.3
  106.2 0.3 copy_bitcast_fusion.1
  106.5 25.2 %all_to_all.15 = bf16[8,128,768]{1,2,0:T(8,128)(2,1)S(1)} all-to-all(bf16[8,128,768]{1,2,0:T(8,128)(2,1)S(1)} %copy_bitcast_fusion.1), channel_id=1, replica_groups=mesh['rep'=8,'row'=8,'col'=8] {'row'}, dimensions={0} | all-to-all | bytes 3145728 | tf_op jit(solution)/shard_map/all_to_all | solution.py:31
  131.7 0.2 convert_reduce_fusion
  131.9 0.1 multiply_convert_fusion
  132.1 0.7 pad_maximum_fusion
  132.8 0.0 copy-start.6
  132.8 0.0 all-gather.5.cloned.1.call-update
  132.8 42.9 %all-gather.5.cloned.1.call-done = bf16[1024,768]{0,1:T(8,128)(2,1)} async-done(((bf16[128,768]{0,1:T(8,128)(2,1)}), bf16[1024,768]{0,1:T(8,128)(2,1)}) %all-gather.5.cloned.1.call-update) | async-done | bytes 1572880 | tf_op jit(solution)/shard_map/all_gather | solution.py:62
  175.7 0.0 copy-start.5
  175.7 2.2 convolution_convert_fusion
  177.9 0.0 copy-done.6
  178.0 0.0 copy-done.5
  178.0 1.0 convolution_convert_fusion.1
  179.0 0.6 copy_bitcast_fusion
  179.6 81.2 %all_to_all.16 = bf16[8,128,1536]{1,2,0:T(8,128)(2,1)} all-to-all(bf16[8,128,1536]{1,2,0:T(8,128)(2,1)S(1)} %copy_bitcast_fusion), channel_id=1, replica_groups=mesh['rep'=8,'row'=8,'col'=8] {'rep'}, dimensions={0} | all-to-all | bytes 6291456 | tf_op jit(solution)/shard_map/all_to_all | solution.py:31
  260.8 2.5 reduce_sum.51
  263.3 0.9 copy.17
  264.2 6.7 %all-to-all-start.2 = ((bf16[8,16,1536]{2,1,0:T(8,128)(2,1)}), bf16[8,16,1536]{2,1,0:T(8,128)(2,1)S(1)}, u32[]{:S(2)}, u32[]{:S(2)}) async-start(bf16[8,16,1536]{2,1,0:T(8,128)(2,1)} %bitcast.2), calls=%async_computation.2 | async-start | bytes 786432 | tf_op jit(solution)/shard_map/all_to_all | solution.py:31
  271.0 0.0 copy-start.4
  271.0 3.4 %fusion = f32[384,768]{1,0:T(8,128)} fusion(bf16[1024,1536]{1,0:T(8,128)(2,1)} %all-gather.3.cloned.1.call-done, bf16[1024,768]{0,1:T(8,128)(2,1)S(1)} %copy-done.5), kind=kOutput, calls=%fused_computation.9 | convolution fusion | flops 603979776 | bytes 3538944 | tf_op jit(solution)/shard_map/dot_general | solution.py:23
  274.3 0.0 copy-done.4
  274.3 0.0 copy-start.1
  274.3 0.0 copy-start.2
  274.3 2.0 fusion.3
  276.4 6.5 %all-to-all-done.2 = bf16[8,16,1536]{2,1,0:T(8,128)(2,1)S(1)} async-done(((bf16[8,16,1536]{2,1,0:T(8,128)(2,1)}), bf16[8,16,1536]{2,1,0:T(8,128)(2,1)S(1)}, u32[]{:S(2)}, u32[]{:S(2)}) %all-to-all-start.2) | async-done | bytes 393248 | tf_op jit(solution)/shard_map/all_to_all | solution.py:31
  282.8 0.1 convert_reduce_fusion.1
  282.9 0.0 copy-done.1
  282.9 0.0 copy-done.2
  282.9 0.7 fusion.22
Async XLA Ops:
  7.2 98.2 %copy-start = (bf16[768,384]{1,0:T(8,128)(2,1)S(1)}, bf16[768,384]{1,0:T(8,128)(2,1)}, u32[]{:S(2)}) copy-start(bf16[768,384]{1,0:T(8,128)(2,1)} %param.6) | copy-start | bytes 1769476
  7.2 95.7 %all-gather.3.cloned.1.call-start = ((), (), s32[]{:S(2)}) async-start(), calls=%async_computation.3 | async-start | bytes 3194880 | tf_op jit(solution)/shard_map/all_gather | solution.py:54
  12.1 163.6 %all-gather.5.cloned.1.call-start = ((), (), s32[]{:S(2)}) async-start(), calls=%async_computation.4 | async-start | bytes 1769472 | tf_op jit(solution)/shard_map/all_gather | solution.py:62
  102.9 2.5 copy-start.3
  132.8 45.2 %copy-start.6 = (bf16[384,768]{1,0:T(8,128)(2,1)S(1)}, bf16[384,768]{1,0:T(8,128)(2,1)}, u32[]{:S(2)}) copy-start(bf16[384,768]{1,0:T(8,128)(2,1)} %param.7) | copy-start | bytes 1769476
  175.7 2.2 copy-start.5
  264.2 18.6 %all-to-all-start.2 = ((bf16[8,16,1536]{2,1,0:T(8,128)(2,1)}), bf16[8,16,1536]{2,1,0:T(8,128)(2,1)S(1)}, u32[]{:S(2)}, u32[]{:S(2)}) async-start(bf16[8,16,1536]{2,1,0:T(8,128)(2,1)} %bitcast.2), calls=%async_computation.2 | async-start | bytes 786432 | tf_op jit(solution)/shard_map/all_to_all | solution.py:31
  271.0 3.4 %copy-start.4 = (bf16[1024,1536]{1,0:T(8,128)(2,1)S(1)}, bf16[1024,1536]{1,0:T(8,128)(2,1)}, u32[]{:S(2)}) copy-start(bf16[1024,1536]{1,0:T(8,128)(2,1)} %all-gather.3.cloned.1.call-done) | copy-start | bytes 9437188
  274.3 8.6 %copy-start.1 = (bf16[1,16,768]{2,1,0:T(8,128)(2,1)S(1)}, bf16[1,16,768]{2,1,0:T(8,128)(2,1)}, u32[]{:S(2)}) copy-start(bf16[1,16,768]{2,1,0:T(8,128)(2,1)} %param.8) | copy-start | bytes 73732
  274.3 8.6 %copy-start.2 = (bf16[1,16,768]{2,1,0:T(8,128)(2,1)S(1)}, bf16[1,16,768]{2,1,0:T(8,128)(2,1)}, u32[]{:S(2)}) copy-start(bf16[1,16,768]{2,1,0:T(8,128)(2,1)} %param.5) | copy-start | bytes 73732
Sparse Core Ops, SparseCore 0:
  12.2 90.5 all-gather.2
  132.9 42.7 all-gather.4

commit v2 on v1

v2 whole, which is shorter than its diff:
```python
import jax
import jax.numpy as jnp
from jax import lax
from jax.sharding import PartitionSpec as P

MBT = 32
CORES = 2

root_coef = 0.7978845608028654
cubic_coef = 0.044715


def gelu_both(values):
    inner = root_coef * (values + cubic_coef * values * values * values)
    tangent = jnp.tanh(inner)
    slope = 0.5 * (1.0 + tangent) + 0.5 * values * (1.0 - tangent * tangent) * root_coef * (
        1.0 + 3.0 * cubic_coef * values * values
    )
    return 0.5 * values * (1.0 + tangent), slope


def product(left, right, left_dim, right_dim):
    return lax.dot_general(
        left, right, (((left_dim,), (right_dim,)), ((), ())), preferred_element_type=jnp.float32
    )


def cut(value, pieces):
    rows, width = value.shape
    return value.reshape(pieces, rows // pieces, width)


def swapped(value, axis, groups=None):
    return lax.all_to_all(value, axis, 0, 0, axis_index_groups=groups, tiled=True)


def added_up(pieces):
    total = pieces[0].astype(jnp.float32)
    for at in range(1, pieces.shape[0]):
        total = total + pieces[at].astype(jnp.float32)
    return total


def spread(value, axis, size, groups=None):
    return swapped(jnp.broadcast_to(value[None], (size, *value.shape)), axis, groups)


def body(inputs, w_in, w_out, cotangent, counts):
    rows_local = inputs.shape[1]
    width = inputs.shape[2]
    units = w_in.shape[1]
    replicas = lax.axis_size("rep")
    columns = lax.axis_size("col")
    row_count = lax.axis_size("row")
    chips = replicas // CORES
    same_core = [[chip * CORES + core for chip in range(chips)] for core in range(CORES)]
    to_mate = [(r, r // CORES * CORES + (r + 1) % CORES) for r in range(replicas)]
    mate = lambda value: lax.ppermute(value, "rep", to_mate)

    tokens_local = inputs.reshape(rows_local, width)
    replica_index = lax.axis_index("rep")
    column_index = lax.axis_index("col")
    own_count = jnp.sum(jnp.where(jnp.arange(replicas) == replica_index, counts, 0))
    token_total = (MBT * jnp.sum(counts)).astype(jnp.float32)
    positions = column_index * rows_local + jnp.arange(rows_local, dtype=jnp.int32)
    kept_mask = (positions // MBT < own_count).astype(jnp.float32)
    scaled = (
        cotangent.reshape(rows_local, width).astype(jnp.float32)
        * kept_mask[:, None]
        / token_total
    ).astype(jnp.bfloat16)

    w_in_mate, w_out_mate = mate(w_in), mate(w_out)

    line = spread(jnp.concatenate([tokens_local, scaled], axis=0), "rep", chips, same_core)
    tokens_line = line[:, :rows_local].reshape(chips * rows_local, width)
    scaled_line = line[:, rows_local:].reshape(chips * rows_local, width)
    line_rows = chips * rows_local
    rows_all = columns * line_rows

    padded = jnp.concatenate([scaled_line, scaled_line[: line_rows // 2]], axis=0)
    scaled_all = lax.all_gather(padded, "col", axis=0)[:, :line_rows].reshape(rows_all, width)

    tokens_all = spread(tokens_line, "col", columns).reshape(rows_all, width)
    hidden_terms = jnp.concatenate(
        [product(tokens_all, w, 1, 0).astype(jnp.bfloat16) for w in (w_in, w_in_mate)], axis=1
    )
    hidden = added_up(swapped(cut(hidden_terms, row_count), "row"))
    active, slope = gelu_both(hidden)
    active, scaled_all = lax.optimization_barrier((active, scaled_all))
    activated = spread(active.astype(jnp.bfloat16), "row", row_count).reshape(rows_all, -1)

    slope_terms = jnp.concatenate(
        [product(scaled_all, w, 1, 1).astype(jnp.bfloat16) for w in (w_out, w_out_mate)], axis=1
    )
    slope_terms, activated = lax.optimization_barrier((slope_terms, activated))
    slope_sum = added_up(swapped(cut(slope_terms, row_count), "row"))
    grad_share = (slope_sum * slope).astype(jnp.bfloat16)

    output_terms = (
        product(activated[:, :units], w_out, 1, 0) + product(activated[:, units:], w_out_mate, 1, 0)
    ).astype(jnp.bfloat16)
    grad_share, output_terms = lax.optimization_barrier((grad_share, output_terms))
    hidden_grad = spread(grad_share, "row", row_count).reshape(rows_all, -1)
    output_line = lax.psum_scatter(output_terms, "col", scatter_dimension=0, tiled=True)

    back_terms = (
        product(hidden_grad[:, :units], w_in, 1, 1) + product(hidden_grad[:, units:], w_in_mate, 1, 1)
    ).astype(jnp.bfloat16)
    back_line = added_up(swapped(cut(back_terms, columns), "col")).astype(jnp.bfloat16)

    ends = jnp.concatenate([cut(output_line, chips), cut(back_line, chips)], axis=1)
    finished = added_up(swapped(ends, "rep", same_core))
    block_output = (tokens_local.astype(jnp.float32) + finished[:rows_local]).astype(jnp.bfloat16)
    input_grad = (scaled.astype(jnp.float32) + finished[rows_local:]).astype(jnp.bfloat16)

    tokens_mate, scaled_mate = mate(tokens_all), mate(scaled_all)
    active_mate, grad_mate = mate(activated[:, units:]), mate(hidden_grad[:, units:])
    w_in_grad = product(tokens_all, hidden_grad[:, :units], 0, 0) + product(
        tokens_mate, grad_mate, 0, 0
    )
    w_out_grad = product(activated[:, :units], scaled_all, 0, 0) + product(
        active_mate, scaled_mate, 0, 0
    )
    return (
        block_output.reshape(1, rows_local, width),
        input_grad.reshape(1, rows_local, width),
        w_in_grad,
        w_out_grad,
    )


def solution(mesh):
    placed = (
        P("rep", "col", "row"),
        P("row", ("rep", "col")),
        P(("rep", "col"), "row"),
        P("rep", "col", "row"),
        P(),
    )
    return jax.shard_map(
        body,
        mesh=mesh,
        in_specs=placed,
        out_specs=(
            P("rep", "col", "row"),
            P("rep", "col", "row"),
            P("row", ("rep", "col")),
            P(("rep", "col"), "row"),
        ),
        check_vma=False,
    )
```

time: 294 us -> 208 us (0.71)
  blocking collectives: 106 us -> 20.5 us
  waiting for transfers between devices: 140 us -> 85 us
  starting transfers between devices: 6.82 us -> 52.7 us
  local copies, waits for them, and re-layouts: 1 us -> 8.51 us
  matrix products: 12 us -> 17.3 us
    all_gather x2 -> x1, waiting for transfers between devices: 134 us -> 11 us  [body(): lax.all_gather(padded, 'col', axis=0)[:, :line_rows]]
    all_to_all x2 -> x1, blocking collectives: 106 us -> 20.5 us  [swapped(): lax.all_to_all(value, axis, 0, 0, axis_index_groups=groups, tiled=True)]
    all_to_all x1 -> x7, waiting for transfers between devices: 6.48 us -> 49.8 us  [swapped(): lax.all_to_all(value, axis, 0, 0, axis_index_groups=groups, tiled=True)]
    all_to_all x1 -> x7, starting transfers between devices: 6.74 us -> 40.7 us  [swapped(): lax.all_to_all(value, axis, 0, 0, axis_index_groups=groups, tiled=True)]
    reduce_scatter x0 -> x1, waiting for transfers between devices: none -> 22 us  [body(): lax.psum_scatter(output_terms, 'col', scatter_dimension=0, tiled=True)]
    ppermute x0 -> x6, starting transfers between devices: none -> 12 us  [body(): mate = lambda value: lax.ppermute(value, 'rep', to_mate)]
    dot_general x6 -> x12, matrix products: 12 us -> 17.3 us  [product(): lax.dot_general(left, right, (((left_dim,), (right_dim,)), ((), ())), pre...]
  transfers between devices with their start and end apart: 3 -> 15, of which waited for: 3 -> 9; matrix products, arithmetic and copies ran while one was open for 2% -> 11% of each run, Pallas kernels for 0% -> 0%
where the time goes in v2:
time: 208 us; the launch traced here: 206 us
  waiting for transfers between devices  85 us (41%)
  starting transfers between devices  52.7 us (25%)
  blocking collectives  20.5 us (10%)
  matrix products  17.3 us (8%)
  between operations  15 us (7%)
  local copies, waits for them, and re-layouts  8.51 us (4%)
  other arithmetic  7.1 us (3%)
    all_to_all x7, waiting for transfers between devices, swapped(): lax.all_to_all(value, axis, 0, 0, axis_index_groups=groups, tiled=True)  49.8 us
    all_to_all x7, starting transfers between devices, swapped(): lax.all_to_all(value, axis, 0, 0, axis_index_groups=groups, tiled=True)  40.7 us
    reduce_scatter x1, waiting for transfers between devices, body(): lax.psum_scatter(output_terms, 'col', scatter_dimension=0, tiled=True)  22 us
    all_to_all x1, blocking collectives, swapped(): lax.all_to_all(value, axis, 0, 0, axis_index_groups=groups, tiled=True)  20.5 us
    dot_general x12, matrix products, product(): lax.dot_general(left, right, (((left_dim,), (right_dim,)), ((), ())), pre...  17.3 us
    ppermute x6, starting transfers between devices, body(): mate = lambda value: lax.ppermute(value, 'rep', to_mate)  12 us
    all_gather x1, waiting for transfers between devices, body(): lax.all_gather(padded, 'col', axis=0)[:, :line_rows]  11 us
  transfers between devices with their start and end apart: 15, of which 9 were waited for; matrix products, arithmetic and copies ran while one was open for 11% of the time, Pallas kernels for 0%

profile of v2, /device:TPU:6, one launch (start us, length us, event | category | flops | bytes accessed | tf_op | source)
XLA Modules:
  0.0 206.2 jit_solution(13910700809125076045)
XLA Ops:
  7.2 1.3 fusion.24
  9.1 0.7 compare_convert_fusion
  9.8 0.8 fusion.21
  10.6 0.7 pad_maximum_fusion.4
  11.4 20.5 %all_to_all.40 = bf16[4,32,768]{2,1,0:T(8,128)(2,1)S(1)} all-to-all(bf16[4,32,768]{2,1,0:T(8,128)(2,1)S(1)} %broadcast_in_dim.15), channel_id=1, replica_groups={{0,128,256,384},{64,192,320,448},{1,129,257,385},{65,193,321,449},{2,13..., dimensions={0} | all-to-all | bytes 393216 | tf_op jit(solution)/shard_map/all_to_all | solution.py:34
  31.9 0.9 broadcast_in_dim.17
  32.9 7.1 %all-to-all-start.1 = ((bf16[8,64,768]{2,1,0:T(8,128)(2,1)}), bf16[8,64,768]{2,1,0:T(8,128)(2,1)}, u32[]{:S(2)}, u32[]{:S(2)}) async-start(bf16[8,64,768]{2,1,0:T(8,128)(2,1)} %broadcast_in_dim.17), calls=%async_computation.1 | async-start | bytes 1572864 | tf_op jit(solution)/shard_map/all_to_all | solution.py:34
  40.0 1.9 collective-permute-start
  42.0 0.7 pad_maximum_fusion.3
  42.7 18.3 %all-to-all-done.1 = bf16[8,64,768]{2,1,0:T(8,128)(2,1)} async-done(((bf16[8,64,768]{2,1,0:T(8,128)(2,1)}), bf16[8,64,768]{2,1,0:T(8,128)(2,1)}, u32[]{:S(2)}, u32[]{:S(2)}) %all-to-all-start.1) | async-done | bytes 786464 | tf_op jit(solution)/shard_map/all_to_all | solution.py:34
  60.9 1.7 convolution_convert_fusion.3
  62.6 1.9 convolution_convert_fusion.2
  64.5 1.2 copy.12
  65.7 6.1 %all-to-all-start.2 = ((bf16[8,64,768]{2,1,0:T(8,128)(2,1)}), bf16[8,64,768]{2,1,0:T(8,128)(2,1)S(1)}, u32[]{:S(2)}, u32[]{:S(2)}) async-start(bf16[8,64,768]{2,1,0:T(8,128)(2,1)} %bitcast.4), calls=%async_computation.2 | async-start | bytes 1572864 | tf_op jit(solution)/shard_map/all_to_all | solution.py:34
  71.7 11.0 %all-gather.3.cloned.1.call-done = bf16[768,768]{1,0:T(8,128)(2,1)} async-done(((bf16[96,768]{1,0:T(8,128)(2,1)}), bf16[768,768]{1,0:T(8,128)(2,1)}) %all-gather.3.cloned.1.call-update) | async-done | bytes 1179664 | tf_op jit(solution)/shard_map/all_gather | solution.py:82
  82.8 1.2 slice.180
  84.2 0.9 broadcast_in_dim.34
  85.1 5.9 %all-to-all-start.3 = ((bf16[8,64,768]{2,1,0:T(8,128)(2,1)}), bf16[8,64,768]{2,1,0:T(8,128)(2,1)S(1)}, u32[]{:S(2)}, u32[]{:S(2)}) async-start(bf16[8,64,768]{2,1,0:T(8,128)(2,1)} %broadcast_in_dim.34), calls=%async_computation.3 | async-start | bytes 1572864 | tf_op jit(solution)/shard_map/all_to_all | solution.py:34
  91.0 1.9 collective-permute-start.1
  93.5 1.5 collective-permute-done.1
  94.9 0.8 copy-done.4
  96.3 2.3 %all-to-all-done.3 = bf16[8,64,768]{2,1,0:T(8,128)(2,1)S(1)} async-done(((bf16[8,64,768]{2,1,0:T(8,128)(2,1)}), bf16[8,64,768]{2,1,0:T(8,128)(2,1)S(1)}, u32[]{:S(2)}, u32[]{:S(2)}) %all-to-all-start.3) | async-done | bytes 786464 | tf_op jit(solution)/shard_map/all_to_all | solution.py:34
  98.6 1.2 copy.13
  99.8 5.4 %all-to-all-start.4 = ((bf16[8,64,768]{2,1,0:T(8,128)(2,1)}), bf16[8,64,768]{2,1,0:T(8,128)(2,1)S(1)}, u32[]{:S(2)}, u32[]{:S(2)}) async-start(bf16[8,64,768]{2,1,0:T(8,128)(2,1)} %bitcast.11), calls=%async_computation.4 | async-start | bytes 1572864 | tf_op jit(solution)/shard_map/all_to_all | solution.py:34
  105.1 0.6 fusion.6
  106.2 1.5 add_convert_fusion.1
  107.7 6.3 %all-to-all-done.4 = bf16[8,64,768]{2,1,0:T(8,128)(2,1)S(1)} async-done(((bf16[8,64,768]{2,1,0:T(8,128)(2,1)}), bf16[8,64,768]{2,1,0:T(8,128)(2,1)S(1)}, u32[]{:S(2)}, u32[]{:S(2)}) %all-to-all-start.4) | async-done | bytes 786464 | tf_op jit(solution)/shard_map/all_to_all | solution.py:34
  114.2 0.9 broadcast_in_dim.35
  115.1 5.3 %all-to-all-start.5 = ((bf16[8,64,768]{2,1,0:T(8,128)(2,1)}), bf16[8,64,768]{2,1,0:T(8,128)(2,1)S(1)}, u32[]{:S(2)}, u32[]{:S(2)}) async-start(bf16[8,64,768]{2,1,0:T(8,128)(2,1)} %broadcast_in_dim.35), calls=%async_computation.6 | async-start | bytes 1572864 | tf_op jit(solution)/shard_map/all_to_all | solution.py:34
  120.4 1.9 collective-permute-start.5
  122.4 7.6 %all-to-all-done.5 = bf16[8,64,768]{2,1,0:T(8,128)(2,1)S(1)} async-done(((bf16[8,64,768]{2,1,0:T(8,128)(2,1)}), bf16[8,64,768]{2,1,0:T(8,128)(2,1)S(1)}, u32[]{:S(2)}, u32[]{:S(2)}) %all-to-all-start.5) | async-done | bytes 786464 | tf_op jit(solution)/shard_map/all_to_all | solution.py:34
  130.0 0.6 fusion.2
  130.5 2.5 %add_convert_fusion = bf16[512,768]{1,0:T(8,128)(2,1)} fusion(f32[512,768]{1,0:T(8,128)S(1)} %fusion.2, bf16[768,384]{1,0:T(8,128)(2,1)} %copy-done.3, bf16[512,768]{1,0:T(8,128)(2,1)S(1)} %bitcast.77), kind=kOutput, calls=%fused_computation | convolution fusion | flops 302776320 | bytes 3342336 | tf_op jit(solution)/shard_map/dot_general | solution.py:23
  133.1 3.7 %all-to-all-start.6 = ((bf16[8,64,768]{2,1,0:T(8,128)(2,1)}), bf16[8,64,768]{2,1,0:T(8,128)(2,1)S(1)}, u32[]{:S(2)}, u32[]{:S(2)}) async-start(bf16[8,64,768]{2,1,0:T(8,128)(2,1)} %bitcast.84), calls=%async_computation.7 | async-start | bytes 1572864 | tf_op jit(solution)/shard_map/all_to_all | solution.py:34
  136.8 0.7 reduce-scatter.2.cloned.1.call-update
  137.6 1.9 collective-permute-start.4
  139.5 2.4 %collective-permute-start.2 = (bf16[512,768]{1,0:T(8,128)(2,1)}, bf16[512,768]{1,0:T(8,128)(2,1)}, u32[]{:S(2)}, u32[]{:S(2)}) collective-permute-start(bf16[512,768]{1,0:T(8,128)(2,1)} %bitcast.3), channel_id=1, source_target_pairs={{0,64},{64,0},{128,192},{192,128},{256,320},{320,256},{384,448},{4... | collective-permute-start | bytes 2359304 | tf_op jit(solution)/shard_map/ppermute | solution.py:58
  142.5 2.6 %convolution_add_fusion = f32[384,768]{1,0:T(8,128)} fusion(f32[384,768]{1,0:T(8,128)S(1)} %fusion.4, bf16[512,384]{1,0:T(8,128)(2,1)S(1)} %collective-permute-done.4, bf16[512,768]{1,0:T(8,128)(2,1)} %collective-permute-done.5), kind=kOutput, calls=%fused_computation.2 | convolution fusion | flops 302284800 | bytes 3538944 | tf_op jit(solution)/shard_map/dot_general | solution.py:23
  145.1 0.8 slice.190
  145.9 1.9 collective-permute-start.3
  147.8 1.7 fusion
  149.6 9.5 %all-to-all-done.6 = bf16[8,64,768]{2,1,0:T(8,128)(2,1)S(1)} async-done(((bf16[8,64,768]{2,1,0:T(8,128)(2,1)}), bf16[8,64,768]{2,1,0:T(8,128)(2,1)S(1)}, u32[]{:S(2)}, u32[]{:S(2)}) %all-to-all-start.6) | async-done | bytes 786464 | tf_op jit(solution)/shard_map/all_to_all | solution.py:34
  159.1 22.0 %reduce-scatter.2.cloned.1.call-done = bf16[64,768]{1,0:T(8,128)(2,1)} async-done(((bf16[512,768]{1,0:T(8,128)(2,1)}), bf16[64,768]{1,0:T(8,128)(2,1)}) %reduce-scatter.2.cloned.1.call-update) | async-done | bytes 98320 | tf_op jit(solution)/shard_map/reduce_scatter | solution.py:105
  181.1 1.6 pad_maximum_fusion.2
  182.7 7.2 %all-to-all-start.7 = ((bf16[4,32,768]{2,1,0:T(8,128)(2,1)}), bf16[4,32,768]{2,1,0:T(8,128)(2,1)S(1)}, u32[]{:S(2)}, u32[]{:S(2)}) async-start(bf16[4,32,768]{2,1,0:T(8,128)(2,1)} %pad_maximum_fusion.2), calls=%async_computation.8 | async-start | bytes 393216 | tf_op jit(solution)/shard_map/all_to_all | solution.py:34
  189.9 2.8 %convolution_add_fusion.1 = f32[768,384]{1,0:T(8,128)} fusion(f32[768,384]{1,0:T(8,128)S(1)} %fusion, bf16[512,768]{1,0:T(8,128)(2,1)} %collective-permute-done.2, bf16[512,384]{1,0:T(8,128)(2,1)S(1)} %collective-permute-done.3), kind=kOutput, calls=%fused_computation.3 | convolution fusion | flops 302284800 | bytes 3538944 | tf_op jit(solution)/shard_map/dot_general | solution.py:23
  192.7 6.0 %all-to-all-done.7 = bf16[4,32,768]{2,1,0:T(8,128)(2,1)S(1)} async-done(((bf16[4,32,768]{2,1,0:T(8,128)(2,1)}), bf16[4,32,768]{2,1,0:T(8,128)(2,1)S(1)}, u32[]{:S(2)}, u32[]{:S(2)}) %all-to-all-start.7) | async-done | bytes 196640 | tf_op jit(solution)/shard_map/all_to_all | solution.py:34
  198.7 0.7 fusion.23
  (37 shorter events, 2.8 us)
Async XLA Ops:
  11.4 28.6 %copy-start.1 = (bf16[768,384]{1,0:T(8,128)(2,1)S(1)}, bf16[768,384]{1,0:T(8,128)(2,1)}, u32[]{:S(2)}) copy-start(bf16[768,384]{1,0:T(8,128)(2,1)} %param.6) | copy-start | bytes 1769476
  32.9 28.0 %all-to-all-start.1 = ((bf16[8,64,768]{2,1,0:T(8,128)(2,1)}), bf16[8,64,768]{2,1,0:T(8,128)(2,1)}, u32[]{:S(2)}, u32[]{:S(2)}) async-start(bf16[8,64,768]{2,1,0:T(8,128)(2,1)} %broadcast_in_dim.17), calls=%async_computation.1 | async-start | bytes 1572864 | tf_op jit(solution)/shard_map/all_to_all | solution.py:34
  40.0 42.8 %all-gather.3.cloned.1.call-start = ((), (), s32[]{:S(2)}) async-start(), calls=%async_computation.10 | async-start | bytes 1327104 | tf_op jit(solution)/shard_map/all_gather | solution.py:82
  40.0 22.6 %collective-permute-start = (bf16[768,384]{1,0:T(8,128)(2,1)S(1)}, bf16[768,384]{1,0:T(8,128)(2,1)S(1)}, u32[]{:S(2)}, u32[]{:S(2)}) collective-permute-start(bf16[768,384]{1,0:T(8,128)(2,1)S(1)} %copy-done.1), channel_id=1, source_target_pairs={{0,64},{64,0},{128,192},{192,128},{256,320},{320,256},{384,448},{4... | collective-permute-start | bytes 1769480 | tf_op jit(solution)/shard_map/ppermute | solution.py:58
  62.6 3.1 %copy-start.3 = (bf16[768,384]{1,0:T(8,128)(2,1)}, bf16[768,384]{1,0:T(8,128)(2,1)S(1)}, u32[]{:S(2)}) copy-start(bf16[768,384]{1,0:T(8,128)(2,1)S(1)} %collective-permute-done) | copy-start | bytes 1769476
  65.7 18.3 %all-to-all-start.2 = ((bf16[8,64,768]{2,1,0:T(8,128)(2,1)}), bf16[8,64,768]{2,1,0:T(8,128)(2,1)S(1)}, u32[]{:S(2)}, u32[]{:S(2)}) async-start(bf16[8,64,768]{2,1,0:T(8,128)(2,1)} %bitcast.4), calls=%async_computation.2 | async-start | bytes 1572864 | tf_op jit(solution)/shard_map/all_to_all | solution.py:34
  84.0 7.1 %copy-start = (bf16[384,768]{1,0:T(8,128)(2,1)S(1)}, bf16[384,768]{1,0:T(8,128)(2,1)}, u32[]{:S(2)}) copy-start(bf16[384,768]{1,0:T(8,128)(2,1)} %param.7) | copy-start | bytes 1769476
  85.1 13.5 %all-to-all-start.3 = ((bf16[8,64,768]{2,1,0:T(8,128)(2,1)}), bf16[8,64,768]{2,1,0:T(8,128)(2,1)S(1)}, u32[]{:S(2)}, u32[]{:S(2)}) async-start(bf16[8,64,768]{2,1,0:T(8,128)(2,1)} %broadcast_in_dim.34), calls=%async_computation.3 | async-start | bytes 1572864 | tf_op jit(solution)/shard_map/all_to_all | solution.py:34
  91.0 3.9 %collective-permute-start.1 = (bf16[384,768]{1,0:T(8,128)(2,1)S(1)}, bf16[384,768]{1,0:T(8,128)(2,1)S(1)}, u32[]{:S(2)}, u32[]{:S(2)}) collective-permute-start(bf16[384,768]{1,0:T(8,128)(2,1)S(1)} %copy-done), channel_id=1, source_target_pairs={{0,64},{64,0},{128,192},{192,128},{256,320},{320,256},{384,448},{4... | collective-permute-start | bytes 1769480 | tf_op jit(solution)/shard_map/ppermute | solution.py:58
  94.9 0.8 copy-start.4
  99.8 14.2 %all-to-all-start.4 = ((bf16[8,64,768]{2,1,0:T(8,128)(2,1)}), bf16[8,64,768]{2,1,0:T(8,128)(2,1)S(1)}, u32[]{:S(2)}, u32[]{:S(2)}) async-start(bf16[8,64,768]{2,1,0:T(8,128)(2,1)} %bitcast.11), calls=%async_computation.4 | async-start | bytes 1572864 | tf_op jit(solution)/shard_map/all_to_all | solution.py:34
  105.1 1.1 copy-start.5
  113.9 16.0 %copy-start.2 = (bf16[768,384]{1,0:T(8,128)(2,1)S(1)}, bf16[768,384]{1,0:T(8,128)(2,1)}, u32[]{:S(2)}) copy-start(bf16[768,384]{1,0:T(8,128)(2,1)} %param.6) | copy-start | bytes 1769476
  115.1 14.8 %all-to-all-start.5 = ((bf16[8,64,768]{2,1,0:T(8,128)(2,1)}), bf16[8,64,768]{2,1,0:T(8,128)(2,1)S(1)}, u32[]{:S(2)}, u32[]{:S(2)}) async-start(bf16[8,64,768]{2,1,0:T(8,128)(2,1)} %broadcast_in_dim.35), calls=%async_computation.6 | async-start | bytes 1572864 | tf_op jit(solution)/shard_map/all_to_all | solution.py:34
  120.4 22.0 %collective-permute-start.5 = (bf16[512,768]{1,0:T(8,128)(2,1)S(1)}, bf16[512,768]{1,0:T(8,128)(2,1)}, u32[]{:S(2)}, u32[]{:S(2)}) collective-permute-start(bf16[512,768]{1,0:T(8,128)(2,1)S(1)} %bitcast.82), channel_id=1, source_target_pairs={{0,64},{64,0},{128,192},{192,128},{256,320},{320,256},{384,448},{4... | collective-permute-start | bytes 2359304 | tf_op jit(solution)/shard_map/ppermute | solution.py:58
  133.1 26.0 %all-to-all-start.6 = ((bf16[8,64,768]{2,1,0:T(8,128)(2,1)}), bf16[8,64,768]{2,1,0:T(8,128)(2,1)S(1)}, u32[]{:S(2)}, u32[]{:S(2)}) async-start(bf16[8,64,768]{2,1,0:T(8,128)(2,1)} %bitcast.84), calls=%async_computation.7 | async-start | bytes 1572864 | tf_op jit(solution)/shard_map/all_to_all | solution.py:34
  136.8 44.3 %reduce-scatter.2.cloned.1.call-start = ((), (), s32[]{:S(2)}) async-start(), calls=%async_computation.9 | async-start | bytes 884736 | tf_op jit(solution)/shard_map/reduce_scatter | solution.py:105
  137.6 4.9 %collective-permute-start.4 = (bf16[512,384]{1,0:T(8,128)(2,1)S(1)}, bf16[512,384]{1,0:T(8,128)(2,1)S(1)}, u32[]{:S(2)}, u32[]{:S(2)}) collective-permute-start(bf16[512,384]{1,0:T(8,128)(2,1)S(1)} %slice.150), channel_id=1, source_target_pairs={{0,64},{64,0},{128,192},{192,128},{256,320},{320,256},{384,448},{4... | collective-permute-start | bytes 1179656 | tf_op jit(solution)/shard_map/ppermute | solution.py:58
  139.5 50.4 %collective-permute-start.2 = (bf16[512,768]{1,0:T(8,128)(2,1)}, bf16[512,768]{1,0:T(8,128)(2,1)}, u32[]{:S(2)}, u32[]{:S(2)}) collective-permute-start(bf16[512,768]{1,0:T(8,128)(2,1)} %bitcast.3), channel_id=1, source_target_pairs={{0,64},{64,0},{128,192},{192,128},{256,320},{320,256},{384,448},{4... | collective-permute-start | bytes 2359304 | tf_op jit(solution)/shard_map/ppermute | solution.py:58
  145.9 44.0 %collective-permute-start.3 = (bf16[512,384]{1,0:T(8,128)(2,1)}, bf16[512,384]{1,0:T(8,128)(2,1)S(1)}, u32[]{:S(2)}, u32[]{:S(2)}) collective-permute-start(bf16[512,384]{1,0:T(8,128)(2,1)} %slice.190), channel_id=1, source_target_pairs={{0,64},{64,0},{128,192},{192,128},{256,320},{320,256},{384,448},{4... | collective-permute-start | bytes 1179656 | tf_op jit(solution)/shard_map/ppermute | solution.py:58
  182.7 15.9 %all-to-all-start.7 = ((bf16[4,32,768]{2,1,0:T(8,128)(2,1)}), bf16[4,32,768]{2,1,0:T(8,128)(2,1)S(1)}, u32[]{:S(2)}, u32[]{:S(2)}) async-start(bf16[4,32,768]{2,1,0:T(8,128)(2,1)} %pad_maximum_fusion.2), calls=%async_computation.8 | async-start | bytes 393216 | tf_op jit(solution)/shard_map/all_to_all | solution.py:34
  189.9 8.8 %copy-start.6 = (bf16[1,16,768]{2,1,0:T(8,128)(2,1)S(1)}, bf16[1,16,768]{2,1,0:T(8,128)(2,1)}, u32[]{:S(2)}) copy-start(bf16[1,16,768]{2,1,0:T(8,128)(2,1)} %param.8) | copy-start | bytes 73732
  189.9 8.8 %copy-start.7 = (bf16[1,16,768]{2,1,0:T(8,128)(2,1)S(1)}, bf16[1,16,768]{2,1,0:T(8,128)(2,1)}, u32[]{:S(2)}) copy-start(bf16[1,16,768]{2,1,0:T(8,128)(2,1)} %param.5) | copy-start | bytes 73732
Sparse Core Ops, SparseCore 0:
  43.4 39.2 all-gather.2
  140.5 40.6 reduce-scatter.1

commit v3 on v2

--- a/solution.py
+++ b/solution.py
@@ -109,19 +109,19 @@
     ).astype(jnp.bfloat16)
     back_line = added_up(swapped(cut(back_terms, columns), "col")).astype(jnp.bfloat16)
 
+    hidden_grad, scaled_all, output_line = lax.optimization_barrier((hidden_grad, scaled_all, output_line))
+    w_out_grad = product(activated[:, :units], scaled_all, 0, 0) + product(
+        mate(activated[:, units:]), mate(scaled_all), 0, 0
+    )
+
+    w_in_grad = product(tokens_all, hidden_grad[:, :units], 0, 0) + product(
+        mate(tokens_all), mate(hidden_grad[:, units:]), 0, 0
+    )
     ends = jnp.concatenate([cut(output_line, chips), cut(back_line, chips)], axis=1)
     finished = added_up(swapped(ends, "rep", same_core))
     block_output = (tokens_local.astype(jnp.float32) + finished[:rows_local]).astype(jnp.bfloat16)
     input_grad = (scaled.astype(jnp.float32) + finished[rows_local:]).astype(jnp.bfloat16)
 
-    tokens_mate, scaled_mate = mate(tokens_all), mate(scaled_all)
-    active_mate, grad_mate = mate(activated[:, units:]), mate(hidden_grad[:, units:])
-    w_in_grad = product(tokens_all, hidden_grad[:, :units], 0, 0) + product(
-        tokens_mate, grad_mate, 0, 0
-    )
-    w_out_grad = product(activated[:, :units], scaled_all, 0, 0) + product(
-        active_mate, scaled_mate, 0, 0
-    )
     return (
         block_output.reshape(1, rows_local, width),
         input_grad.reshape(1, rows_local, width),

time: 208 us -> 207 us (level)
    all_to_all x7, waiting for transfers between devices: 49.8 us -> 43.4 us  [swapped(): lax.all_to_all(value, axis, 0, 0, axis_index_groups=groups, tiled=True)]
    reduce_scatter x1, waiting for transfers between devices: 22 us -> 27.2 us  [body(): lax.psum_scatter(output_terms, 'col', scatter_dimension=0, tiled=True)]
    all_gather x1, waiting for transfers between devices: 11 us -> 13.4 us  [body(): lax.all_gather(padded, 'col', axis=0)[:, :line_rows]]
  transfers between devices with their start and end apart: 15 -> 15, of which waited for: 9 -> 8; matrix products, arithmetic and copies ran while one was open for 11% -> 11% of each run, Pallas kernels for 0% -> 0%
where the time goes in v3:
time: 207 us; the launch traced here: 206 us
  waiting for transfers between devices  85.1 us (41%)
  starting transfers between devices  53.1 us (26%)
  blocking collectives  20.5 us (10%)
  matrix products  16.2 us (8%)
  between operations  15 us (7%)
  local copies, waits for them, and re-layouts  9.62 us (5%)
  other arithmetic  6.19 us (3%)
    all_to_all x7, waiting for transfers between devices, swapped(): lax.all_to_all(value, axis, 0, 0, axis_index_groups=groups, tiled=True)  43.4 us
    all_to_all x7, starting transfers between devices, swapped(): lax.all_to_all(value, axis, 0, 0, axis_index_groups=groups, tiled=True)  40.6 us
    reduce_scatter x1, waiting for transfers between devices, body(): lax.psum_scatter(output_terms, 'col', scatter_dimension=0, tiled=True)  27.2 us
    all_to_all x1, blocking collectives, swapped(): lax.all_to_all(value, axis, 0, 0, axis_index_groups=groups, tiled=True)  20.5 us
    dot_general x12, matrix products, product(): lax.dot_general(left, right, (((left_dim,), (right_dim,)), ((), ())), pre...  16.2 us
    all_gather x1, waiting for transfers between devices, body(): lax.all_gather(padded, 'col', axis=0)[:, :line_rows]  13.4 us
    ppermute x6, starting transfers between devices, body(): mate = lambda value: lax.ppermute(value, 'rep', to_mate)  12.5 us
  transfers between devices with their start and end apart: 15, of which 8 were waited for; matrix products, arithmetic and copies ran while one was open for 11% of the time, Pallas kernels for 0%

profile of v3, /device:TPU:6, one launch (start us, length us, event | category | flops | bytes accessed | tf_op | source)
XLA Modules:
  0.0 205.7 jit_solution(4667438962013766883)
XLA Ops:
  7.2 1.3 fusion.25
  9.1 0.7 compare_convert_fusion
  9.8 0.8 fusion.22
  10.6 0.7 pad_maximum_fusion.4
  11.4 20.5 %all_to_all.40 = bf16[4,32,768]{2,1,0:T(8,128)(2,1)S(1)} all-to-all(bf16[4,32,768]{2,1,0:T(8,128)(2,1)S(1)} %broadcast_in_dim.15), channel_id=1, replica_groups={{0,128,256,384},{64,192,320,448},{1,129,257,385},{65,193,321,449},{2,13..., dimensions={0} | all-to-all | bytes 393216 | tf_op jit(solution)/shard_map/all_to_all | solution.py:34
  31.9 0.9 broadcast_in_dim.17
  32.9 7.1 %all-to-all-start.1 = ((bf16[8,64,768]{2,1,0:T(8,128)(2,1)}), bf16[8,64,768]{2,1,0:T(8,128)(2,1)S(1)}, u32[]{:S(2)}, u32[]{:S(2)}) async-start(bf16[8,64,768]{2,1,0:T(8,128)(2,1)} %broadcast_in_dim.17), calls=%async_computation.1 | async-start | bytes 1572864 | tf_op jit(solution)/shard_map/all_to_all | solution.py:34
  40.0 1.9 collective-permute-start
  42.0 0.7 pad_maximum_fusion.3
  42.7 18.1 %all-to-all-done.1 = bf16[8,64,768]{2,1,0:T(8,128)(2,1)S(1)} async-done(((bf16[8,64,768]{2,1,0:T(8,128)(2,1)}), bf16[8,64,768]{2,1,0:T(8,128)(2,1)S(1)}, u32[]{:S(2)}, u32[]{:S(2)}) %all-to-all-start.1) | async-done | bytes 786464 | tf_op jit(solution)/shard_map/all_to_all | solution.py:34
  61.3 0.5 convolution_convert_fusion.2
  62.2 1.2 copy.12
  63.3 6.1 %all-to-all-start.2 = ((bf16[8,64,768]{2,1,0:T(8,128)(2,1)}), bf16[8,64,768]{2,1,0:T(8,128)(2,1)S(1)}, u32[]{:S(2)}, u32[]{:S(2)}) async-start(bf16[8,64,768]{2,1,0:T(8,128)(2,1)} %bitcast.4), calls=%async_computation.2 | async-start | bytes 1572864 | tf_op jit(solution)/shard_map/all_to_all | solution.py:34
  69.4 13.4 %all-gather.3.cloned.1.call-done = bf16[768,768]{1,0:T(8,128)(2,1)} async-done(((bf16[96,768]{1,0:T(8,128)(2,1)}), bf16[768,768]{1,0:T(8,128)(2,1)}) %all-gather.3.cloned.1.call-update) | async-done | bytes 1179664 | tf_op jit(solution)/shard_map/all_gather | solution.py:82
  82.8 2.1 %slice.186 = bf16[8,64,768]{2,1,0:T(8,128)(2,1)} slice(bf16[8,96,768]{2,1,0:T(8,128)(2,1)} %bitcast.85), slice={[0:8], [0:64], [0:768]} | slice | bytes 1572864 | tf_op jit(solution)/shard_map/slice | solution.py:82
  85.0 0.9 broadcast_in_dim.34
  86.0 5.9 %all-to-all-start.3 = ((bf16[8,64,768]{2,1,0:T(8,128)(2,1)}), bf16[8,64,768]{2,1,0:T(8,128)(2,1)S(1)}, u32[]{:S(2)}, u32[]{:S(2)}) async-start(bf16[8,64,768]{2,1,0:T(8,128)(2,1)} %broadcast_in_dim.34), calls=%async_computation.3 | async-start | bytes 1572864 | tf_op jit(solution)/shard_map/all_to_all | solution.py:34
  91.9 1.9 collective-permute-start.1
  93.8 1.6 convolution_convert_fusion.1
  95.8 0.8 copy-done.5
  96.6 1.6 convolution_convert_fusion
  98.3 1.2 all-to-all-done.3
  99.5 1.2 copy.13
  100.6 5.4 %all-to-all-start.4 = ((bf16[8,64,768]{2,1,0:T(8,128)(2,1)}), bf16[8,64,768]{2,1,0:T(8,128)(2,1)S(1)}, u32[]{:S(2)}, u32[]{:S(2)}) async-start(bf16[8,64,768]{2,1,0:T(8,128)(2,1)} %bitcast.11), calls=%async_computation.4 | async-start | bytes 1572864 | tf_op jit(solution)/shard_map/all_to_all | solution.py:34
  106.0 0.6 fusion.7
  107.1 1.5 add_convert_fusion.1
  108.5 7.3 %all-to-all-done.4 = bf16[8,64,768]{2,1,0:T(8,128)(2,1)S(1)} async-done(((bf16[8,64,768]{2,1,0:T(8,128)(2,1)}), bf16[8,64,768]{2,1,0:T(8,128)(2,1)S(1)}, u32[]{:S(2)}, u32[]{:S(2)}) %all-to-all-start.4) | async-done | bytes 786464 | tf_op jit(solution)/shard_map/all_to_all | solution.py:34
  116.0 0.9 broadcast_in_dim.35
  117.0 5.4 %all-to-all-start.5 = ((bf16[8,64,768]{2,1,0:T(8,128)(2,1)}), bf16[8,64,768]{2,1,0:T(8,128)(2,1)S(1)}, u32[]{:S(2)}, u32[]{:S(2)}) async-start(bf16[8,64,768]{2,1,0:T(8,128)(2,1)} %broadcast_in_dim.35), calls=%async_computation.5 | async-start | bytes 1572864 | tf_op jit(solution)/shard_map/all_to_all | solution.py:34
  122.3 0.7 reduce-scatter.2.cloned.1.call-update
  123.1 9.7 %all-to-all-done.5 = bf16[8,64,768]{2,1,0:T(8,128)(2,1)S(1)} async-done(((bf16[8,64,768]{2,1,0:T(8,128)(2,1)}), bf16[8,64,768]{2,1,0:T(8,128)(2,1)S(1)}, u32[]{:S(2)}, u32[]{:S(2)}) %all-to-all-start.5) | async-done | bytes 786464 | tf_op jit(solution)/shard_map/all_to_all | solution.py:34
  132.8 0.6 fusion.1
  133.4 1.5 add_convert_fusion
  134.9 3.7 %all-to-all-start.6 = ((bf16[8,64,768]{2,1,0:T(8,128)(2,1)}), bf16[8,64,768]{2,1,0:T(8,128)(2,1)S(1)}, u32[]{:S(2)}, u32[]{:S(2)}) async-start(bf16[8,64,768]{2,1,0:T(8,128)(2,1)} %bitcast.84), calls=%async_computation.7 | async-start | bytes 1572864 | tf_op jit(solution)/shard_map/all_to_all | solution.py:34
  138.6 1.9 collective-permute-start.2
  140.5 0.8 slice.154
  141.3 2.4 %collective-permute-start.4 = (bf16[512,384]{1,0:T(8,128)(2,1)}, bf16[512,384]{1,0:T(8,128)(2,1)}, u32[]{:S(2)}, u32[]{:S(2)}) collective-permute-start(bf16[512,384]{1,0:T(8,128)(2,1)} %slice.154), channel_id=1, source_target_pairs={{0,64},{64,0},{128,192},{192,128},{256,320},{320,256},{384,448},{4... | collective-permute-start | bytes 1179656 | tf_op jit(solution)/shard_map/ppermute | solution.py:58
  143.7 27.2 %reduce-scatter.2.cloned.1.call-done = bf16[64,768]{1,0:T(8,128)(2,1)} async-done(((bf16[512,768]{1,0:T(8,128)(2,1)}), bf16[64,768]{1,0:T(8,128)(2,1)}) %reduce-scatter.2.cloned.1.call-update) | async-done | bytes 98320 | tf_op jit(solution)/shard_map/reduce_scatter | solution.py:105
  170.9 1.9 collective-permute-start.3
  172.8 0.6 fusion.3
  173.4 2.4 %collective-permute-start.5 = (bf16[512,768]{1,0:T(8,128)(2,1)}, bf16[512,768]{1,0:T(8,128)(2,1)}, u32[]{:S(2)}, u32[]{:S(2)}) collective-permute-start(bf16[512,768]{1,0:T(8,128)(2,1)} %bitcast.9), channel_id=1, source_target_pairs={{0,64},{64,0},{128,192},{192,128},{256,320},{320,256},{384,448},{4... | collective-permute-start | bytes 2359304 | tf_op jit(solution)/shard_map/ppermute | solution.py:58
  175.8 1.6 fusion.5
  177.5 2.8 %convolution_add_fusion.1 = f32[768,384]{1,0:T(8,128)} fusion(f32[768,384]{1,0:T(8,128)S(1)} %fusion.3, bf16[512,768]{1,0:T(8,128)(2,1)} %collective-permute-done.2, bf16[512,384]{1,0:T(8,128)(2,1)S(1)} %collective-permute-done.3), kind=kOutput, calls=%fused_computation.3 | convolution fusion | flops 302284800 | bytes 3538944 | tf_op jit(solution)/shard_map/dot_general | solution.py:23
  180.4 0.7 pad_maximum_fusion.2
  181.1 7.1 %all-to-all-start.7 = ((bf16[4,32,768]{2,1,0:T(8,128)(2,1)}), bf16[4,32,768]{2,1,0:T(8,128)(2,1)S(1)}, u32[]{:S(2)}, u32[]{:S(2)}) async-start(bf16[4,32,768]{2,1,0:T(8,128)(2,1)} %pad_maximum_fusion.2), calls=%async_computation.8 | async-start | bytes 393216 | tf_op jit(solution)/shard_map/all_to_all | solution.py:34
  188.2 2.8 %convolution_add_fusion = f32[384,768]{1,0:T(8,128)} fusion(f32[384,768]{1,0:T(8,128)S(1)} %fusion.5, bf16[512,384]{1,0:T(8,128)(2,1)} %collective-permute-done.4, bf16[512,768]{1,0:T(8,128)(2,1)} %collective-permute-done.5), kind=kOutput, calls=%fused_computation.2 | convolution fusion | flops 302284800 | bytes 3538944 | tf_op jit(solution)/shard_map/dot_general | solution.py:23
  191.0 7.1 %all-to-all-done.7 = bf16[4,32,768]{2,1,0:T(8,128)(2,1)S(1)} async-done(((bf16[4,32,768]{2,1,0:T(8,128)(2,1)}), bf16[4,32,768]{2,1,0:T(8,128)(2,1)S(1)}, u32[]{:S(2)}, u32[]{:S(2)}) %all-to-all-start.7) | async-done | bytes 196640 | tf_op jit(solution)/shard_map/all_to_all | solution.py:34
  198.2 0.7 fusion.24
  (41 shorter events, 2.4 us)
Async XLA Ops:
  11.4 28.6 %copy-start.1 = (bf16[768,384]{1,0:T(8,128)(2,1)S(1)}, bf16[768,384]{1,0:T(8,128)(2,1)}, u32[]{:S(2)}) copy-start(bf16[768,384]{1,0:T(8,128)(2,1)} %param.6) | copy-start | bytes 1769476
  32.9 27.9 %all-to-all-start.1 = ((bf16[8,64,768]{2,1,0:T(8,128)(2,1)}), bf16[8,64,768]{2,1,0:T(8,128)(2,1)S(1)}, u32[]{:S(2)}, u32[]{:S(2)}) async-start(bf16[8,64,768]{2,1,0:T(8,128)(2,1)} %broadcast_in_dim.17), calls=%async_computation.1 | async-start | bytes 1572864 | tf_op jit(solution)/shard_map/all_to_all | solution.py:34
  40.0 42.8 %all-gather.3.cloned.1.call-start = ((), (), s32[]{:S(2)}) async-start(), calls=%async_computation.10 | async-start | bytes 1327104 | tf_op jit(solution)/shard_map/all_gather | solution.py:82
  40.0 21.3 %collective-permute-start = (bf16[768,384]{1,0:T(8,128)(2,1)S(1)}, bf16[768,384]{1,0:T(8,128)(2,1)S(1)}, u32[]{:S(2)}, u32[]{:S(2)}) collective-permute-start(bf16[768,384]{1,0:T(8,128)(2,1)S(1)} %copy-done.1), channel_id=1, source_target_pairs={{0,64},{64,0},{128,192},{192,128},{256,320},{320,256},{384,448},{4... | collective-permute-start | bytes 1769480 | tf_op jit(solution)/shard_map/ppermute | solution.py:58
  61.3 0.8 copy-start.3
  63.3 21.6 %all-to-all-start.2 = ((bf16[8,64,768]{2,1,0:T(8,128)(2,1)}), bf16[8,64,768]{2,1,0:T(8,128)(2,1)S(1)}, u32[]{:S(2)}, u32[]{:S(2)}) async-start(bf16[8,64,768]{2,1,0:T(8,128)(2,1)} %bitcast.4), calls=%async_computation.2 | async-start | bytes 1572864 | tf_op jit(solution)/shard_map/all_to_all | solution.py:34
  84.9 7.0 %copy-start = (bf16[384,768]{1,0:T(8,128)(2,1)S(1)}, bf16[384,768]{1,0:T(8,128)(2,1)}, u32[]{:S(2)}) copy-start(bf16[384,768]{1,0:T(8,128)(2,1)} %param.7) | copy-start | bytes 1769476
  86.0 13.5 %all-to-all-start.3 = ((bf16[8,64,768]{2,1,0:T(8,128)(2,1)}), bf16[8,64,768]{2,1,0:T(8,128)(2,1)S(1)}, u32[]{:S(2)}, u32[]{:S(2)}) async-start(bf16[8,64,768]{2,1,0:T(8,128)(2,1)} %broadcast_in_dim.34), calls=%async_computation.3 | async-start | bytes 1572864 | tf_op jit(solution)/shard_map/all_to_all | solution.py:34
  91.9 3.9 %collective-permute-start.1 = (bf16[384,768]{1,0:T(8,128)(2,1)S(1)}, bf16[384,768]{1,0:T(8,128)(2,1)S(1)}, u32[]{:S(2)}, u32[]{:S(2)}) collective-permute-start(bf16[384,768]{1,0:T(8,128)(2,1)S(1)} %copy-done), channel_id=1, source_target_pairs={{0,64},{64,0},{128,192},{192,128},{256,320},{320,256},{384,448},{4... | collective-permute-start | bytes 1769480 | tf_op jit(solution)/shard_map/ppermute | solution.py:58
  95.8 0.8 copy-start.5
  100.6 15.2 %all-to-all-start.4 = ((bf16[8,64,768]{2,1,0:T(8,128)(2,1)}), bf16[8,64,768]{2,1,0:T(8,128)(2,1)S(1)}, u32[]{:S(2)}, u32[]{:S(2)}) async-start(bf16[8,64,768]{2,1,0:T(8,128)(2,1)} %bitcast.11), calls=%async_computation.4 | async-start | bytes 1572864 | tf_op jit(solution)/shard_map/all_to_all | solution.py:34
  106.0 1.1 copy-start.6
  116.0 16.8 %copy-start.2 = (bf16[768,384]{1,0:T(8,128)(2,1)S(1)}, bf16[768,384]{1,0:T(8,128)(2,1)}, u32[]{:S(2)}) copy-start(bf16[768,384]{1,0:T(8,128)(2,1)} %param.6) | copy-start | bytes 1769476
  117.0 15.8 %all-to-all-start.5 = ((bf16[8,64,768]{2,1,0:T(8,128)(2,1)}), bf16[8,64,768]{2,1,0:T(8,128)(2,1)S(1)}, u32[]{:S(2)}, u32[]{:S(2)}) async-start(bf16[8,64,768]{2,1,0:T(8,128)(2,1)} %broadcast_in_dim.35), calls=%async_computation.5 | async-start | bytes 1572864 | tf_op jit(solution)/shard_map/all_to_all | solution.py:34
  122.3 11.0 %copy-start.4 = (bf16[768,384]{1,0:T(8,128)(2,1)S(1)}, bf16[768,384]{1,0:T(8,128)(2,1)}, u32[]{:S(2)}) copy-start(bf16[768,384]{1,0:T(8,128)(2,1)} %copy-done.3) | copy-start | bytes 1769476
  122.3 48.5 %reduce-scatter.2.cloned.1.call-start = ((), (), s32[]{:S(2)}) async-start(), calls=%async_computation.9 | async-start | bytes 884736 | tf_op jit(solution)/shard_map/reduce_scatter | solution.py:105
  134.9 45.4 %all-to-all-start.6 = ((bf16[8,64,768]{2,1,0:T(8,128)(2,1)}), bf16[8,64,768]{2,1,0:T(8,128)(2,1)S(1)}, u32[]{:S(2)}, u32[]{:S(2)}) async-start(bf16[8,64,768]{2,1,0:T(8,128)(2,1)} %bitcast.84), calls=%async_computation.7 | async-start | bytes 1572864 | tf_op jit(solution)/shard_map/all_to_all | solution.py:34
  138.6 38.9 %collective-permute-start.2 = (bf16[512,768]{1,0:T(8,128)(2,1)S(1)}, bf16[512,768]{1,0:T(8,128)(2,1)}, u32[]{:S(2)}, u32[]{:S(2)}) collective-permute-start(bf16[512,768]{1,0:T(8,128)(2,1)S(1)} %bitcast.82), channel_id=1, source_target_pairs={{0,64},{64,0},{128,192},{192,128},{256,320},{320,256},{384,448},{4... | collective-permute-start | bytes 2359304 | tf_op jit(solution)/shard_map/ppermute | solution.py:58
  141.3 46.9 %collective-permute-start.4 = (bf16[512,384]{1,0:T(8,128)(2,1)}, bf16[512,384]{1,0:T(8,128)(2,1)}, u32[]{:S(2)}, u32[]{:S(2)}) collective-permute-start(bf16[512,384]{1,0:T(8,128)(2,1)} %slice.154), channel_id=1, source_target_pairs={{0,64},{64,0},{128,192},{192,128},{256,320},{320,256},{384,448},{4... | collective-permute-start | bytes 1179656 | tf_op jit(solution)/shard_map/ppermute | solution.py:58
  170.9 6.6 %collective-permute-start.3 = (bf16[512,384]{1,0:T(8,128)(2,1)S(1)}, bf16[512,384]{1,0:T(8,128)(2,1)S(1)}, u32[]{:S(2)}, u32[]{:S(2)}) collective-permute-start(bf16[512,384]{1,0:T(8,128)(2,1)S(1)} %slice.174), channel_id=1, source_target_pairs={{0,64},{64,0},{128,192},{192,128},{256,320},{320,256},{384,448},{4... | collective-permute-start | bytes 1179656 | tf_op jit(solution)/shard_map/ppermute | solution.py:58
  173.4 14.8 %collective-permute-start.5 = (bf16[512,768]{1,0:T(8,128)(2,1)}, bf16[512,768]{1,0:T(8,128)(2,1)}, u32[]{:S(2)}, u32[]{:S(2)}) collective-permute-start(bf16[512,768]{1,0:T(8,128)(2,1)} %bitcast.9), channel_id=1, source_target_pairs={{0,64},{64,0},{128,192},{192,128},{256,320},{320,256},{384,448},{4... | collective-permute-start | bytes 2359304 | tf_op jit(solution)/shard_map/ppermute | solution.py:58
  177.5 2.9 %copy-start.9 = (bf16[64,768]{1,0:T(8,128)(2,1)S(1)}, bf16[64,768]{1,0:T(8,128)(2,1)}, u32[]{:S(2)}) copy-start(bf16[64,768]{1,0:T(8,128)(2,1)} %reduce-scatter.2.cloned.1.call-done) | copy-start | bytes 294916
  181.1 17.0 %all-to-all-start.7 = ((bf16[4,32,768]{2,1,0:T(8,128)(2,1)}), bf16[4,32,768]{2,1,0:T(8,128)(2,1)S(1)}, u32[]{:S(2)}, u32[]{:S(2)}) async-start(bf16[4,32,768]{2,1,0:T(8,128)(2,1)} %pad_maximum_fusion.2), calls=%async_computation.8 | async-start | bytes 393216 | tf_op jit(solution)/shard_map/all_to_all | solution.py:34
  188.2 10.0 %copy-start.7 = (bf16[1,16,768]{2,1,0:T(8,128)(2,1)S(1)}, bf16[1,16,768]{2,1,0:T(8,128)(2,1)}, u32[]{:S(2)}) copy-start(bf16[1,16,768]{2,1,0:T(8,128)(2,1)} %param.8) | copy-start | bytes 73732
  188.2 10.0 %copy-start.8 = (bf16[1,16,768]{2,1,0:T(8,128)(2,1)S(1)}, bf16[1,16,768]{2,1,0:T(8,128)(2,1)}, u32[]{:S(2)}) copy-start(bf16[1,16,768]{2,1,0:T(8,128)(2,1)} %param.5) | copy-start | bytes 73732
Sparse Core Ops, SparseCore 0:
  43.4 39.3 all-gather.2
  126.6 44.2 reduce-scatter.1

commit v4 on v3

--- a/solution.py
+++ b/solution.py
@@ -81,42 +81,59 @@
     padded = jnp.concatenate([scaled_line, scaled_line[: line_rows // 2]], axis=0)
     scaled_all = lax.all_gather(padded, "col", axis=0)[:, :line_rows].reshape(rows_all, width)
 
-    tokens_all = spread(tokens_line, "col", columns).reshape(rows_all, width)
-    hidden_terms = jnp.concatenate(
-        [product(tokens_all, w, 1, 0).astype(jnp.bfloat16) for w in (w_in, w_in_mate)], axis=1
-    )
+    def forward(line):
+        everyone = spread(line, "col", columns).reshape(rows_all, width)
+        return everyone, hidden_part(everyone)
+
+    def forward_plain(line):
+        everyone = lax.all_gather(line, "col", axis=0, tiled=True)
+        return everyone, hidden_part(everyone)
+
+    def hidden_part(everyone):
+        return jnp.concatenate(
+            [product(everyone, w, 1, 0).astype(jnp.bfloat16) for w in (w_in, w_in_mate)], axis=1
+        )
+
+    some_kept = jnp.sum(counts) > 0
+    tokens_all, hidden_terms = lax.cond(some_kept, forward, forward_plain, tokens_line)
     hidden = added_up(swapped(cut(hidden_terms, row_count), "row"))
     active, slope = gelu_both(hidden)
-    active, scaled_all = lax.optimization_barrier((active, scaled_all))
-    activated = spread(active.astype(jnp.bfloat16), "row", row_count).reshape(rows_all, -1)
-
     slope_terms = jnp.concatenate(
         [product(scaled_all, w, 1, 1).astype(jnp.bfloat16) for w in (w_out, w_out_mate)], axis=1
     )
-    slope_terms, activated = lax.optimization_barrier((slope_terms, activated))
-    slope_sum = added_up(swapped(cut(slope_terms, row_count), "row"))
-    grad_share = (slope_sum * slope).astype(jnp.bfloat16)
-
+    share = jnp.broadcast_to(active.astype(jnp.bfloat16)[None], (row_count, *active.shape))
+    mixed = swapped(jnp.concatenate([share, cut(slope_terms, row_count)], axis=2), "row")
+    activated = mixed[:, :, : active.shape[1]].reshape(rows_all, -1)
+    grad_share = (added_up(mixed[:, :, active.shape[1] :]) * slope).astype(jnp.bfloat16)
     output_terms = (
         product(activated[:, :units], w_out, 1, 0) + product(activated[:, units:], w_out_mate, 1, 0)
     ).astype(jnp.bfloat16)
     grad_share, output_terms = lax.optimization_barrier((grad_share, output_terms))
-    hidden_grad = spread(grad_share, "row", row_count).reshape(rows_all, -1)
     output_line = lax.psum_scatter(output_terms, "col", scatter_dimension=0, tiled=True)
 
-    back_terms = (
-        product(hidden_grad[:, :units], w_in, 1, 1) + product(hidden_grad[:, units:], w_in_mate, 1, 1)
-    ).astype(jnp.bfloat16)
-    back_line = added_up(swapped(cut(back_terms, columns), "col")).astype(jnp.bfloat16)
+    def backward(share):
+        hidden_grad = spread(share, "row", row_count).reshape(rows_all, -1)
+        back_terms = (
+            product(hidden_grad[:, :units], w_in, 1, 1)
+            + product(hidden_grad[:, units:], w_in_mate, 1, 1)
+        ).astype(jnp.bfloat16)
+        back_line = added_up(swapped(cut(back_terms, columns), "col")).astype(jnp.bfloat16)
+        w_out_grad = product(activated[:, :units], scaled_all, 0, 0) + product(
+            mate(activated[:, units:]), mate(scaled_all), 0, 0
+        )
+        w_in_grad = product(tokens_all, hidden_grad[:, :units], 0, 0) + product(
+            mate(tokens_all), mate(hidden_grad[:, units:]), 0, 0
+        )
+        return back_line, w_in_grad, w_out_grad
 
-    hidden_grad, scaled_all, output_line = lax.optimization_barrier((hidden_grad, scaled_all, output_line))
-    w_out_grad = product(activated[:, :units], scaled_all, 0, 0) + product(
-        mate(activated[:, units:]), mate(scaled_all), 0, 0
-    )
+    def nothing(share):
+        return (
+            jnp.zeros((line_rows, width), jnp.bfloat16),
+            jnp.zeros((width, units), jnp.float32),
+            jnp.zeros((units, width), jnp.float32),
+        )
 
-    w_in_grad = product(tokens_all, hidden_grad[:, :units], 0, 0) + product(
-        mate(tokens_all), mate(hidden_grad[:, units:]), 0, 0
-    )
+    back_line, w_in_grad, w_out_grad = lax.cond(some_kept, backward, nothing, grad_share)
     ends = jnp.concatenate([cut(output_line, chips), cut(back_line, chips)], axis=1)
     finished = added_up(swapped(ends, "rep", same_core))
     block_output = (tokens_local.astype(jnp.float32) + finished[:rows_local]).astype(jnp.bfloat16)

time: 207 us -> 187 us (0.903)
  waiting for transfers between devices: 85.1 us -> 29.1 us
  blocking collectives: 20.5 us -> 69.3 us
  starting transfers between devices: 53.1 us -> 41.4 us
  local copies, waits for them, and re-layouts: 9.62 us -> 6.34 us
    all_to_all x1 -> x3, blocking collectives: 20.5 us -> 69.3 us  [swapped(): lax.all_to_all(value, axis, 0, 0, axis_index_groups=groups, tiled=True)]
    reduce_scatter x1, waiting for transfers between devices: 27.2 us -> 0.02 us  [body(): lax.psum_scatter(output_terms, 'col', scatter_dimension=0, tiled=True)]
    all_to_all x7 -> x4, waiting for transfers between devices: 43.4 us -> 29 us  [swapped(): lax.all_to_all(value, axis, 0, 0, axis_index_groups=groups, tiled=True)]
    all_gather x1, waiting for transfers between devices: 13.4 us -> 0.02 us  [body(): lax.all_gather(padded, 'col', axis=0)[:, :line_rows]]
    all_to_all x7 -> x4, starting transfers between devices: 40.6 us -> 29.4 us  [swapped(): lax.all_to_all(value, axis, 0, 0, axis_index_groups=groups, tiled=True)]
  transfers between devices with their start and end apart: 15 -> 12, of which waited for: 8 -> 4; matrix products, arithmetic and copies ran while one was open for 11% -> 10% of each run, Pallas kernels for 0% -> 0%
where the time goes in v4:
time: 187 us; the launch traced here: 185 us
  blocking collectives  69.3 us (37%)
  starting transfers between devices  41.4 us (22%)
  waiting for transfers between devices  29.1 us (16%)
  matrix products  16.2 us (9%)
  between operations  15.6 us (8%)
  other arithmetic  6.6 us (4%)
  local copies, waits for them, and re-layouts  6.34 us (3%)
    all_to_all x3, blocking collectives, swapped(): lax.all_to_all(value, axis, 0, 0, axis_index_groups=groups, tiled=True)  69.3 us
    all_to_all x4, starting transfers between devices, swapped(): lax.all_to_all(value, axis, 0, 0, axis_index_groups=groups, tiled=True)  29.4 us
    all_to_all x4, waiting for transfers between devices, swapped(): lax.all_to_all(value, axis, 0, 0, axis_index_groups=groups, tiled=True)  29 us
    dot_general x12, matrix products, product(): lax.dot_general(left, right, (((left_dim,), (right_dim,)), ((), ())), pre...  16.2 us
    ppermute x6, starting transfers between devices, body(): mate = lambda value: lax.ppermute(value, 'rep', to_mate)  12 us
  transfers between devices with their start and end apart: 12, of which 4 were waited for; matrix products, arithmetic and copies ran while one was open for 10% of the time, Pallas kernels for 0%

profile of v4, /device:TPU:6, one launch (start us, length us, event | category | flops | bytes accessed | tf_op | source)
XLA Modules:
  0.0 184.6 jit_solution(8218283465735064157)
XLA Ops:
  7.2 1.4 fusion.33
  9.2 0.7 compare_convert_fusion
  9.9 0.8 fusion.30
  10.7 0.7 pad_maximum_fusion.6
  11.4 0.7 broadcast_in_dim.20
  12.1 10.3 %all-to-all-start.3 = ((bf16[4,32,768]{2,1,0:T(8,128)(2,1)}), bf16[4,32,768]{2,1,0:T(8,128)(2,1)S(1)}, u32[]{:S(2)}, u32[]{:S(2)}) async-start(bf16[4,32,768]{2,1,0:T(8,128)(2,1)} %broadcast_in_dim.20), calls=%async_computation.3 | async-start | bytes 393216 | tf_op jit(solution)/shard_map/all_to_all | solution.py:34
  22.4 1.9 %collective-permute-start.4 = (bf16[768,384]{1,0:T(8,128)(2,1)}, bf16[768,384]{1,0:T(8,128)(2,1)}, u32[]{:S(2)}, u32[]{:S(2)}) collective-permute-start(bf16[768,384]{1,0:T(8,128)(2,1)} %param.10), channel_id=1, source_target_pairs={{0,64},{64,0},{128,192},{192,128},{256,320},{320,256},{384,448},{4... | collective-permute-start | bytes 1769480 | tf_op jit(solution)/shard_map/ppermute | solution.py:58
  24.3 8.0 %all-to-all-done.3 = bf16[4,32,768]{2,1,0:T(8,128)(2,1)S(1)} async-done(((bf16[4,32,768]{2,1,0:T(8,128)(2,1)}), bf16[4,32,768]{2,1,0:T(8,128)(2,1)S(1)}, u32[]{:S(2)}, u32[]{:S(2)}) %all-to-all-start.3) | async-done | bytes 196640 | tf_op jit(solution)/shard_map/all_to_all | solution.py:34
  32.4 0.7 pad_maximum_fusion.5
  33.8 36.7 %conditional.2 = (bf16[512,768]{1,0:T(8,128)(2,1)}, bf16[512,768]{0,1:T(8,128)(2,1)S(1)}) conditional(s32[]{:T(128)} %convert_element_type.231, (bf16[4,16,768]{2,1,0:T(8,128)(2,1)S(1)}, bf16[768,384]{1,0:T(8,128)(2,1)S(1)}, bf16[768,384]{1,0:T(8,128)(2,1)}) %tuple.46, (bf16[4,16,768]{2,1,0:T(8,128)(2,1)S(1)}, bf16[768,384]{1,0:T(8,128)(2,1)S(1)}, ...), branch_computations={%region_2.3_spmd, %region_3.4_spmd} | conditional | flops 605945856 | bytes 7569424 | solution.py:98
  33.8 33.1 %all_to_all.32 = bf16[8,64,768]{2,1,0:T(8,128)(2,1)} all-to-all(bf16[8,64,768]{2,1,0:T(8,128)(2,1)S(1)} %broadcast_in_dim.8), channel_id=1, replica_groups=mesh['rep'=8,'row'=8,'col'=8] {'col'}, dimensions={0} | all-to-all | bytes 1572864 | tf_op jit(solution)/shard_map/cond/branch_1_fun/all_to_all | solution.py:34
  67.0 1.8 convolution_convert_fusion.2
  68.8 1.6 convolution_convert_fusion.3
  70.5 1.2 copy.11
  71.7 7.2 %all-to-all-start.4 = ((bf16[8,64,768]{2,1,0:T(8,128)(2,1)}), bf16[8,64,768]{2,1,0:T(8,128)(2,1)S(1)}, u32[]{:S(2)}, u32[]{:S(2)}) async-start(bf16[8,64,768]{2,1,0:T(8,128)(2,1)} %bitcast.8), calls=%async_computation.4 | async-start | bytes 1572864 | tf_op jit(solution)/shard_map/all_to_all | solution.py:34
  78.9 1.9 %collective-permute-start.5 = (bf16[384,768]{1,0:T(8,128)(2,1)S(1)}, bf16[384,768]{1,0:T(8,128)(2,1)S(1)}, u32[]{:S(2)}, u32[]{:S(2)}) collective-permute-start(bf16[384,768]{1,0:T(8,128)(2,1)S(1)} %copy-done), channel_id=1, source_target_pairs={{0,64},{64,0},{128,192},{192,128},{256,320},{320,256},{384,448},{4... | collective-permute-start | bytes 1769480 | tf_op jit(solution)/shard_map/ppermute | solution.py:58
  80.8 5.6 %all-to-all-done.4 = bf16[8,64,768]{2,1,0:T(8,128)(2,1)S(1)} async-done(((bf16[8,64,768]{2,1,0:T(8,128)(2,1)}), bf16[8,64,768]{2,1,0:T(8,128)(2,1)S(1)}, u32[]{:S(2)}, u32[]{:S(2)}) %all-to-all-start.4) | async-done | bytes 786464 | tf_op jit(solution)/shard_map/all_to_all | solution.py:34
  86.5 0.2 fusion.24
  86.7 1.2 slice.197
  87.9 0.5 convolution_convert_fusion.5
  88.4 0.8 copy-done.4
  89.2 0.5 convolution_convert_fusion.4
  89.8 0.3 copy.12
  90.1 0.1 pad_maximum_fusion.2
  90.2 19.4 %all_to_all.33 = bf16[8,64,1536]{2,1,0:T(8,128)(2,1)S(1)} all-to-all(bf16[8,64,1536]{2,1,0:T(8,128)(2,1)S(1)} %pad_maximum_fusion.2), channel_id=1, replica_groups=mesh['rep'=8,'row'=8,'col'=8] {'row'}, dimensions={0} | all-to-all | bytes 3145728 | tf_op jit(solution)/shard_map/all_to_all | solution.py:34
  109.8 1.0 copy-done.1
  110.8 0.6 fusion.8
  111.3 1.5 add_convert_fusion.2
  112.8 0.2 fusion.21
  113.1 46.2 %conditional.3 = (f32[768,384]{1,0:T(8,128)}, f32[384,768]{1,0:T(8,128)}, bf16[4,16,768]{2,1,0:T(8,128)(2,1)S(1)}) conditional(s32[]{:T(128)} %convert_element_type.231, () %tuple.29, (bf16[64,768]{1,0:T(8,128)(2,1)S(1)}, bf16[512,768]{1,0:T(8,128)(2,1)}, bf16[512,768]{1,0:T(8,128)(2,1)S(1)}, bf16[512,768]{1,0:T(8,128)(2,1)S(1)}, ...), branch_computations={%region_5.6_spmd, %region_6.7_spmd} | conditional | flops 1814102016 | bytes 37552404 | solution.py:136
  113.1 0.9 broadcast_in_dim.14
  114.0 5.8 %all-to-all-start.1 = ((bf16[8,64,768]{2,1,0:T(8,128)(2,1)}), bf16[8,64,768]{2,1,0:T(8,128)(2,1)S(1)}, u32[]{:S(2)}, u32[]{:S(2)}) async-start(bf16[8,64,768]{2,1,0:T(8,128)(2,1)} %broadcast_in_dim.14), calls=%async_computation.1 | async-start | bytes 1572864 | tf_op jit(solution)/shard_map/cond/branch_1_fun/all_to_all | solution.py:34
  119.9 1.9 %collective-permute-start.3 = (bf16[512,768]{1,0:T(8,128)(2,1)S(1)}, bf16[512,768]{1,0:T(8,128)(2,1)}, u32[]{:S(2)}, u32[]{:S(2)}) collective-permute-start(bf16[512,768]{1,0:T(8,128)(2,1)S(1)} %get-tuple-element.35), channel_id=1, source_target_pairs={{0,64},{64,0},{128,192},{192,128},{256,320},{320,256},{384,448},{4... | collective-permute-start | bytes 2359304 | tf_op jit(solution)/shard_map/cond/branch_1_fun/ppermute | solution.py:58
  121.8 5.7 %all-to-all-done.1 = bf16[8,64,768]{2,1,0:T(8,128)(2,1)S(1)} async-done(((bf16[8,64,768]{2,1,0:T(8,128)(2,1)}), bf16[8,64,768]{2,1,0:T(8,128)(2,1)S(1)}, u32[]{:S(2)}, u32[]{:S(2)}) %all-to-all-start.1) | async-done | bytes 786464 | tf_op jit(solution)/shard_map/cond/branch_1_fun/all_to_all | solution.py:34
  127.5 0.6 fusion.2
  128.1 2.6 %add_convert_fusion = bf16[512,768]{1,0:T(8,128)(2,1)} fusion(f32[512,768]{1,0:T(8,128)S(1)} %fusion.2, bf16[768,384]{1,0:T(8,128)(2,1)} %get-tuple-element.37, bf16[512,768]{1,0:T(8,128)(2,1)S(1)} %bitcast.83), kind=kOutput, calls=%fused_computation.6 | convolution fusion | flops 302776320 | bytes 3342336 | tf_op jit(solution)/shard_map/cond/branch_1_fun/dot_general | solution.py:23
  130.6 6.0 %all-to-all-start.2 = ((bf16[8,64,768]{2,1,0:T(8,128)(2,1)}), bf16[8,64,768]{2,1,0:T(8,128)(2,1)S(1)}, u32[]{:S(2)}, u32[]{:S(2)}) async-start(bf16[8,64,768]{2,1,0:T(8,128)(2,1)} %bitcast.89), calls=%async_computation.2 | async-start | bytes 1572864 | tf_op jit(solution)/shard_map/cond/branch_1_fun/all_to_all | solution.py:34
  136.7 1.9 %collective-permute-start.2 = (bf16[512,384]{1,0:T(8,128)(2,1)S(1)}, bf16[512,384]{1,0:T(8,128)(2,1)S(1)}, u32[]{:S(2)}, u32[]{:S(2)}) collective-permute-start(bf16[512,384]{1,0:T(8,128)(2,1)S(1)} %slice.103), channel_id=1, source_target_pairs={{0,64},{64,0},{128,192},{192,128},{256,320},{320,256},{384,448},{4... | collective-permute-start | bytes 1179656 | tf_op jit(solution)/shard_map/cond/branch_1_fun/ppermute | solution.py:58
  138.6 2.4 %collective-permute-start = (bf16[512,768]{1,0:T(8,128)(2,1)}, bf16[512,768]{1,0:T(8,128)(2,1)S(1)}, u32[]{:S(2)}, u32[]{:S(2)}) collective-permute-start(bf16[512,768]{1,0:T(8,128)(2,1)} %get-tuple-element.32), channel_id=1, source_target_pairs={{0,64},{64,0},{128,192},{192,128},{256,320},{320,256},{384,448},{4... | collective-permute-start | bytes 2359304 | tf_op jit(solution)/shard_map/cond/branch_1_fun/ppermute | solution.py:58
  141.0 0.5 fusion
  141.6 1.9 %collective-permute-start.1 = (bf16[512,384]{1,0:T(8,128)(2,1)S(1)}, bf16[512,384]{1,0:T(8,128)(2,1)S(1)}, u32[]{:S(2)}, u32[]{:S(2)}) collective-permute-start(bf16[512,384]{1,0:T(8,128)(2,1)S(1)} %slice.177), channel_id=1, source_target_pairs={{0,64},{64,0},{128,192},{192,128},{256,320},{320,256},{384,448},{4... | collective-permute-start | bytes 1179656 | tf_op jit(solution)/shard_map/cond/branch_1_fun/ppermute | solution.py:58
  143.5 2.6 %convolution_add_fusion = f32[384,768]{1,0:T(8,128)} fusion(f32[384,768]{1,0:T(8,128)S(1)} %fusion, bf16[512,384]{1,0:T(8,128)(2,1)S(1)} %collective-permute-done.2, bf16[512,768]{1,0:T(8,128)(2,1)} %collective-permute-done.3), kind=kOutput, calls=%fused_computation.7 | convolution fusion | flops 302284800 | bytes 3538944 | tf_op jit(solution)/shard_map/cond/branch_1_fun/dot_general | solution.py:23
  146.2 1.7 fusion.4
  147.9 1.6 convolution_add_fusion.1
  149.5 9.7 %all-to-all-done.2 = bf16[8,64,768]{2,1,0:T(8,128)(2,1)S(1)} async-done(((bf16[8,64,768]{2,1,0:T(8,128)(2,1)}), bf16[8,64,768]{2,1,0:T(8,128)(2,1)S(1)}, u32[]{:S(2)}, u32[]{:S(2)}) %all-to-all-start.2) | async-done | bytes 786464 | tf_op jit(solution)/shard_map/cond/branch_1_fun/all_to_all | solution.py:34
  159.4 0.9 pad_maximum_fusion.4
  160.3 16.8 %all_to_all.34 = bf16[4,32,768]{2,1,0:T(8,128)(2,1)S(1)} all-to-all(bf16[4,32,768]{2,1,0:T(8,128)(2,1)S(1)} %pad_maximum_fusion.4), channel_id=1, replica_groups={{0,128,256,384},{64,192,320,448},{1,129,257,385},{65,193,321,449},{2,13..., dimensions={0} | all-to-all | bytes 393216 | tf_op jit(solution)/shard_map/all_to_all | solution.py:34
  177.1 0.7 fusion.32
  (37 shorter events, 0.6 us)
Async XLA Ops:
  7.2 26.6 %copy-start.2 = (bf16[768,384]{1,0:T(8,128)(2,1)S(1)}, bf16[768,384]{1,0:T(8,128)(2,1)}, u32[]{:S(2)}) copy-start(bf16[768,384]{1,0:T(8,128)(2,1)} %param.10) | copy-start | bytes 1769476
  12.1 20.2 %all-to-all-start.3 = ((bf16[4,32,768]{2,1,0:T(8,128)(2,1)}), bf16[4,32,768]{2,1,0:T(8,128)(2,1)S(1)}, u32[]{:S(2)}, u32[]{:S(2)}) async-start(bf16[4,32,768]{2,1,0:T(8,128)(2,1)} %broadcast_in_dim.20), calls=%async_computation.3 | async-start | bytes 393216 | tf_op jit(solution)/shard_map/all_to_all | solution.py:34
  22.4 64.3 %all-gather.3.cloned.1.call-start = ((), (), s32[]{:S(2)}) async-start(), calls=%async_computation.9 | async-start | bytes 1327104 | tf_op jit(solution)/shard_map/all_gather | solution.py:82
  22.4 11.3 %collective-permute-start.4 = (bf16[768,384]{1,0:T(8,128)(2,1)}, bf16[768,384]{1,0:T(8,128)(2,1)}, u32[]{:S(2)}, u32[]{:S(2)}) collective-permute-start(bf16[768,384]{1,0:T(8,128)(2,1)} %param.10), channel_id=1, source_target_pairs={{0,64},{64,0},{128,192},{192,128},{256,320},{320,256},{384,448},{4... | collective-permute-start | bytes 1769480 | tf_op jit(solution)/shard_map/ppermute | solution.py:58
  70.5 8.4 %copy-start = (bf16[384,768]{1,0:T(8,128)(2,1)S(1)}, bf16[384,768]{1,0:T(8,128)(2,1)}, u32[]{:S(2)}) copy-start(bf16[384,768]{1,0:T(8,128)(2,1)} %param.11) | copy-start | bytes 1769476
  71.7 14.8 %all-to-all-start.4 = ((bf16[8,64,768]{2,1,0:T(8,128)(2,1)}), bf16[8,64,768]{2,1,0:T(8,128)(2,1)S(1)}, u32[]{:S(2)}, u32[]{:S(2)}) async-start(bf16[8,64,768]{2,1,0:T(8,128)(2,1)} %bitcast.8), calls=%async_computation.4 | async-start | bytes 1572864 | tf_op jit(solution)/shard_map/all_to_all | solution.py:34
  78.9 80.4 %reduce-scatter.2.cloned.1.call-start = ((), (), s32[]{:S(2)}) async-start(), calls=%async_computation.8 | async-start | bytes 884736 | tf_op jit(solution)/shard_map/reduce_scatter | solution.py:112
  78.9 9.5 %collective-permute-start.5 = (bf16[384,768]{1,0:T(8,128)(2,1)S(1)}, bf16[384,768]{1,0:T(8,128)(2,1)S(1)}, u32[]{:S(2)}, u32[]{:S(2)}) collective-permute-start(bf16[384,768]{1,0:T(8,128)(2,1)S(1)} %copy-done), channel_id=1, source_target_pairs={{0,64},{64,0},{128,192},{192,128},{256,320},{320,256},{384,448},{4... | collective-permute-start | bytes 1769480 | tf_op jit(solution)/shard_map/ppermute | solution.py:58
  88.4 0.8 copy-start.4
  109.7 1.1 copy-start.1
  109.7 1.6 copy-start.5
  113.1 64.0 %copy-start.6 = (bf16[1,16,768]{2,1,0:T(8,128)(2,1)S(1)}, bf16[1,16,768]{2,1,0:T(8,128)(2,1)}, u32[]{:S(2)}) copy-start(bf16[1,16,768]{2,1,0:T(8,128)(2,1)} %param.12) | copy-start | bytes 73732
  113.1 64.0 %copy-start.7 = (bf16[1,16,768]{2,1,0:T(8,128)(2,1)S(1)}, bf16[1,16,768]{2,1,0:T(8,128)(2,1)}, u32[]{:S(2)}) copy-start(bf16[1,16,768]{2,1,0:T(8,128)(2,1)} %param.9) | copy-start | bytes 73732
  113.1 14.4 %copy-start.3 = (bf16[768,384]{1,0:T(8,128)(2,1)S(1)}, bf16[768,384]{1,0:T(8,128)(2,1)}, u32[]{:S(2)}) copy-start(bf16[768,384]{1,0:T(8,128)(2,1)} %get-tuple-element.36) | copy-start | bytes 1769476 | tf_op jit(solution)/shard_map/cond
  114.0 13.4 %all-to-all-start.1 = ((bf16[8,64,768]{2,1,0:T(8,128)(2,1)}), bf16[8,64,768]{2,1,0:T(8,128)(2,1)S(1)}, u32[]{:S(2)}, u32[]{:S(2)}) async-start(bf16[8,64,768]{2,1,0:T(8,128)(2,1)} %broadcast_in_dim.14), calls=%async_computation.1 | async-start | bytes 1572864 | tf_op jit(solution)/shard_map/cond/branch_1_fun/all_to_all | solution.py:34
  119.9 23.6 %collective-permute-start.3 = (bf16[512,768]{1,0:T(8,128)(2,1)S(1)}, bf16[512,768]{1,0:T(8,128)(2,1)}, u32[]{:S(2)}, u32[]{:S(2)}) collective-permute-start(bf16[512,768]{1,0:T(8,128)(2,1)S(1)} %get-tuple-element.35), channel_id=1, source_target_pairs={{0,64},{64,0},{128,192},{192,128},{256,320},{320,256},{384,448},{4... | collective-permute-start | bytes 2359304 | tf_op jit(solution)/shard_map/cond/branch_1_fun/ppermute | solution.py:58
  130.6 28.6 %all-to-all-start.2 = ((bf16[8,64,768]{2,1,0:T(8,128)(2,1)}), bf16[8,64,768]{2,1,0:T(8,128)(2,1)S(1)}, u32[]{:S(2)}, u32[]{:S(2)}) async-start(bf16[8,64,768]{2,1,0:T(8,128)(2,1)} %bitcast.89), calls=%async_computation.2 | async-start | bytes 1572864 | tf_op jit(solution)/shard_map/cond/branch_1_fun/all_to_all | solution.py:34
  136.7 6.8 %collective-permute-start.2 = (bf16[512,384]{1,0:T(8,128)(2,1)S(1)}, bf16[512,384]{1,0:T(8,128)(2,1)S(1)}, u32[]{:S(2)}, u32[]{:S(2)}) collective-permute-start(bf16[512,384]{1,0:T(8,128)(2,1)S(1)} %slice.103), channel_id=1, source_target_pairs={{0,64},{64,0},{128,192},{192,128},{256,320},{320,256},{384,448},{4... | collective-permute-start | bytes 1179656 | tf_op jit(solution)/shard_map/cond/branch_1_fun/ppermute | solution.py:58
  138.6 9.3 %collective-permute-start = (bf16[512,768]{1,0:T(8,128)(2,1)}, bf16[512,768]{1,0:T(8,128)(2,1)S(1)}, u32[]{:S(2)}, u32[]{:S(2)}) collective-permute-start(bf16[512,768]{1,0:T(8,128)(2,1)} %get-tuple-element.32), channel_id=1, source_target_pairs={{0,64},{64,0},{128,192},{192,128},{256,320},{320,256},{384,448},{4... | collective-permute-start | bytes 2359304 | tf_op jit(solution)/shard_map/cond/branch_1_fun/ppermute | solution.py:58
  141.6 6.3 %collective-permute-start.1 = (bf16[512,384]{1,0:T(8,128)(2,1)S(1)}, bf16[512,384]{1,0:T(8,128)(2,1)S(1)}, u32[]{:S(2)}, u32[]{:S(2)}) collective-permute-start(bf16[512,384]{1,0:T(8,128)(2,1)S(1)} %slice.177), channel_id=1, source_target_pairs={{0,64},{64,0},{128,192},{192,128},{256,320},{320,256},{384,448},{4... | collective-permute-start | bytes 1179656 | tf_op jit(solution)/shard_map/cond/branch_1_fun/ppermute | solution.py:58
Sparse Core Ops, SparseCore 0:
  33.2 44.2 all-gather.2
  113.2 42.6 reduce-scatter.1

commit v5 on v3

v5 whole, which is shorter than its diff:
```python
import jax
import jax.numpy as jnp
from jax import lax
from jax.sharding import PartitionSpec as P

MBT = 32
CORES = 2

root_coef = 0.7978845608028654
cubic_coef = 0.044715


def gelu_both(values):
    inner = root_coef * (values + cubic_coef * values * values * values)
    tangent = jnp.tanh(inner)
    slope = 0.5 * (1.0 + tangent) + 0.5 * values * (1.0 - tangent * tangent) * root_coef * (
        1.0 + 3.0 * cubic_coef * values * values
    )
    return 0.5 * values * (1.0 + tangent), slope


def product(left, right, left_dim, right_dim):
    return lax.dot_general(
        left, right, (((left_dim,), (right_dim,)), ((), ())), preferred_element_type=jnp.float32
    )


def cut(value, pieces):
    rows, width = value.shape
    return value.reshape(pieces, rows // pieces, width)


def swapped(value, axis):
    return lax.all_to_all(value, axis, 0, 0, tiled=True)


def added_up(pieces):
    total = pieces[0].astype(jnp.float32)
    for at in range(1, len(pieces)):
        total = total + pieces[at].astype(jnp.float32)
    return total


def spread(value, axis, size):
    return swapped(jnp.broadcast_to(value[None], (size, *value.shape)), axis)


def body(inputs, w_in, w_out, cotangent, counts):
    rows_local = inputs.shape[1]
    width = inputs.shape[2]
    units = w_in.shape[1]
    replicas = lax.axis_size("rep")
    columns = lax.axis_size("col")
    row_count = lax.axis_size("row")
    chips = replicas // CORES
    to_mate = [(r, r // CORES * CORES + (r + 1) % CORES) for r in range(replicas)]
    mate = lambda value: lax.ppermute(value, "rep", to_mate)

    tokens_local = inputs.reshape(rows_local, width)
    replica_index = lax.axis_index("rep")
    column_index = lax.axis_index("col")
    own_count = jnp.sum(jnp.where(jnp.arange(replicas) == replica_index, counts, 0))
    token_total = (MBT * jnp.sum(counts)).astype(jnp.float32)
    positions = column_index * rows_local + jnp.arange(rows_local, dtype=jnp.int32)
    kept_mask = (positions // MBT < own_count).astype(jnp.float32)
    scaled = (
        cotangent.reshape(rows_local, width).astype(jnp.float32)
        * kept_mask[:, None]
        / token_total
    ).astype(jnp.bfloat16)

    w_in_mate, w_out_mate = mate(w_in), mate(w_out)

    onward = lambda value, k: lax.ppermute(
        value, "rep", [(r, (r + k * CORES) % replicas) for r in range(replicas)]
    )
    scaled_ring = spread(scaled, "col", columns)
    tokens_line = jnp.stack([tokens_local] + [onward(tokens_local, k) for k in range(1, chips)])
    rows_all = columns * chips * rows_local
    tokens_all = spread(tokens_line.reshape(-1, width), "col", columns).reshape(rows_all, width)
    scaled_all = jnp.stack(
        [scaled_ring] + [onward(scaled_ring, k) for k in range(1, chips)], axis=1
    ).reshape(rows_all, width)

    def pair(left, rights, right_dim):
        return [product(left, w, 1, right_dim).astype(jnp.bfloat16) for w in rights]

    terms = jnp.concatenate(
        pair(tokens_all, (w_in, w_in_mate), 0) + pair(scaled_all, (w_out, w_out_mate), 1), axis=1
    )
    sums = added_up(swapped(cut(terms, row_count), "row"))
    active, slope = gelu_both(sums[:, : 2 * units])
    shares = jnp.concatenate(
        [active.astype(jnp.bfloat16), (sums[:, 2 * units :] * slope).astype(jnp.bfloat16)], axis=1
    )
    shares_all = spread(shares, "row", row_count).reshape(rows_all, 4 * units)
    active_own, active_other, grad_own, grad_other = [
        shares_all[:, at * units : (at + 1) * units] for at in range(4)
    ]

    back_terms = (
        product(grad_own, w_in, 1, 1) + product(grad_other, w_in_mate, 1, 1)
    ).astype(jnp.bfloat16)
    output_terms = (
        product(active_own, w_out, 1, 0) + product(active_other, w_out_mate, 1, 0)
    ).astype(jnp.bfloat16)

    output_line = added_up(swapped(cut(output_terms, columns), "col")).astype(jnp.bfloat16)
    back_blocks = back_terms.reshape(columns, chips, rows_local, width)
    back_ring = added_up(
        [back_blocks[:, 0]] + [onward(back_blocks[:, k], chips - k) for k in range(1, chips)]
    ).astype(jnp.bfloat16)
    output_blocks = output_line.reshape(chips, rows_local, width)
    mixed = added_up(
        [output_blocks[0]] + [onward(output_blocks[k], chips - k) for k in range(1, chips)]
    )
    back = added_up(swapped(back_ring, "col"))
    block_output = (tokens_local.astype(jnp.float32) + mixed).astype(jnp.bfloat16)
    input_grad = (scaled.astype(jnp.float32) + back).astype(jnp.bfloat16)

    w_in_grad = product(tokens_all, grad_own, 0, 0) + product(
        mate(tokens_all), mate(grad_other), 0, 0
    )
    w_out_grad = product(active_own, scaled_all, 0, 0) + product(
        mate(active_other), mate(scaled_all), 0, 0
    )
    return (
        block_output.reshape(1, rows_local, width),
        input_grad.reshape(1, rows_local, width),
        w_in_grad,
        w_out_grad,
    )


def solution(mesh):
    placed = (
        P("rep", "col", "row"),
        P("row", ("rep", "col")),
        P(("rep", "col"), "row"),
        P("rep", "col", "row"),
        P(),
    )
    return jax.shard_map(
        body,
        mesh=mesh,
        in_specs=placed,
        out_specs=(
            P("rep", "col", "row"),
            P("rep", "col", "row"),
            P("row", ("rep", "col")),
            P(("rep", "col"), "row"),
        ),
        check_vma=False,
    )
```

time: 207 us -> 200 us (0.966)
  waiting for transfers between devices: 85.1 us -> 28.2 us
  starting transfers between devices: 53.1 us -> 108 us
  between operations: 15 us -> 1.72 us
  blocking collectives: 20.5 us -> 28.8 us
  local copies, waits for them, and re-layouts: 9.62 us -> 5.78 us
  other arithmetic: 6.19 us -> 8.37 us
    ppermute x0 -> x12, starting transfers between devices: none -> 61.4 us  [body(): lax.ppermute(value, 'rep', [(r, (r + k * CORES) % replicas) for r in rang...]
    all_to_all x7 -> x5, waiting for transfers between devices: 43.4 us -> 15.4 us  [swapped(): return lax.all_to_all(value, axis, 0, 0, tiled=True)]
    reduce_scatter x1 -> x0, waiting for transfers between devices: 27.2 us -> none  [body(): lax.psum_scatter(output_terms, 'col', scatter_dimension=0, tiled=True)]
    all_gather x1 -> x0, waiting for transfers between devices: 13.4 us -> none  [body(): lax.all_gather(padded, 'col', axis=0)[:, :line_rows]]
    ppermute x0 -> x12, waiting for transfers between devices: none -> 12.8 us  [body(): lax.ppermute(value, 'rep', [(r, (r + k * CORES) % replicas) for r in rang...]
    all_to_all x1, blocking collectives: 20.5 us -> 28.8 us  [swapped(): return lax.all_to_all(value, axis, 0, 0, tiled=True)]
    all_to_all x7 -> x5, starting transfers between devices: 40.6 us -> 34.5 us  [swapped(): return lax.all_to_all(value, axis, 0, 0, tiled=True)]
    slice x5 -> x2, local copies, waits for them, and re-layouts: 2.92 us -> 0.09 us  [the longest x1 0.08 us: body(): shares_all[:, at * units:(at + 1) * units]]
  transfers between devices with their start and end apart: 15 -> 23, of which waited for: 8 -> 6; matrix products, arithmetic and copies ran while one was open for 11% -> 10% of each run, Pallas kernels for 0% -> 0%
where the time goes in v5:
time: 200 us; the launch traced here: 198 us
  starting transfers between devices  108 us (54%)
  blocking collectives  28.8 us (14%)
  waiting for transfers between devices  28.2 us (14%)
  matrix products  16.2 us (8%)
  other arithmetic  8.37 us (4%)
  local copies, waits for them, and re-layouts  5.78 us (3%)
    ppermute x12, starting transfers between devices, body(): lax.ppermute(value, 'rep', [(r, (r + k * CORES) % replicas) for r in rang...  61.4 us
    all_to_all x5, starting transfers between devices, swapped(): return lax.all_to_all(value, axis, 0, 0, tiled=True)  34.5 us
    all_to_all x1, blocking collectives, swapped(): return lax.all_to_all(value, axis, 0, 0, tiled=True)  28.8 us
    dot_general x12, matrix products, product(): lax.dot_general(left, right, (((left_dim,), (right_dim,)), ((), ())), pre...  16.2 us
    all_to_all x5, waiting for transfers between devices, swapped(): return lax.all_to_all(value, axis, 0, 0, tiled=True)  15.4 us
    ppermute x12, waiting for transfers between devices, body(): lax.ppermute(value, 'rep', [(r, (r + k * CORES) % replicas) for r in rang...  12.8 us
    ppermute x6, starting transfers between devices, body(): mate = lambda value: lax.ppermute(value, 'rep', to_mate)  12.5 us
  transfers between devices with their start and end apart: 23, of which 6 were waited for; matrix products, arithmetic and copies ran while one was open for 10% of the time, Pallas kernels for 0%

profile of v5, /device:TPU:6, one launch (start us, length us, event | category | flops | bytes accessed | tf_op | source)
XLA Modules:
  0.0 197.5 jit_solution(6322994513018017419)
XLA Ops:
  0.6 1.3 fusion.22
  3.3 0.8 fusion.23
  4.8 7.2 %all-to-all-start.1 = ((bf16[8,16,768]{2,1,0:T(8,128)(2,1)}), bf16[8,16,768]{2,1,0:T(8,128)(2,1)S(1)}, u32[]{:S(2)}, u32[]{:S(2)}) async-start(bf16[8,16,768]{2,1,0:T(8,128)(2,1)} %broadcast_in_dim.30), calls=%async_computation.1 | async-start | bytes 393216 | tf_op jit(solution)/shard_map/all_to_all | solution.py:34
  12.0 10.9 %collective-permute-start.2 = (bf16[16,768]{1,0:T(8,128)(2,1)}, bf16[16,768]{1,0:T(8,128)(2,1)S(1)}, u32[]{:S(2)}, u32[]{:S(2)}) collective-permute-start(bf16[16,768]{1,0:T(8,128)(2,1)} %bitcast.96), channel_id=1, source_target_pairs={{0,384},{64,448},{128,0},{192,64},{256,128},{320,192},{384,256},{4... | collective-permute-start | bytes 73736 | tf_op jit(solution)/shard_map/ppermute | solution.py:74
  22.9 1.9 collective-permute-start.1
  24.9 4.8 %collective-permute-start = (bf16[16,768]{1,0:T(8,128)(2,1)}, bf16[16,768]{1,0:T(8,128)(2,1)S(1)}, u32[]{:S(2)}, u32[]{:S(2)}) collective-permute-start(bf16[16,768]{1,0:T(8,128)(2,1)} %bitcast.98), channel_id=1, source_target_pairs={{0,128},{64,192},{128,256},{192,320},{256,384},{320,448},{384,0},{... | collective-permute-start | bytes 73736 | tf_op jit(solution)/shard_map/ppermute | solution.py:74
  29.7 3.6 %collective-permute-done.1 = bf16[16,768]{1,0:T(8,128)(2,1)S(1)} collective-permute-done((bf16[16,768]{1,0:T(8,128)(2,1)}, bf16[16,768]{1,0:T(8,128)(2,1)S(1)}, u32[]{:S(2)}, u32[]{:S(2)}) %collective-permute-start.1) | collective-permute-done | bytes 24608 | tf_op jit(solution)/shard_map/ppermute | solution.py:74
  33.3 0.8 pad_maximum_fusion.3
  34.1 0.9 broadcast_in_dim.27
  35.0 7.2 %all-to-all-start = ((bf16[8,64,768]{2,1,0:T(8,128)(2,1)}), bf16[8,64,768]{2,1,0:T(8,128)(2,1)S(1)}, u32[]{:S(2)}, u32[]{:S(2)}) async-start(bf16[8,64,768]{2,1,0:T(8,128)(2,1)} %broadcast_in_dim.27), calls=%async_computation | async-start | bytes 1572864 | tf_op jit(solution)/shard_map/all_to_all | solution.py:34
  42.3 3.8 %collective-permute-start.6 = (bf16[8,16,768]{2,1,0:T(8,128)(2,1)S(1)}, bf16[8,16,768]{2,1,0:T(8,128)(2,1)S(1)}, u32[]{:S(2)}, u32[]{:S(2)}) collective-permute-start(bf16[8,16,768]{2,1,0:T(8,128)(2,1)S(1)} %all-to-all-done.1), channel_id=1, source_target_pairs={{0,384},{64,448},{128,0},{192,64},{256,128},{320,192},{384,256},{4... | collective-permute-start | bytes 589832 | tf_op jit(solution)/shard_map/ppermute | solution.py:74
  46.1 5.5 %collective-permute-start.5 = (bf16[8,16,768]{2,1,0:T(8,128)(2,1)S(1)}, bf16[8,16,768]{2,1,0:T(8,128)(2,1)S(1)}, u32[]{:S(2)}, u32[]{:S(2)}) collective-permute-start(bf16[8,16,768]{2,1,0:T(8,128)(2,1)S(1)} %all-to-all-done.1), channel_id=1, source_target_pairs={{0,256},{64,320},{128,384},{192,448},{256,0},{320,64},{384,128},{4... | collective-permute-start | bytes 589832 | tf_op jit(solution)/shard_map/ppermute | solution.py:74
  51.6 4.8 %collective-permute-start.4 = (bf16[8,16,768]{2,1,0:T(8,128)(2,1)S(1)}, bf16[8,16,768]{2,1,0:T(8,128)(2,1)S(1)}, u32[]{:S(2)}, u32[]{:S(2)}) collective-permute-start(bf16[8,16,768]{2,1,0:T(8,128)(2,1)S(1)} %all-to-all-done.1), channel_id=1, source_target_pairs={{0,128},{64,192},{128,256},{192,320},{256,384},{320,448},{384,0},{... | collective-permute-start | bytes 589832 | tf_op jit(solution)/shard_map/ppermute | solution.py:74
  56.4 1.9 collective-permute-start.7
  58.4 2.4 %collective-permute-start.3 = (bf16[768,384]{1,0:T(8,128)(2,1)S(1)}, bf16[768,384]{1,0:T(8,128)(2,1)S(1)}, u32[]{:S(2)}, u32[]{:S(2)}) collective-permute-start(bf16[768,384]{1,0:T(8,128)(2,1)S(1)} %copy-done.4), channel_id=1, source_target_pairs={{0,64},{64,0},{128,192},{192,128},{256,320},{320,256},{384,448},{4... | collective-permute-start | bytes 1769480 | tf_op jit(solution)/shard_map/ppermute | solution.py:57
  60.8 1.0 collective-permute-done.5
  61.8 1.3 collective-permute-done.4
  63.1 1.0 pad_maximum_fusion.1
  64.0 1.6 convolution_convert_fusion.1
  65.7 0.8 copy-done.6
  66.5 1.6 convolution_convert_fusion
  69.0 0.8 copy-done.5
  71.2 28.8 %all_to_all.30 = bf16[8,64,1536]{2,1,0:T(8,128)(2,1)S(1)} all-to-all(bf16[8,64,1536]{2,1,0:T(8,128)(2,1)S(1)} %bitcast.83), channel_id=1, replica_groups=mesh['rep'=8,'row'=8,'col'=8] {'row'}, dimensions={0} | all-to-all | bytes 3145728 | tf_op jit(solution)/shard_map/all_to_all | solution.py:34
  100.4 1.3 broadcast_in_dim.31
  101.7 6.0 %all-to-all-start.3 = ((bf16[8,64,1536]{2,1,0:T(8,128)(2,1)}), bf16[8,64,1536]{2,1,0:T(8,128)(2,1)S(1)}, u32[]{:S(2)}, u32[]{:S(2)}) async-start(bf16[8,64,1536]{2,1,0:T(8,128)(2,1)} %broadcast_in_dim.31), calls=%async_computation.3 | async-start | bytes 3145728 | tf_op jit(solution)/shard_map/all_to_all | solution.py:34
  107.8 1.9 collective-permute-start.17
  109.7 15.4 %all-to-all-done.3 = bf16[8,64,1536]{2,1,0:T(8,128)(2,1)S(1)} async-done(((bf16[8,64,1536]{2,1,0:T(8,128)(2,1)}), bf16[8,64,1536]{2,1,0:T(8,128)(2,1)S(1)}, u32[]{:S(2)}, u32[]{:S(2)}) %all-to-all-start.3) | async-done | bytes 1572896 | tf_op jit(solution)/shard_map/all_to_all | solution.py:34
  125.6 1.7 fusion.5
  127.4 1.5 add_convert_fusion.1
  128.8 6.9 %all-to-all-start.4 = ((bf16[8,64,768]{2,1,0:T(8,128)(2,1)}), bf16[8,64,768]{2,1,0:T(8,128)(2,1)}, u32[]{:S(2)}, u32[]{:S(2)}) async-start(bf16[8,64,768]{2,1,0:T(8,128)(2,1)} %bitcast.88), calls=%async_computation.4 | async-start | bytes 1572864 | tf_op jit(solution)/shard_map/all_to_all | solution.py:34
  135.8 1.7 add_convert_fusion
  137.5 4.1 %collective-permute-start.13 = (bf16[8,16,768]{2,1,0:T(8,128)(2,1)S(1)}, bf16[8,16,768]{2,1,0:T(8,128)(2,1)S(1)}, u32[]{:S(2)}, u32[]{:S(2)}) collective-permute-start(bf16[8,16,768]{2,1,0:T(8,128)(2,1)S(1)} %get-tuple-element.10), channel_id=1, source_target_pairs={{0,128},{64,192},{128,256},{192,320},{256,384},{320,448},{384,0},{... | collective-permute-start | bytes 589832 | tf_op jit(solution)/shard_map/ppermute | solution.py:74
  141.6 4.9 %collective-permute-start.12 = (bf16[8,16,768]{2,1,0:T(8,128)(2,1)S(1)}, bf16[8,16,768]{2,1,0:T(8,128)(2,1)S(1)}, u32[]{:S(2)}, u32[]{:S(2)}) collective-permute-start(bf16[8,16,768]{2,1,0:T(8,128)(2,1)S(1)} %get-tuple-element.9), channel_id=1, source_target_pairs={{0,256},{64,320},{128,384},{192,448},{256,0},{320,64},{384,128},{4... | collective-permute-start | bytes 589832 | tf_op jit(solution)/shard_map/ppermute | solution.py:74
  146.5 6.0 %collective-permute-start.11 = (bf16[8,16,768]{2,1,0:T(8,128)(2,1)S(1)}, bf16[8,16,768]{2,1,0:T(8,128)(2,1)S(1)}, u32[]{:S(2)}, u32[]{:S(2)}) collective-permute-start(bf16[8,16,768]{2,1,0:T(8,128)(2,1)S(1)} %get-tuple-element.8), channel_id=1, source_target_pairs={{0,384},{64,448},{128,0},{192,64},{256,128},{320,192},{384,256},{4... | collective-permute-start | bytes 589832 | tf_op jit(solution)/shard_map/ppermute | solution.py:74
  152.6 1.9 collective-permute-start.16
  155.2 2.4 %collective-permute-start.14 = (bf16[512,768]{1,0:T(8,128)(2,1)S(1)}, bf16[512,768]{1,0:T(8,128)(2,1)S(1)}, u32[]{:S(2)}, u32[]{:S(2)}) collective-permute-start(bf16[512,768]{1,0:T(8,128)(2,1)S(1)} %bitcast.87), channel_id=1, source_target_pairs={{0,64},{64,0},{128,192},{192,128},{256,320},{320,256},{384,448},{4... | collective-permute-start | bytes 2359304 | tf_op jit(solution)/shard_map/ppermute | solution.py:57
  157.6 1.9 collective-permute-start.15
  159.6 6.2 %collective-permute-done.11 = bf16[8,16,768]{2,1,0:T(8,128)(2,1)S(1)} collective-permute-done((bf16[8,16,768]{2,1,0:T(8,128)(2,1)S(1)}, bf16[8,16,768]{2,1,0:T(8,128)(2,1)S(1)}, u32[]{:S(2)}, u32[]{:S(2)}) %collective-permute-start.11) | collective-permute-done | bytes 196640 | tf_op jit(solution)/shard_map/ppermute | solution.py:74
  165.7 0.8 fusion.2
  166.5 1.6 fusion.27
  168.2 2.7 %convolution_add_fusion = f32[384,768]{1,0:T(8,128)} fusion(f32[384,768]{1,0:T(8,128)S(1)} %fusion.27, bf16[512,768]{1,0:T(8,128)(2,1)} %bitcast.14, bf16[512,1536]{1,0:T(8,128)(2,1)S(1)} %bitcast.82), kind=kOutput, calls=%fused_computation.3 | convolution fusion | flops 302284800 | bytes 3538944 | tf_op jit(solution)/shard_map/dot_general | solution.py:23
  170.8 1.6 convolution_add_fusion.1
  172.4 7.0 %all-to-all-start.5 = ((bf16[8,16,768]{2,1,0:T(8,128)(2,1)}), bf16[8,16,768]{2,1,0:T(8,128)(2,1)S(1)}, u32[]{:S(2)}, u32[]{:S(2)}) async-start(bf16[8,16,768]{2,1,0:T(8,128)(2,1)} %fusion.2), calls=%async_computation.5 | async-start | bytes 393216 | tf_op jit(solution)/shard_map/all_to_all | solution.py:34
  179.5 1.3 add_convert_fusion.2
  180.8 3.9 %collective-permute-start.10 = (bf16[16,768]{1,0:T(8,128)(2,1)S(1)}, bf16[16,768]{1,0:T(8,128)(2,1)S(1)}, u32[]{:S(2)}, u32[]{:S(2)}) collective-permute-start(bf16[16,768]{1,0:T(8,128)(2,1)S(1)} %get-tuple-element.15), channel_id=1, source_target_pairs={{0,128},{64,192},{128,256},{192,320},{256,384},{320,448},{384,0},{... | collective-permute-start | bytes 73736 | tf_op jit(solution)/shard_map/ppermute | solution.py:74
  184.7 5.3 %collective-permute-start.9 = (bf16[16,768]{1,0:T(8,128)(2,1)S(1)}, bf16[16,768]{1,0:T(8,128)(2,1)S(1)}, u32[]{:S(2)}, u32[]{:S(2)}) collective-permute-start(bf16[16,768]{1,0:T(8,128)(2,1)S(1)} %get-tuple-element.14), channel_id=1, source_target_pairs={{0,256},{64,320},{128,384},{192,448},{256,0},{320,64},{384,128},{4... | collective-permute-start | bytes 73736 | tf_op jit(solution)/shard_map/ppermute | solution.py:74
  190.0 5.4 %collective-permute-start.8 = (bf16[16,768]{1,0:T(8,128)(2,1)S(1)}, bf16[16,768]{1,0:T(8,128)(2,1)S(1)}, u32[]{:S(2)}, u32[]{:S(2)}) collective-permute-start(bf16[16,768]{1,0:T(8,128)(2,1)S(1)} %get-tuple-element.13), channel_id=1, source_target_pairs={{0,384},{64,448},{128,0},{192,64},{256,128},{320,192},{384,256},{4... | collective-permute-start | bytes 73736 | tf_op jit(solution)/shard_map/ppermute | solution.py:74
  196.1 0.8 collective-permute-done.8
  (51 shorter events, 6.6 us)
Async XLA Ops:
  4.8 51.7 %copy-start.2 = (bf16[384,768]{1,0:T(8,128)(2,1)S(1)}, bf16[384,768]{1,0:T(8,128)(2,1)}, u32[]{:S(2)}) copy-start(bf16[384,768]{1,0:T(8,128)(2,1)} %param.7) | copy-start | bytes 1769476
  4.8 53.6 %copy-start.4 = (bf16[768,384]{1,0:T(8,128)(2,1)S(1)}, bf16[768,384]{1,0:T(8,128)(2,1)}, u32[]{:S(2)}) copy-start(bf16[768,384]{1,0:T(8,128)(2,1)} %param.6) | copy-start | bytes 1769476
  4.8 29.3 %all-to-all-start.1 = ((bf16[8,16,768]{2,1,0:T(8,128)(2,1)}), bf16[8,16,768]{2,1,0:T(8,128)(2,1)S(1)}, u32[]{:S(2)}, u32[]{:S(2)}) async-start(bf16[8,16,768]{2,1,0:T(8,128)(2,1)} %broadcast_in_dim.30), calls=%async_computation.1 | async-start | bytes 393216 | tf_op jit(solution)/shard_map/all_to_all | solution.py:34
  12.0 17.7 %collective-permute-start.2 = (bf16[16,768]{1,0:T(8,128)(2,1)}, bf16[16,768]{1,0:T(8,128)(2,1)S(1)}, u32[]{:S(2)}, u32[]{:S(2)}) collective-permute-start(bf16[16,768]{1,0:T(8,128)(2,1)} %bitcast.96), channel_id=1, source_target_pairs={{0,384},{64,448},{128,0},{192,64},{256,128},{320,192},{384,256},{4... | collective-permute-start | bytes 73736 | tf_op jit(solution)/shard_map/ppermute | solution.py:74
  22.9 10.4 %collective-permute-start.1 = (bf16[16,768]{1,0:T(8,128)(2,1)}, bf16[16,768]{1,0:T(8,128)(2,1)S(1)}, u32[]{:S(2)}, u32[]{:S(2)}) collective-permute-start(bf16[16,768]{1,0:T(8,128)(2,1)} %bitcast.97), channel_id=1, source_target_pairs={{0,256},{64,320},{128,384},{192,448},{256,0},{320,64},{384,128},{4... | collective-permute-start | bytes 73736 | tf_op jit(solution)/shard_map/ppermute | solution.py:74
  24.9 8.4 %collective-permute-start = (bf16[16,768]{1,0:T(8,128)(2,1)}, bf16[16,768]{1,0:T(8,128)(2,1)S(1)}, u32[]{:S(2)}, u32[]{:S(2)}) collective-permute-start(bf16[16,768]{1,0:T(8,128)(2,1)} %bitcast.98), channel_id=1, source_target_pairs={{0,128},{64,192},{128,256},{192,320},{256,384},{320,448},{384,0},{... | collective-permute-start | bytes 73736 | tf_op jit(solution)/shard_map/ppermute | solution.py:74
  35.0 33.1 %all-to-all-start = ((bf16[8,64,768]{2,1,0:T(8,128)(2,1)}), bf16[8,64,768]{2,1,0:T(8,128)(2,1)S(1)}, u32[]{:S(2)}, u32[]{:S(2)}) async-start(bf16[8,64,768]{2,1,0:T(8,128)(2,1)} %broadcast_in_dim.27), calls=%async_computation | async-start | bytes 1572864 | tf_op jit(solution)/shard_map/all_to_all | solution.py:34
  42.3 18.5 %collective-permute-start.6 = (bf16[8,16,768]{2,1,0:T(8,128)(2,1)S(1)}, bf16[8,16,768]{2,1,0:T(8,128)(2,1)S(1)}, u32[]{:S(2)}, u32[]{:S(2)}) collective-permute-start(bf16[8,16,768]{2,1,0:T(8,128)(2,1)S(1)} %all-to-all-done.1), channel_id=1, source_target_pairs={{0,384},{64,448},{128,0},{192,64},{256,128},{320,192},{384,256},{4... | collective-permute-start | bytes 589832 | tf_op jit(solution)/shard_map/ppermute | solution.py:74
  46.1 15.7 %collective-permute-start.5 = (bf16[8,16,768]{2,1,0:T(8,128)(2,1)S(1)}, bf16[8,16,768]{2,1,0:T(8,128)(2,1)S(1)}, u32[]{:S(2)}, u32[]{:S(2)}) collective-permute-start(bf16[8,16,768]{2,1,0:T(8,128)(2,1)S(1)} %all-to-all-done.1), channel_id=1, source_target_pairs={{0,256},{64,320},{128,384},{192,448},{256,0},{320,64},{384,128},{4... | collective-permute-start | bytes 589832 | tf_op jit(solution)/shard_map/ppermute | solution.py:74
  51.6 11.5 %collective-permute-start.4 = (bf16[8,16,768]{2,1,0:T(8,128)(2,1)S(1)}, bf16[8,16,768]{2,1,0:T(8,128)(2,1)S(1)}, u32[]{:S(2)}, u32[]{:S(2)}) collective-permute-start(bf16[8,16,768]{2,1,0:T(8,128)(2,1)S(1)} %all-to-all-done.1), channel_id=1, source_target_pairs={{0,128},{64,192},{128,256},{192,320},{256,384},{320,448},{384,0},{... | collective-permute-start | bytes 589832 | tf_op jit(solution)/shard_map/ppermute | solution.py:74
  56.4 9.2 %collective-permute-start.7 = (bf16[384,768]{1,0:T(8,128)(2,1)S(1)}, bf16[384,768]{1,0:T(8,128)(2,1)S(1)}, u32[]{:S(2)}, u32[]{:S(2)}) collective-permute-start(bf16[384,768]{1,0:T(8,128)(2,1)S(1)} %copy-done.2), channel_id=1, source_target_pairs={{0,64},{64,0},{128,192},{192,128},{256,320},{320,256},{384,448},{4... | collective-permute-start | bytes 1769480 | tf_op jit(solution)/shard_map/ppermute | solution.py:57
  58.4 10.3 %collective-permute-start.3 = (bf16[768,384]{1,0:T(8,128)(2,1)S(1)}, bf16[768,384]{1,0:T(8,128)(2,1)S(1)}, u32[]{:S(2)}, u32[]{:S(2)}) collective-permute-start(bf16[768,384]{1,0:T(8,128)(2,1)S(1)} %copy-done.4), channel_id=1, source_target_pairs={{0,64},{64,0},{128,192},{192,128},{256,320},{320,256},{384,448},{4... | collective-permute-start | bytes 1769480 | tf_op jit(solution)/shard_map/ppermute | solution.py:57
  65.7 0.8 copy-start.6
  68.2 0.9 copy-start
  69.0 0.8 copy-start.5
  101.7 23.3 %copy-start.3 = (bf16[384,768]{1,0:T(8,128)(2,1)S(1)}, bf16[384,768]{1,0:T(8,128)(2,1)}, u32[]{:S(2)}) copy-start(bf16[384,768]{1,0:T(8,128)(2,1)} %param.7) | copy-start | bytes 1769476
  101.7 23.3 %all-to-all-start.3 = ((bf16[8,64,1536]{2,1,0:T(8,128)(2,1)}), bf16[8,64,1536]{2,1,0:T(8,128)(2,1)S(1)}, u32[]{:S(2)}, u32[]{:S(2)}) async-start(bf16[8,64,1536]{2,1,0:T(8,128)(2,1)} %broadcast_in_dim.31), calls=%async_computation.3 | async-start | bytes 3145728 | tf_op jit(solution)/shard_map/all_to_all | solution.py:34
  107.8 58.7 %collective-permute-start.17 = (bf16[512,768]{1,0:T(8,128)(2,1)}, bf16[512,768]{1,0:T(8,128)(2,1)}, u32[]{:S(2)}, u32[]{:S(2)}) collective-permute-start(bf16[512,768]{1,0:T(8,128)(2,1)} %bitcast.14), channel_id=1, source_target_pairs={{0,64},{64,0},{128,192},{192,128},{256,320},{320,256},{384,448},{4... | collective-permute-start | bytes 2359304 | tf_op jit(solution)/shard_map/ppermute | solution.py:57
  125.6 1.7 copy-start.7
  128.8 43.6 %all-to-all-start.4 = ((bf16[8,64,768]{2,1,0:T(8,128)(2,1)}), bf16[8,64,768]{2,1,0:T(8,128)(2,1)}, u32[]{:S(2)}, u32[]{:S(2)}) async-start(bf16[8,64,768]{2,1,0:T(8,128)(2,1)} %bitcast.88), calls=%async_computation.4 | async-start | bytes 1572864 | tf_op jit(solution)/shard_map/all_to_all | solution.py:34
  137.4 17.1 %copy-start.1 = (bf16[8,64,768]{2,1,0:T(8,128)(2,1)S(1)}, bf16[8,64,768]{2,1,0:T(8,128)(2,1)}, u32[]{:S(2)}) copy-start(bf16[8,64,768]{2,1,0:T(8,128)(2,1)} %copy-done) | copy-start | bytes 2359300
  137.5 17.7 %collective-permute-start.13 = (bf16[8,16,768]{2,1,0:T(8,128)(2,1)S(1)}, bf16[8,16,768]{2,1,0:T(8,128)(2,1)S(1)}, u32[]{:S(2)}, u32[]{:S(2)}) collective-permute-start(bf16[8,16,768]{2,1,0:T(8,128)(2,1)S(1)} %get-tuple-element.10), channel_id=1, source_target_pairs={{0,128},{64,192},{128,256},{192,320},{256,384},{320,448},{384,0},{... | collective-permute-start | bytes 589832 | tf_op jit(solution)/shard_map/ppermute | solution.py:74
  141.6 16.0 %collective-permute-start.12 = (bf16[8,16,768]{2,1,0:T(8,128)(2,1)S(1)}, bf16[8,16,768]{2,1,0:T(8,128)(2,1)S(1)}, u32[]{:S(2)}, u32[]{:S(2)}) collective-permute-start(bf16[8,16,768]{2,1,0:T(8,128)(2,1)S(1)} %get-tuple-element.9), channel_id=1, source_target_pairs={{0,256},{64,320},{128,384},{192,448},{256,0},{320,64},{384,128},{4... | collective-permute-start | bytes 589832 | tf_op jit(solution)/shard_map/ppermute | solution.py:74
  146.5 19.2 %collective-permute-start.11 = (bf16[8,16,768]{2,1,0:T(8,128)(2,1)S(1)}, bf16[8,16,768]{2,1,0:T(8,128)(2,1)S(1)}, u32[]{:S(2)}, u32[]{:S(2)}) collective-permute-start(bf16[8,16,768]{2,1,0:T(8,128)(2,1)S(1)} %get-tuple-element.8), channel_id=1, source_target_pairs={{0,384},{64,448},{128,0},{192,64},{256,128},{320,192},{384,256},{4... | collective-permute-start | bytes 589832 | tf_op jit(solution)/shard_map/ppermute | solution.py:74
  152.6 13.9 %collective-permute-start.16 = (bf16[512,384]{1,0:T(8,128)(2,1)S(1)}, bf16[512,384]{1,0:T(8,128)(2,1)S(1)}, u32[]{:S(2)}, u32[]{:S(2)}) collective-permute-start(bf16[512,384]{1,0:T(8,128)(2,1)S(1)} %get-tuple-element.6), channel_id=1, source_target_pairs={{0,64},{64,0},{128,192},{192,128},{256,320},{320,256},{384,448},{4... | collective-permute-start | bytes 1179656 | tf_op jit(solution)/shard_map/ppermute | solution.py:57
  155.2 15.6 %collective-permute-start.14 = (bf16[512,768]{1,0:T(8,128)(2,1)S(1)}, bf16[512,768]{1,0:T(8,128)(2,1)S(1)}, u32[]{:S(2)}, u32[]{:S(2)}) collective-permute-start(bf16[512,768]{1,0:T(8,128)(2,1)S(1)} %bitcast.87), channel_id=1, source_target_pairs={{0,64},{64,0},{128,192},{192,128},{256,320},{320,256},{384,448},{4... | collective-permute-start | bytes 2359304 | tf_op jit(solution)/shard_map/ppermute | solution.py:57
  157.6 13.2 %collective-permute-start.15 = (bf16[512,384]{1,0:T(8,128)(2,1)S(1)}, bf16[512,384]{1,0:T(8,128)(2,1)S(1)}, u32[]{:S(2)}, u32[]{:S(2)}) collective-permute-start(bf16[512,384]{1,0:T(8,128)(2,1)S(1)} %get-tuple-element.7), channel_id=1, source_target_pairs={{0,64},{64,0},{128,192},{192,128},{256,320},{320,256},{384,448},{4... | collective-permute-start | bytes 1179656 | tf_op jit(solution)/shard_map/ppermute | solution.py:57
  170.8 24.6 %copy-start.9 = (bf16[1,16,768]{2,1,0:T(8,128)(2,1)S(1)}, bf16[1,16,768]{2,1,0:T(8,128)(2,1)}, u32[]{:S(2)}) copy-start(bf16[1,16,768]{2,1,0:T(8,128)(2,1)} %param.8) | copy-start | bytes 73732
  172.4 24.5 %copy-start.8 = (bf16[1,16,768]{2,1,0:T(8,128)(2,1)S(1)}, bf16[1,16,768]{2,1,0:T(8,128)(2,1)}, u32[]{:S(2)}) copy-start(bf16[1,16,768]{2,1,0:T(8,128)(2,1)} %param.5) | copy-start | bytes 73732
  172.4 23.0 %all-to-all-start.5 = ((bf16[8,16,768]{2,1,0:T(8,128)(2,1)}), bf16[8,16,768]{2,1,0:T(8,128)(2,1)S(1)}, u32[]{:S(2)}, u32[]{:S(2)}) async-start(bf16[8,16,768]{2,1,0:T(8,128)(2,1)} %fusion.2), calls=%async_computation.5 | async-start | bytes 393216 | tf_op jit(solution)/shard_map/all_to_all | solution.py:34
  180.8 15.3 %collective-permute-start.10 = (bf16[16,768]{1,0:T(8,128)(2,1)S(1)}, bf16[16,768]{1,0:T(8,128)(2,1)S(1)}, u32[]{:S(2)}, u32[]{:S(2)}) collective-permute-start(bf16[16,768]{1,0:T(8,128)(2,1)S(1)} %get-tuple-element.15), channel_id=1, source_target_pairs={{0,128},{64,192},{128,256},{192,320},{256,384},{320,448},{384,0},{... | collective-permute-start | bytes 73736 | tf_op jit(solution)/shard_map/ppermute | solution.py:74
  184.7 11.4 %collective-permute-start.9 = (bf16[16,768]{1,0:T(8,128)(2,1)S(1)}, bf16[16,768]{1,0:T(8,128)(2,1)S(1)}, u32[]{:S(2)}, u32[]{:S(2)}) collective-permute-start(bf16[16,768]{1,0:T(8,128)(2,1)S(1)} %get-tuple-element.14), channel_id=1, source_target_pairs={{0,256},{64,320},{128,384},{192,448},{256,0},{320,64},{384,128},{4... | collective-permute-start | bytes 73736 | tf_op jit(solution)/shard_map/ppermute | solution.py:74
  190.0 6.9 %collective-permute-start.8 = (bf16[16,768]{1,0:T(8,128)(2,1)S(1)}, bf16[16,768]{1,0:T(8,128)(2,1)S(1)}, u32[]{:S(2)}, u32[]{:S(2)}) collective-permute-start(bf16[16,768]{1,0:T(8,128)(2,1)S(1)} %get-tuple-element.13), channel_id=1, source_target_pairs={{0,384},{64,448},{128,0},{192,64},{256,128},{320,192},{384,256},{4... | collective-permute-start | bytes 73736 | tf_op jit(solution)/shard_map/ppermute | solution.py:74

commit v6 on v4

--- a/solution.py
+++ b/solution.py
@@ -64,38 +64,51 @@
     token_total = (MBT * jnp.sum(counts)).astype(jnp.float32)
     positions = column_index * rows_local + jnp.arange(rows_local, dtype=jnp.int32)
     kept_mask = (positions // MBT < own_count).astype(jnp.float32)
-    scaled = (
-        cotangent.reshape(rows_local, width).astype(jnp.float32)
-        * kept_mask[:, None]
-        / token_total
-    ).astype(jnp.bfloat16)
-
     w_in_mate, w_out_mate = mate(w_in), mate(w_out)
 
-    line = spread(jnp.concatenate([tokens_local, scaled], axis=0), "rep", chips, same_core)
-    tokens_line = line[:, :rows_local].reshape(chips * rows_local, width)
-    scaled_line = line[:, rows_local:].reshape(chips * rows_local, width)
     line_rows = chips * rows_local
     rows_all = columns * line_rows
 
-    padded = jnp.concatenate([scaled_line, scaled_line[: line_rows // 2]], axis=0)
+    plane = [
+        [(chip * CORES + core) * columns + column for column in range(columns) for chip in range(chips)]
+        for core in range(CORES)
+    ]
+    tokens_all = spread(tokens_local, ("rep", "col"), columns * chips, plane).reshape(rows_all, width)
+
+    onward = lambda value, k: lax.ppermute(
+        value, "rep", [(r, (r + k * CORES) % replicas) for r in range(replicas)]
+    )
+    some_kept = jnp.sum(counts) > 0
+
+    def gradient_line(cotangent_block):
+        scaled = (
+            cotangent_block.reshape(rows_local, width).astype(jnp.float32)
+            * kept_mask[:, None]
+            / token_total
+        ).astype(jnp.bfloat16)
+        near = [scaled] + [onward(scaled, k) for k in range(1, chips)]
+        back = lax.rem(lax.div(replica_index, CORES) + chips, chips)
+        ordered = []
+        for place in range(chips):
+            steps = lax.rem(back - place + chips, chips)
+            block = near[0]
+            for k in range(1, chips):
+                block = jnp.where(steps == k, near[k], block)
+            ordered.append(block)
+        return scaled, jnp.concatenate(ordered + ordered[: chips // 2], axis=0)
+
+    def no_gradient_line(cotangent_block):
+        return (
+            jnp.zeros((rows_local, width), jnp.bfloat16),
+            jnp.zeros((line_rows * 3 // 2, width), jnp.bfloat16),
+        )
+
+    scaled, padded = lax.cond(some_kept, gradient_line, no_gradient_line, cotangent)
     scaled_all = lax.all_gather(padded, "col", axis=0)[:, :line_rows].reshape(rows_all, width)
 
-    def forward(line):
-        everyone = spread(line, "col", columns).reshape(rows_all, width)
-        return everyone, hidden_part(everyone)
-
-    def forward_plain(line):
-        everyone = lax.all_gather(line, "col", axis=0, tiled=True)
-        return everyone, hidden_part(everyone)
-
-    def hidden_part(everyone):
-        return jnp.concatenate(
-            [product(everyone, w, 1, 0).astype(jnp.bfloat16) for w in (w_in, w_in_mate)], axis=1
-        )
-
-    some_kept = jnp.sum(counts) > 0
-    tokens_all, hidden_terms = lax.cond(some_kept, forward, forward_plain, tokens_line)
+    hidden_terms = jnp.concatenate(
+        [product(tokens_all, w, 1, 0).astype(jnp.bfloat16) for w in (w_in, w_in_mate)], axis=1
+    )
     hidden = added_up(swapped(cut(hidden_terms, row_count), "row"))
     active, slope = gelu_both(hidden)
     slope_terms = jnp.concatenate(

time: 187 us -> 193 us (1.032)
  blocking collectives: 69.3 us -> 37.3 us
  waiting for transfers between devices: 29.1 us -> 47.5 us
  starting transfers between devices: 41.4 us -> 58.1 us
  local copies, waits for them, and re-layouts: 6.34 us -> 9.38 us
    all_to_all x3 -> x2, blocking collectives: 69.3 us -> 37.3 us  [swapped(): lax.all_to_all(value, axis, 0, 0, axis_index_groups=groups, tiled=True)]
    all_gather x1, waiting for transfers between devices: 0.02 us -> 22.7 us  [body(): lax.all_gather(padded, 'col', axis=0)[:, :line_rows]]
    ppermute x0 -> x3, starting transfers between devices: none -> 14.3 us  [body(): lax.ppermute(value, 'rep', [(r, (r + k * CORES) % replicas) for r in rang...]
    all_to_all x4, waiting for transfers between devices: 29 us -> 14.7 us  [swapped(): lax.all_to_all(value, axis, 0, 0, axis_index_groups=groups, tiled=True)]
    ppermute x0 -> x3, waiting for transfers between devices: none -> 8.47 us  [body(): lax.ppermute(value, 'rep', [(r, (r + k * CORES) % replicas) for r in rang...]
    cond x0 -> x4, other arithmetic: none -> 2.5 us
    all_to_all x4, starting transfers between devices: 29.4 us -> 31.7 us  [swapped(): lax.all_to_all(value, axis, 0, 0, axis_index_groups=groups, tiled=True)]
  transfers between devices with their start and end apart: 12 -> 15, of which waited for: 4 -> 6; matrix products, arithmetic and copies ran while one was open for 10% -> 13% of each run, Pallas kernels for 0% -> 0%
where the time goes in v6:
time: 193 us; the launch traced here: 191 us
  starting transfers between devices  58.1 us (30%)
  waiting for transfers between devices  47.5 us (25%)
  blocking collectives  37.3 us (19%)
  matrix products  17 us (9%)
  between operations  15.6 us (8%)
  local copies, waits for them, and re-layouts  9.38 us (5%)
  other arithmetic  6.16 us (3%)
    all_to_all x2, blocking collectives, swapped(): lax.all_to_all(value, axis, 0, 0, axis_index_groups=groups, tiled=True)  37.3 us
    all_to_all x4, starting transfers between devices, swapped(): lax.all_to_all(value, axis, 0, 0, axis_index_groups=groups, tiled=True)  31.7 us
    all_gather x1, waiting for transfers between devices, body(): lax.all_gather(padded, 'col', axis=0)[:, :line_rows]  22.7 us
    dot_general x12, matrix products, product(): lax.dot_general(left, right, (((left_dim,), (right_dim,)), ((), ())), pre...  17 us
    all_to_all x4, waiting for transfers between devices, swapped(): lax.all_to_all(value, axis, 0, 0, axis_index_groups=groups, tiled=True)  14.7 us
    ppermute x3, starting transfers between devices, body(): lax.ppermute(value, 'rep', [(r, (r + k * CORES) % replicas) for r in rang...  14.3 us
    ppermute x6, starting transfers between devices, body(): mate = lambda value: lax.ppermute(value, 'rep', to_mate)  12 us
    ppermute x3, waiting for transfers between devices, body(): lax.ppermute(value, 'rep', [(r, (r + k * CORES) % replicas) for r in rang...  8.47 us
  transfers between devices with their start and end apart: 15, of which 6 were waited for; matrix products, arithmetic and copies ran while one was open for 13% of the time, Pallas kernels for 0%

profile of v6, /device:TPU:6, one launch (start us, length us, event | category | flops | bytes accessed | tf_op | source)
XLA Modules:
  0.0 191.3 jit_solution(3581035142396294423)
XLA Ops:
  7.2 1.7 broadcast_in_dim.13
  8.9 16.1 %all-to-all-start.2 = ((bf16[32,16,768]{2,1,0:T(8,128)(2,1)}), bf16[32,16,768]{2,1,0:T(8,128)(2,1)S(1)}, u32[]{:S(2)}, u32[]{:S(2)}) async-start(bf16[32,16,768]{2,1,0:T(8,128)(2,1)} %broadcast_in_dim.13), calls=%async_computation.2 | async-start | bytes 1572864 | tf_op jit(solution)/shard_map/all_to_all | solution.py:34
  25.0 0.6 fusion.33
  27.0 0.7 compare_convert_fusion
  27.6 26.7 %conditional.2 = (bf16[96,768]{1,0:T(8,128)(2,1)}, f32[16,768]{1,0:T(8,128)S(1)}) conditional(s32[]{:T(128)} %convert_element_type.235, () %tuple.29, (s32[]{:T(128)}, bf16[1,16,768]{2,1,0:T(8,128)(2,1)S(1)}, f32[16]{0:T(128)S(1)}, f32[]{:T(128)}) %tuple.51), branch_computations={%region_2.3_spmd, %region_3.4_spmd} | conditional | flops 208948 | bytes 1032954 | solution.py:106
  27.7 5.8 %collective-permute-start = (bf16[16,768]{1,0:T(8,128)(2,1)S(1)}, bf16[16,768]{1,0:T(8,128)(2,1)S(1)}, u32[]{:S(2)}, u32[]{:S(2)}) collective-permute-start(bf16[16,768]{1,0:T(8,128)(2,1)S(1)} %get-tuple-element.55), channel_id=1, source_target_pairs={{0,384},{64,448},{128,0},{192,64},{256,128},{320,192},{384,256},{4... | collective-permute-start | bytes 73736 | tf_op jit(solution)/shard_map/cond/branch_1_fun/ppermute | solution.py:78
  33.5 4.3 %collective-permute-start.1 = (bf16[16,768]{1,0:T(8,128)(2,1)S(1)}, bf16[16,768]{1,0:T(8,128)(2,1)S(1)}, u32[]{:S(2)}, u32[]{:S(2)}) collective-permute-start(bf16[16,768]{1,0:T(8,128)(2,1)S(1)} %get-tuple-element.55), channel_id=1, source_target_pairs={{0,256},{64,320},{128,384},{192,448},{256,0},{320,64},{384,128},{4... | collective-permute-start | bytes 73736 | tf_op jit(solution)/shard_map/cond/branch_1_fun/ppermute | solution.py:78
  37.8 4.3 %collective-permute-start.2 = (bf16[16,768]{1,0:T(8,128)(2,1)S(1)}, bf16[16,768]{1,0:T(8,128)(2,1)S(1)}, u32[]{:S(2)}, u32[]{:S(2)}) collective-permute-start(bf16[16,768]{1,0:T(8,128)(2,1)S(1)} %get-tuple-element.55), channel_id=1, source_target_pairs={{0,128},{64,192},{128,256},{192,320},{256,384},{320,448},{384,0},{... | collective-permute-start | bytes 73736 | tf_op jit(solution)/shard_map/cond/branch_1_fun/ppermute | solution.py:78
  42.2 5.4 %collective-permute-done = bf16[16,768]{1,0:T(8,128)(2,1)S(1)} collective-permute-done((bf16[16,768]{1,0:T(8,128)(2,1)S(1)}, bf16[16,768]{1,0:T(8,128)(2,1)S(1)}, u32[]{:S(2)}, u32[]{:S(2)}) %collective-permute-start) | collective-permute-done | bytes 24608 | tf_op jit(solution)/shard_map/cond/branch_1_fun/ppermute | solution.py:78
  47.6 3.0 %collective-permute-done.1 = bf16[16,768]{1,0:T(8,128)(2,1)S(1)} collective-permute-done((bf16[16,768]{1,0:T(8,128)(2,1)S(1)}, bf16[16,768]{1,0:T(8,128)(2,1)S(1)}, u32[]{:S(2)}, u32[]{:S(2)}) %collective-permute-start.1) | collective-permute-done | bytes 24608 | tf_op jit(solution)/shard_map/cond/branch_1_fun/ppermute | solution.py:78
  50.6 0.6 constant_dynamic-update-slice_fusion.3
  51.3 0.6 constant_dynamic-update-slice_fusion.2
  51.9 0.6 select_dynamic-update-slice_fusion.1
  52.5 0.6 select_dynamic-update-slice_fusion
  53.1 0.6 constant_dynamic-update-slice_fusion.1
  53.7 0.6 constant_dynamic-update-slice_fusion
  54.4 1.9 %collective-permute-start.7 = (bf16[768,384]{1,0:T(8,128)(2,1)S(1)}, bf16[768,384]{1,0:T(8,128)(2,1)}, u32[]{:S(2)}, u32[]{:S(2)}) collective-permute-start(bf16[768,384]{1,0:T(8,128)(2,1)S(1)} %copy-done.2), channel_id=1, source_target_pairs={{0,64},{64,0},{128,192},{192,128},{256,320},{320,256},{384,448},{4... | collective-permute-start | bytes 1769480 | tf_op jit(solution)/shard_map/ppermute | solution.py:58
  56.9 1.6 collective-permute-done.7
  58.4 1.6 convolution_convert_fusion.2
  60.1 1.2 copy.12
  61.2 5.3 %all-to-all-start.3 = ((bf16[8,64,768]{2,1,0:T(8,128)(2,1)}), bf16[8,64,768]{2,1,0:T(8,128)(2,1)S(1)}, u32[]{:S(2)}, u32[]{:S(2)}) async-start(bf16[8,64,768]{2,1,0:T(8,128)(2,1)} %bitcast.6), calls=%async_computation.3 | async-start | bytes 1572864 | tf_op jit(solution)/shard_map/all_to_all | solution.py:34
  66.5 1.9 %collective-permute-start.8 = (bf16[384,768]{1,0:T(8,128)(2,1)S(1)}, bf16[384,768]{1,0:T(8,128)(2,1)S(1)}, u32[]{:S(2)}, u32[]{:S(2)}) collective-permute-start(bf16[384,768]{1,0:T(8,128)(2,1)S(1)} %copy-done), channel_id=1, source_target_pairs={{0,64},{64,0},{128,192},{192,128},{256,320},{320,256},{384,448},{4... | collective-permute-start | bytes 1769480 | tf_op jit(solution)/shard_map/ppermute | solution.py:58
  68.4 22.7 %all-gather.3.cloned.1.call-done = bf16[768,768]{1,0:T(8,128)(2,1)} async-done(((bf16[96,768]{1,0:T(8,128)(2,1)}), bf16[768,768]{1,0:T(8,128)(2,1)}) %all-gather.3.cloned.1.call-update) | async-done | bytes 1179664 | tf_op jit(solution)/shard_map/all_gather | solution.py:107
  91.1 2.1 %slice.177 = bf16[8,64,768]{2,1,0:T(8,128)(2,1)} slice(bf16[8,96,768]{2,1,0:T(8,128)(2,1)} %bitcast.82), slice={[0:8], [0:64], [0:768]} | slice | bytes 1572864 | tf_op jit(solution)/shard_map/slice | solution.py:107
  93.2 1.6 convolution_convert_fusion.1
  94.9 0.8 copy-done.4
  95.7 1.6 convolution_convert_fusion
  98.1 20.9 %all_to_all.28 = bf16[8,64,1536]{2,1,0:T(8,128)(2,1)S(1)} all-to-all(bf16[8,64,1536]{2,1,0:T(8,128)(2,1)S(1)} %pad_maximum_fusion), channel_id=1, replica_groups=mesh['rep'=8,'row'=8,'col'=8] {'row'}, dimensions={0} | all-to-all | bytes 3145728 | tf_op jit(solution)/shard_map/all_to_all | solution.py:34
  119.0 1.0 copy-done.1
  120.6 1.5 add_convert_fusion.2
  122.3 44.1 %conditional.3 = (f32[768,384]{1,0:T(8,128)}, f32[384,768]{1,0:T(8,128)}, bf16[4,16,768]{2,1,0:T(8,128)(2,1)S(1)}) conditional(s32[]{:T(128)} %convert_element_type.235, () %tuple.32, (bf16[64,768]{1,0:T(8,128)(2,1)S(1)}, bf16[512,768]{1,0:T(8,128)(2,1)S(1)}, bf16[512,768]{1,0:T(8,128)(2,1)S(1)}, bf16[512,768]{1,0:T(8,128)(2,1)}, ...), branch_computations={%region_5.6_spmd, %region_6.7_spmd} | conditional | flops 1814102016 | bytes 37552404 | solution.py:149
  122.3 0.9 broadcast_in_dim.3
  123.3 5.9 %all-to-all-start = ((bf16[8,64,768]{2,1,0:T(8,128)(2,1)}), bf16[8,64,768]{2,1,0:T(8,128)(2,1)S(1)}, u32[]{:S(2)}, u32[]{:S(2)}) async-start(bf16[8,64,768]{2,1,0:T(8,128)(2,1)} %broadcast_in_dim.3), calls=%async_computation | async-start | bytes 1572864 | tf_op jit(solution)/shard_map/cond/branch_1_fun/all_to_all | solution.py:34
  129.2 1.9 collective-permute-start.6
  131.1 5.7 %all-to-all-done = bf16[8,64,768]{2,1,0:T(8,128)(2,1)S(1)} async-done(((bf16[8,64,768]{2,1,0:T(8,128)(2,1)}), bf16[8,64,768]{2,1,0:T(8,128)(2,1)S(1)}, u32[]{:S(2)}, u32[]{:S(2)}) %all-to-all-start) | async-done | bytes 786464 | tf_op jit(solution)/shard_map/cond/branch_1_fun/all_to_all | solution.py:34
  137.3 2.6 %add_convert_fusion = bf16[512,768]{1,0:T(8,128)(2,1)} fusion(f32[512,768]{1,0:T(8,128)S(1)} %fusion.4, bf16[768,384]{1,0:T(8,128)(2,1)} %get-tuple-element.31, bf16[512,768]{1,0:T(8,128)(2,1)S(1)} %bitcast.74), kind=kOutput, calls=%fused_computation.11 | convolution fusion | flops 302776320 | bytes 3342336 | tf_op jit(solution)/shard_map/cond/branch_1_fun/dot_general | solution.py:23
  139.9 4.4 %all-to-all-start.1 = ((bf16[8,64,768]{2,1,0:T(8,128)(2,1)}), bf16[8,64,768]{2,1,0:T(8,128)(2,1)S(1)}, u32[]{:S(2)}, u32[]{:S(2)}) async-start(bf16[8,64,768]{2,1,0:T(8,128)(2,1)} %bitcast.80), calls=%async_computation.1 | async-start | bytes 1572864 | tf_op jit(solution)/shard_map/cond/branch_1_fun/all_to_all | solution.py:34
  144.4 1.9 %collective-permute-start.5 = (bf16[512,384]{1,0:T(8,128)(2,1)S(1)}, bf16[512,384]{1,0:T(8,128)(2,1)S(1)}, u32[]{:S(2)}, u32[]{:S(2)}) collective-permute-start(bf16[512,384]{1,0:T(8,128)(2,1)S(1)} %slice.94), channel_id=1, source_target_pairs={{0,64},{64,0},{128,192},{192,128},{256,320},{320,256},{384,448},{4... | collective-permute-start | bytes 1179656 | tf_op jit(solution)/shard_map/cond/branch_1_fun/ppermute | solution.py:58
  146.3 2.4 %collective-permute-start.3 = (bf16[512,768]{1,0:T(8,128)(2,1)S(1)}, bf16[512,768]{1,0:T(8,128)(2,1)S(1)}, u32[]{:S(2)}, u32[]{:S(2)}) collective-permute-start(bf16[512,768]{1,0:T(8,128)(2,1)S(1)} %get-tuple-element.26), channel_id=1, source_target_pairs={{0,64},{64,0},{128,192},{192,128},{256,320},{320,256},{384,448},{4... | collective-permute-start | bytes 2359304 | tf_op jit(solution)/shard_map/cond/branch_1_fun/ppermute | solution.py:58
  148.7 1.6 fusion.2
  150.4 1.9 %collective-permute-start.4 = (bf16[512,384]{1,0:T(8,128)(2,1)S(1)}, bf16[512,384]{1,0:T(8,128)(2,1)S(1)}, u32[]{:S(2)}, u32[]{:S(2)}) collective-permute-start(bf16[512,384]{1,0:T(8,128)(2,1)S(1)} %slice.160), channel_id=1, source_target_pairs={{0,64},{64,0},{128,192},{192,128},{256,320},{320,256},{384,448},{4... | collective-permute-start | bytes 1179656 | tf_op jit(solution)/shard_map/cond/branch_1_fun/ppermute | solution.py:58
  152.3 2.7 %convolution_add_fusion = f32[384,768]{1,0:T(8,128)} fusion(f32[384,768]{1,0:T(8,128)S(1)} %fusion.2, bf16[512,384]{1,0:T(8,128)(2,1)S(1)} %collective-permute-done.5, bf16[512,768]{1,0:T(8,128)(2,1)} %collective-permute-done.6), kind=kOutput, calls=%fused_computation.12 | convolution fusion | flops 302284800 | bytes 3538944 | tf_op jit(solution)/shard_map/cond/branch_1_fun/dot_general | solution.py:23
  155.0 0.6 fusion.6
  155.6 1.6 convolution_add_fusion.1
  157.2 9.1 %all-to-all-done.1 = bf16[8,64,768]{2,1,0:T(8,128)(2,1)S(1)} async-done(((bf16[8,64,768]{2,1,0:T(8,128)(2,1)}), bf16[8,64,768]{2,1,0:T(8,128)(2,1)S(1)}, u32[]{:S(2)}, u32[]{:S(2)}) %all-to-all-start.1) | async-done | bytes 786464 | tf_op jit(solution)/shard_map/cond/branch_1_fun/all_to_all | solution.py:34
  166.4 0.9 pad_maximum_fusion.3
  167.3 16.4 %all_to_all.29 = bf16[4,32,768]{2,1,0:T(8,128)(2,1)S(1)} all-to-all(bf16[4,32,768]{2,1,0:T(8,128)(2,1)S(1)} %pad_maximum_fusion.3), channel_id=1, replica_groups={{0,128,256,384},{64,192,320,448},{1,129,257,385},{65,193,321,449},{2,13..., dimensions={0} | all-to-all | bytes 393216 | tf_op jit(solution)/shard_map/all_to_all | solution.py:34
  183.8 0.6 fusion.32
  (45 shorter events, 3.1 us)
Async XLA Ops:
  7.2 17.9 %copy-start.8 = (s32[8]{0:T(128)S(1)}, s32[8]{0:T(128)}, u32[]{:S(2)}) copy-start(s32[8]{0:T(128)} %param.13) | copy-start | bytes 100
  7.2 20.5 %copy-start.7 = (bf16[1,16,768]{2,1,0:T(8,128)(2,1)S(1)}, bf16[1,16,768]{2,1,0:T(8,128)(2,1)}, u32[]{:S(2)}) copy-start(bf16[1,16,768]{2,1,0:T(8,128)(2,1)} %param.12) | copy-start | bytes 73732
  8.9 45.5 %copy-start.2 = (bf16[768,384]{1,0:T(8,128)(2,1)S(1)}, bf16[768,384]{1,0:T(8,128)(2,1)}, u32[]{:S(2)}) copy-start(bf16[768,384]{1,0:T(8,128)(2,1)} %param.10) | copy-start | bytes 1769476
  8.9 47.4 %all-to-all-start.2 = ((bf16[32,16,768]{2,1,0:T(8,128)(2,1)}), bf16[32,16,768]{2,1,0:T(8,128)(2,1)S(1)}, u32[]{:S(2)}, u32[]{:S(2)}) async-start(bf16[32,16,768]{2,1,0:T(8,128)(2,1)} %broadcast_in_dim.13), calls=%async_computation.2 | async-start | bytes 1572864 | tf_op jit(solution)/shard_map/all_to_all | solution.py:34
  25.0 66.2 %all-gather.3.cloned.1.call-start = ((), (), s32[]{:S(2)}) async-start(), calls=%async_computation.8 | async-start | bytes 1327104 | tf_op jit(solution)/shard_map/all_gather | solution.py:107
  27.7 19.8 %collective-permute-start = (bf16[16,768]{1,0:T(8,128)(2,1)S(1)}, bf16[16,768]{1,0:T(8,128)(2,1)S(1)}, u32[]{:S(2)}, u32[]{:S(2)}) collective-permute-start(bf16[16,768]{1,0:T(8,128)(2,1)S(1)} %get-tuple-element.55), channel_id=1, source_target_pairs={{0,384},{64,448},{128,0},{192,64},{256,128},{320,192},{384,256},{4... | collective-permute-start | bytes 73736 | tf_op jit(solution)/shard_map/cond/branch_1_fun/ppermute | solution.py:78
  33.5 17.1 %collective-permute-start.1 = (bf16[16,768]{1,0:T(8,128)(2,1)S(1)}, bf16[16,768]{1,0:T(8,128)(2,1)S(1)}, u32[]{:S(2)}, u32[]{:S(2)}) collective-permute-start(bf16[16,768]{1,0:T(8,128)(2,1)S(1)} %get-tuple-element.55), channel_id=1, source_target_pairs={{0,256},{64,320},{128,384},{192,448},{256,0},{320,64},{384,128},{4... | collective-permute-start | bytes 73736 | tf_op jit(solution)/shard_map/cond/branch_1_fun/ppermute | solution.py:78
  37.8 12.8 %collective-permute-start.2 = (bf16[16,768]{1,0:T(8,128)(2,1)S(1)}, bf16[16,768]{1,0:T(8,128)(2,1)S(1)}, u32[]{:S(2)}, u32[]{:S(2)}) collective-permute-start(bf16[16,768]{1,0:T(8,128)(2,1)S(1)} %get-tuple-element.55), channel_id=1, source_target_pairs={{0,128},{64,192},{128,256},{192,320},{256,384},{320,448},{384,0},{... | collective-permute-start | bytes 73736 | tf_op jit(solution)/shard_map/cond/branch_1_fun/ppermute | solution.py:78
  54.4 4.0 %collective-permute-start.7 = (bf16[768,384]{1,0:T(8,128)(2,1)S(1)}, bf16[768,384]{1,0:T(8,128)(2,1)}, u32[]{:S(2)}, u32[]{:S(2)}) collective-permute-start(bf16[768,384]{1,0:T(8,128)(2,1)S(1)} %copy-done.2), channel_id=1, source_target_pairs={{0,64},{64,0},{128,192},{192,128},{256,320},{320,256},{384,448},{4... | collective-permute-start | bytes 1769480 | tf_op jit(solution)/shard_map/ppermute | solution.py:58
  60.1 6.5 %copy-start = (bf16[384,768]{1,0:T(8,128)(2,1)S(1)}, bf16[384,768]{1,0:T(8,128)(2,1)}, u32[]{:S(2)}) copy-start(bf16[384,768]{1,0:T(8,128)(2,1)} %param.11) | copy-start | bytes 1769476
  61.2 36.5 %all-to-all-start.3 = ((bf16[8,64,768]{2,1,0:T(8,128)(2,1)}), bf16[8,64,768]{2,1,0:T(8,128)(2,1)S(1)}, u32[]{:S(2)}, u32[]{:S(2)}) async-start(bf16[8,64,768]{2,1,0:T(8,128)(2,1)} %bitcast.6), calls=%async_computation.3 | async-start | bytes 1572864 | tf_op jit(solution)/shard_map/all_to_all | solution.py:34
  66.5 99.9 %reduce-scatter.2.cloned.1.call-start = ((), (), s32[]{:S(2)}) async-start(), calls=%async_computation.7 | async-start | bytes 884736 | tf_op jit(solution)/shard_map/reduce_scatter | solution.py:125
  66.5 28.4 %collective-permute-start.8 = (bf16[384,768]{1,0:T(8,128)(2,1)S(1)}, bf16[384,768]{1,0:T(8,128)(2,1)S(1)}, u32[]{:S(2)}, u32[]{:S(2)}) collective-permute-start(bf16[384,768]{1,0:T(8,128)(2,1)S(1)} %copy-done), channel_id=1, source_target_pairs={{0,64},{64,0},{128,192},{192,128},{256,320},{320,256},{384,448},{4... | collective-permute-start | bytes 1769480 | tf_op jit(solution)/shard_map/ppermute | solution.py:58
  94.9 0.8 copy-start.4
  118.9 1.1 copy-start.1
  119.0 1.6 copy-start.5
  122.3 61.5 %copy-start.6 = (bf16[1,16,768]{2,1,0:T(8,128)(2,1)S(1)}, bf16[1,16,768]{2,1,0:T(8,128)(2,1)}, u32[]{:S(2)}) copy-start(bf16[1,16,768]{2,1,0:T(8,128)(2,1)} %param.9) | copy-start | bytes 73732
  122.3 14.4 %copy-start.3 = (bf16[768,384]{1,0:T(8,128)(2,1)S(1)}, bf16[768,384]{1,0:T(8,128)(2,1)}, u32[]{:S(2)}) copy-start(bf16[768,384]{1,0:T(8,128)(2,1)} %get-tuple-element.30) | copy-start | bytes 1769476 | tf_op jit(solution)/shard_map/cond
  123.3 13.5 %all-to-all-start = ((bf16[8,64,768]{2,1,0:T(8,128)(2,1)}), bf16[8,64,768]{2,1,0:T(8,128)(2,1)S(1)}, u32[]{:S(2)}, u32[]{:S(2)}) async-start(bf16[8,64,768]{2,1,0:T(8,128)(2,1)} %broadcast_in_dim.3), calls=%async_computation | async-start | bytes 1572864 | tf_op jit(solution)/shard_map/cond/branch_1_fun/all_to_all | solution.py:34
  129.2 23.2 %collective-permute-start.6 = (bf16[512,768]{1,0:T(8,128)(2,1)}, bf16[512,768]{1,0:T(8,128)(2,1)}, u32[]{:S(2)}, u32[]{:S(2)}) collective-permute-start(bf16[512,768]{1,0:T(8,128)(2,1)} %get-tuple-element.29), channel_id=1, source_target_pairs={{0,64},{64,0},{128,192},{192,128},{256,320},{320,256},{384,448},{4... | collective-permute-start | bytes 2359304 | tf_op jit(solution)/shard_map/cond/branch_1_fun/ppermute | solution.py:58
  139.9 26.4 %all-to-all-start.1 = ((bf16[8,64,768]{2,1,0:T(8,128)(2,1)}), bf16[8,64,768]{2,1,0:T(8,128)(2,1)S(1)}, u32[]{:S(2)}, u32[]{:S(2)}) async-start(bf16[8,64,768]{2,1,0:T(8,128)(2,1)} %bitcast.80), calls=%async_computation.1 | async-start | bytes 1572864 | tf_op jit(solution)/shard_map/cond/branch_1_fun/all_to_all | solution.py:34
  144.4 8.0 %collective-permute-start.5 = (bf16[512,384]{1,0:T(8,128)(2,1)S(1)}, bf16[512,384]{1,0:T(8,128)(2,1)S(1)}, u32[]{:S(2)}, u32[]{:S(2)}) collective-permute-start(bf16[512,384]{1,0:T(8,128)(2,1)S(1)} %slice.94), channel_id=1, source_target_pairs={{0,64},{64,0},{128,192},{192,128},{256,320},{320,256},{384,448},{4... | collective-permute-start | bytes 1179656 | tf_op jit(solution)/shard_map/cond/branch_1_fun/ppermute | solution.py:58
  146.3 9.3 %collective-permute-start.3 = (bf16[512,768]{1,0:T(8,128)(2,1)S(1)}, bf16[512,768]{1,0:T(8,128)(2,1)S(1)}, u32[]{:S(2)}, u32[]{:S(2)}) collective-permute-start(bf16[512,768]{1,0:T(8,128)(2,1)S(1)} %get-tuple-element.26), channel_id=1, source_target_pairs={{0,64},{64,0},{128,192},{192,128},{256,320},{320,256},{384,448},{4... | collective-permute-start | bytes 2359304 | tf_op jit(solution)/shard_map/cond/branch_1_fun/ppermute | solution.py:58
  150.4 5.2 %collective-permute-start.4 = (bf16[512,384]{1,0:T(8,128)(2,1)S(1)}, bf16[512,384]{1,0:T(8,128)(2,1)S(1)}, u32[]{:S(2)}, u32[]{:S(2)}) collective-permute-start(bf16[512,384]{1,0:T(8,128)(2,1)S(1)} %slice.160), channel_id=1, source_target_pairs={{0,64},{64,0},{128,192},{192,128},{256,320},{320,256},{384,448},{4... | collective-permute-start | bytes 1179656 | tf_op jit(solution)/shard_map/cond/branch_1_fun/ppermute | solution.py:58
Sparse Core Ops, SparseCore 0:
  54.5 36.6 all-gather.2
  122.4 43.1 reduce-scatter.1

commit v7 on v4

--- a/solution.py
+++ b/solution.py
@@ -1,10 +1,13 @@
 import jax
 import jax.numpy as jnp
 from jax import lax
+from jax.experimental import pallas as pl
+from jax.experimental.pallas import tpu as pltpu
 from jax.sharding import PartitionSpec as P
 
 MBT = 32
 CORES = 2
+VMEM = 24 << 20
 
 root_coef = 0.7978845608028654
 cubic_coef = 0.044715
@@ -23,6 +26,68 @@
     return lax.dot_general(
         left, right, (((left_dim,), (right_dim,)), ((), ())), preferred_element_type=jnp.float32
     )
+
+
+def paired(blocks, half, own, other, turned):
+    count, rows, width = blocks.shape
+    rows //= 2
+    columns = own.shape[0] if turned else own.shape[1]
+    step = count // 4
+
+    def kernel(left_ref, own_ref, other_ref, out_ref):
+        for at in range(4):
+            left = left_ref[at * step : (at + 1) * step].reshape(step * rows, width)
+            for place, right_ref in enumerate((own_ref, other_ref)):
+                out_ref[
+                    at * step * rows : (at + 1) * step * rows,
+                    place * columns : (place + 1) * columns,
+                ] = product(left, right_ref[...], 1, 1 if turned else 0).astype(jnp.bfloat16)
+
+    return pl.pallas_call(
+        kernel,
+        grid=(1,),
+        in_specs=[
+            pl.BlockSpec((count, rows, width), lambda i: (0, half, 0)),
+            pl.BlockSpec(own.shape, lambda i: (0, 0)),
+            pl.BlockSpec(other.shape, lambda i: (0, 0)),
+        ],
+        out_specs=pl.BlockSpec((count * rows, 2 * columns), lambda i: (0, 0)),
+        out_shape=jax.ShapeDtypeStruct((count * rows, 2 * columns), jnp.bfloat16),
+        compiler_params=pltpu.CompilerParams(vmem_limit_bytes=VMEM),
+        cost_estimate=pl.CostEstimate(
+            flops=4 * count * rows * width * columns, bytes_accessed=4 << 20, transcendentals=0
+        ),
+    )(blocks, own, other)
+
+
+def joined(blocks, own, other, turned):
+    count, rows, _ = blocks.shape
+    units, width = own.shape[::-1] if turned else own.shape
+    step = count // 4
+
+    def kernel(left_ref, own_ref, other_ref, out_ref):
+        for at in range(4):
+            left = left_ref[at * step : (at + 1) * step].reshape(step * rows, 2 * units)
+            dim = 1 if turned else 0
+            total = product(left[:, :units], own_ref[...], 1, dim)
+            total = total + product(left[:, units:], other_ref[...], 1, dim)
+            out_ref[at * step * rows : (at + 1) * step * rows] = total.astype(jnp.bfloat16)
+
+    return pl.pallas_call(
+        kernel,
+        grid=(1,),
+        in_specs=[
+            pl.BlockSpec((count, rows, 2 * units), lambda i: (0, 0, 0)),
+            pl.BlockSpec(own.shape, lambda i: (0, 0)),
+            pl.BlockSpec(other.shape, lambda i: (0, 0)),
+        ],
+        out_specs=pl.BlockSpec((count * rows, width), lambda i: (0, 0)),
+        out_shape=jax.ShapeDtypeStruct((count * rows, width), jnp.bfloat16),
+        compiler_params=pltpu.CompilerParams(vmem_limit_bytes=VMEM),
+        cost_estimate=pl.CostEstimate(
+            flops=4 * count * rows * width * units, bytes_accessed=4 << 20, transcendentals=0
+        ),
+    )(blocks, own, other)
 
 
 def cut(value, pieces):
@@ -72,51 +137,34 @@
 
     w_in_mate, w_out_mate = mate(w_in), mate(w_out)
 
-    line = spread(jnp.concatenate([tokens_local, scaled], axis=0), "rep", chips, same_core)
-    tokens_line = line[:, :rows_local].reshape(chips * rows_local, width)
-    scaled_line = line[:, rows_local:].reshape(chips * rows_local, width)
     line_rows = chips * rows_local
     rows_all = columns * line_rows
 
-    padded = jnp.concatenate([scaled_line, scaled_line[: line_rows // 2]], axis=0)
-    scaled_all = lax.all_gather(padded, "col", axis=0)[:, :line_rows].reshape(rows_all, width)
-
-    def forward(line):
-        everyone = spread(line, "col", columns).reshape(rows_all, width)
-        return everyone, hidden_part(everyone)
-
-    def forward_plain(line):
-        everyone = lax.all_gather(line, "col", axis=0, tiled=True)
-        return everyone, hidden_part(everyone)
-
-    def hidden_part(everyone):
-        return jnp.concatenate(
-            [product(everyone, w, 1, 0).astype(jnp.bfloat16) for w in (w_in, w_in_mate)], axis=1
-        )
-
-    some_kept = jnp.sum(counts) > 0
-    tokens_all, hidden_terms = lax.cond(some_kept, forward, forward_plain, tokens_line)
+    plane = [
+        [(chip * CORES + core) * columns + column for column in range(columns) for chip in range(chips)]
+        for core in range(CORES)
+    ]
+    both = jnp.concatenate([tokens_local, scaled], axis=0)
+    everyone = spread(both, ("rep", "col"), columns * chips, plane)
+    hidden_terms = paired(everyone, 0, w_in, w_in_mate, False)
+    slope_terms = paired(everyone, 1, w_out, w_out_mate, True)
+
     hidden = added_up(swapped(cut(hidden_terms, row_count), "row"))
     active, slope = gelu_both(hidden)
-    slope_terms = jnp.concatenate(
-        [product(scaled_all, w, 1, 1).astype(jnp.bfloat16) for w in (w_out, w_out_mate)], axis=1
-    )
     share = jnp.broadcast_to(active.astype(jnp.bfloat16)[None], (row_count, *active.shape))
     mixed = swapped(jnp.concatenate([share, cut(slope_terms, row_count)], axis=2), "row")
     activated = mixed[:, :, : active.shape[1]].reshape(rows_all, -1)
     grad_share = (added_up(mixed[:, :, active.shape[1] :]) * slope).astype(jnp.bfloat16)
-    output_terms = (
-        product(activated[:, :units], w_out, 1, 0) + product(activated[:, units:], w_out_mate, 1, 0)
-    ).astype(jnp.bfloat16)
-    grad_share, output_terms = lax.optimization_barrier((grad_share, output_terms))
+    output_terms = joined(mixed, w_out, w_out_mate, False)
     output_line = lax.psum_scatter(output_terms, "col", scatter_dimension=0, tiled=True)
+    tokens_all, scaled_all = [
+        everyone[:, at * rows_local : (at + 1) * rows_local].reshape(rows_all, width) for at in (0, 1)
+    ]
 
     def backward(share):
-        hidden_grad = spread(share, "row", row_count).reshape(rows_all, -1)
-        back_terms = (
-            product(hidden_grad[:, :units], w_in, 1, 1)
-            + product(hidden_grad[:, units:], w_in_mate, 1, 1)
-        ).astype(jnp.bfloat16)
+        shares = spread(share, "row", row_count)
+        back_terms = joined(shares, w_in, w_in_mate, True)
+        hidden_grad = shares.reshape(rows_all, -1)
         back_line = added_up(swapped(cut(back_terms, columns), "col")).astype(jnp.bfloat16)
         w_out_grad = product(activated[:, :units], scaled_all, 0, 0) + product(
             mate(activated[:, units:]), mate(scaled_all), 0, 0
@@ -133,7 +181,7 @@
             jnp.zeros((units, width), jnp.float32),
         )
 
-    back_line, w_in_grad, w_out_grad = lax.cond(some_kept, backward, nothing, grad_share)
+    back_line, w_in_grad, w_out_grad = lax.cond(jnp.sum(counts) > 0, backward, nothing, grad_share)
     ends = jnp.concatenate([cut(output_line, chips), cut(back_line, chips)], axis=1)
     finished = added_up(swapped(ends, "rep", same_core))
     block_output = (tokens_local.astype(jnp.float32) + finished[:rows_local]).astype(jnp.bfloat16)

time: 187 us -> 191 us (1.021)
  blocking collectives: 69.3 us -> 35.6 us
  waiting for transfers between devices: 29.1 us -> 56.3 us
  starting transfers between devices: 41.4 us -> 53.2 us
  matrix products: 16.2 us -> 6.49 us
  Pallas kernels: 0 us -> 7.62 us
  other arithmetic: 6.6 us -> 10.3 us
    all_to_all x3 -> x2, blocking collectives: 69.3 us -> 35.6 us  [swapped(): lax.all_to_all(value, axis, 0, 0, axis_index_groups=groups, tiled=True)]
    all_to_all x4, waiting for transfers between devices: 29 us -> 52.4 us  [swapped(): lax.all_to_all(value, axis, 0, 0, axis_index_groups=groups, tiled=True)]
    all_to_all x4, starting transfers between devices: 29.4 us -> 41.1 us  [swapped(): lax.all_to_all(value, axis, 0, 0, axis_index_groups=groups, tiled=True)]
    dot_general x12 -> x4, matrix products: 16.2 us -> 6.49 us  [product(): lax.dot_general(left, right, (((left_dim,), (right_dim,)), ((), ())), pre...]
    pallas_call x0 -> x4, Pallas kernels: none -> 7.62 us  [the longest x2 4.36 us: joined(): pl.pallas_call(kernel, grid=(1,), in_specs=[pl.BlockSpec((count, rows, 2...]
    ppermute x6, waiting for transfers between devices: 0.02 us -> 3.95 us  [body(): mate = lambda value: lax.ppermute(value, 'rep', to_mate)]
  transfers between devices with their start and end apart: 12 -> 11, of which waited for: 4 -> 6; matrix products, arithmetic and copies ran while one was open for 10% -> 6% of each run, Pallas kernels for 0% -> 2%
where the time goes in v7:
time: 191 us; the launch traced here: 190 us
  waiting for transfers between devices  56.3 us (29%)
  starting transfers between devices  53.2 us (28%)
  blocking collectives  35.6 us (19%)
  between operations  15.5 us (8%)
  other arithmetic  10.3 us (5%)
  Pallas kernels  7.62 us (4%)
  matrix products  6.49 us (3%)
  local copies, waits for them, and re-layouts  4.94 us (3%)
    all_to_all x4, waiting for transfers between devices, swapped(): lax.all_to_all(value, axis, 0, 0, axis_index_groups=groups, tiled=True)  52.4 us
    all_to_all x4, starting transfers between devices, swapped(): lax.all_to_all(value, axis, 0, 0, axis_index_groups=groups, tiled=True)  41.1 us
    all_to_all x2, blocking collectives, swapped(): lax.all_to_all(value, axis, 0, 0, axis_index_groups=groups, tiled=True)  35.6 us
    ppermute x6, starting transfers between devices, body(): mate = lambda value: lax.ppermute(value, 'rep', to_mate)  12.1 us
    dot_general x4, matrix products, product(): lax.dot_general(left, right, (((left_dim,), (right_dim,)), ((), ())), pre...  6.49 us
    pallas_call x2, Pallas kernels, joined(): pl.pallas_call(kernel, grid=(1,), in_specs=[pl.BlockSpec((count, rows, 2...  4.36 us
    ppermute x6, waiting for transfers between devices, body(): mate = lambda value: lax.ppermute(value, 'rep', to_mate)  3.95 us
  transfers between devices with their start and end apart: 11, of which 6 were waited for; matrix products, arithmetic and copies ran while one was open for 6% of the time, Pallas kernels for 2%

profile of v7, /device:TPU:6, one launch (start us, length us, event | category | flops | bytes accessed | tf_op | source)
XLA Modules:
  0.0 190.2 jit_solution(3364429220149580294)
XLA Ops:
  7.2 1.3 fusion.27
  9.1 0.7 compare_convert_fusion
  9.8 0.8 fusion.24
  10.6 0.7 pad_maximum_fusion.2
  11.3 1.3 broadcast_in_dim.13
  12.7 16.1 %all-to-all-start.2 = ((bf16[32,32,768]{2,1,0:T(8,128)(2,1)}), bf16[32,32,768]{2,1,0:T(8,128)(2,1)S(1)}, u32[]{:S(2)}, u32[]{:S(2)}) async-start(bf16[32,32,768]{2,1,0:T(8,128)(2,1)} %broadcast_in_dim.13), calls=%async_computation.2 | async-start | bytes 3145728 | tf_op jit(solution)/shard_map/all_to_all | solution.py:99
  28.8 1.9 %collective-permute-start.4 = (bf16[768,384]{1,0:T(8,128)(2,1)S(1)}, bf16[768,384]{1,0:T(8,128)(2,1)S(1)}, u32[]{:S(2)}, u32[]{:S(2)}) collective-permute-start(bf16[768,384]{1,0:T(8,128)(2,1)S(1)} %copy-done.4), channel_id=1, source_target_pairs={{0,64},{64,0},{128,192},{192,128},{256,320},{320,256},{384,448},{4... | collective-permute-start | bytes 1769480 | tf_op jit(solution)/shard_map/ppermute | solution.py:123
  30.7 2.0 %collective-permute-done.4.other_ref = bf16[768,384]{1,0:T(8,128)(2,1)S(1)} collective-permute-done((bf16[768,384]{1,0:T(8,128)(2,1)S(1)}, bf16[768,384]{1,0:T(8,128)(2,1)S(1)}, u32[]{:S(2)}, u32[]{:S(2)}) %collective-permute-start.4) | collective-permute-done | bytes 589856 | tf_op jit(solution)/shard_map/ppermute | solution.py:123
  32.7 36.7 %all-to-all-done.2.left_ref = bf16[32,32,768]{2,1,0:T(8,128)(2,1)S(1)} async-done(((bf16[32,32,768]{2,1,0:T(8,128)(2,1)}), bf16[32,32,768]{2,1,0:T(8,128)(2,1)S(1)}, u32[]{:S(2)}, u32[]{:S(2)}) %all-to-all-start.2) | async-done | bytes 1572896 | tf_op jit(solution)/shard_map/all_to_all | solution.py:99
  69.4 1.9 shard_map.84
  71.3 5.3 %all-to-all-start.3 = ((bf16[8,64,768]{2,1,0:T(8,128)(2,1)}), bf16[8,64,768]{2,1,0:T(8,128)(2,1)}, u32[]{:S(2)}, u32[]{:S(2)}) async-start(bf16[8,64,768]{2,1,0:T(8,128)(2,1)} %bitcast.8), calls=%async_computation.3 | async-start | bytes 1572864 | tf_op jit(solution)/shard_map/all_to_all | solution.py:99
  76.6 1.9 %collective-permute-start.5 = (bf16[384,768]{1,0:T(8,128)(2,1)S(1)}, bf16[384,768]{1,0:T(8,128)(2,1)S(1)}, u32[]{:S(2)}, u32[]{:S(2)}) collective-permute-start(bf16[384,768]{1,0:T(8,128)(2,1)S(1)} %copy-done), channel_id=1, source_target_pairs={{0,64},{64,0},{128,192},{192,128},{256,320},{320,256},{384,448},{4... | collective-permute-start | bytes 1769480 | tf_op jit(solution)/shard_map/ppermute | solution.py:123
  78.5 2.0 %collective-permute-done.5.other_ref = bf16[384,768]{1,0:T(8,128)(2,1)S(1)} collective-permute-done((bf16[384,768]{1,0:T(8,128)(2,1)S(1)}, bf16[384,768]{1,0:T(8,128)(2,1)S(1)}, u32[]{:S(2)}, u32[]{:S(2)}) %collective-permute-start.5) | collective-permute-done | bytes 589856 | tf_op jit(solution)/shard_map/ppermute | solution.py:123
  80.5 1.4 shard_map.85
  81.9 2.8 %all-to-all-done.3 = bf16[8,64,768]{2,1,0:T(8,128)(2,1)} async-done(((bf16[8,64,768]{2,1,0:T(8,128)(2,1)}), bf16[8,64,768]{2,1,0:T(8,128)(2,1)}, u32[]{:S(2)}, u32[]{:S(2)}) %all-to-all-start.3) | async-done | bytes 786464 | tf_op jit(solution)/shard_map/all_to_all | solution.py:99
  84.7 2.0 %fusion.18 = (bf16[64,768]{1,0:T(8,128)(2,1)S(1)}, f32[1,64,768]{2,1,0:T(8,128)}) fusion(bf16[8,64,768]{2,1,0:T(8,128)(2,1)} %all-to-all-done.3), kind=kLoop, calls=%fused_computation.29 | loop fusion | flops 1179648 | bytes 1081344 | tf_op jit(solution)/shard_map/broadcast_in_dim | solution.py:154
  86.7 0.1 broadcast_in_dim.28
  86.8 0.1 pad_maximum_fusion
  86.9 22.1 %all_to_all.28.left_ref = bf16[8,64,1536]{2,1,0:T(8,128)(2,1)S(1)} all-to-all(bf16[8,64,1536]{2,1,0:T(8,128)(2,1)S(1)} %pad_maximum_fusion), channel_id=1, replica_groups=mesh['rep'=8,'row'=8,'col'=8] {'row'}, dimensions={0} | all-to-all | bytes 3145728 | tf_op jit(solution)/shard_map/all_to_all | solution.py:99
  109.0 1.2 copy-done.1
  110.1 1.9 shard_map.86
  112.0 0.0 reduce-scatter.2.cloned.1.call-update
  112.8 1.5 fusion.15
  114.3 53.1 %conditional.1 = (f32[768,384]{1,0:T(8,128)}, f32[384,768]{1,0:T(8,128)}, bf16[4,16,768]{2,1,0:T(8,128)(2,1)}) conditional(s32[]{:T(128)} %convert_element_type.220, () %tuple.18, (bf16[32,32,768]{2,1,0:T(8,128)(2,1)S(1)}, bf16[64,768]{1,0:T(8,128)(2,1)S(1)}, bf16[8,64,1536]{2,1,0:T(8,128)(2,1)}, bf16[768,384]{1,0:T(8,128)(2,1)S(1)}, ...), branch_computations={%region_3.4_spmd, %region_4.5_spmd} | conditional | flops 1813315584 | bytes 47644976 | solution.py:184
  114.3 1.0 broadcast_in_dim.2
  115.3 5.8 %all-to-all-start = ((bf16[8,64,768]{2,1,0:T(8,128)(2,1)}), bf16[8,64,768]{2,1,0:T(8,128)(2,1)S(1)}, u32[]{:S(2)}, u32[]{:S(2)}) async-start(bf16[8,64,768]{2,1,0:T(8,128)(2,1)} %broadcast_in_dim.2), calls=%async_computation | async-start | bytes 1572864 | tf_op jit(solution)/shard_map/cond/branch_1_fun/all_to_all | solution.py:99
  121.1 1.3 fusion.28
  122.4 1.9 %collective-permute-start.3 = (bf16[512,768]{1,0:T(8,128)(2,1)}, bf16[512,768]{1,0:T(8,128)(2,1)}, u32[]{:S(2)}, u32[]{:S(2)}) collective-permute-start(bf16[512,768]{1,0:T(8,128)(2,1)} %bitcast.3), channel_id=1, source_target_pairs={{0,64},{64,0},{128,192},{192,128},{256,320},{320,256},{384,448},{4... | collective-permute-start | bytes 2359304 | tf_op jit(solution)/shard_map/cond/branch_1_fun/ppermute | solution.py:123
  124.3 4.4 %all-to-all-done.left_ref = bf16[8,64,768]{2,1,0:T(8,128)(2,1)S(1)} async-done(((bf16[8,64,768]{2,1,0:T(8,128)(2,1)}), bf16[8,64,768]{2,1,0:T(8,128)(2,1)S(1)}, u32[]{:S(2)}, u32[]{:S(2)}) %all-to-all-start) | async-done | bytes 786464 | tf_op jit(solution)/shard_map/cond/branch_1_fun/all_to_all | solution.py:99
  128.7 2.5 %branch_1_fun.1 = bf16[512,768]{1,0:T(8,128)(2,1)} custom-call(bf16[8,64,768]{2,1,0:T(8,128)(2,1)S(1)} %all-to-all-done.left_ref, bf16[768,384]{1,0:T(8,128)(2,1)S(1)} %get-tuple-element.21.own_ref, bf16[768,384]{1,0:T(8,128)(2,1)S(1)} %get-tuple-element.22.other_ref), custom_call_target="tpu_custom_call" | custom-call | flops 603979776 | bytes 4194304 | tf_op jit(solution)/shard_map/cond/branch_1_fun/pallas_call | solution.py:76
  131.2 13.8 %all-to-all-start.1 = ((bf16[8,64,768]{2,1,0:T(8,128)(2,1)}), bf16[8,64,768]{2,1,0:T(8,128)(2,1)S(1)}, u32[]{:S(2)}, u32[]{:S(2)}) async-start(bf16[8,64,768]{2,1,0:T(8,128)(2,1)} %bitcast.4), calls=%async_computation.1 | async-start | bytes 1572864 | tf_op jit(solution)/shard_map/cond/branch_1_fun/all_to_all | solution.py:99
  145.0 0.0 copy-start.3
  145.0 0.1 slice.93
  145.2 2.1 %collective-permute-start.2 = (bf16[512,384]{1,0:T(8,128)(2,1)S(1)}, bf16[512,384]{1,0:T(8,128)(2,1)S(1)}, u32[]{:S(2)}, u32[]{:S(2)}) collective-permute-start(bf16[512,384]{1,0:T(8,128)(2,1)S(1)} %slice.156), channel_id=1, source_target_pairs={{0,64},{64,0},{128,192},{192,128},{256,320},{320,256},{384,448},{4... | collective-permute-start | bytes 1179656 | tf_op jit(solution)/shard_map/cond/branch_1_fun/ppermute | solution.py:123
  147.2 2.4 %collective-permute-start = (bf16[512,768]{1,0:T(8,128)(2,1)S(1)}, bf16[512,768]{1,0:T(8,128)(2,1)S(1)}, u32[]{:S(2)}, u32[]{:S(2)}) collective-permute-start(bf16[512,768]{1,0:T(8,128)(2,1)S(1)} %bitcast.63), channel_id=1, source_target_pairs={{0,64},{64,0},{128,192},{192,128},{256,320},{320,256},{384,448},{4... | collective-permute-start | bytes 2359304 | tf_op jit(solution)/shard_map/cond/branch_1_fun/ppermute | solution.py:123
  149.6 1.6 fusion
  151.3 1.9 %collective-permute-start.1 = (bf16[512,384]{1,0:T(8,128)(2,1)S(1)}, bf16[512,384]{1,0:T(8,128)(2,1)S(1)}, u32[]{:S(2)}, u32[]{:S(2)}) collective-permute-start(bf16[512,384]{1,0:T(8,128)(2,1)S(1)} %slice.154), channel_id=1, source_target_pairs={{0,64},{64,0},{128,192},{192,128},{256,320},{320,256},{384,448},{4... | collective-permute-start | bytes 1179656 | tf_op jit(solution)/shard_map/cond/branch_1_fun/ppermute | solution.py:123
  153.3 0.0 collective-permute-done.3
  153.3 2.6 %convolution_add_fusion = f32[384,768]{1,0:T(8,128)} fusion(f32[384,768]{1,0:T(8,128)S(1)} %fusion, bf16[512,384]{1,0:T(8,128)(2,1)S(1)} %collective-permute-done.2, bf16[512,768]{1,0:T(8,128)(2,1)} %collective-permute-done.3), kind=kOutput, calls=%fused_computation | convolution fusion | flops 302284800 | bytes 3538944 | tf_op jit(solution)/shard_map/cond/branch_1_fun/dot_general | solution.py:26
  155.9 0.6 fusion.2
  156.5 0.0 collective-permute-done
  156.5 0.0 collective-permute-done.1
  156.5 1.6 convolution_add_fusion.1
  158.2 8.5 %all-to-all-done.1 = bf16[8,64,768]{2,1,0:T(8,128)(2,1)S(1)} async-done(((bf16[8,64,768]{2,1,0:T(8,128)(2,1)}), bf16[8,64,768]{2,1,0:T(8,128)(2,1)S(1)}, u32[]{:S(2)}, u32[]{:S(2)}) %all-to-all-start.1) | async-done | bytes 786464 | tf_op jit(solution)/shard_map/cond/branch_1_fun/all_to_all | solution.py:99
  166.7 0.7 add_convert_fusion
  167.4 1.0 pad_maximum_fusion.1
  168.4 13.5 %all_to_all.29 = bf16[4,32,768]{2,1,0:T(8,128)(2,1)S(1)} all-to-all(bf16[4,32,768]{2,1,0:T(8,128)(2,1)S(1)} %pad_maximum_fusion.1), channel_id=1, replica_groups={{0,128,256,384},{64,192,320,448},{1,129,257,385},{65,193,321,449},{2,13..., dimensions={0} | all-to-all | bytes 393216 | tf_op jit(solution)/shard_map/all_to_all | solution.py:99
  181.9 1.4 fusion.26
  (20 shorter events, 0.1 us)
Async XLA Ops:
  12.7 16.1 %copy-start.4 = (bf16[768,384]{1,0:T(8,128)(2,1)S(1)}, bf16[768,384]{1,0:T(8,128)(2,1)}, u32[]{:S(2)}) copy-start(bf16[768,384]{1,0:T(8,128)(2,1)} %own_ref.3) | copy-start | bytes 1769476
  12.7 56.7 %all-to-all-start.2 = ((bf16[32,32,768]{2,1,0:T(8,128)(2,1)}), bf16[32,32,768]{2,1,0:T(8,128)(2,1)S(1)}, u32[]{:S(2)}, u32[]{:S(2)}) async-start(bf16[32,32,768]{2,1,0:T(8,128)(2,1)} %broadcast_in_dim.13), calls=%async_computation.2 | async-start | bytes 3145728 | tf_op jit(solution)/shard_map/all_to_all | solution.py:99
  28.8 3.9 %collective-permute-start.4 = (bf16[768,384]{1,0:T(8,128)(2,1)S(1)}, bf16[768,384]{1,0:T(8,128)(2,1)S(1)}, u32[]{:S(2)}, u32[]{:S(2)}) collective-permute-start(bf16[768,384]{1,0:T(8,128)(2,1)S(1)} %copy-done.4), channel_id=1, source_target_pairs={{0,64},{64,0},{128,192},{192,128},{256,320},{320,256},{384,448},{4... | collective-permute-start | bytes 1769480 | tf_op jit(solution)/shard_map/ppermute | solution.py:123
  32.7 38.6 %copy-start.6 = (bf16[768,384]{1,0:T(8,128)(2,1)}, bf16[768,384]{1,0:T(8,128)(2,1)S(1)}, u32[]{:S(2)}) copy-start(bf16[768,384]{1,0:T(8,128)(2,1)S(1)} %collective-permute-done.4.other_ref) | copy-start | bytes 1769476
  71.3 5.3 %copy-start = (bf16[384,768]{1,0:T(8,128)(2,1)S(1)}, bf16[384,768]{1,0:T(8,128)(2,1)}, u32[]{:S(2)}) copy-start(bf16[384,768]{1,0:T(8,128)(2,1)} %own_ref.5) | copy-start | bytes 1769476
  71.3 13.4 %all-to-all-start.3 = ((bf16[8,64,768]{2,1,0:T(8,128)(2,1)}), bf16[8,64,768]{2,1,0:T(8,128)(2,1)}, u32[]{:S(2)}, u32[]{:S(2)}) async-start(bf16[8,64,768]{2,1,0:T(8,128)(2,1)} %bitcast.8), calls=%async_computation.3 | async-start | bytes 1572864 | tf_op jit(solution)/shard_map/all_to_all | solution.py:99
  76.6 90.8 %reduce-scatter.2.cloned.1.call-start = ((), (), s32[]{:S(2)}) async-start(), calls=%async_computation.7 | async-start | bytes 884736 | tf_op jit(solution)/shard_map/reduce_scatter | solution.py:159
  76.6 3.9 %collective-permute-start.5 = (bf16[384,768]{1,0:T(8,128)(2,1)S(1)}, bf16[384,768]{1,0:T(8,128)(2,1)S(1)}, u32[]{:S(2)}, u32[]{:S(2)}) collective-permute-start(bf16[384,768]{1,0:T(8,128)(2,1)S(1)} %copy-done), channel_id=1, source_target_pairs={{0,64},{64,0},{128,192},{192,128},{256,320},{320,256},{384,448},{4... | collective-permute-start | bytes 1769480 | tf_op jit(solution)/shard_map/ppermute | solution.py:123
  109.0 1.2 copy-start.1
  112.0 2.3 %copy-start.5 = (bf16[768,384]{1,0:T(8,128)(2,1)S(1)}, bf16[768,384]{1,0:T(8,128)(2,1)}, u32[]{:S(2)}) copy-start(bf16[768,384]{1,0:T(8,128)(2,1)} %own_ref.3) | copy-start | bytes 1769476
  112.0 2.3 %copy-start.7 = (bf16[768,384]{1,0:T(8,128)(2,1)S(1)}, bf16[768,384]{1,0:T(8,128)(2,1)}, u32[]{:S(2)}) copy-start(bf16[768,384]{1,0:T(8,128)(2,1)} %copy-done.6) | copy-start | bytes 1769476
  115.3 13.4 %all-to-all-start = ((bf16[8,64,768]{2,1,0:T(8,128)(2,1)}), bf16[8,64,768]{2,1,0:T(8,128)(2,1)S(1)}, u32[]{:S(2)}, u32[]{:S(2)}) async-start(bf16[8,64,768]{2,1,0:T(8,128)(2,1)} %broadcast_in_dim.2), calls=%async_computation | async-start | bytes 1572864 | tf_op jit(solution)/shard_map/cond/branch_1_fun/all_to_all | solution.py:99
  122.4 30.9 %collective-permute-start.3 = (bf16[512,768]{1,0:T(8,128)(2,1)}, bf16[512,768]{1,0:T(8,128)(2,1)}, u32[]{:S(2)}, u32[]{:S(2)}) collective-permute-start(bf16[512,768]{1,0:T(8,128)(2,1)} %bitcast.3), channel_id=1, source_target_pairs={{0,64},{64,0},{128,192},{192,128},{256,320},{320,256},{384,448},{4... | collective-permute-start | bytes 2359304 | tf_op jit(solution)/shard_map/cond/branch_1_fun/ppermute | solution.py:123
  131.2 13.8 %copy-start.2 = (bf16[8,64,1536]{2,1,0:T(8,128)(2,1)S(1)}, bf16[8,64,1536]{2,1,0:T(8,128)(2,1)}, u32[]{:S(2)}) copy-start(bf16[8,64,1536]{2,1,0:T(8,128)(2,1)} %get-tuple-element.20) | copy-start | bytes 4718596 | tf_op jit(solution)/shard_map/cond
  131.2 35.5 %all-to-all-start.1 = ((bf16[8,64,768]{2,1,0:T(8,128)(2,1)}), bf16[8,64,768]{2,1,0:T(8,128)(2,1)S(1)}, u32[]{:S(2)}, u32[]{:S(2)}) async-start(bf16[8,64,768]{2,1,0:T(8,128)(2,1)} %bitcast.4), calls=%async_computation.1 | async-start | bytes 1572864 | tf_op jit(solution)/shard_map/cond/branch_1_fun/all_to_all | solution.py:99
  145.0 2.2 %copy-start.3 = (bf16[32,16,768]{2,1,0:T(8,128)(2,1)S(1)}, bf16[32,16,768]{2,1,0:T(8,128)(2,1)}, u32[]{:S(2)}) copy-start(bf16[32,16,768]{2,1,0:T(8,128)(2,1)} %get-tuple-element.38) | copy-start | bytes 2359300 | tf_op jit(solution)/shard_map/cond
  145.2 8.1 %collective-permute-start.2 = (bf16[512,384]{1,0:T(8,128)(2,1)S(1)}, bf16[512,384]{1,0:T(8,128)(2,1)S(1)}, u32[]{:S(2)}, u32[]{:S(2)}) collective-permute-start(bf16[512,384]{1,0:T(8,128)(2,1)S(1)} %slice.156), channel_id=1, source_target_pairs={{0,64},{64,0},{128,192},{192,128},{256,320},{320,256},{384,448},{4... | collective-permute-start | bytes 1179656 | tf_op jit(solution)/shard_map/cond/branch_1_fun/ppermute | solution.py:123
  147.2 9.3 %collective-permute-start = (bf16[512,768]{1,0:T(8,128)(2,1)S(1)}, bf16[512,768]{1,0:T(8,128)(2,1)S(1)}, u32[]{:S(2)}, u32[]{:S(2)}) collective-permute-start(bf16[512,768]{1,0:T(8,128)(2,1)S(1)} %bitcast.63), channel_id=1, source_target_pairs={{0,64},{64,0},{128,192},{192,128},{256,320},{320,256},{384,448},{4... | collective-permute-start | bytes 2359304 | tf_op jit(solution)/shard_map/cond/branch_1_fun/ppermute | solution.py:123
  151.3 5.2 %collective-permute-start.1 = (bf16[512,384]{1,0:T(8,128)(2,1)S(1)}, bf16[512,384]{1,0:T(8,128)(2,1)S(1)}, u32[]{:S(2)}, u32[]{:S(2)}) collective-permute-start(bf16[512,384]{1,0:T(8,128)(2,1)S(1)} %slice.154), channel_id=1, source_target_pairs={{0,64},{64,0},{128,192},{192,128},{256,320},{320,256},{384,448},{4... | collective-permute-start | bytes 1179656 | tf_op jit(solution)/shard_map/cond/branch_1_fun/ppermute | solution.py:123
Sparse Core Ops, SparseCore 0:
  112.2 44.5 reduce-scatter.1

commit v8 on v7

--- a/solution.py
+++ b/solution.py
@@ -28,9 +28,44 @@
     )
 
 
-def paired(blocks, half, own, other, turned):
-    count, rows, width = blocks.shape
-    rows //= 2
+def prepared(tokens, cotangent, counts, copies):
+    _, rows, width = tokens.shape
+
+    def kernel(counts_ref, tokens_ref, cotangent_ref, send_ref, scaled_ref):
+        own_count = counts_ref[lax.axis_index("rep")]
+        total = counts_ref[0]
+        for replica in range(1, counts.shape[0]):
+            total = total + counts_ref[replica]
+        token_total = (MBT * total).astype(jnp.float32)
+        positions = lax.axis_index("col") * rows + lax.broadcasted_iota(
+            jnp.int32, (rows, width), 0
+        )
+        kept_mask = (positions < MBT * own_count).astype(jnp.float32)
+        scaled = (cotangent_ref[0].astype(jnp.float32) * kept_mask / token_total).astype(
+            jnp.bfloat16
+        )
+        scaled_ref[...] = scaled
+        for copy in range(copies):
+            send_ref[copy, :rows] = tokens_ref[0]
+            send_ref[copy, rows:] = scaled
+
+    return pl.pallas_call(
+        kernel,
+        in_specs=[
+            pl.BlockSpec(memory_space=pltpu.SMEM),
+            pl.BlockSpec(memory_space=pltpu.VMEM),
+            pl.BlockSpec(memory_space=pltpu.VMEM),
+        ],
+        out_specs=[pl.BlockSpec(memory_space=pltpu.VMEM), pl.BlockSpec(memory_space=pltpu.VMEM)],
+        out_shape=[
+            jax.ShapeDtypeStruct((copies, 2 * rows, width), jnp.bfloat16),
+            jax.ShapeDtypeStruct((rows, width), jnp.bfloat16),
+        ],
+    )(counts, tokens, cotangent)
+
+
+def paired(blocks, rows, own, other, turned):
+    count, _, width = blocks.shape
     columns = own.shape[0] if turned else own.shape[1]
     step = count // 4
 
@@ -47,7 +82,7 @@
         kernel,
         grid=(1,),
         in_specs=[
-            pl.BlockSpec((count, rows, width), lambda i: (0, half, 0)),
+            pl.BlockSpec((count, rows, width), lambda i: (0, 0, 0)),
             pl.BlockSpec(own.shape, lambda i: (0, 0)),
             pl.BlockSpec(other.shape, lambda i: (0, 0)),
         ],
@@ -123,31 +158,30 @@
     mate = lambda value: lax.ppermute(value, "rep", to_mate)
 
     tokens_local = inputs.reshape(rows_local, width)
-    replica_index = lax.axis_index("rep")
-    column_index = lax.axis_index("col")
-    own_count = jnp.sum(jnp.where(jnp.arange(replicas) == replica_index, counts, 0))
-    token_total = (MBT * jnp.sum(counts)).astype(jnp.float32)
-    positions = column_index * rows_local + jnp.arange(rows_local, dtype=jnp.int32)
-    kept_mask = (positions // MBT < own_count).astype(jnp.float32)
-    scaled = (
-        cotangent.reshape(rows_local, width).astype(jnp.float32)
-        * kept_mask[:, None]
-        / token_total
-    ).astype(jnp.bfloat16)
+    send, scaled = prepared(inputs, cotangent, counts, chips)
 
     w_in_mate, w_out_mate = mate(w_in), mate(w_out)
 
+    line = swapped(send, "rep", same_core)
+    tokens_line = line[:, :rows_local].reshape(chips * rows_local, width)
+    scaled_line = line[:, rows_local:].reshape(chips * rows_local, width)
     line_rows = chips * rows_local
     rows_all = columns * line_rows
 
-    plane = [
-        [(chip * CORES + core) * columns + column for column in range(columns) for chip in range(chips)]
-        for core in range(CORES)
-    ]
-    both = jnp.concatenate([tokens_local, scaled], axis=0)
-    everyone = spread(both, ("rep", "col"), columns * chips, plane)
-    hidden_terms = paired(everyone, 0, w_in, w_in_mate, False)
-    slope_terms = paired(everyone, 1, w_out, w_out_mate, True)
+    padded = jnp.concatenate([scaled_line, scaled_line[: line_rows // 2]], axis=0)
+    scaled_blocks = lax.all_gather(padded, "col", axis=0)
+
+    def forward(line):
+        blocks = spread(line, "col", columns)
+        return blocks, paired(blocks, line_rows, w_in, w_in_mate, False)
+
+    def forward_plain(line):
+        blocks = lax.all_gather(line, "col", axis=0)
+        return blocks, paired(blocks, line_rows, w_in, w_in_mate, False)
+
+    some_kept = jnp.sum(counts) > 0
+    tokens_blocks, hidden_terms = lax.cond(some_kept, forward, forward_plain, tokens_line)
+    slope_terms = paired(scaled_blocks, line_rows, w_out, w_out_mate, True)
 
     hidden = added_up(swapped(cut(hidden_terms, row_count), "row"))
     active, slope = gelu_both(hidden)
@@ -157,9 +191,8 @@
     grad_share = (added_up(mixed[:, :, active.shape[1] :]) * slope).astype(jnp.bfloat16)
     output_terms = joined(mixed, w_out, w_out_mate, False)
     output_line = lax.psum_scatter(output_terms, "col", scatter_dimension=0, tiled=True)
-    tokens_all, scaled_all = [
-        everyone[:, at * rows_local : (at + 1) * rows_local].reshape(rows_all, width) for at in (0, 1)
-    ]
+    tokens_all = tokens_blocks.reshape(rows_all, width)
+    scaled_all = scaled_blocks[:, :line_rows].reshape(rows_all, width)
 
     def backward(share):
         shares = spread(share, "row", row_count)
@@ -181,7 +214,7 @@
             jnp.zeros((units, width), jnp.float32),
         )
 
-    back_line, w_in_grad, w_out_grad = lax.cond(jnp.sum(counts) > 0, backward, nothing, grad_share)
+    back_line, w_in_grad, w_out_grad = lax.cond(some_kept, backward, nothing, grad_share)
     ends = jnp.concatenate([cut(output_line, chips), cut(back_line, chips)], axis=1)
     finished = added_up(swapped(ends, "rep", same_core))
     block_output = (tokens_local.astype(jnp.float32) + finished[:rows_local]).astype(jnp.bfloat16)

time: 191 us -> 182 us (0.953)
  blocking collectives: 35.6 us -> 70.9 us
  waiting for transfers between devices: 56.3 us -> 27 us
  starting transfers between devices: 53.2 us -> 39.5 us
  other arithmetic: 10.3 us -> 5.31 us
  Pallas kernels: 7.62 us -> 12.6 us
    all_to_all x2 -> x3, blocking collectives: 35.6 us -> 70.9 us  [swapped(): lax.all_to_all(value, axis, 0, 0, axis_index_groups=groups, tiled=True)]
    all_to_all x4, waiting for transfers between devices: 52.4 us -> 27 us  [swapped(): lax.all_to_all(value, axis, 0, 0, axis_index_groups=groups, tiled=True)]
    all_to_all x4, starting transfers between devices: 41.1 us -> 27.6 us  [swapped(): lax.all_to_all(value, axis, 0, 0, axis_index_groups=groups, tiled=True)]
    ppermute x6, waiting for transfers between devices: 3.95 us -> 0.02 us  [body(): mate = lambda value: lax.ppermute(value, 'rep', to_mate)]
    pallas_call x2, Pallas kernels: 3.26 us -> 5.7 us  [paired(): pl.pallas_call(kernel, grid=(1,), in_specs=[pl.BlockSpec((count, rows, wi...]
  transfers between devices with their start and end apart: 11 -> 12, of which waited for: 6 -> 4; matrix products, arithmetic and copies ran while one was open for 6% -> 8% of each run, Pallas kernels for 2% -> 4%
where the time goes in v8:
time: 182 us; the launch traced here: 181 us
  blocking collectives  70.9 us (39%)
  starting transfers between devices  39.5 us (22%)
  waiting for transfers between devices  27 us (15%)
  between operations  14.8 us (8%)
  Pallas kernels  12.6 us (7%)
  matrix products  7.64 us (4%)
  other arithmetic  5.31 us (3%)
  local copies, waits for them, and re-layouts  3.29 us (2%)
    all_to_all x3, blocking collectives, swapped(): lax.all_to_all(value, axis, 0, 0, axis_index_groups=groups, tiled=True)  70.9 us
    all_to_all x4, starting transfers between devices, swapped(): lax.all_to_all(value, axis, 0, 0, axis_index_groups=groups, tiled=True)  27.6 us
    all_to_all x4, waiting for transfers between devices, swapped(): lax.all_to_all(value, axis, 0, 0, axis_index_groups=groups, tiled=True)  27 us
    ppermute x6, starting transfers between devices, body(): mate = lambda value: lax.ppermute(value, 'rep', to_mate)  12 us
    dot_general x4, matrix products, product(): lax.dot_general(left, right, (((left_dim,), (right_dim,)), ((), ())), pre...  7.64 us
    pallas_call x2, Pallas kernels, paired(): pl.pallas_call(kernel, grid=(1,), in_specs=[pl.BlockSpec((count, rows, wi...  5.7 us
    pallas_call x2, Pallas kernels, joined(): pl.pallas_call(kernel, grid=(1,), in_specs=[pl.BlockSpec((count, rows, 2...  5.4 us
  transfers between devices with their start and end apart: 12, of which 4 were waited for; matrix products, arithmetic and copies ran while one was open for 8% of the time, Pallas kernels for 4%

profile of v8, /device:TPU:6, one launch (start us, length us, event | category | flops | bytes accessed | tf_op | source)
XLA Modules:
  0.0 181.3 jit_solution(3843875962523776880)
XLA Ops:
  7.2 0.0 copy-start.1
  7.2 1.5 shard_map.84
  8.7 10.3 %all-to-all-start.3 = ((bf16[4,32,768]{2,1,0:T(8,128)(2,1)}), bf16[4,32,768]{2,1,0:T(8,128)(2,1)S(1)}, u32[]{:S(2)}, u32[]{:S(2)}) async-start(bf16[4,32,768]{2,1,0:T(8,128)(2,1)} %get-tuple-element.55), calls=%async_computation.3 | async-start | bytes 393216 | tf_op jit(solution)/shard_map/all_to_all | solution.py:134
  19.0 1.9 %collective-permute-start.4 = (bf16[768,384]{1,0:T(8,128)(2,1)}, bf16[768,384]{1,0:T(8,128)(2,1)}, u32[]{:S(2)}, u32[]{:S(2)}) collective-permute-start(bf16[768,384]{1,0:T(8,128)(2,1)} %param.10), channel_id=1, source_target_pairs={{0,64},{64,0},{128,192},{192,128},{256,320},{320,256},{384,448},{4... | collective-permute-start | bytes 1769480 | tf_op jit(solution)/shard_map/ppermute | solution.py:158
  20.9 8.0 %all-to-all-done.3 = bf16[4,32,768]{2,1,0:T(8,128)(2,1)S(1)} async-done(((bf16[4,32,768]{2,1,0:T(8,128)(2,1)}), bf16[4,32,768]{2,1,0:T(8,128)(2,1)S(1)}, u32[]{:S(2)}, u32[]{:S(2)}) %all-to-all-start.3) | async-done | bytes 196640 | tf_op jit(solution)/shard_map/all_to_all | solution.py:134
  29.0 0.7 pad_maximum_fusion.2
  29.7 0.0 all-gather.3.cloned.1.call-update
  29.7 0.6 reduce_sum.9
  31.0 37.5 %conditional.2 = (bf16[512,768]{1,0:T(8,128)(2,1)}, bf16[512,768]{1,0:T(8,128)(2,1)}) conditional(s32[]{:T(128)} %convert_element_type.192, (bf16[4,32,768]{2,1,0:T(8,128)(2,1)S(1)}, bf16[768,384]{1,0:T(8,128)(2,1)S(1)}, bf16[768,384]{1,0:T(8,128)(2,1)}) %tuple.41, (bf16[4,32,768]{2,1,0:T(8,128)(2,1)S(1)}, bf16[768,384]{1,0:T(8,128)(2,1)S(1)}, ...), branch_computations={%region_1.0_spmd, %region_2.0_spmd} | conditional | flops 603979776 | bytes 6848528 | solution.py:183
  31.0 0.1 broadcast_in_dim.6
  31.1 34.3 %all_to_all.32.left_ref = bf16[8,64,768]{2,1,0:T(8,128)(2,1)} all-to-all(bf16[8,64,768]{2,1,0:T(8,128)(2,1)S(1)} %broadcast_in_dim.6), channel_id=1, replica_groups=mesh['rep'=8,'row'=8,'col'=8] {'col'}, dimensions={0} | all-to-all | bytes 1572864 | tf_op jit(solution)/shard_map/cond/branch_1_fun/all_to_all | solution.py:134
  65.4 3.2 %branch_1_fun.2 = bf16[512,768]{1,0:T(8,128)(2,1)} custom-call(bf16[8,64,768]{2,1,0:T(8,128)(2,1)} %all_to_all.32.left_ref, bf16[768,384]{1,0:T(8,128)(2,1)S(1)} %get-tuple-element.36.own_ref, bf16[768,384]{1,0:T(8,128)(2,1)} %get-tuple-element.37.other_ref), custom_call_target="tpu_custom_call" | custom-call | flops 603979776 | bytes 4194304 | tf_op jit(solution)/shard_map/cond/branch_1_fun/pallas_call | solution.py:81
  68.6 6.4 %all-to-all-start.4 = ((bf16[8,64,768]{2,1,0:T(8,128)(2,1)}), bf16[8,64,768]{2,1,0:T(8,128)(2,1)S(1)}, u32[]{:S(2)}, u32[]{:S(2)}) async-start(bf16[8,64,768]{2,1,0:T(8,128)(2,1)} %bitcast.9), calls=%async_computation.4 | async-start | bytes 1572864 | tf_op jit(solution)/shard_map/all_to_all | solution.py:134
  75.0 1.9 %collective-permute-start.5 = (bf16[384,768]{1,0:T(8,128)(2,1)S(1)}, bf16[384,768]{1,0:T(8,128)(2,1)S(1)}, u32[]{:S(2)}, u32[]{:S(2)}) collective-permute-start(bf16[384,768]{1,0:T(8,128)(2,1)S(1)} %copy-done), channel_id=1, source_target_pairs={{0,64},{64,0},{128,192},{192,128},{256,320},{320,256},{384,448},{4... | collective-permute-start | bytes 1769480 | tf_op jit(solution)/shard_map/ppermute | solution.py:158
  76.9 5.6 %all-to-all-done.4 = bf16[8,64,768]{2,1,0:T(8,128)(2,1)S(1)} async-done(((bf16[8,64,768]{2,1,0:T(8,128)(2,1)}), bf16[8,64,768]{2,1,0:T(8,128)(2,1)S(1)}, u32[]{:S(2)}, u32[]{:S(2)}) %all-to-all-start.4) | async-done | bytes 786464 | tf_op jit(solution)/shard_map/all_to_all | solution.py:134
  82.6 0.2 fusion.18
  82.7 0.0 all-gather.3.cloned.1.call-done
  82.8 2.5 %shard_map.85 = bf16[512,768]{1,0:T(8,128)(2,1)S(1)} custom-call(bf16[8,96,768]{2,1,0:T(8,128)(2,1)} %bitcast.50, bf16[384,768]{1,0:T(8,128)(2,1)S(1)} %copy-done, bf16[384,768]{1,0:T(8,128)(2,1)S(1)} %collective-permute-done.5.other_ref), custom_call_target="tpu_custom_call" | custom-call | flops 603979776 | bytes 4194304 | tf_op jit(solution)/shard_map/pallas_call | solution.py:81
  85.3 0.1 broadcast_in_dim.22
  85.4 0.1 pad_maximum_fusion
  85.5 20.8 %all_to_all.33.left_ref = bf16[8,64,1536]{2,1,0:T(8,128)(2,1)S(1)} all-to-all(bf16[8,64,1536]{2,1,0:T(8,128)(2,1)S(1)} %pad_maximum_fusion), channel_id=1, replica_groups=mesh['rep'=8,'row'=8,'col'=8] {'row'}, dimensions={0} | all-to-all | bytes 3145728 | tf_op jit(solution)/shard_map/all_to_all | solution.py:134
  106.3 1.9 %shard_map.86 = bf16[512,768]{1,0:T(8,128)(2,1)} custom-call(bf16[8,64,1536]{2,1,0:T(8,128)(2,1)S(1)} %all_to_all.33.left_ref, bf16[384,768]{1,0:T(8,128)(2,1)S(1)} %copy-done, bf16[384,768]{1,0:T(8,128)(2,1)S(1)} %collective-permute-done.5.other_ref), custom_call_target="tpu_custom_call" | custom-call | flops 603979776 | bytes 4194304 | tf_op jit(solution)/shard_map/pallas_call | solution.py:111
  108.2 0.0 reduce-scatter.2.cloned.1.call-update
  108.2 0.2 fusion.15
  108.5 0.0 copy-start.2
  108.5 48.0 %conditional.3 = (f32[768,384]{1,0:T(8,128)}, f32[384,768]{1,0:T(8,128)}, bf16[4,16,768]{2,1,0:T(8,128)(2,1)S(1)}) conditional(s32[]{:T(128)} %convert_element_type.192, () %tuple.29, (bf16[64,768]{1,0:T(8,128)(2,1)S(1)}, bf16[512,768]{1,0:T(8,128)(2,1)}, bf16[8,64,1536]{2,1,0:T(8,128)(2,1)S(1)}, bf16[8,96,768]{2,1,0:T(8,128)(2,1)}, ...), branch_computations={%region_4.0_spmd, %region_5.0_spmd} | conditional | flops 1813315584 | bytes 36634872 | solution.py:217
  108.5 0.9 broadcast_in_dim.10
  109.4 5.8 %all-to-all-start.1 = ((bf16[8,64,768]{2,1,0:T(8,128)(2,1)}), bf16[8,64,768]{2,1,0:T(8,128)(2,1)S(1)}, u32[]{:S(2)}, u32[]{:S(2)}) async-start(bf16[8,64,768]{2,1,0:T(8,128)(2,1)} %broadcast_in_dim.10), calls=%async_computation.1 | async-start | bytes 1572864 | tf_op jit(solution)/shard_map/cond/branch_1_fun/all_to_all | solution.py:134
  115.3 2.1 %slice.105 = bf16[8,64,768]{2,1,0:T(8,128)(2,1)} slice(bf16[8,96,768]{2,1,0:T(8,128)(2,1)} %get-tuple-element.41), slice={[0:8], [0:64], [0:768]} | slice | bytes 1572864 | tf_op jit(solution)/shard_map/slice | solution.py:195
  117.3 1.9 %collective-permute-start.3 = (bf16[512,768]{1,0:T(8,128)(2,1)}, bf16[512,768]{1,0:T(8,128)(2,1)}, u32[]{:S(2)}, u32[]{:S(2)}) collective-permute-start(bf16[512,768]{1,0:T(8,128)(2,1)} %bitcast.6), channel_id=1, source_target_pairs={{0,64},{64,0},{128,192},{192,128},{256,320},{320,256},{384,448},{4... | collective-permute-start | bytes 2359304 | tf_op jit(solution)/shard_map/cond/branch_1_fun/ppermute | solution.py:158
  119.3 3.6 %all-to-all-done.1.left_ref = bf16[8,64,768]{2,1,0:T(8,128)(2,1)S(1)} async-done(((bf16[8,64,768]{2,1,0:T(8,128)(2,1)}), bf16[8,64,768]{2,1,0:T(8,128)(2,1)S(1)}, u32[]{:S(2)}, u32[]{:S(2)}) %all-to-all-start.1) | async-done | bytes 786464 | tf_op jit(solution)/shard_map/cond/branch_1_fun/all_to_all | solution.py:134
  122.9 3.5 %branch_1_fun.3 = bf16[512,768]{1,0:T(8,128)(2,1)} custom-call(bf16[8,64,768]{2,1,0:T(8,128)(2,1)S(1)} %all-to-all-done.1.left_ref, bf16[768,384]{1,0:T(8,128)(2,1)S(1)} %get-tuple-element.42.own_ref, bf16[768,384]{1,0:T(8,128)(2,1)} %get-tuple-element.43.other_ref), custom_call_target="tpu_custom_call" | custom-call | flops 603979776 | bytes 4194304 | tf_op jit(solution)/shard_map/cond/branch_1_fun/pallas_call | solution.py:111
  126.4 5.0 %all-to-all-start.2 = ((bf16[8,64,768]{2,1,0:T(8,128)(2,1)}), bf16[8,64,768]{2,1,0:T(8,128)(2,1)}, u32[]{:S(2)}, u32[]{:S(2)}) async-start(bf16[8,64,768]{2,1,0:T(8,128)(2,1)} %bitcast.7), calls=%async_computation.2 | async-start | bytes 1572864 | tf_op jit(solution)/shard_map/cond/branch_1_fun/all_to_all | solution.py:134
  131.4 0.1 slice.103
  131.5 1.9 %collective-permute-start.2 = (bf16[512,384]{1,0:T(8,128)(2,1)S(1)}, bf16[512,384]{1,0:T(8,128)(2,1)S(1)}, u32[]{:S(2)}, u32[]{:S(2)}) collective-permute-start(bf16[512,384]{1,0:T(8,128)(2,1)S(1)} %slice.172), channel_id=1, source_target_pairs={{0,64},{64,0},{128,192},{192,128},{256,320},{320,256},{384,448},{4... | collective-permute-start | bytes 1179656 | tf_op jit(solution)/shard_map/cond/branch_1_fun/ppermute | solution.py:158
  133.4 2.4 %collective-permute-start = (bf16[512,768]{1,0:T(8,128)(2,1)}, bf16[512,768]{1,0:T(8,128)(2,1)S(1)}, u32[]{:S(2)}, u32[]{:S(2)}) collective-permute-start(bf16[512,768]{1,0:T(8,128)(2,1)} %get-tuple-element.38), channel_id=1, source_target_pairs={{0,64},{64,0},{128,192},{192,128},{256,320},{320,256},{384,448},{4... | collective-permute-start | bytes 2359304 | tf_op jit(solution)/shard_map/cond/branch_1_fun/ppermute | solution.py:158
  135.8 1.6 fusion
  137.5 1.9 %collective-permute-start.1 = (bf16[512,384]{1,0:T(8,128)(2,1)S(1)}, bf16[512,384]{1,0:T(8,128)(2,1)S(1)}, u32[]{:S(2)}, u32[]{:S(2)}) collective-permute-start(bf16[512,384]{1,0:T(8,128)(2,1)S(1)} %slice.170), channel_id=1, source_target_pairs={{0,64},{64,0},{128,192},{192,128},{256,320},{320,256},{384,448},{4... | collective-permute-start | bytes 1179656 | tf_op jit(solution)/shard_map/cond/branch_1_fun/ppermute | solution.py:158
  139.5 2.7 %convolution_add_fusion = f32[384,768]{1,0:T(8,128)} fusion(f32[384,768]{1,0:T(8,128)S(1)} %fusion, bf16[512,384]{1,0:T(8,128)(2,1)S(1)} %collective-permute-done.2, bf16[512,768]{1,0:T(8,128)(2,1)} %collective-permute-done.3), kind=kOutput, calls=%fused_computation | convolution fusion | flops 302284800 | bytes 3538944 | tf_op jit(solution)/shard_map/cond/branch_1_fun/dot_general | solution.py:26
  142.1 1.7 fusion.2
  143.9 1.6 convolution_add_fusion.1
  145.5 9.7 %all-to-all-done.2 = bf16[8,64,768]{2,1,0:T(8,128)(2,1)} async-done(((bf16[8,64,768]{2,1,0:T(8,128)(2,1)}), bf16[8,64,768]{2,1,0:T(8,128)(2,1)}, u32[]{:S(2)}, u32[]{:S(2)}) %all-to-all-start.2) | async-done | bytes 786464 | tf_op jit(solution)/shard_map/cond/branch_1_fun/all_to_all | solution.py:134
  155.2 1.3 add_convert_fusion
  156.5 0.0 reduce-scatter.2.cloned.1.call-done
  156.5 0.9 pad_maximum_fusion.1
  157.5 15.7 %all_to_all.34 = bf16[4,32,768]{2,1,0:T(8,128)(2,1)S(1)} all-to-all(bf16[4,32,768]{2,1,0:T(8,128)(2,1)S(1)} %pad_maximum_fusion.1), channel_id=1, replica_groups={{0,128,256,384},{64,192,320,448},{1,129,257,385},{65,193,321,449},{2,13..., dimensions={0} | all-to-all | bytes 393216 | tf_op jit(solution)/shard_map/all_to_all | solution.py:134
  173.2 0.6 fusion.21
  173.9 0.6 fusion.22
  (22 shorter events, 0.2 us)
Async XLA Ops:
  7.2 22.5 %copy-start.4 = (s32[8]{0:T(128)S(1)}, s32[8]{0:T(128)}, u32[]{:S(2)}) copy-start(s32[8]{0:T(128)} %counts_ref.1) | copy-start | bytes 100
  7.2 23.8 %copy-start.1 = (bf16[768,384]{1,0:T(8,128)(2,1)S(1)}, bf16[768,384]{1,0:T(8,128)(2,1)}, u32[]{:S(2)}) copy-start(bf16[768,384]{1,0:T(8,128)(2,1)} %param.10) | copy-start | bytes 1769476
  8.7 20.2 %all-to-all-start.3 = ((bf16[4,32,768]{2,1,0:T(8,128)(2,1)}), bf16[4,32,768]{2,1,0:T(8,128)(2,1)S(1)}, u32[]{:S(2)}, u32[]{:S(2)}) async-start(bf16[4,32,768]{2,1,0:T(8,128)(2,1)} %get-tuple-element.55), calls=%async_computation.3 | async-start | bytes 393216 | tf_op jit(solution)/shard_map/all_to_all | solution.py:134
  19.0 63.7 %all-gather.3.cloned.1.call-start = ((), (), s32[]{:S(2)}) async-start(), calls=%async_computation.9 | async-start | bytes 1327104 | tf_op jit(solution)/shard_map/all_gather | solution.py:172
  19.0 12.0 %collective-permute-start.4 = (bf16[768,384]{1,0:T(8,128)(2,1)}, bf16[768,384]{1,0:T(8,128)(2,1)}, u32[]{:S(2)}, u32[]{:S(2)}) collective-permute-start(bf16[768,384]{1,0:T(8,128)(2,1)} %param.10), channel_id=1, source_target_pairs={{0,64},{64,0},{128,192},{192,128},{256,320},{320,256},{384,448},{4... | collective-permute-start | bytes 1769480 | tf_op jit(solution)/shard_map/ppermute | solution.py:158
  68.6 6.4 %copy-start = (bf16[384,768]{1,0:T(8,128)(2,1)S(1)}, bf16[384,768]{1,0:T(8,128)(2,1)}, u32[]{:S(2)}) copy-start(bf16[384,768]{1,0:T(8,128)(2,1)} %own_ref.3) | copy-start | bytes 1769476
  68.6 14.0 %all-to-all-start.4 = ((bf16[8,64,768]{2,1,0:T(8,128)(2,1)}), bf16[8,64,768]{2,1,0:T(8,128)(2,1)S(1)}, u32[]{:S(2)}, u32[]{:S(2)}) async-start(bf16[8,64,768]{2,1,0:T(8,128)(2,1)} %bitcast.9), calls=%async_computation.4 | async-start | bytes 1572864 | tf_op jit(solution)/shard_map/all_to_all | solution.py:134
  75.0 81.6 %reduce-scatter.2.cloned.1.call-start = ((), (), s32[]{:S(2)}) async-start(), calls=%async_computation.8 | async-start | bytes 884736 | tf_op jit(solution)/shard_map/reduce_scatter | solution.py:193
  75.0 7.7 %collective-permute-start.5 = (bf16[384,768]{1,0:T(8,128)(2,1)S(1)}, bf16[384,768]{1,0:T(8,128)(2,1)S(1)}, u32[]{:S(2)}, u32[]{:S(2)}) collective-permute-start(bf16[384,768]{1,0:T(8,128)(2,1)S(1)} %copy-done), channel_id=1, source_target_pairs={{0,64},{64,0},{128,192},{192,128},{256,320},{320,256},{384,448},{4... | collective-permute-start | bytes 1769480 | tf_op jit(solution)/shard_map/ppermute | solution.py:158
  108.5 64.8 %copy-start.2 = (bf16[1,16,768]{2,1,0:T(8,128)(2,1)S(1)}, bf16[1,16,768]{2,1,0:T(8,128)(2,1)}, u32[]{:S(2)}) copy-start(bf16[1,16,768]{2,1,0:T(8,128)(2,1)} %tokens_ref.1) | copy-start | bytes 73732
  109.4 13.4 %all-to-all-start.1 = ((bf16[8,64,768]{2,1,0:T(8,128)(2,1)}), bf16[8,64,768]{2,1,0:T(8,128)(2,1)S(1)}, u32[]{:S(2)}, u32[]{:S(2)}) async-start(bf16[8,64,768]{2,1,0:T(8,128)(2,1)} %broadcast_in_dim.10), calls=%async_computation.1 | async-start | bytes 1572864 | tf_op jit(solution)/shard_map/cond/branch_1_fun/all_to_all | solution.py:134
  117.3 22.1 %collective-permute-start.3 = (bf16[512,768]{1,0:T(8,128)(2,1)}, bf16[512,768]{1,0:T(8,128)(2,1)}, u32[]{:S(2)}, u32[]{:S(2)}) collective-permute-start(bf16[512,768]{1,0:T(8,128)(2,1)} %bitcast.6), channel_id=1, source_target_pairs={{0,64},{64,0},{128,192},{192,128},{256,320},{320,256},{384,448},{4... | collective-permute-start | bytes 2359304 | tf_op jit(solution)/shard_map/cond/branch_1_fun/ppermute | solution.py:158
  126.4 28.8 %all-to-all-start.2 = ((bf16[8,64,768]{2,1,0:T(8,128)(2,1)}), bf16[8,64,768]{2,1,0:T(8,128)(2,1)}, u32[]{:S(2)}, u32[]{:S(2)}) async-start(bf16[8,64,768]{2,1,0:T(8,128)(2,1)} %bitcast.7), calls=%async_computation.2 | async-start | bytes 1572864 | tf_op jit(solution)/shard_map/cond/branch_1_fun/all_to_all | solution.py:134
  131.5 8.0 %collective-permute-start.2 = (bf16[512,384]{1,0:T(8,128)(2,1)S(1)}, bf16[512,384]{1,0:T(8,128)(2,1)S(1)}, u32[]{:S(2)}, u32[]{:S(2)}) collective-permute-start(bf16[512,384]{1,0:T(8,128)(2,1)S(1)} %slice.172), channel_id=1, source_target_pairs={{0,64},{64,0},{128,192},{192,128},{256,320},{320,256},{384,448},{4... | collective-permute-start | bytes 1179656 | tf_op jit(solution)/shard_map/cond/branch_1_fun/ppermute | solution.py:158
  133.4 10.4 %collective-permute-start = (bf16[512,768]{1,0:T(8,128)(2,1)}, bf16[512,768]{1,0:T(8,128)(2,1)S(1)}, u32[]{:S(2)}, u32[]{:S(2)}) collective-permute-start(bf16[512,768]{1,0:T(8,128)(2,1)} %get-tuple-element.38), channel_id=1, source_target_pairs={{0,64},{64,0},{128,192},{192,128},{256,320},{320,256},{384,448},{4... | collective-permute-start | bytes 2359304 | tf_op jit(solution)/shard_map/cond/branch_1_fun/ppermute | solution.py:158
  137.5 6.4 %collective-permute-start.1 = (bf16[512,384]{1,0:T(8,128)(2,1)S(1)}, bf16[512,384]{1,0:T(8,128)(2,1)S(1)}, u32[]{:S(2)}, u32[]{:S(2)}) collective-permute-start(bf16[512,384]{1,0:T(8,128)(2,1)S(1)} %slice.170), channel_id=1, source_target_pairs={{0,64},{64,0},{128,192},{192,128},{256,320},{320,256},{384,448},{4... | collective-permute-start | bytes 1179656 | tf_op jit(solution)/shard_map/cond/branch_1_fun/ppermute | solution.py:158
  156.5 17.4 %copy-start.3 = (bf16[16,768]{1,0:T(8,128)(2,1)S(1)}, bf16[16,768]{1,0:T(8,128)(2,1)}, u32[]{:S(2)}) copy-start(bf16[16,768]{1,0:T(8,128)(2,1)} %get-tuple-element.59) | copy-start | bytes 73732
Sparse Core Ops, SparseCore 0:
  29.8 44.3 all-gather.2
  108.3 42.5 reduce-scatter.1

commit v9 on v8

--- a/solution.py
+++ b/solution.py
@@ -168,7 +168,7 @@
     line_rows = chips * rows_local
     rows_all = columns * line_rows
 
-    padded = jnp.concatenate([scaled_line, scaled_line[: line_rows // 2]], axis=0)
+    padded = jnp.concatenate([scaled_line, scaled_line[: line_rows * 3 // 8]], axis=0)
     scaled_blocks = lax.all_gather(padded, "col", axis=0)
 
     def forward(line):
@@ -180,7 +180,7 @@
         return blocks, paired(blocks, line_rows, w_in, w_in_mate, False)
 
     some_kept = jnp.sum(counts) > 0
-    tokens_blocks, hidden_terms = lax.cond(some_kept, forward, forward_plain, tokens_line)
+    tokens_blocks, hidden_terms = lax.cond(some_kept, forward_plain, forward, tokens_line)
     slope_terms = paired(scaled_blocks, line_rows, w_out, w_out_mate, True)
 
     hidden = added_up(swapped(cut(hidden_terms, row_count), "row"))

time: 182 us -> 176 us (0.967)
  blocking collectives: 70.9 us -> 65.8 us
    all_to_all x3 -> x2, blocking collectives: 70.9 us -> 35.4 us  [swapped(): lax.all_to_all(value, axis, 0, 0, axis_index_groups=groups, tiled=True)]
    all_gather x0 -> x1, blocking collectives: none -> 30.4 us  [forward_plain(): blocks = lax.all_gather(line, 'col', axis=0)]
where the time goes in v9:
time: 176 us; the launch traced here: 175 us
  blocking collectives  65.8 us (37%)
  starting transfers between devices  38.6 us (22%)
  waiting for transfers between devices  25.5 us (14%)
  between operations  14.8 us (8%)
  Pallas kernels  12.6 us (7%)
  matrix products  7.62 us (4%)
  other arithmetic  5.97 us (3%)
  local copies, waits for them, and re-layouts  4.03 us (2%)
    all_to_all x2, blocking collectives, swapped(): lax.all_to_all(value, axis, 0, 0, axis_index_groups=groups, tiled=True)  35.4 us
    all_gather x1, blocking collectives, forward_plain(): blocks = lax.all_gather(line, 'col', axis=0)  30.4 us
    all_to_all x4, starting transfers between devices, swapped(): lax.all_to_all(value, axis, 0, 0, axis_index_groups=groups, tiled=True)  26.7 us
    all_to_all x4, waiting for transfers between devices, swapped(): lax.all_to_all(value, axis, 0, 0, axis_index_groups=groups, tiled=True)  25.4 us
    ppermute x6, starting transfers between devices, body(): mate = lambda value: lax.ppermute(value, 'rep', to_mate)  12 us
    dot_general x4, matrix products, product(): lax.dot_general(left, right, (((left_dim,), (right_dim,)), ((), ())), pre...  7.62 us
    pallas_call x2, Pallas kernels, paired(): pl.pallas_call(kernel, grid=(1,), in_specs=[pl.BlockSpec((count, rows, wi...  5.72 us
    pallas_call x2, Pallas kernels, joined(): pl.pallas_call(kernel, grid=(1,), in_specs=[pl.BlockSpec((count, rows, 2...  5.37 us
  transfers between devices with their start and end apart: 12, of which 4 were waited for; matrix products, arithmetic and copies ran while one was open for 8% of the time, Pallas kernels for 4%

profile of v9, /device:TPU:6, one launch (start us, length us, event | category | flops | bytes accessed | tf_op | source)
XLA Modules:
  0.0 175.2 jit_solution(12116866880368490657)
XLA Ops:
  7.2 1.5 shard_map.84
  8.6 10.3 %all-to-all-start.3 = ((bf16[4,32,768]{2,1,0:T(8,128)(2,1)}), bf16[4,32,768]{2,1,0:T(8,128)(2,1)S(1)}, u32[]{:S(2)}, u32[]{:S(2)}) async-start(bf16[4,32,768]{2,1,0:T(8,128)(2,1)} %get-tuple-element.55), calls=%async_computation.3 | async-start | bytes 393216 | tf_op jit(solution)/shard_map/all_to_all | solution.py:134
  18.9 1.9 %collective-permute-start.4 = (bf16[768,384]{1,0:T(8,128)(2,1)}, bf16[768,384]{1,0:T(8,128)(2,1)}, u32[]{:S(2)}, u32[]{:S(2)}) collective-permute-start(bf16[768,384]{1,0:T(8,128)(2,1)} %param.10), channel_id=1, source_target_pairs={{0,64},{64,0},{128,192},{192,128},{256,320},{320,256},{384,448},{4... | collective-permute-start | bytes 1769480 | tf_op jit(solution)/shard_map/ppermute | solution.py:158
  20.9 8.0 %all-to-all-done.3 = bf16[4,32,768]{2,1,0:T(8,128)(2,1)S(1)} async-done(((bf16[4,32,768]{2,1,0:T(8,128)(2,1)}), bf16[4,32,768]{2,1,0:T(8,128)(2,1)S(1)}, u32[]{:S(2)}, u32[]{:S(2)}) %all-to-all-start.3) | async-done | bytes 196640 | tf_op jit(solution)/shard_map/all_to_all | solution.py:134
  28.9 0.7 pad_maximum_fusion.2
  29.6 0.0 all-gather.3.cloned.1.call-update
  29.6 1.3 reduce_sum.9
  31.6 33.7 %conditional.2 = (bf16[512,768]{1,0:T(8,128)(2,1)}, bf16[512,768]{1,0:T(8,128)(2,1)}) conditional(s32[]{:T(128)} %convert_element_type.192, (bf16[4,32,768]{2,1,0:T(8,128)(2,1)S(1)}, bf16[768,384]{1,0:T(8,128)(2,1)}, bf16[768,384]{1,0:T(8,128)(2,1)}) %tuple.28, (bf16[4,32,768]{2,1,0:T(8,128)(2,1)S(1)}, bf16[768,384]{1,0:T(8,128)(2,1)}, ...), branch_computations={%region_1.0_spmd, %region_2.0_spmd} | conditional | flops 603979776 | bytes 9207852 | solution.py:183
  31.6 0.0 copy-start.3
  31.6 30.4 %all_gather.6.left_ref = bf16[8,64,768]{2,1,0:T(8,128)(2,1)} all-gather(bf16[1,64,768]{2,1,0:T(8,128)(2,1)S(1)} %bitcast.56), channel_id=1, replica_groups=mesh['rep'=8,'row'=8,'col'=8] {'col'}, dimensions={0}, use_global_device_ids=true | all-gather | bytes 884736 | tf_op jit(solution)/shard_map/cond/branch_1_fun/all_gather | solution.py:179
  62.0 3.2 %branch_1_fun.2 = bf16[512,768]{1,0:T(8,128)(2,1)} custom-call(bf16[8,64,768]{2,1,0:T(8,128)(2,1)} %all_gather.6.left_ref, bf16[768,384]{1,0:T(8,128)(2,1)S(1)} %copy-done.3, bf16[768,384]{1,0:T(8,128)(2,1)} %get-tuple-element.37.other_ref), custom_call_target="tpu_custom_call" | custom-call | flops 603979776 | bytes 4194304 | tf_op jit(solution)/shard_map/cond/branch_1_fun/pallas_call | solution.py:81
  65.2 5.1 %all-to-all-start.4 = ((bf16[8,64,768]{2,1,0:T(8,128)(2,1)}), bf16[8,64,768]{2,1,0:T(8,128)(2,1)S(1)}, u32[]{:S(2)}, u32[]{:S(2)}) async-start(bf16[8,64,768]{2,1,0:T(8,128)(2,1)} %bitcast.9), calls=%async_computation.4 | async-start | bytes 1572864 | tf_op jit(solution)/shard_map/all_to_all | solution.py:134
  70.3 1.9 %collective-permute-start.5 = (bf16[384,768]{1,0:T(8,128)(2,1)S(1)}, bf16[384,768]{1,0:T(8,128)(2,1)S(1)}, u32[]{:S(2)}, u32[]{:S(2)}) collective-permute-start(bf16[384,768]{1,0:T(8,128)(2,1)S(1)} %copy-done), channel_id=1, source_target_pairs={{0,64},{64,0},{128,192},{192,128},{256,320},{320,256},{384,448},{4... | collective-permute-start | bytes 1769480 | tf_op jit(solution)/shard_map/ppermute | solution.py:158
  72.2 5.6 %all-to-all-done.4 = bf16[8,64,768]{2,1,0:T(8,128)(2,1)S(1)} async-done(((bf16[8,64,768]{2,1,0:T(8,128)(2,1)}), bf16[8,64,768]{2,1,0:T(8,128)(2,1)S(1)}, u32[]{:S(2)}, u32[]{:S(2)}) %all-to-all-start.4) | async-done | bytes 786464 | tf_op jit(solution)/shard_map/all_to_all | solution.py:134
  77.9 0.2 fusion.18
  78.0 0.0 all-gather.3.cloned.1.call-done
  78.1 2.5 %shard_map.85 = bf16[512,768]{1,0:T(8,128)(2,1)S(1)} custom-call(bf16[8,88,768]{2,1,0:T(8,128)(2,1)} %bitcast.49, bf16[384,768]{1,0:T(8,128)(2,1)S(1)} %copy-done, bf16[384,768]{1,0:T(8,128)(2,1)S(1)} %collective-permute-done.5.other_ref), custom_call_target="tpu_custom_call" | custom-call | flops 603979776 | bytes 4194304 | tf_op jit(solution)/shard_map/pallas_call | solution.py:81
  80.6 0.1 broadcast_in_dim.22
  80.7 0.1 pad_maximum_fusion
  80.8 20.8 %all_to_all.33.left_ref = bf16[8,64,1536]{2,1,0:T(8,128)(2,1)S(1)} all-to-all(bf16[8,64,1536]{2,1,0:T(8,128)(2,1)S(1)} %pad_maximum_fusion), channel_id=1, replica_groups=mesh['rep'=8,'row'=8,'col'=8] {'row'}, dimensions={0} | all-to-all | bytes 3145728 | tf_op jit(solution)/shard_map/all_to_all | solution.py:134
  101.6 1.9 %shard_map.86 = bf16[512,768]{1,0:T(8,128)(2,1)} custom-call(bf16[8,64,1536]{2,1,0:T(8,128)(2,1)S(1)} %all_to_all.33.left_ref, bf16[384,768]{1,0:T(8,128)(2,1)S(1)} %copy-done, bf16[384,768]{1,0:T(8,128)(2,1)S(1)} %collective-permute-done.5.other_ref), custom_call_target="tpu_custom_call" | custom-call | flops 603979776 | bytes 4194304 | tf_op jit(solution)/shard_map/pallas_call | solution.py:111
  103.5 0.0 reduce-scatter.2.cloned.1.call-update
  103.5 0.2 fusion.15
  103.8 0.8 copy-done.1
  104.6 46.9 %conditional.3 = (f32[768,384]{1,0:T(8,128)}, f32[384,768]{1,0:T(8,128)}, bf16[4,16,768]{2,1,0:T(8,128)(2,1)S(1)}) conditional(s32[]{:T(128)} %convert_element_type.192, () %tuple.29, (bf16[64,768]{1,0:T(8,128)(2,1)S(1)}, bf16[512,768]{1,0:T(8,128)(2,1)}, bf16[8,64,1536]{2,1,0:T(8,128)(2,1)S(1)}, bf16[8,88,768]{2,1,0:T(8,128)(2,1)}, ...), branch_computations={%region_4.0_spmd, %region_5.0_spmd} | conditional | flops 1813315584 | bytes 36634872 | solution.py:217
  104.6 0.9 broadcast_in_dim.10
  105.5 5.8 %all-to-all-start.1 = ((bf16[8,64,768]{2,1,0:T(8,128)(2,1)}), bf16[8,64,768]{2,1,0:T(8,128)(2,1)S(1)}, u32[]{:S(2)}, u32[]{:S(2)}) async-start(bf16[8,64,768]{2,1,0:T(8,128)(2,1)} %broadcast_in_dim.10), calls=%async_computation.1 | async-start | bytes 1572864 | tf_op jit(solution)/shard_map/cond/branch_1_fun/all_to_all | solution.py:134
  111.4 2.1 %slice.102 = bf16[8,64,768]{2,1,0:T(8,128)(2,1)} slice(bf16[8,88,768]{2,1,0:T(8,128)(2,1)} %get-tuple-element.41), slice={[0:8], [0:64], [0:768]} | slice | bytes 1572864 | tf_op jit(solution)/shard_map/slice | solution.py:195
  113.4 1.9 %collective-permute-start.3 = (bf16[512,768]{1,0:T(8,128)(2,1)}, bf16[512,768]{1,0:T(8,128)(2,1)}, u32[]{:S(2)}, u32[]{:S(2)}) collective-permute-start(bf16[512,768]{1,0:T(8,128)(2,1)} %bitcast.6), channel_id=1, source_target_pairs={{0,64},{64,0},{128,192},{192,128},{256,320},{320,256},{384,448},{4... | collective-permute-start | bytes 2359304 | tf_op jit(solution)/shard_map/cond/branch_1_fun/ppermute | solution.py:158
  115.3 3.6 %all-to-all-done.1.left_ref = bf16[8,64,768]{2,1,0:T(8,128)(2,1)S(1)} async-done(((bf16[8,64,768]{2,1,0:T(8,128)(2,1)}), bf16[8,64,768]{2,1,0:T(8,128)(2,1)S(1)}, u32[]{:S(2)}, u32[]{:S(2)}) %all-to-all-start.1) | async-done | bytes 786464 | tf_op jit(solution)/shard_map/cond/branch_1_fun/all_to_all | solution.py:134
  118.9 3.5 %branch_1_fun.3 = bf16[512,768]{1,0:T(8,128)(2,1)} custom-call(bf16[8,64,768]{2,1,0:T(8,128)(2,1)S(1)} %all-to-all-done.1.left_ref, bf16[768,384]{1,0:T(8,128)(2,1)S(1)} %get-tuple-element.42.own_ref, bf16[768,384]{1,0:T(8,128)(2,1)} %get-tuple-element.43.other_ref), custom_call_target="tpu_custom_call" | custom-call | flops 603979776 | bytes 4194304 | tf_op jit(solution)/shard_map/cond/branch_1_fun/pallas_call | solution.py:111
  122.4 5.4 %all-to-all-start.2 = ((bf16[8,64,768]{2,1,0:T(8,128)(2,1)}), bf16[8,64,768]{2,1,0:T(8,128)(2,1)}, u32[]{:S(2)}, u32[]{:S(2)}) async-start(bf16[8,64,768]{2,1,0:T(8,128)(2,1)} %bitcast.7), calls=%async_computation.2 | async-start | bytes 1572864 | tf_op jit(solution)/shard_map/cond/branch_1_fun/all_to_all | solution.py:134
  127.9 0.1 slice.100
  128.0 1.9 %collective-permute-start.2 = (bf16[512,384]{1,0:T(8,128)(2,1)S(1)}, bf16[512,384]{1,0:T(8,128)(2,1)S(1)}, u32[]{:S(2)}, u32[]{:S(2)}) collective-permute-start(bf16[512,384]{1,0:T(8,128)(2,1)S(1)} %slice.167), channel_id=1, source_target_pairs={{0,64},{64,0},{128,192},{192,128},{256,320},{320,256},{384,448},{4... | collective-permute-start | bytes 1179656 | tf_op jit(solution)/shard_map/cond/branch_1_fun/ppermute | solution.py:158
  129.9 2.4 %collective-permute-start = (bf16[512,768]{1,0:T(8,128)(2,1)}, bf16[512,768]{1,0:T(8,128)(2,1)S(1)}, u32[]{:S(2)}, u32[]{:S(2)}) collective-permute-start(bf16[512,768]{1,0:T(8,128)(2,1)} %get-tuple-element.38), channel_id=1, source_target_pairs={{0,64},{64,0},{128,192},{192,128},{256,320},{320,256},{384,448},{4... | collective-permute-start | bytes 2359304 | tf_op jit(solution)/shard_map/cond/branch_1_fun/ppermute | solution.py:158
  132.3 1.6 fusion
  134.0 1.9 %collective-permute-start.1 = (bf16[512,384]{1,0:T(8,128)(2,1)S(1)}, bf16[512,384]{1,0:T(8,128)(2,1)S(1)}, u32[]{:S(2)}, u32[]{:S(2)}) collective-permute-start(bf16[512,384]{1,0:T(8,128)(2,1)S(1)} %slice.165), channel_id=1, source_target_pairs={{0,64},{64,0},{128,192},{192,128},{256,320},{320,256},{384,448},{4... | collective-permute-start | bytes 1179656 | tf_op jit(solution)/shard_map/cond/branch_1_fun/ppermute | solution.py:158
  136.0 2.6 %convolution_add_fusion = f32[384,768]{1,0:T(8,128)} fusion(f32[384,768]{1,0:T(8,128)S(1)} %fusion, bf16[512,384]{1,0:T(8,128)(2,1)S(1)} %collective-permute-done.2, bf16[512,768]{1,0:T(8,128)(2,1)} %collective-permute-done.3), kind=kOutput, calls=%fused_computation | convolution fusion | flops 302284800 | bytes 3538944 | tf_op jit(solution)/shard_map/cond/branch_1_fun/dot_general | solution.py:26
  138.6 1.7 fusion.2
  140.4 1.6 convolution_add_fusion.1
  142.0 8.2 %all-to-all-done.2 = bf16[8,64,768]{2,1,0:T(8,128)(2,1)} async-done(((bf16[8,64,768]{2,1,0:T(8,128)(2,1)}), bf16[8,64,768]{2,1,0:T(8,128)(2,1)}, u32[]{:S(2)}, u32[]{:S(2)}) %all-to-all-start.2) | async-done | bytes 786464 | tf_op jit(solution)/shard_map/cond/branch_1_fun/all_to_all | solution.py:134
  150.2 1.3 add_convert_fusion
  151.5 0.0 copy-start.5
  151.5 0.0 reduce-scatter.2.cloned.1.call-done
  151.5 0.9 pad_maximum_fusion.1
  152.4 14.6 %all_to_all.34 = bf16[4,32,768]{2,1,0:T(8,128)(2,1)S(1)} all-to-all(bf16[4,32,768]{2,1,0:T(8,128)(2,1)S(1)} %pad_maximum_fusion.1), channel_id=1, replica_groups={{0,128,256,384},{64,192,320,448},{1,129,257,385},{65,193,321,449},{2,13..., dimensions={0} | all-to-all | bytes 393216 | tf_op jit(solution)/shard_map/all_to_all | solution.py:134
  167.1 0.6 fusion.21
  167.7 0.6 fusion.22
  (21 shorter events, 0.2 us)
Async XLA Ops:
  8.6 20.2 %all-to-all-start.3 = ((bf16[4,32,768]{2,1,0:T(8,128)(2,1)}), bf16[4,32,768]{2,1,0:T(8,128)(2,1)S(1)}, u32[]{:S(2)}, u32[]{:S(2)}) async-start(bf16[4,32,768]{2,1,0:T(8,128)(2,1)} %get-tuple-element.55), calls=%async_computation.3 | async-start | bytes 393216 | tf_op jit(solution)/shard_map/all_to_all | solution.py:134
  18.9 59.1 %all-gather.3.cloned.1.call-start = ((), (), s32[]{:S(2)}) async-start(), calls=%async_computation.9 | async-start | bytes 1216512 | tf_op jit(solution)/shard_map/all_gather | solution.py:172
  18.9 12.6 %collective-permute-start.4 = (bf16[768,384]{1,0:T(8,128)(2,1)}, bf16[768,384]{1,0:T(8,128)(2,1)}, u32[]{:S(2)}, u32[]{:S(2)}) collective-permute-start(bf16[768,384]{1,0:T(8,128)(2,1)} %param.10), channel_id=1, source_target_pairs={{0,64},{64,0},{128,192},{192,128},{256,320},{320,256},{384,448},{4... | collective-permute-start | bytes 1769480 | tf_op jit(solution)/shard_map/ppermute | solution.py:158
  31.6 30.5 %copy-start.3 = (bf16[768,384]{1,0:T(8,128)(2,1)S(1)}, bf16[768,384]{1,0:T(8,128)(2,1)}, u32[]{:S(2)}) copy-start(bf16[768,384]{1,0:T(8,128)(2,1)} %get-tuple-element.36.own_ref) | copy-start | bytes 1769476 | tf_op jit(solution)/shard_map/cond
  65.2 5.1 %copy-start = (bf16[384,768]{1,0:T(8,128)(2,1)S(1)}, bf16[384,768]{1,0:T(8,128)(2,1)}, u32[]{:S(2)}) copy-start(bf16[384,768]{1,0:T(8,128)(2,1)} %own_ref.3) | copy-start | bytes 1769476
  65.2 12.6 %all-to-all-start.4 = ((bf16[8,64,768]{2,1,0:T(8,128)(2,1)}), bf16[8,64,768]{2,1,0:T(8,128)(2,1)S(1)}, u32[]{:S(2)}, u32[]{:S(2)}) async-start(bf16[8,64,768]{2,1,0:T(8,128)(2,1)} %bitcast.9), calls=%async_computation.4 | async-start | bytes 1572864 | tf_op jit(solution)/shard_map/all_to_all | solution.py:134
  70.3 81.2 %reduce-scatter.2.cloned.1.call-start = ((), (), s32[]{:S(2)}) async-start(), calls=%async_computation.8 | async-start | bytes 884736 | tf_op jit(solution)/shard_map/reduce_scatter | solution.py:193
  70.3 7.7 %collective-permute-start.5 = (bf16[384,768]{1,0:T(8,128)(2,1)S(1)}, bf16[384,768]{1,0:T(8,128)(2,1)S(1)}, u32[]{:S(2)}, u32[]{:S(2)}) collective-permute-start(bf16[384,768]{1,0:T(8,128)(2,1)S(1)} %copy-done), channel_id=1, source_target_pairs={{0,64},{64,0},{128,192},{192,128},{256,320},{320,256},{384,448},{4... | collective-permute-start | bytes 1769480 | tf_op jit(solution)/shard_map/ppermute | solution.py:158
  103.5 1.1 copy-start.1
  104.6 62.5 %copy-start.4 = (bf16[1,16,768]{2,1,0:T(8,128)(2,1)S(1)}, bf16[1,16,768]{2,1,0:T(8,128)(2,1)}, u32[]{:S(2)}) copy-start(bf16[1,16,768]{2,1,0:T(8,128)(2,1)} %tokens_ref.1) | copy-start | bytes 73732
  105.5 13.4 %all-to-all-start.1 = ((bf16[8,64,768]{2,1,0:T(8,128)(2,1)}), bf16[8,64,768]{2,1,0:T(8,128)(2,1)S(1)}, u32[]{:S(2)}, u32[]{:S(2)}) async-start(bf16[8,64,768]{2,1,0:T(8,128)(2,1)} %broadcast_in_dim.10), calls=%async_computation.1 | async-start | bytes 1572864 | tf_op jit(solution)/shard_map/cond/branch_1_fun/all_to_all | solution.py:134
  113.4 22.5 %collective-permute-start.3 = (bf16[512,768]{1,0:T(8,128)(2,1)}, bf16[512,768]{1,0:T(8,128)(2,1)}, u32[]{:S(2)}, u32[]{:S(2)}) collective-permute-start(bf16[512,768]{1,0:T(8,128)(2,1)} %bitcast.6), channel_id=1, source_target_pairs={{0,64},{64,0},{128,192},{192,128},{256,320},{320,256},{384,448},{4... | collective-permute-start | bytes 2359304 | tf_op jit(solution)/shard_map/cond/branch_1_fun/ppermute | solution.py:158
  122.4 27.7 %all-to-all-start.2 = ((bf16[8,64,768]{2,1,0:T(8,128)(2,1)}), bf16[8,64,768]{2,1,0:T(8,128)(2,1)}, u32[]{:S(2)}, u32[]{:S(2)}) async-start(bf16[8,64,768]{2,1,0:T(8,128)(2,1)} %bitcast.7), calls=%async_computation.2 | async-start | bytes 1572864 | tf_op jit(solution)/shard_map/cond/branch_1_fun/all_to_all | solution.py:134
  128.0 8.0 %collective-permute-start.2 = (bf16[512,384]{1,0:T(8,128)(2,1)S(1)}, bf16[512,384]{1,0:T(8,128)(2,1)S(1)}, u32[]{:S(2)}, u32[]{:S(2)}) collective-permute-start(bf16[512,384]{1,0:T(8,128)(2,1)S(1)} %slice.167), channel_id=1, source_target_pairs={{0,64},{64,0},{128,192},{192,128},{256,320},{320,256},{384,448},{4... | collective-permute-start | bytes 1179656 | tf_op jit(solution)/shard_map/cond/branch_1_fun/ppermute | solution.py:158
  129.9 10.4 %collective-permute-start = (bf16[512,768]{1,0:T(8,128)(2,1)}, bf16[512,768]{1,0:T(8,128)(2,1)S(1)}, u32[]{:S(2)}, u32[]{:S(2)}) collective-permute-start(bf16[512,768]{1,0:T(8,128)(2,1)} %get-tuple-element.38), channel_id=1, source_target_pairs={{0,64},{64,0},{128,192},{192,128},{256,320},{320,256},{384,448},{4... | collective-permute-start | bytes 2359304 | tf_op jit(solution)/shard_map/cond/branch_1_fun/ppermute | solution.py:158
  134.0 6.3 %collective-permute-start.1 = (bf16[512,384]{1,0:T(8,128)(2,1)S(1)}, bf16[512,384]{1,0:T(8,128)(2,1)S(1)}, u32[]{:S(2)}, u32[]{:S(2)}) collective-permute-start(bf16[512,384]{1,0:T(8,128)(2,1)S(1)} %slice.165), channel_id=1, source_target_pairs={{0,64},{64,0},{128,192},{192,128},{256,320},{320,256},{384,448},{4... | collective-permute-start | bytes 1179656 | tf_op jit(solution)/shard_map/cond/branch_1_fun/ppermute | solution.py:158
  151.5 16.2 %copy-start.5 = (bf16[16,768]{1,0:T(8,128)(2,1)S(1)}, bf16[16,768]{1,0:T(8,128)(2,1)}, u32[]{:S(2)}) copy-start(bf16[16,768]{1,0:T(8,128)(2,1)} %get-tuple-element.59) | copy-start | bytes 73732
Sparse Core Ops, SparseCore 0:
  29.7 38.0 all-gather.2
  103.7 39.3 reduce-scatter.1

commit v10 on v9

--- a/solution.py
+++ b/solution.py
@@ -123,6 +123,27 @@
             flops=4 * count * rows * width * units, bytes_accessed=4 << 20, transcendentals=0
         ),
     )(blocks, own, other)
+
+
+def packed(pieces, finished, copies):
+    count, total_rows, width = pieces.shape
+    rows = total_rows // copies
+
+    def kernel(pieces_ref, finished_ref, send_ref):
+        for copy in range(copies):
+            here = slice(copy * rows, (copy + 1) * rows)
+            total = pieces_ref[0, here].astype(jnp.float32)
+            for at in range(1, count):
+                total = total + pieces_ref[at, here].astype(jnp.float32)
+            send_ref[copy, :rows] = finished_ref[here]
+            send_ref[copy, rows:] = total.astype(jnp.bfloat16)
+
+    return pl.pallas_call(
+        kernel,
+        in_specs=[pl.BlockSpec(memory_space=pltpu.VMEM), pl.BlockSpec(memory_space=pltpu.VMEM)],
+        out_specs=pl.BlockSpec(memory_space=pltpu.VMEM),
+        out_shape=jax.ShapeDtypeStruct((copies, 2 * rows, width), jnp.bfloat16),
+    )(pieces, finished)
 
 
 def cut(value, pieces):
@@ -179,11 +200,13 @@
         blocks = lax.all_gather(line, "col", axis=0)
         return blocks, paired(blocks, line_rows, w_in, w_in_mate, False)
 
-    some_kept = jnp.sum(counts) > 0
-    tokens_blocks, hidden_terms = lax.cond(some_kept, forward_plain, forward, tokens_line)
+    in_grid = lax.axis_index("col") >= 0
+    tokens_blocks, hidden_terms = lax.cond(in_grid, forward_plain, forward, tokens_line)
     slope_terms = paired(scaled_blocks, line_rows, w_out, w_out_mate, True)
 
-    hidden = added_up(swapped(cut(hidden_terms, row_count), "row"))
+    hidden_pieces = swapped(cut(hidden_terms, row_count), "row")
+    hidden_pieces, slope_terms = lax.optimization_barrier((hidden_pieces, slope_terms))
+    hidden = added_up(hidden_pieces)
     active, slope = gelu_both(hidden)
     share = jnp.broadcast_to(active.astype(jnp.bfloat16)[None], (row_count, *active.shape))
     mixed = swapped(jnp.concatenate([share, cut(slope_terms, row_count)], axis=2), "row")
@@ -195,27 +218,25 @@
     scaled_all = scaled_blocks[:, :line_rows].reshape(rows_all, width)
 
     def backward(share):
-        shares = spread(share, "row", row_count)
+        return backward_parts(spread(share, "row", row_count))
+
+    def backward_plain(share):
+        return backward_parts(lax.all_gather(share, "row", axis=0))
+
+    def backward_parts(shares):
         back_terms = joined(shares, w_in, w_in_mate, True)
         hidden_grad = shares.reshape(rows_all, -1)
-        back_line = added_up(swapped(cut(back_terms, columns), "col")).astype(jnp.bfloat16)
+        back_pieces = swapped(cut(back_terms, columns), "col")
         w_out_grad = product(activated[:, :units], scaled_all, 0, 0) + product(
             mate(activated[:, units:]), mate(scaled_all), 0, 0
         )
         w_in_grad = product(tokens_all, hidden_grad[:, :units], 0, 0) + product(
             mate(tokens_all), mate(hidden_grad[:, units:]), 0, 0
         )
-        return back_line, w_in_grad, w_out_grad
-
-    def nothing(share):
-        return (
-            jnp.zeros((line_rows, width), jnp.bfloat16),
-            jnp.zeros((width, units), jnp.float32),
-            jnp.zeros((units, width), jnp.float32),
-        )
-
-    back_line, w_in_grad, w_out_grad = lax.cond(some_kept, backward, nothing, grad_share)
-    ends = jnp.concatenate([cut(output_line, chips), cut(back_line, chips)], axis=1)
+        return back_pieces, w_in_grad, w_out_grad
+
+    back_pieces, w_in_grad, w_out_grad = lax.cond(in_grid, backward, backward_plain, grad_share)
+    ends = packed(back_pieces, output_line, chips)
     finished = added_up(swapped(ends, "rep", same_core))
     block_output = (tokens_local.astype(jnp.float32) + finished[:rows_local]).astype(jnp.bfloat16)
     input_grad = (scaled.astype(jnp.float32) + finished[rows_local:]).astype(jnp.bfloat16)

time: 176 us -> 178 us (1.011)
  other arithmetic: 5.97 us -> 2.46 us
  waiting for transfers between devices: 25.5 us -> 28.8 us
  blocking collectives: 65.8 us -> 68.6 us
  matrix products: 7.62 us -> 5.48 us
    pallas_call x0 -> x1, Pallas kernels: none -> 2.36 us  [packed(): pl.pallas_call(kernel, in_specs=[pl.BlockSpec(memory_space=pltpu.VMEM), p...]
    dot_general x4, matrix products: 7.62 us -> 5.48 us  [product(): lax.dot_general(left, right, (((left_dim,), (right_dim,)), ((), ())), pre...]
    all_to_all x2, blocking collectives: 35.4 us -> 37.5 us  [swapped(): lax.all_to_all(value, axis, 0, 0, axis_index_groups=groups, tiled=True)]
    ppermute x6, waiting for transfers between devices: 0.02 us -> 1.98 us  [body(): mate = lambda value: lax.ppermute(value, 'rep', to_mate)]
  transfers between devices with their start and end apart: 12 -> 12, of which waited for: 4 -> 5; matrix products, arithmetic and copies ran while one was open for 8% -> 5% of each run, Pallas kernels for 4% -> 5%
where the time goes in v10:
time: 178 us; the launch traced here: 177 us
  blocking collectives  68.6 us (39%)
  starting transfers between devices  38.7 us (22%)
  waiting for transfers between devices  28.8 us (16%)
  between operations  14.1 us (8%)
  Pallas kernels  13.8 us (8%)
  matrix products  5.48 us (3%)
  local copies, waits for them, and re-layouts  4.34 us (2%)
  other arithmetic  2.46 us (1%)
    all_to_all x2, blocking collectives, swapped(): lax.all_to_all(value, axis, 0, 0, axis_index_groups=groups, tiled=True)  37.5 us
    all_gather x1, blocking collectives, forward_plain(): blocks = lax.all_gather(line, 'col', axis=0)  31.1 us
    all_to_all x4, waiting for transfers between devices, swapped(): lax.all_to_all(value, axis, 0, 0, axis_index_groups=groups, tiled=True)  26.8 us
    all_to_all x4, starting transfers between devices, swapped(): lax.all_to_all(value, axis, 0, 0, axis_index_groups=groups, tiled=True)  26.7 us
    ppermute x6, starting transfers between devices, body(): mate = lambda value: lax.ppermute(value, 'rep', to_mate)  12 us
    dot_general x4, matrix products, product(): lax.dot_general(left, right, (((left_dim,), (right_dim,)), ((), ())), pre...  5.48 us
    pallas_call x2, Pallas kernels, joined(): pl.pallas_call(kernel, grid=(1,), in_specs=[pl.BlockSpec((count, rows, 2...  5.39 us
    pallas_call x2, Pallas kernels, paired(): pl.pallas_call(kernel, grid=(1,), in_specs=[pl.BlockSpec((count, rows, wi...  4.57 us
  transfers between devices with their start and end apart: 12, of which 5 were waited for; matrix products, arithmetic and copies ran while one was open for 5% of the time, Pallas kernels for 5%

profile of v10, /device:TPU:6, one launch (start us, length us, event | category | flops | bytes accessed | tf_op | source)
XLA Modules:
  0.0 176.5 jit_solution(11793560224722653200)
XLA Ops:
  7.2 1.5 shard_map.84
  8.6 10.3 %all-to-all-start.4 = ((bf16[4,32,768]{2,1,0:T(8,128)(2,1)}), bf16[4,32,768]{2,1,0:T(8,128)(2,1)S(1)}, u32[]{:S(2)}, u32[]{:S(2)}) async-start(bf16[4,32,768]{2,1,0:T(8,128)(2,1)} %get-tuple-element.70), calls=%async_computation.4 | async-start | bytes 393216 | tf_op jit(solution)/shard_map/all_to_all | solution.py:155
  18.9 1.9 %collective-permute-start.8 = (bf16[768,384]{1,0:T(8,128)(2,1)}, bf16[768,384]{1,0:T(8,128)(2,1)}, u32[]{:S(2)}, u32[]{:S(2)}) collective-permute-start(bf16[768,384]{1,0:T(8,128)(2,1)} %param.10), channel_id=1, source_target_pairs={{0,64},{64,0},{128,192},{192,128},{256,320},{320,256},{384,448},{4... | collective-permute-start | bytes 1769480 | tf_op jit(solution)/shard_map/ppermute | solution.py:179
  20.9 8.0 %all-to-all-done.4 = bf16[4,32,768]{2,1,0:T(8,128)(2,1)S(1)} async-done(((bf16[4,32,768]{2,1,0:T(8,128)(2,1)}), bf16[4,32,768]{2,1,0:T(8,128)(2,1)S(1)}, u32[]{:S(2)}, u32[]{:S(2)}) %all-to-all-start.4) | async-done | bytes 196640 | tf_op jit(solution)/shard_map/all_to_all | solution.py:155
  28.9 0.7 pad_maximum_fusion.1
  29.6 0.0 all-gather.4.cloned.1.call-update
  29.6 34.3 %conditional.2 = (bf16[512,768]{1,0:T(8,128)(2,1)}, bf16[512,768]{1,0:T(8,128)(2,1)}) conditional(s32[]{:T(128)} %convert_element_type.140, (bf16[4,32,768]{2,1,0:T(8,128)(2,1)S(1)}, bf16[768,384]{1,0:T(8,128)(2,1)}, bf16[768,384]{1,0:T(8,128)(2,1)}) %tuple.27, (bf16[4,32,768]{2,1,0:T(8,128)(2,1)S(1)}, bf16[768,384]{1,0:T(8,128)(2,1)}, ...), branch_computations={%region_0.0_spmd, %region_1.0_spmd} | conditional | flops 603979776 | bytes 9207852 | solution.py:204
  29.6 0.0 copy-start.7
  29.7 31.1 %all_gather.10.left_ref = bf16[8,64,768]{2,1,0:T(8,128)(2,1)} all-gather(bf16[1,64,768]{2,1,0:T(8,128)(2,1)S(1)} %bitcast.65), channel_id=1, replica_groups=mesh['rep'=8,'row'=8,'col'=8] {'col'}, dimensions={0}, use_global_device_ids=true | all-gather | bytes 884736 | tf_op jit(solution)/shard_map/cond/branch_1_fun/all_gather | solution.py:200
  60.8 3.2 %branch_1_fun.2 = bf16[512,768]{1,0:T(8,128)(2,1)} custom-call(bf16[8,64,768]{2,1,0:T(8,128)(2,1)} %all_gather.10.left_ref, bf16[768,384]{1,0:T(8,128)(2,1)S(1)} %copy-done.7, bf16[768,384]{1,0:T(8,128)(2,1)} %get-tuple-element.44.other_ref), custom_call_target="tpu_custom_call" | custom-call | flops 603979776 | bytes 4194304 | tf_op jit(solution)/shard_map/cond/branch_1_fun/pallas_call | solution.py:81
  64.0 5.1 %all-to-all-start.5 = ((bf16[8,64,768]{2,1,0:T(8,128)(2,1)}), bf16[8,64,768]{2,1,0:T(8,128)(2,1)S(1)}, u32[]{:S(2)}, u32[]{:S(2)}) async-start(bf16[8,64,768]{2,1,0:T(8,128)(2,1)} %bitcast.8), calls=%async_computation.5 | async-start | bytes 1572864 | tf_op jit(solution)/shard_map/all_to_all | solution.py:155
  69.1 1.9 %collective-permute-start.9 = (bf16[384,768]{1,0:T(8,128)(2,1)S(1)}, bf16[384,768]{1,0:T(8,128)(2,1)S(1)}, u32[]{:S(2)}, u32[]{:S(2)}) collective-permute-start(bf16[384,768]{1,0:T(8,128)(2,1)S(1)} %copy-done.2), channel_id=1, source_target_pairs={{0,64},{64,0},{128,192},{192,128},{256,320},{320,256},{384,448},{4... | collective-permute-start | bytes 1769480 | tf_op jit(solution)/shard_map/ppermute | solution.py:179
  71.0 2.0 %collective-permute-done.9.other_ref = bf16[384,768]{1,0:T(8,128)(2,1)S(1)} collective-permute-done((bf16[384,768]{1,0:T(8,128)(2,1)S(1)}, bf16[384,768]{1,0:T(8,128)(2,1)S(1)}, u32[]{:S(2)}, u32[]{:S(2)}) %collective-permute-start.9) | collective-permute-done | bytes 589856 | tf_op jit(solution)/shard_map/ppermute | solution.py:179
  73.0 1.4 copy-done
  74.4 1.4 shard_map.85
  75.9 0.8 all-to-all-done.5
  76.6 0.2 fusion.22
  76.8 0.1 broadcast_in_dim.22
  76.9 0.1 pad_maximum_fusion
  77.0 0.0 copy-start.4
  77.0 24.2 %all_to_all.37.left_ref = bf16[8,64,1536]{2,1,0:T(8,128)(2,1)S(1)} all-to-all(bf16[8,64,1536]{2,1,0:T(8,128)(2,1)S(1)} %pad_maximum_fusion), channel_id=1, replica_groups=mesh['rep'=8,'row'=8,'col'=8] {'row'}, dimensions={0} | all-to-all | bytes 3145728 | tf_op jit(solution)/shard_map/all_to_all | solution.py:155
  101.2 1.9 %shard_map.86 = bf16[512,768]{1,0:T(8,128)(2,1)} custom-call(bf16[8,64,1536]{2,1,0:T(8,128)(2,1)S(1)} %all_to_all.37.left_ref, bf16[384,768]{1,0:T(8,128)(2,1)S(1)} %copy-done.2, bf16[384,768]{1,0:T(8,128)(2,1)S(1)} %copy-done.4), custom_call_target="tpu_custom_call" | custom-call | flops 603979776 | bytes 4194304 | tf_op jit(solution)/shard_map/pallas_call | solution.py:111
  103.1 0.0 reduce-scatter.2.cloned.1.call-update
  103.2 0.9 slice.167
  104.1 0.1 slice.166
  104.2 0.2 fusion.19
  104.4 0.8 copy-done.5
  105.2 47.6 %conditional.3 = (bf16[8,64,768]{2,1,0:T(8,128)(2,1)}, f32[768,384]{1,0:T(8,128)S(1)}, f32[384,768]{1,0:T(8,128)}) conditional(s32[]{:T(128)} %convert_element_type.140, (bf16[64,768]{1,0:T(8,128)(2,1)S(1)}, bf16[768,384]{1,0:T(8,128)(2,1)S(1)}, bf16[768,384]{1,0:T(8,128)(2,1)}, bf16[512,768]{1,0:T(8,128)(2,1)}, bf16[512,768]{1,0:T(8,128)(2,1)S(1)}, ...), branch_computations={%region_2.0_spmd, %region_3.0_spmd} | conditional | flops 1812529152 | bytes 35750164 | solution.py:238
  105.2 0.9 broadcast_in_dim.10
  106.1 5.9 %all-to-all-start.2 = ((bf16[8,64,768]{2,1,0:T(8,128)(2,1)}), bf16[8,64,768]{2,1,0:T(8,128)(2,1)S(1)}, u32[]{:S(2)}, u32[]{:S(2)}) async-start(bf16[8,64,768]{2,1,0:T(8,128)(2,1)} %broadcast_in_dim.10), calls=%async_computation.2 | async-start | bytes 1572864 | tf_op jit(solution)/shard_map/cond/branch_1_fun/all_to_all | solution.py:155
  112.0 1.9 %collective-permute-start.7 = (bf16[512,768]{1,0:T(8,128)(2,1)S(1)}, bf16[512,768]{1,0:T(8,128)(2,1)}, u32[]{:S(2)}, u32[]{:S(2)}) collective-permute-start(bf16[512,768]{1,0:T(8,128)(2,1)S(1)} %copy-done.9), channel_id=1, source_target_pairs={{0,64},{64,0},{128,192},{192,128},{256,320},{320,256},{384,448},{4... | collective-permute-start | bytes 2359304 | tf_op jit(solution)/shard_map/cond/branch_1_fun/ppermute | solution.py:179
  113.9 6.9 %all-to-all-done.2.left_ref = bf16[8,64,768]{2,1,0:T(8,128)(2,1)S(1)} async-done(((bf16[8,64,768]{2,1,0:T(8,128)(2,1)}), bf16[8,64,768]{2,1,0:T(8,128)(2,1)S(1)}, u32[]{:S(2)}, u32[]{:S(2)}) %all-to-all-start.2) | async-done | bytes 786464 | tf_op jit(solution)/shard_map/cond/branch_1_fun/all_to_all | solution.py:155
  120.8 3.5 %branch_1_fun.3 = bf16[512,768]{1,0:T(8,128)(2,1)} custom-call(bf16[8,64,768]{2,1,0:T(8,128)(2,1)S(1)} %all-to-all-done.2.left_ref, bf16[768,384]{1,0:T(8,128)(2,1)S(1)} %get-tuple-element.52.own_ref, bf16[768,384]{1,0:T(8,128)(2,1)} %get-tuple-element.53.other_ref), custom_call_target="tpu_custom_call" | custom-call | flops 603979776 | bytes 4194304 | tf_op jit(solution)/shard_map/cond/branch_1_fun/pallas_call | solution.py:111
  124.3 5.4 %all-to-all-start.3 = ((bf16[8,64,768]{2,1,0:T(8,128)(2,1)}), bf16[8,64,768]{2,1,0:T(8,128)(2,1)}, u32[]{:S(2)}, u32[]{:S(2)}) async-start(bf16[8,64,768]{2,1,0:T(8,128)(2,1)} %bitcast.6), calls=%async_computation.3 | async-start | bytes 1572864 | tf_op jit(solution)/shard_map/cond/branch_1_fun/all_to_all | solution.py:155
  129.8 1.9 %collective-permute-start.6 = (bf16[512,384]{1,0:T(8,128)(2,1)S(1)}, bf16[512,384]{1,0:T(8,128)(2,1)S(1)}, u32[]{:S(2)}, u32[]{:S(2)}) collective-permute-start(bf16[512,384]{1,0:T(8,128)(2,1)S(1)} %slice.95), channel_id=1, source_target_pairs={{0,64},{64,0},{128,192},{192,128},{256,320},{320,256},{384,448},{4... | collective-permute-start | bytes 1179656 | tf_op jit(solution)/shard_map/cond/branch_1_fun/ppermute | solution.py:179
  131.8 2.4 %collective-permute-start.4 = (bf16[512,768]{1,0:T(8,128)(2,1)}, bf16[512,768]{1,0:T(8,128)(2,1)S(1)}, u32[]{:S(2)}, u32[]{:S(2)}) collective-permute-start(bf16[512,768]{1,0:T(8,128)(2,1)} %get-tuple-element.54), channel_id=1, source_target_pairs={{0,64},{64,0},{128,192},{192,128},{256,320},{320,256},{384,448},{4... | collective-permute-start | bytes 2359304 | tf_op jit(solution)/shard_map/cond/branch_1_fun/ppermute | solution.py:179
  134.2 0.5 fusion.6
  134.7 1.9 %collective-permute-start.5 = (bf16[512,384]{1,0:T(8,128)(2,1)S(1)}, bf16[512,384]{1,0:T(8,128)(2,1)S(1)}, u32[]{:S(2)}, u32[]{:S(2)}) collective-permute-start(bf16[512,384]{1,0:T(8,128)(2,1)S(1)} %slice.155), channel_id=1, source_target_pairs={{0,64},{64,0},{128,192},{192,128},{256,320},{320,256},{384,448},{4... | collective-permute-start | bytes 1179656 | tf_op jit(solution)/shard_map/cond/branch_1_fun/ppermute | solution.py:179
  136.6 0.0 collective-permute-done.6
  136.7 2.6 %convolution_add_fusion.2 = f32[384,768]{1,0:T(8,128)} fusion(f32[384,768]{1,0:T(8,128)S(1)} %fusion.6, bf16[512,384]{1,0:T(8,128)(2,1)S(1)} %collective-permute-done.6, bf16[512,768]{1,0:T(8,128)(2,1)} %collective-permute-done.7), kind=kOutput, calls=%fused_computation.6 | convolution fusion | flops 302284800 | bytes 3538944 | tf_op jit(solution)/shard_map/cond/branch_1_fun/dot_general | solution.py:26
  139.3 1.7 fusion.4
  141.1 0.6 convolution_add_fusion.3
  141.7 11.1 %all-to-all-done.3 = bf16[8,64,768]{2,1,0:T(8,128)(2,1)} async-done(((bf16[8,64,768]{2,1,0:T(8,128)(2,1)}), bf16[8,64,768]{2,1,0:T(8,128)(2,1)}, u32[]{:S(2)}, u32[]{:S(2)}) %all-to-all-start.3) | async-done | bytes 786464 | tf_op jit(solution)/shard_map/cond/branch_1_fun/all_to_all | solution.py:155
  152.8 0.0 reduce-scatter.2.cloned.1.call-done.finished_ref
  152.8 2.4 %shard_map.87 = bf16[4,32,768]{2,1,0:T(8,128)(2,1)} custom-call(bf16[8,64,768]{2,1,0:T(8,128)(2,1)} %get-tuple-element.75.pieces_ref, bf16[64,768]{1,0:T(8,128)(2,1)} %reduce-scatter.2.cloned.1.call-done.finished_ref), custom_call_target="tpu_custom_call" | custom-call | tf_op jit(solution)/shard_map/pallas_call | solution.py:141
  155.1 13.3 %all_to_all.38 = bf16[4,32,768]{2,1,0:T(8,128)(2,1)S(1)} all-to-all(bf16[4,32,768]{2,1,0:T(8,128)(2,1)} %shard_map.87), channel_id=1, replica_groups={{0,128,256,384},{64,192,320,448},{1,129,257,385},{65,193,321,449},{2,13..., dimensions={0} | all-to-all | bytes 393216 | tf_op jit(solution)/shard_map/all_to_all | solution.py:155
  168.5 0.6 fusion.25
  169.1 0.6 fusion.26
  (31 shorter events, 0.2 us)
Async XLA Ops:
  8.6 20.2 %all-to-all-start.4 = ((bf16[4,32,768]{2,1,0:T(8,128)(2,1)}), bf16[4,32,768]{2,1,0:T(8,128)(2,1)S(1)}, u32[]{:S(2)}, u32[]{:S(2)}) async-start(bf16[4,32,768]{2,1,0:T(8,128)(2,1)} %get-tuple-element.70), calls=%async_computation.4 | async-start | bytes 393216 | tf_op jit(solution)/shard_map/all_to_all | solution.py:155
  18.9 54.0 %all-gather.4.cloned.1.call-start = ((), (), s32[]{:S(2)}) async-start(), calls=%async_computation.10 | async-start | bytes 1216512 | tf_op jit(solution)/shard_map/all_gather | solution.py:193
  18.9 10.7 %collective-permute-start.8 = (bf16[768,384]{1,0:T(8,128)(2,1)}, bf16[768,384]{1,0:T(8,128)(2,1)}, u32[]{:S(2)}, u32[]{:S(2)}) collective-permute-start(bf16[768,384]{1,0:T(8,128)(2,1)} %param.10), channel_id=1, source_target_pairs={{0,64},{64,0},{128,192},{192,128},{256,320},{320,256},{384,448},{4... | collective-permute-start | bytes 1769480 | tf_op jit(solution)/shard_map/ppermute | solution.py:179
  29.6 31.1 %copy-start.7 = (bf16[768,384]{1,0:T(8,128)(2,1)S(1)}, bf16[768,384]{1,0:T(8,128)(2,1)}, u32[]{:S(2)}) copy-start(bf16[768,384]{1,0:T(8,128)(2,1)} %get-tuple-element.43.own_ref) | copy-start | bytes 1769476 | tf_op jit(solution)/shard_map/cond
  64.0 5.1 %copy-start.2 = (bf16[384,768]{1,0:T(8,128)(2,1)S(1)}, bf16[384,768]{1,0:T(8,128)(2,1)}, u32[]{:S(2)}) copy-start(bf16[384,768]{1,0:T(8,128)(2,1)} %own_ref.3) | copy-start | bytes 1769476
  64.0 12.7 %all-to-all-start.5 = ((bf16[8,64,768]{2,1,0:T(8,128)(2,1)}), bf16[8,64,768]{2,1,0:T(8,128)(2,1)S(1)}, u32[]{:S(2)}, u32[]{:S(2)}) async-start(bf16[8,64,768]{2,1,0:T(8,128)(2,1)} %bitcast.8), calls=%async_computation.5 | async-start | bytes 1572864 | tf_op jit(solution)/shard_map/all_to_all | solution.py:155
  69.1 83.7 %reduce-scatter.2.cloned.1.call-start = ((), (), s32[]{:S(2)}) async-start(), calls=%async_computation.9 | async-start | bytes 884736 | tf_op jit(solution)/shard_map/reduce_scatter | solution.py:216
  69.1 3.9 %collective-permute-start.9 = (bf16[384,768]{1,0:T(8,128)(2,1)S(1)}, bf16[384,768]{1,0:T(8,128)(2,1)S(1)}, u32[]{:S(2)}, u32[]{:S(2)}) collective-permute-start(bf16[384,768]{1,0:T(8,128)(2,1)S(1)} %copy-done.2), channel_id=1, source_target_pairs={{0,64},{64,0},{128,192},{192,128},{256,320},{320,256},{384,448},{4... | collective-permute-start | bytes 1769480 | tf_op jit(solution)/shard_map/ppermute | solution.py:179
  73.0 2.9 %copy-start.3 = (bf16[384,768]{1,0:T(8,128)(2,1)}, bf16[384,768]{1,0:T(8,128)(2,1)S(1)}, u32[]{:S(2)}) copy-start(bf16[384,768]{1,0:T(8,128)(2,1)S(1)} %collective-permute-done.9.other_ref) | copy-start | bytes 1769476
  73.0 1.4 copy-start
  77.0 24.2 %copy-start.4 = (bf16[384,768]{1,0:T(8,128)(2,1)S(1)}, bf16[384,768]{1,0:T(8,128)(2,1)}, u32[]{:S(2)}) copy-start(bf16[384,768]{1,0:T(8,128)(2,1)} %copy-done.3) | copy-start | bytes 1769476
  101.2 1.9 %copy-start.1 = (bf16[704,768]{1,0:T(8,128)(2,1)S(1)}, bf16[704,768]{1,0:T(8,128)(2,1)}, u32[]{:S(2)}) copy-start(bf16[704,768]{1,0:T(8,128)(2,1)} %all-gather.4.cloned.1.call-done) | copy-start | bytes 3244036
  104.1 1.1 copy-start.5
  105.2 6.8 %copy-start.9 = (bf16[512,768]{1,0:T(8,128)(2,1)S(1)}, bf16[512,768]{1,0:T(8,128)(2,1)}, u32[]{:S(2)}) copy-start(bf16[512,768]{1,0:T(8,128)(2,1)} %get-tuple-element.56) | copy-start | bytes 2359300 | tf_op jit(solution)/shard_map/cond
  106.1 14.7 %all-to-all-start.2 = ((bf16[8,64,768]{2,1,0:T(8,128)(2,1)}), bf16[8,64,768]{2,1,0:T(8,128)(2,1)S(1)}, u32[]{:S(2)}, u32[]{:S(2)}) async-start(bf16[8,64,768]{2,1,0:T(8,128)(2,1)} %broadcast_in_dim.10), calls=%async_computation.2 | async-start | bytes 1572864 | tf_op jit(solution)/shard_map/cond/branch_1_fun/all_to_all | solution.py:155
  112.0 24.7 %collective-permute-start.7 = (bf16[512,768]{1,0:T(8,128)(2,1)S(1)}, bf16[512,768]{1,0:T(8,128)(2,1)}, u32[]{:S(2)}, u32[]{:S(2)}) collective-permute-start(bf16[512,768]{1,0:T(8,128)(2,1)S(1)} %copy-done.9), channel_id=1, source_target_pairs={{0,64},{64,0},{128,192},{192,128},{256,320},{320,256},{384,448},{4... | collective-permute-start | bytes 2359304 | tf_op jit(solution)/shard_map/cond/branch_1_fun/ppermute | solution.py:179
  124.3 28.4 %all-to-all-start.3 = ((bf16[8,64,768]{2,1,0:T(8,128)(2,1)}), bf16[8,64,768]{2,1,0:T(8,128)(2,1)}, u32[]{:S(2)}, u32[]{:S(2)}) async-start(bf16[8,64,768]{2,1,0:T(8,128)(2,1)} %bitcast.6), calls=%async_computation.3 | async-start | bytes 1572864 | tf_op jit(solution)/shard_map/cond/branch_1_fun/all_to_all | solution.py:155
  129.8 6.8 %collective-permute-start.6 = (bf16[512,384]{1,0:T(8,128)(2,1)S(1)}, bf16[512,384]{1,0:T(8,128)(2,1)S(1)}, u32[]{:S(2)}, u32[]{:S(2)}) collective-permute-start(bf16[512,384]{1,0:T(8,128)(2,1)S(1)} %slice.95), channel_id=1, source_target_pairs={{0,64},{64,0},{128,192},{192,128},{256,320},{320,256},{384,448},{4... | collective-permute-start | bytes 1179656 | tf_op jit(solution)/shard_map/cond/branch_1_fun/ppermute | solution.py:179
  131.8 9.3 %collective-permute-start.4 = (bf16[512,768]{1,0:T(8,128)(2,1)}, bf16[512,768]{1,0:T(8,128)(2,1)S(1)}, u32[]{:S(2)}, u32[]{:S(2)}) collective-permute-start(bf16[512,768]{1,0:T(8,128)(2,1)} %get-tuple-element.54), channel_id=1, source_target_pairs={{0,64},{64,0},{128,192},{192,128},{256,320},{320,256},{384,448},{4... | collective-permute-start | bytes 2359304 | tf_op jit(solution)/shard_map/cond/branch_1_fun/ppermute | solution.py:179
  134.7 6.3 %collective-permute-start.5 = (bf16[512,384]{1,0:T(8,128)(2,1)S(1)}, bf16[512,384]{1,0:T(8,128)(2,1)S(1)}, u32[]{:S(2)}, u32[]{:S(2)}) collective-permute-start(bf16[512,384]{1,0:T(8,128)(2,1)S(1)} %slice.155), channel_id=1, source_target_pairs={{0,64},{64,0},{128,192},{192,128},{256,320},{320,256},{384,448},{4... | collective-permute-start | bytes 1179656 | tf_op jit(solution)/shard_map/cond/branch_1_fun/ppermute | solution.py:179
  152.8 16.9 %copy-start.10 = (f32[768,384]{1,0:T(8,128)}, f32[768,384]{1,0:T(8,128)S(1)}, u32[]{:S(2)}) copy-start(f32[768,384]{1,0:T(8,128)S(1)} %get-tuple-element.68) | copy-start | bytes 3538948
  152.8 15.7 %copy-start.11 = (bf16[1,16,768]{2,1,0:T(8,128)(2,1)S(1)}, bf16[1,16,768]{2,1,0:T(8,128)(2,1)}, u32[]{:S(2)}) copy-start(bf16[1,16,768]{2,1,0:T(8,128)(2,1)} %tokens_ref.1) | copy-start | bytes 73732
  152.8 16.3 %copy-start.12 = (bf16[16,768]{1,0:T(8,128)(2,1)S(1)}, bf16[16,768]{1,0:T(8,128)(2,1)}, u32[]{:S(2)}) copy-start(bf16[16,768]{1,0:T(8,128)(2,1)} %get-tuple-element.76) | copy-start | bytes 73732
Sparse Core Ops, SparseCore 0:
  29.7 39.5 all-gather.3
  103.3 38.2 reduce-scatter.1

commit v11 on v9

v11 whole, which is shorter than its diff:
```python
import jax
import jax.numpy as jnp
from jax import lax
from jax.experimental import pallas as pl
from jax.experimental.pallas import tpu as pltpu
from jax.sharding import PartitionSpec as P

MBT = 32
CORES = 2
VMEM = 24 << 20

root_coef = 0.7978845608028654
cubic_coef = 0.044715


def gelu_both(values):
    inner = root_coef * (values + cubic_coef * values * values * values)
    tangent = jnp.tanh(inner)
    slope = 0.5 * (1.0 + tangent) + 0.5 * values * (1.0 - tangent * tangent) * root_coef * (
        1.0 + 3.0 * cubic_coef * values * values
    )
    return 0.5 * values * (1.0 + tangent), slope


def product(left, right, left_dim, right_dim):
    return lax.dot_general(
        left, right, (((left_dim,), (right_dim,)), ((), ())), preferred_element_type=jnp.float32
    )


def prepared(tokens, cotangent, counts, copies):
    _, rows, width = tokens.shape

    def kernel(counts_ref, tokens_ref, cotangent_ref, send_ref, scaled_ref):
        own_count = counts_ref[lax.axis_index("rep")]
        total = counts_ref[0]
        for replica in range(1, counts.shape[0]):
            total = total + counts_ref[replica]
        token_total = (MBT * total).astype(jnp.float32)
        positions = lax.axis_index("col") * rows + lax.broadcasted_iota(
            jnp.int32, (rows, width), 0
        )
        kept_mask = (positions < MBT * own_count).astype(jnp.float32)
        scaled = (cotangent_ref[0].astype(jnp.float32) * kept_mask / token_total).astype(
            jnp.bfloat16
        )
        scaled_ref[...] = scaled
        for copy in range(copies):
            send_ref[copy, :rows] = tokens_ref[0]
            send_ref[copy, rows:] = scaled

    return pl.pallas_call(
        kernel,
        in_specs=[
            pl.BlockSpec(memory_space=pltpu.SMEM),
            pl.BlockSpec(memory_space=pltpu.VMEM),
            pl.BlockSpec(memory_space=pltpu.VMEM),
        ],
        out_specs=[pl.BlockSpec(memory_space=pltpu.VMEM), pl.BlockSpec(memory_space=pltpu.VMEM)],
        out_shape=[
            jax.ShapeDtypeStruct((copies, 2 * rows, width), jnp.bfloat16),
            jax.ShapeDtypeStruct((rows, width), jnp.bfloat16),
        ],
    )(counts, tokens, cotangent)


def whole(array):
    return pl.BlockSpec(array.shape, lambda i: (0,) * len(array.shape))


def inward(blocks, w_in, w_in_mate, w_out, w_out_mate):
    places, chips, rows, width = blocks.shape
    rows //= 2
    units = w_in.shape[1]
    step = places // 4
    height = step * chips * rows

    def kernel(blocks_ref, in_ref, in_mate_ref, out_ref, out_mate_ref, terms_ref):
        for at in range(4):
            here = slice(at * step, (at + 1) * step)
            lines = slice(at * height, (at + 1) * height)
            tokens = blocks_ref[here, :, :rows].reshape(height, width)
            scaled = blocks_ref[here, :, rows:].reshape(height, width)
            for place, (left, right, dim) in enumerate(
                (
                    (tokens, in_ref, 0),
                    (tokens, in_mate_ref, 0),
                    (scaled, out_ref, 1),
                    (scaled, out_mate_ref, 1),
                )
            ):
                terms_ref[lines, place * units : (place + 1) * units] = product(
                    left, right[...], 1, dim
                ).astype(jnp.bfloat16)

    total = places * chips * rows
    weights = (w_in, w_in_mate, w_out, w_out_mate)
    return pl.pallas_call(
        kernel,
        grid=(1,),
        in_specs=[whole(blocks)] + [whole(w) for w in weights],
        out_specs=pl.BlockSpec((total, 4 * units), lambda i: (0, 0)),
        out_shape=jax.ShapeDtypeStruct((total, 4 * units), jnp.bfloat16),
        compiler_params=pltpu.CompilerParams(vmem_limit_bytes=VMEM),
        cost_estimate=pl.CostEstimate(
            flops=8 * total * width * units, bytes_accessed=6 << 20, transcendentals=0
        ),
    )(blocks, *weights)


def outward(shares, w_in, w_in_mate, w_out, w_out_mate):
    total = shares.shape[0] * shares.shape[1]
    units = shares.shape[2] // 4
    width = w_in.shape[0]
    step = shares.shape[0] // 4
    height = total // 4

    def kernel(shares_ref, in_ref, in_mate_ref, out_ref, out_mate_ref, terms_ref):
        for at in range(4):
            left = shares_ref[at * step : (at + 1) * step].reshape(height, 4 * units)
            part = [left[:, k * units : (k + 1) * units] for k in range(4)]
            lines = slice(at * height, (at + 1) * height)
            mixed = product(part[0], out_ref[...], 1, 0) + product(part[1], out_mate_ref[...], 1, 0)
            terms_ref[lines, :width] = mixed.astype(jnp.bfloat16)
            back = product(part[2], in_ref[...], 1, 1) + product(part[3], in_mate_ref[...], 1, 1)
            terms_ref[lines, width:] = back.astype(jnp.bfloat16)

    weights = (w_in, w_in_mate, w_out, w_out_mate)
    return pl.pallas_call(
        kernel,
        grid=(1,),
        in_specs=[whole(shares)] + [whole(w) for w in weights],
        out_specs=pl.BlockSpec((total, 2 * width), lambda i: (0, 0)),
        out_shape=jax.ShapeDtypeStruct((total, 2 * width), jnp.bfloat16),
        compiler_params=pltpu.CompilerParams(vmem_limit_bytes=VMEM),
        cost_estimate=pl.CostEstimate(
            flops=8 * total * width * units, bytes_accessed=6 << 20, transcendentals=0
        ),
    )(shares, *weights)


def cut(value, pieces):
    rows, width = value.shape
    return value.reshape(pieces, rows // pieces, width)


def swapped(value, axis, groups=None):
    return lax.all_to_all(value, axis, 0, 0, axis_index_groups=groups, tiled=True)


def added_up(pieces):
    total = pieces[0].astype(jnp.float32)
    for at in range(1, pieces.shape[0]):
        total = total + pieces[at].astype(jnp.float32)
    return total


def spread(value, axis, size, groups=None):
    return swapped(jnp.broadcast_to(value[None], (size, *value.shape)), axis, groups)


def body(inputs, w_in, w_out, cotangent, counts):
    rows_local = inputs.shape[1]
    width = inputs.shape[2]
    units = w_in.shape[1]
    replicas = lax.axis_size("rep")
    columns = lax.axis_size("col")
    row_count = lax.axis_size("row")
    chips = replicas // CORES
    same_core = [[chip * CORES + core for chip in range(chips)] for core in range(CORES)]
    to_mate = [(r, r // CORES * CORES + (r + 1) % CORES) for r in range(replicas)]
    mate = lambda value: lax.ppermute(value, "rep", to_mate)

    tokens_local = inputs.reshape(rows_local, width)
    send, scaled = prepared(inputs, cotangent, counts, chips)

    w_in_mate, w_out_mate = mate(w_in), mate(w_out)

    weights = (w_in, w_in_mate, w_out, w_out_mate)

    rows_all = columns * chips * rows_local
    blocks = spread(swapped(send, "rep", same_core), "col", columns)
    terms = inward(blocks, *weights)
    sums = added_up(swapped(cut(terms, row_count), "row"))
    active, slope = gelu_both(sums[:, : 2 * units])
    share = jnp.concatenate(
        [active.astype(jnp.bfloat16), (sums[:, 2 * units :] * slope).astype(jnp.bfloat16)], axis=1
    )
    shares = spread(share, "row", row_count)
    ends = outward(shares, *weights)
    ends_line = added_up(swapped(cut(ends, columns), "col")).astype(jnp.bfloat16)
    finished = added_up(swapped(cut(ends_line, chips), "rep", same_core))
    block_output = (tokens_local.astype(jnp.float32) + finished[:, :width]).astype(jnp.bfloat16)
    input_grad = (scaled.astype(jnp.float32) + finished[:, width:]).astype(jnp.bfloat16)

    blocks_mate = mate(blocks)
    tokens_all, scaled_all, tokens_mate, scaled_mate = [
        b[:, :, at : at + rows_local].reshape(rows_all, width)
        for b in (blocks, blocks_mate)
        for at in (0, rows_local)
    ]
    shares = shares.reshape(rows_all, 4 * units)
    part = lambda k: shares[:, k * units : (k + 1) * units]
    from_mate = mate(jnp.concatenate([part(1), part(3)], axis=1))
    w_in_grad = product(tokens_all, part(2), 0, 0) + product(
        tokens_mate, from_mate[:, units:], 0, 0
    )
    w_out_grad = product(part(0), scaled_all, 0, 0) + product(
        from_mate[:, :units], scaled_mate, 0, 0
    )
    return (
        block_output.reshape(1, rows_local, width),
        input_grad.reshape(1, rows_local, width),
        w_in_grad,
        w_out_grad,
    )


def solution(mesh):
    placed = (
        P("rep", "col", "row"),
        P("row", ("rep", "col")),
        P(("rep", "col"), "row"),
        P("rep", "col", "row"),
        P(),
    )
    return jax.shard_map(
        body,
        mesh=mesh,
        in_specs=placed,
        out_specs=(
            P("rep", "col", "row"),
            P("rep", "col", "row"),
            P("row", ("rep", "col")),
            P(("rep", "col"), "row"),
        ),
        check_vma=False,
    )
```

time: 176 us -> 183 us (1.040)
  waiting for transfers between devices: 25.5 us -> 67.9 us
  starting transfers between devices: 38.6 us -> 23.7 us
  between operations: 14.8 us -> 0.89 us
  Pallas kernels: 12.6 us -> 6.06 us
  matrix products: 7.62 us -> 4.22 us
  blocking collectives: 65.8 us -> 68.6 us
  local copies, waits for them, and re-layouts: 4.03 us -> 6.67 us
  other arithmetic: 5.97 us -> 3.43 us
    all_to_all x4 -> x3, waiting for transfers between devices: 25.4 us -> 65.7 us  [swapped(): lax.all_to_all(value, axis, 0, 0, axis_index_groups=groups, tiled=True)]
    all_to_all x2 -> x3, blocking collectives: 35.4 us -> 68.6 us  [swapped(): lax.all_to_all(value, axis, 0, 0, axis_index_groups=groups, tiled=True)]
    all_gather x1 -> x0, blocking collectives: 30.4 us -> none  [forward_plain(): blocks = lax.all_gather(line, 'col', axis=0)]
    all_to_all x4 -> x3, starting transfers between devices: 26.7 us -> 15 us  [swapped(): lax.all_to_all(value, axis, 0, 0, axis_index_groups=groups, tiled=True)]
    pallas_call x4 -> x2, Pallas kernels: 11.1 us -> 4.58 us  [the longest x1 2.33 us: outward(): pl.pallas_call(kernel, grid=(1,), in_specs=[whole(shares)] + [whole(w) fo...]
    dot_general x4, matrix products: 7.62 us -> 4.22 us  [product(): lax.dot_general(left, right, (((left_dim,), (right_dim,)), ((), ())), pre...]
    ppermute x6 -> x4, starting transfers between devices: 12 us -> 8.65 us  [body(): mate = lambda value: lax.ppermute(value, 'rep', to_mate)]
    unnamed x8 -> x30, local copies, waits for them, and re-layouts: 0.82 us -> 3.94 us
  transfers between devices with their start and end apart: 12 -> 7, of which waited for: 4 -> 5; matrix products, arithmetic and copies ran while one was open for 8% -> 3% of each run, Pallas kernels for 4% -> 0%
where the time goes in v11:
time: 183 us; the launch traced here: 181 us
  blocking collectives  68.6 us (37%)
  waiting for transfers between devices  67.9 us (37%)
  starting transfers between devices  23.7 us (13%)
  local copies, waits for them, and re-layouts  6.67 us (4%)
  Pallas kernels  6.06 us (3%)
  matrix products  4.22 us (2%)
  other arithmetic  3.43 us (2%)
    all_to_all x3, blocking collectives, swapped(): lax.all_to_all(value, axis, 0, 0, axis_index_groups=groups, tiled=True)  68.6 us
    all_to_all x3, waiting for transfers between devices, swapped(): lax.all_to_all(value, axis, 0, 0, axis_index_groups=groups, tiled=True)  65.7 us
    all_to_all x3, starting transfers between devices, swapped(): lax.all_to_all(value, axis, 0, 0, axis_index_groups=groups, tiled=True)  15 us
    ppermute x4, starting transfers between devices, body(): mate = lambda value: lax.ppermute(value, 'rep', to_mate)  8.65 us
    dot_general x4, matrix products, product(): lax.dot_general(left, right, (((left_dim,), (right_dim,)), ((), ())), pre...  4.22 us
    unnamed x30, local copies, waits for them, and re-layouts  3.94 us
  transfers between devices with their start and end apart: 7, of which 5 were waited for; matrix products, arithmetic and copies ran while one was open for 3% of the time, Pallas kernels for 0%

profile of v11, /device:TPU:6, one launch (start us, length us, event | category | flops | bytes accessed | tf_op | source)
XLA Modules:
  0.0 181.4 jit_solution(7409667294766234823)
XLA Ops:
  0.6 1.5 shard_map.84
  2.1 20.6 %all_to_all.30 = bf16[4,32,768]{2,1,0:T(8,128)(2,1)S(1)} all-to-all(bf16[4,32,768]{2,1,0:T(8,128)(2,1)} %get-tuple-element.6), channel_id=1, replica_groups={{0,128,256,384},{64,192,320,448},{1,129,257,385},{65,193,321,449},{2,13..., dimensions={0} | all-to-all | bytes 393216 | tf_op jit(solution)/shard_map/all_to_all | solution.py:148
  22.7 1.4 broadcast_in_dim.4
  24.1 7.2 %all-to-all-start.1 = ((bf16[8,4,32,768]{3,2,1,0:T(8,128)(2,1)}), bf16[8,4,32,768]{3,2,1,0:T(8,128)(2,1)S(1)}, u32[]{:S(2)}, u32[]{:S(2)}) async-start(bf16[8,4,32,768]{3,2,1,0:T(8,128)(2,1)} %broadcast_in_dim.4), calls=%async_computation.1 | async-start | bytes 3145728 | tf_op jit(solution)/shard_map/all_to_all | solution.py:148
  31.3 0.0 copy-done.1
  31.3 1.9 %collective-permute-start = (bf16[768,384]{1,0:T(8,128)(2,1)S(1)}, bf16[768,384]{1,0:T(8,128)(2,1)S(1)}, u32[]{:S(2)}, u32[]{:S(2)}) collective-permute-start(bf16[768,384]{1,0:T(8,128)(2,1)S(1)} %copy-done.1), channel_id=1, source_target_pairs={{0,64},{64,0},{128,192},{192,128},{256,320},{320,256},{384,448},{4... | collective-permute-start | bytes 1769480 | tf_op jit(solution)/shard_map/ppermute | solution.py:172
  33.3 0.0 copy-done.3
  33.3 2.4 %collective-permute-start.1 = (bf16[384,768]{1,0:T(8,128)(2,1)S(1)}, bf16[384,768]{1,0:T(8,128)(2,1)S(1)}, u32[]{:S(2)}, u32[]{:S(2)}) collective-permute-start(bf16[384,768]{1,0:T(8,128)(2,1)S(1)} %copy-done.3), channel_id=1, source_target_pairs={{0,64},{64,0},{128,192},{192,128},{256,320},{320,256},{384,448},{4... | collective-permute-start | bytes 1769480 | tf_op jit(solution)/shard_map/ppermute | solution.py:172
  35.7 0.0 collective-permute-done.in_mate_ref
  35.7 0.0 copy-start.5
  35.7 1.6 collective-permute-done.1.out_mate_ref
  37.3 0.8 copy-done.7
  38.1 30.6 %all-to-all-done.1.blocks_ref = bf16[8,4,32,768]{3,2,1,0:T(8,128)(2,1)S(1)} async-done(((bf16[8,4,32,768]{3,2,1,0:T(8,128)(2,1)}), bf16[8,4,32,768]{3,2,1,0:T(8,128)(2,1)S(1)}, u32[]{:S(2)}, u32[]{:S(2)}) %all-to-all-start.1) | async-done | bytes 1572896 | tf_op jit(solution)/shard_map/all_to_all | solution.py:148
  68.7 1.1 copy-done.8
  69.7 2.3 %shard_map.85 = bf16[512,1536]{1,0:T(8,128)(2,1)S(1)} custom-call(bf16[8,4,32,768]{3,2,1,0:T(8,128)(2,1)S(1)} %all-to-all-done.1.blocks_ref, bf16[768,384]{1,0:T(8,128)(2,1)S(1)} %copy-done.1, bf16[768,384]{1,0:T(8,128)(2,1)S(1)} %collective-permute-done.in_mate_ref, bf16[384,768]{1,0:T(8,128)(2,1)S(1)} %copy-done.3, bf16[384,768]{1,0:T(8,128)(2,1)S(1)} %copy-done.8), custom_call_target="tpu_custom_call" | custom-call | flops 1207959552 | bytes 6291456 | tf_op jit(solution)/shard_map/pallas_call | solution.py:98
  72.0 0.0 copy-done.5
  72.0 25.1 %all_to_all.31 = bf16[8,64,1536]{2,1,0:T(8,128)(2,1)S(1)} all-to-all(bf16[8,64,1536]{2,1,0:T(8,128)(2,1)S(1)} %bitcast.27), channel_id=1, replica_groups=mesh['rep'=8,'row'=8,'col'=8] {'row'}, dimensions={0} | all-to-all | bytes 3145728 | tf_op jit(solution)/shard_map/all_to_all | solution.py:148
  97.1 0.2 add_bitcast_fusion
  97.3 0.1 multiply_convert_fusion
  97.5 0.1 broadcast_in_dim.5
  97.6 0.0 copy-start.2
  97.6 0.0 copy-start.4
  97.6 0.0 copy-start.6
  97.7 0.0 copy-start.9
  97.7 22.8 %all_to_all.32.shares_ref = bf16[8,64,1536]{2,1,0:T(8,128)(2,1)S(1)} all-to-all(bf16[8,64,1536]{2,1,0:T(8,128)(2,1)S(1)} %broadcast_in_dim.5), channel_id=1, replica_groups=mesh['rep'=8,'row'=8,'col'=8] {'row'}, dimensions={0} | all-to-all | bytes 3145728 | tf_op jit(solution)/shard_map/all_to_all | solution.py:148
  120.5 0.0 copy-done.4
  120.5 2.3 %shard_map.86 = bf16[512,1536]{1,0:T(8,128)(2,1)S(1)} custom-call(bf16[8,64,1536]{2,1,0:T(8,128)(2,1)S(1)} %all_to_all.32.shares_ref, bf16[768,384]{1,0:T(8,128)(2,1)S(1)} %copy-done.2, bf16[768,384]{1,0:T(8,128)(2,1)S(1)} %copy-done.6, bf16[384,768]{1,0:T(8,128)(2,1)S(1)} %copy-done.4, bf16[384,768]{1,0:T(8,128)(2,1)S(1)} %copy-done.9), custom_call_target="tpu_custom_call" | custom-call | flops 1207959552 | bytes 6291456 | tf_op jit(solution)/shard_map/pallas_call | solution.py:129
  122.9 1.1 copy-done
  124.0 4.3 %all-to-all-start.4 = ((bf16[8,64,1536]{2,1,0:T(8,128)(2,1)}), bf16[8,64,1536]{2,1,0:T(8,128)(2,1)}, u32[]{:S(2)}, u32[]{:S(2)}) async-start(bf16[8,64,1536]{2,1,0:T(8,128)(2,1)} %bitcast.26), calls=%async_computation.4 | async-start | bytes 3145728 | tf_op jit(solution)/shard_map/all_to_all | solution.py:148
  128.3 1.9 %collective-permute-start.2 = (bf16[8,4,32,768]{3,2,1,0:T(8,128)(2,1)S(1)}, bf16[8,4,32,768]{3,2,1,0:T(8,128)(2,1)S(1)}, u32[]{:S(2)}, u32[]{:S(2)}) collective-permute-start(bf16[8,4,32,768]{3,2,1,0:T(8,128)(2,1)S(1)} %all-to-all-done.1.blocks_ref), channel_id=1, source_target_pairs={{0,64},{64,0},{128,192},{192,128},{256,320},{320,256},{384,448},{4... | collective-permute-start | bytes 4718600 | tf_op jit(solution)/shard_map/ppermute | solution.py:172
  130.2 0.1 fusion.18
  130.4 0.1 fusion.19
  130.5 0.1 pad_maximum_fusion
  130.6 2.4 %collective-permute-start.3 = (bf16[512,768]{1,0:T(8,128)(2,1)S(1)}, bf16[512,768]{1,0:T(8,128)(2,1)S(1)}, u32[]{:S(2)}, u32[]{:S(2)}) collective-permute-start(bf16[512,768]{1,0:T(8,128)(2,1)S(1)} %pad_maximum_fusion), channel_id=1, source_target_pairs={{0,64},{64,0},{128,192},{192,128},{256,320},{320,256},{384,448},{4... | collective-permute-start | bytes 2359304 | tf_op jit(solution)/shard_map/ppermute | solution.py:172
  133.0 0.6 collective-permute-done.2
  133.6 1.0 fusion.17
  134.6 0.6 fusion.4
  135.2 0.5 fusion.1
  135.7 0.0 collective-permute-done.3
  135.7 0.9 copy-done.11
  136.6 1.6 convolution_add_fusion.1
  138.2 27.8 %all-to-all-done.4 = bf16[8,64,1536]{2,1,0:T(8,128)(2,1)} async-done(((bf16[8,64,1536]{2,1,0:T(8,128)(2,1)}), bf16[8,64,1536]{2,1,0:T(8,128)(2,1)}, u32[]{:S(2)}, u32[]{:S(2)}) %all-to-all-start.4) | async-done | bytes 1572896 | tf_op jit(solution)/shard_map/all_to_all | solution.py:148
  166.0 2.4 %add_convert_fusion = bf16[1,64,1536]{2,1,0:T(8,128)(2,1)} fusion(bf16[8,64,1536]{2,1,0:T(8,128)(2,1)} %all-to-all-done.4), kind=kLoop, calls=%fused_computation.9 | loop fusion | flops 1572864 | bytes 1769472 | tf_op jit(solution)/shard_map/convert_element_type | solution.py:191
  168.4 3.5 %all-to-all-start.5 = ((bf16[4,16,1536]{2,1,0:T(8,128)(2,1)}), bf16[4,16,1536]{2,1,0:T(8,128)(2,1)S(1)}, u32[]{:S(2)}, u32[]{:S(2)}) async-start(bf16[4,16,1536]{2,1,0:T(8,128)(2,1)} %bitcast.4), calls=%async_computation.5 | async-start | bytes 393216 | tf_op jit(solution)/shard_map/all_to_all | solution.py:148
  171.9 0.0 copy-start.14
  171.9 1.5 convolution_add_fusion
  173.4 7.3 %all-to-all-done.5 = bf16[4,16,1536]{2,1,0:T(8,128)(2,1)S(1)} async-done(((bf16[4,16,1536]{2,1,0:T(8,128)(2,1)}), bf16[4,16,1536]{2,1,0:T(8,128)(2,1)S(1)}, u32[]{:S(2)}, u32[]{:S(2)}) %all-to-all-start.5) | async-done | bytes 196640 | tf_op jit(solution)/shard_map/all_to_all | solution.py:148
  180.7 0.6 fusion.16
  (18 shorter events, 0.1 us)
Async XLA Ops:
  24.1 7.2 %copy-start.1 = (bf16[768,384]{1,0:T(8,128)(2,1)S(1)}, bf16[768,384]{1,0:T(8,128)(2,1)}, u32[]{:S(2)}) copy-start(bf16[768,384]{1,0:T(8,128)(2,1)} %in_ref.3) | copy-start | bytes 1769476
  24.1 9.2 %copy-start.3 = (bf16[384,768]{1,0:T(8,128)(2,1)S(1)}, bf16[384,768]{1,0:T(8,128)(2,1)}, u32[]{:S(2)}) copy-start(bf16[384,768]{1,0:T(8,128)(2,1)} %out_ref.3) | copy-start | bytes 1769476
  24.1 44.6 %all-to-all-start.1 = ((bf16[8,4,32,768]{3,2,1,0:T(8,128)(2,1)}), bf16[8,4,32,768]{3,2,1,0:T(8,128)(2,1)S(1)}, u32[]{:S(2)}, u32[]{:S(2)}) async-start(bf16[8,4,32,768]{3,2,1,0:T(8,128)(2,1)} %broadcast_in_dim.4), calls=%async_computation.1 | async-start | bytes 3145728 | tf_op jit(solution)/shard_map/all_to_all | solution.py:148
  31.3 4.4 %collective-permute-start = (bf16[768,384]{1,0:T(8,128)(2,1)S(1)}, bf16[768,384]{1,0:T(8,128)(2,1)S(1)}, u32[]{:S(2)}, u32[]{:S(2)}) collective-permute-start(bf16[768,384]{1,0:T(8,128)(2,1)S(1)} %copy-done.1), channel_id=1, source_target_pairs={{0,64},{64,0},{128,192},{192,128},{256,320},{320,256},{384,448},{4... | collective-permute-start | bytes 1769480 | tf_op jit(solution)/shard_map/ppermute | solution.py:172
  33.3 4.0 %collective-permute-start.1 = (bf16[384,768]{1,0:T(8,128)(2,1)S(1)}, bf16[384,768]{1,0:T(8,128)(2,1)S(1)}, u32[]{:S(2)}, u32[]{:S(2)}) collective-permute-start(bf16[384,768]{1,0:T(8,128)(2,1)S(1)} %copy-done.3), channel_id=1, source_target_pairs={{0,64},{64,0},{128,192},{192,128},{256,320},{320,256},{384,448},{4... | collective-permute-start | bytes 1769480 | tf_op jit(solution)/shard_map/ppermute | solution.py:172
  35.7 36.3 %copy-start.5 = (bf16[768,384]{1,0:T(8,128)(2,1)}, bf16[768,384]{1,0:T(8,128)(2,1)S(1)}, u32[]{:S(2)}) copy-start(bf16[768,384]{1,0:T(8,128)(2,1)S(1)} %collective-permute-done.in_mate_ref) | copy-start | bytes 1769476
  37.3 0.8 copy-start.7
  68.7 1.1 copy-start.8
  97.6 22.9 %copy-start.2 = (bf16[768,384]{1,0:T(8,128)(2,1)S(1)}, bf16[768,384]{1,0:T(8,128)(2,1)}, u32[]{:S(2)}) copy-start(bf16[768,384]{1,0:T(8,128)(2,1)} %in_ref.3) | copy-start | bytes 1769476
  97.6 22.9 %copy-start.4 = (bf16[384,768]{1,0:T(8,128)(2,1)S(1)}, bf16[384,768]{1,0:T(8,128)(2,1)}, u32[]{:S(2)}) copy-start(bf16[384,768]{1,0:T(8,128)(2,1)} %out_ref.3) | copy-start | bytes 1769476
  97.6 22.9 %copy-start.6 = (bf16[768,384]{1,0:T(8,128)(2,1)S(1)}, bf16[768,384]{1,0:T(8,128)(2,1)}, u32[]{:S(2)}) copy-start(bf16[768,384]{1,0:T(8,128)(2,1)} %copy-done.5) | copy-start | bytes 1769476
  97.7 22.9 %copy-start.9 = (bf16[384,768]{1,0:T(8,128)(2,1)S(1)}, bf16[384,768]{1,0:T(8,128)(2,1)}, u32[]{:S(2)}) copy-start(bf16[384,768]{1,0:T(8,128)(2,1)} %copy-done.7) | copy-start | bytes 1769476
  122.9 1.1 copy-start
  124.0 42.0 %all-to-all-start.4 = ((bf16[8,64,1536]{2,1,0:T(8,128)(2,1)}), bf16[8,64,1536]{2,1,0:T(8,128)(2,1)}, u32[]{:S(2)}, u32[]{:S(2)}) async-start(bf16[8,64,1536]{2,1,0:T(8,128)(2,1)} %bitcast.26), calls=%async_computation.4 | async-start | bytes 3145728 | tf_op jit(solution)/shard_map/all_to_all | solution.py:148
  128.3 5.3 %collective-permute-start.2 = (bf16[8,4,32,768]{3,2,1,0:T(8,128)(2,1)S(1)}, bf16[8,4,32,768]{3,2,1,0:T(8,128)(2,1)S(1)}, u32[]{:S(2)}, u32[]{:S(2)}) collective-permute-start(bf16[8,4,32,768]{3,2,1,0:T(8,128)(2,1)S(1)} %all-to-all-done.1.blocks_ref), channel_id=1, source_target_pairs={{0,64},{64,0},{128,192},{192,128},{256,320},{320,256},{384,448},{4... | collective-permute-start | bytes 4718600 | tf_op jit(solution)/shard_map/ppermute | solution.py:172
  130.6 5.2 %collective-permute-start.3 = (bf16[512,768]{1,0:T(8,128)(2,1)S(1)}, bf16[512,768]{1,0:T(8,128)(2,1)S(1)}, u32[]{:S(2)}, u32[]{:S(2)}) collective-permute-start(bf16[512,768]{1,0:T(8,128)(2,1)S(1)} %pad_maximum_fusion), channel_id=1, source_target_pairs={{0,64},{64,0},{128,192},{192,128},{256,320},{320,256},{384,448},{4... | collective-permute-start | bytes 2359304 | tf_op jit(solution)/shard_map/ppermute | solution.py:172
  135.7 0.9 copy-start.11
  138.2 33.6 %copy-start.10 = (bf16[8,4,16,768]{3,2,1,0:T(8,128)(2,1)S(1)}, bf16[8,4,16,768]{3,2,1,0:T(8,128)(2,1)}, u32[]{:S(2)}) copy-start(bf16[8,4,16,768]{3,2,1,0:T(8,128)(2,1)} %get-tuple-element.8) | copy-start | bytes 2359300
  138.2 33.6 %copy-start.12 = (bf16[512,768]{1,0:T(8,128)(2,1)S(1)}, bf16[512,768]{1,0:T(8,128)(2,1)}, u32[]{:S(2)}) copy-start(bf16[512,768]{1,0:T(8,128)(2,1)} %copy-done.11) | copy-start | bytes 2359300
  168.4 12.3 %all-to-all-start.5 = ((bf16[4,16,1536]{2,1,0:T(8,128)(2,1)}), bf16[4,16,1536]{2,1,0:T(8,128)(2,1)S(1)}, u32[]{:S(2)}, u32[]{:S(2)}) async-start(bf16[4,16,1536]{2,1,0:T(8,128)(2,1)} %bitcast.4), calls=%async_computation.5 | async-start | bytes 393216 | tf_op jit(solution)/shard_map/all_to_all | solution.py:148
  171.9 8.9 %copy-start.13 = (bf16[1,16,768]{2,1,0:T(8,128)(2,1)S(1)}, bf16[1,16,768]{2,1,0:T(8,128)(2,1)}, u32[]{:S(2)}) copy-start(bf16[1,16,768]{2,1,0:T(8,128)(2,1)} %tokens_ref.1) | copy-start | bytes 73732
  171.9 8.9 %copy-start.14 = (bf16[16,768]{1,0:T(8,128)(2,1)S(1)}, bf16[16,768]{1,0:T(8,128)(2,1)}, u32[]{:S(2)}) copy-start(bf16[16,768]{1,0:T(8,128)(2,1)} %get-tuple-element.7) | copy-start | bytes 73732

commit v12 on v9

--- a/solution.py
+++ b/solution.py
@@ -168,58 +168,39 @@
     line_rows = chips * rows_local
     rows_all = columns * line_rows
 
-    padded = jnp.concatenate([scaled_line, scaled_line[: line_rows * 3 // 8]], axis=0)
-    scaled_blocks = lax.all_gather(padded, "col", axis=0)
-
-    def forward(line):
-        blocks = spread(line, "col", columns)
-        return blocks, paired(blocks, line_rows, w_in, w_in_mate, False)
-
-    def forward_plain(line):
-        blocks = lax.all_gather(line, "col", axis=0)
-        return blocks, paired(blocks, line_rows, w_in, w_in_mate, False)
-
-    some_kept = jnp.sum(counts) > 0
-    tokens_blocks, hidden_terms = lax.cond(some_kept, forward_plain, forward, tokens_line)
+    tokens_blocks = lax.all_gather(tokens_line, "col", axis=0)
+    hidden_terms = paired(tokens_blocks, line_rows, w_in, w_in_mate, False)
+    hidden_terms, scaled_line = lax.optimization_barrier((hidden_terms, scaled_line))
+    scaled_blocks = lax.all_gather(scaled_line, "col", axis=0)
     slope_terms = paired(scaled_blocks, line_rows, w_out, w_out_mate, True)
-
-    hidden = added_up(swapped(cut(hidden_terms, row_count), "row"))
+    hidden_pieces = swapped(cut(hidden_terms, row_count), "row")
+    hidden_pieces, slope_terms = lax.optimization_barrier((hidden_pieces, slope_terms))
+
+    hidden = added_up(hidden_pieces)
     active, slope = gelu_both(hidden)
     share = jnp.broadcast_to(active.astype(jnp.bfloat16)[None], (row_count, *active.shape))
     mixed = swapped(jnp.concatenate([share, cut(slope_terms, row_count)], axis=2), "row")
     activated = mixed[:, :, : active.shape[1]].reshape(rows_all, -1)
     grad_share = (added_up(mixed[:, :, active.shape[1] :]) * slope).astype(jnp.bfloat16)
     output_terms = joined(mixed, w_out, w_out_mate, False)
-    output_line = lax.psum_scatter(output_terms, "col", scatter_dimension=0, tiled=True)
     tokens_all = tokens_blocks.reshape(rows_all, width)
     scaled_all = scaled_blocks[:, :line_rows].reshape(rows_all, width)
 
-    def backward(share):
-        shares = spread(share, "row", row_count)
-        back_terms = joined(shares, w_in, w_in_mate, True)
-        hidden_grad = shares.reshape(rows_all, -1)
-        back_line = added_up(swapped(cut(back_terms, columns), "col")).astype(jnp.bfloat16)
-        w_out_grad = product(activated[:, :units], scaled_all, 0, 0) + product(
-            mate(activated[:, units:]), mate(scaled_all), 0, 0
-        )
-        w_in_grad = product(tokens_all, hidden_grad[:, :units], 0, 0) + product(
-            mate(tokens_all), mate(hidden_grad[:, units:]), 0, 0
-        )
-        return back_line, w_in_grad, w_out_grad
-
-    def nothing(share):
-        return (
-            jnp.zeros((line_rows, width), jnp.bfloat16),
-            jnp.zeros((width, units), jnp.float32),
-            jnp.zeros((units, width), jnp.float32),
-        )
-
-    back_line, w_in_grad, w_out_grad = lax.cond(some_kept, backward, nothing, grad_share)
-    ends = jnp.concatenate([cut(output_line, chips), cut(back_line, chips)], axis=1)
-    finished = added_up(swapped(ends, "rep", same_core))
-    block_output = (tokens_local.astype(jnp.float32) + finished[:rows_local]).astype(jnp.bfloat16)
-    input_grad = (scaled.astype(jnp.float32) + finished[rows_local:]).astype(jnp.bfloat16)
-
+    shares = spread(grad_share, "row", row_count)
+    back_terms = joined(shares, w_in, w_in_mate, True)
+    hidden_grad = shares.reshape(rows_all, -1)
+    ends = jnp.concatenate([output_terms, back_terms], axis=1)
+    ends_line = added_up(swapped(cut(ends, columns), "col")).astype(jnp.bfloat16)
+    finished = added_up(swapped(cut(ends_line, chips), "rep", same_core))
+    block_output = (tokens_local.astype(jnp.float32) + finished[:, :width]).astype(jnp.bfloat16)
+    input_grad = (scaled.astype(jnp.float32) + finished[:, width:]).astype(jnp.bfloat16)
+
+    w_out_grad = product(activated[:, :units], scaled_all, 0, 0) + product(
+        mate(activated[:, units:]), mate(scaled_all), 0, 0
+    )
+    w_in_grad = product(tokens_all, hidden_grad[:, :units], 0, 0) + product(
+        mate(tokens_all), mate(hidden_grad[:, units:]), 0, 0
+    )
     return (
         block_output.reshape(1, rows_local, width),
         input_grad.reshape(1, rows_local, width),

time: 176 us -> 183 us (1.040)
  between operations: 14.8 us -> 0.89 us
  waiting for transfers between devices: 25.5 us -> 38.1 us
  blocking collectives: 65.8 us -> 73.3 us
  Pallas kernels: 12.6 us -> 7.36 us
  local copies, waits for them, and re-layouts: 4.03 us -> 8.74 us
  starting transfers between devices: 38.6 us -> 42.8 us
  matrix products: 7.62 us -> 5.23 us
    all_gather x1 -> x2, blocking collectives: 30.4 us -> 53.7 us  [the longest x1 27.6 us: body(): tokens_blocks = lax.all_gather(tokens_line, 'col', axis=0)]
    all_to_all x2 -> x1, blocking collectives: 35.4 us -> 19.6 us  [swapped(): lax.all_to_all(value, axis, 0, 0, axis_index_groups=groups, tiled=True)]
    all_to_all x4 -> x5, waiting for transfers between devices: 25.4 us -> 38.1 us  [swapped(): lax.all_to_all(value, axis, 0, 0, axis_index_groups=groups, tiled=True)]
    unnamed x8 -> x28, local copies, waits for them, and re-layouts: 0.82 us -> 6.86 us
    all_to_all x4 -> x5, starting transfers between devices: 26.7 us -> 30.2 us  [swapped(): lax.all_to_all(value, axis, 0, 0, axis_index_groups=groups, tiled=True)]
    pallas_call x2, Pallas kernels: 5.37 us -> 2.55 us  [joined(): pl.pallas_call(kernel, grid=(1,), in_specs=[pl.BlockSpec((count, rows, 2...]
    pallas_call x2, Pallas kernels: 5.72 us -> 3.27 us  [paired(): pl.pallas_call(kernel, grid=(1,), in_specs=[pl.BlockSpec((count, rows, wi...]
    dot_general x4, matrix products: 7.62 us -> 5.23 us  [product(): lax.dot_general(left, right, (((left_dim,), (right_dim,)), ((), ())), pre...]
  transfers between devices with their start and end apart: 12 -> 11, of which waited for: 4 -> 4; matrix products, arithmetic and copies ran while one was open for 8% -> 5% of each run, Pallas kernels for 4% -> 1%
where the time goes in v12:
time: 183 us; the launch traced here: 181 us
  blocking collectives  73.3 us (40%)
  starting transfers between devices  42.8 us (23%)
  waiting for transfers between devices  38.1 us (21%)
  local copies, waits for them, and re-layouts  8.74 us (5%)
  Pallas kernels  7.36 us (4%)
  matrix products  5.23 us (3%)
  other arithmetic  4.79 us (3%)
    all_to_all x5, waiting for transfers between devices, swapped(): lax.all_to_all(value, axis, 0, 0, axis_index_groups=groups, tiled=True)  38.1 us
    all_to_all x5, starting transfers between devices, swapped(): lax.all_to_all(value, axis, 0, 0, axis_index_groups=groups, tiled=True)  30.2 us
    all_gather x1, blocking collectives, body(): tokens_blocks = lax.all_gather(tokens_line, 'col', axis=0)  27.6 us
    all_gather x1, blocking collectives, body(): scaled_blocks = lax.all_gather(scaled_line, 'col', axis=0)  26.1 us
    all_to_all x1, blocking collectives, swapped(): lax.all_to_all(value, axis, 0, 0, axis_index_groups=groups, tiled=True)  19.6 us
    ppermute x6, starting transfers between devices, body(): mate = lambda value: lax.ppermute(value, 'rep', to_mate)  12.6 us
    unnamed x28, local copies, waits for them, and re-layouts  6.86 us
    dot_general x4, matrix products, product(): lax.dot_general(left, right, (((left_dim,), (right_dim,)), ((), ())), pre...  5.23 us
  transfers between devices with their start and end apart: 11, of which 4 were waited for; matrix products, arithmetic and copies ran while one was open for 5% of the time, Pallas kernels for 1%

profile of v12, /device:TPU:6, one launch (start us, length us, event | category | flops | bytes accessed | tf_op | source)
XLA Modules:
  0.0 181.2 jit_solution(17953395944236426780)
XLA Ops:
  0.6 0.0 copy-start.8
  0.6 1.5 shard_map.84
  2.2 10.3 %all-to-all-start = ((bf16[4,32,768]{2,1,0:T(8,128)(2,1)}), bf16[4,32,768]{2,1,0:T(8,128)(2,1)S(1)}, u32[]{:S(2)}, u32[]{:S(2)}) async-start(bf16[4,32,768]{2,1,0:T(8,128)(2,1)} %get-tuple-element.10), calls=%async_computation | async-start | bytes 393216 | tf_op jit(solution)/shard_map/all_to_all | solution.py:134
  12.5 1.9 %collective-permute-start = (bf16[768,384]{1,0:T(8,128)(2,1)}, bf16[768,384]{1,0:T(8,128)(2,1)S(1)}, u32[]{:S(2)}, u32[]{:S(2)}) collective-permute-start(bf16[768,384]{1,0:T(8,128)(2,1)} %own_ref.7), channel_id=1, source_target_pairs={{0,64},{64,0},{128,192},{192,128},{256,320},{320,256},{384,448},{4... | collective-permute-start | bytes 1769480 | tf_op jit(solution)/shard_map/ppermute | solution.py:158
  14.4 8.0 %all-to-all-done = bf16[4,32,768]{2,1,0:T(8,128)(2,1)S(1)} async-done(((bf16[4,32,768]{2,1,0:T(8,128)(2,1)}), bf16[4,32,768]{2,1,0:T(8,128)(2,1)S(1)}, u32[]{:S(2)}, u32[]{:S(2)}) %all-to-all-start) | async-done | bytes 196640 | tf_op jit(solution)/shard_map/all_to_all | solution.py:134
  22.4 27.6 %all_gather.9.left_ref = bf16[8,64,768]{2,1,0:T(8,128)(2,1)S(1)} all-gather(bf16[1,64,768]{2,1,0:T(8,128)(2,1)S(1)} %bitcast.39), channel_id=1, replica_groups=mesh['rep'=8,'row'=8,'col'=8] {'col'}, dimensions={0}, use_global_device_ids=true | all-gather | bytes 884736 | tf_op jit(solution)/shard_map/all_gather | solution.py:171
  50.1 1.9 %shard_map.85 = bf16[512,768]{1,0:T(8,128)(2,1)} custom-call(bf16[8,64,768]{2,1,0:T(8,128)(2,1)S(1)} %all_gather.9.left_ref, bf16[768,384]{1,0:T(8,128)(2,1)S(1)} %copy-done.8, bf16[768,384]{1,0:T(8,128)(2,1)S(1)} %collective-permute-done.other_ref), custom_call_target="tpu_custom_call" | custom-call | flops 603979776 | bytes 4194304 | tf_op jit(solution)/shard_map/pallas_call | solution.py:81
  52.0 5.3 %all-to-all-start.1 = ((bf16[8,64,768]{2,1,0:T(8,128)(2,1)}), bf16[8,64,768]{2,1,0:T(8,128)(2,1)S(1)}, u32[]{:S(2)}, u32[]{:S(2)}) async-start(bf16[8,64,768]{2,1,0:T(8,128)(2,1)} %bitcast.3), calls=%async_computation.1 | async-start | bytes 1572864 | tf_op jit(solution)/shard_map/all_to_all | solution.py:134
  57.2 1.9 %collective-permute-start.1 = (bf16[384,768]{1,0:T(8,128)(2,1)S(1)}, bf16[384,768]{1,0:T(8,128)(2,1)S(1)}, u32[]{:S(2)}, u32[]{:S(2)}) collective-permute-start(bf16[384,768]{1,0:T(8,128)(2,1)S(1)} %copy-done.4), channel_id=1, source_target_pairs={{0,64},{64,0},{128,192},{192,128},{256,320},{320,256},{384,448},{4... | collective-permute-start | bytes 1769480 | tf_op jit(solution)/shard_map/ppermute | solution.py:158
  59.2 26.1 %all-gather = bf16[512,768]{1,0:T(8,128)(2,1)S(1)} all-gather(bf16[64,768]{1,0:T(8,128)(2,1)S(1)} %bitcast.38), channel_id=2, replica_groups=mesh['rep'=8,'row'=8,'col'=8] {'col'}, dimensions={0}, use_global_device_ids=true | all-gather | bytes 884736 | tf_op jit(solution)/shard_map/all_gather | solution.py:174
  85.3 1.4 shard_map.86
  86.7 0.9 copy-done
  87.6 0.8 copy-done.6
  88.4 0.2 fusion.11
  88.6 0.1 broadcast_in_dim.17
  88.6 0.1 pad_maximum_fusion
  88.7 19.6 %all_to_all.30.left_ref = bf16[8,64,1536]{2,1,0:T(8,128)(2,1)S(1)} all-to-all(bf16[8,64,1536]{2,1,0:T(8,128)(2,1)S(1)} %pad_maximum_fusion), channel_id=1, replica_groups=mesh['rep'=8,'row'=8,'col'=8] {'row'}, dimensions={0} | all-to-all | bytes 3145728 | tf_op jit(solution)/shard_map/all_to_all | solution.py:134
  108.3 0.2 fusion.12
  108.6 0.9 broadcast_in_dim.19
  109.5 5.9 %all-to-all-start.3 = ((bf16[8,64,768]{2,1,0:T(8,128)(2,1)}), bf16[8,64,768]{2,1,0:T(8,128)(2,1)S(1)}, u32[]{:S(2)}, u32[]{:S(2)}) async-start(bf16[8,64,768]{2,1,0:T(8,128)(2,1)} %broadcast_in_dim.19), calls=%async_computation.3 | async-start | bytes 1572864 | tf_op jit(solution)/shard_map/all_to_all | solution.py:134
  115.4 1.1 copy-done.5
  116.5 1.1 copy-done.7
  117.5 1.0 shard_map.87
  118.5 0.0 copy-start.2
  118.5 0.9 copy-done.2
  119.4 3.6 %all-to-all-done.3.left_ref = bf16[8,64,768]{2,1,0:T(8,128)(2,1)S(1)} async-done(((bf16[8,64,768]{2,1,0:T(8,128)(2,1)}), bf16[8,64,768]{2,1,0:T(8,128)(2,1)S(1)}, u32[]{:S(2)}, u32[]{:S(2)}) %all-to-all-start.3) | async-done | bytes 786464 | tf_op jit(solution)/shard_map/all_to_all | solution.py:134
  123.0 1.1 copy-done.9
  124.0 1.1 copy-done.11
  125.1 1.6 shard_map.88
  126.7 1.3 pad_maximum_fusion.1
  128.0 5.4 %all-to-all-start.4 = ((bf16[8,64,1536]{2,1,0:T(8,128)(2,1)}), bf16[8,64,1536]{2,1,0:T(8,128)(2,1)}, u32[]{:S(2)}, u32[]{:S(2)}) async-start(bf16[8,64,1536]{2,1,0:T(8,128)(2,1)} %bitcast.35), calls=%async_computation.4 | async-start | bytes 3145728 | tf_op jit(solution)/shard_map/all_to_all | solution.py:134
  133.3 2.1 %collective-permute-start.5 = (bf16[512,768]{1,0:T(8,128)(2,1)}, bf16[512,768]{1,0:T(8,128)(2,1)S(1)}, u32[]{:S(2)}, u32[]{:S(2)}) collective-permute-start(bf16[512,768]{1,0:T(8,128)(2,1)} %copy-done), channel_id=1, source_target_pairs={{0,64},{64,0},{128,192},{192,128},{256,320},{320,256},{384,448},{4... | collective-permute-start | bytes 2359304 | tf_op jit(solution)/shard_map/ppermute | solution.py:158
  135.4 0.1 slice.183
  135.5 2.4 %collective-permute-start.4 = (bf16[512,384]{1,0:T(8,128)(2,1)S(1)}, bf16[512,384]{1,0:T(8,128)(2,1)S(1)}, u32[]{:S(2)}, u32[]{:S(2)}) collective-permute-start(bf16[512,384]{1,0:T(8,128)(2,1)S(1)} %slice.185), channel_id=1, source_target_pairs={{0,64},{64,0},{128,192},{192,128},{256,320},{320,256},{384,448},{4... | collective-permute-start | bytes 1179656 | tf_op jit(solution)/shard_map/ppermute | solution.py:158
  137.9 1.9 %collective-permute-start.2 = (bf16[512,768]{1,0:T(8,128)(2,1)S(1)}, bf16[512,768]{1,0:T(8,128)(2,1)S(1)}, u32[]{:S(2)}, u32[]{:S(2)}) collective-permute-start(bf16[512,768]{1,0:T(8,128)(2,1)S(1)} %bitcast.31), channel_id=1, source_target_pairs={{0,64},{64,0},{128,192},{192,128},{256,320},{320,256},{384,448},{4... | collective-permute-start | bytes 2359304 | tf_op jit(solution)/shard_map/ppermute | solution.py:158
  139.8 0.5 fusion
  140.4 1.5 convolution_add_fusion
  141.9 0.8 slice.182
  142.7 2.4 %collective-permute-start.3 = (bf16[512,384]{1,0:T(8,128)(2,1)}, bf16[512,384]{1,0:T(8,128)(2,1)}, u32[]{:S(2)}, u32[]{:S(2)}) collective-permute-start(bf16[512,384]{1,0:T(8,128)(2,1)} %slice.182), channel_id=1, source_target_pairs={{0,64},{64,0},{128,192},{192,128},{256,320},{320,256},{384,448},{4... | collective-permute-start | bytes 1179656 | tf_op jit(solution)/shard_map/ppermute | solution.py:158
  145.1 0.6 fusion.2
  145.7 20.1 %all-to-all-done.4 = bf16[8,64,1536]{2,1,0:T(8,128)(2,1)} async-done(((bf16[8,64,1536]{2,1,0:T(8,128)(2,1)}), bf16[8,64,1536]{2,1,0:T(8,128)(2,1)}, u32[]{:S(2)}, u32[]{:S(2)}) %all-to-all-start.4) | async-done | bytes 1572896 | tf_op jit(solution)/shard_map/all_to_all | solution.py:134
  165.8 2.4 %add_convert_fusion = bf16[1,64,1536]{2,1,0:T(8,128)(2,1)} fusion(bf16[8,64,1536]{2,1,0:T(8,128)(2,1)} %all-to-all-done.4), kind=kLoop, calls=%fused_computation.8 | loop fusion | flops 1572864 | bytes 1769472 | tf_op jit(solution)/shard_map/convert_element_type | solution.py:193
  168.2 3.4 %all-to-all-start.5 = ((bf16[4,16,1536]{2,1,0:T(8,128)(2,1)}), bf16[4,16,1536]{2,1,0:T(8,128)(2,1)S(1)}, u32[]{:S(2)}, u32[]{:S(2)}) async-start(bf16[4,16,1536]{2,1,0:T(8,128)(2,1)} %bitcast.9), calls=%async_computation.5 | async-start | bytes 393216 | tf_op jit(solution)/shard_map/all_to_all | solution.py:134
  171.5 0.0 copy-start.12
  171.5 0.0 copy-start.13
  171.6 2.6 %convolution_add_fusion.1 = f32[768,384]{1,0:T(8,128)} fusion(f32[768,384]{1,0:T(8,128)S(1)} %fusion.2, bf16[512,768]{1,0:T(8,128)(2,1)S(1)} %collective-permute-done.2, bf16[512,384]{1,0:T(8,128)(2,1)} %collective-permute-done.3), kind=kOutput, calls=%fused_computation.3 | convolution fusion | flops 302284800 | bytes 3538944 | tf_op jit(solution)/shard_map/dot_general | solution.py:26
  174.2 6.3 %all-to-all-done.5 = bf16[4,16,1536]{2,1,0:T(8,128)(2,1)S(1)} async-done(((bf16[4,16,1536]{2,1,0:T(8,128)(2,1)}), bf16[4,16,1536]{2,1,0:T(8,128)(2,1)S(1)}, u32[]{:S(2)}, u32[]{:S(2)}) %all-to-all-start.5) | async-done | bytes 196640 | tf_op jit(solution)/shard_map/all_to_all | solution.py:134
  180.6 0.6 fusion.16
  (27 shorter events, 0.1 us)
Async XLA Ops:
  0.6 49.5 %copy-start.8 = (bf16[768,384]{1,0:T(8,128)(2,1)S(1)}, bf16[768,384]{1,0:T(8,128)(2,1)}, u32[]{:S(2)}) copy-start(bf16[768,384]{1,0:T(8,128)(2,1)} %own_ref.7) | copy-start | bytes 1769476
  2.2 20.2 %all-to-all-start = ((bf16[4,32,768]{2,1,0:T(8,128)(2,1)}), bf16[4,32,768]{2,1,0:T(8,128)(2,1)S(1)}, u32[]{:S(2)}, u32[]{:S(2)}) async-start(bf16[4,32,768]{2,1,0:T(8,128)(2,1)} %get-tuple-element.10), calls=%async_computation | async-start | bytes 393216 | tf_op jit(solution)/shard_map/all_to_all | solution.py:134
  12.5 37.6 %collective-permute-start = (bf16[768,384]{1,0:T(8,128)(2,1)}, bf16[768,384]{1,0:T(8,128)(2,1)S(1)}, u32[]{:S(2)}, u32[]{:S(2)}) collective-permute-start(bf16[768,384]{1,0:T(8,128)(2,1)} %own_ref.7), channel_id=1, source_target_pairs={{0,64},{64,0},{128,192},{192,128},{256,320},{320,256},{384,448},{4... | collective-permute-start | bytes 1769480 | tf_op jit(solution)/shard_map/ppermute | solution.py:158
  50.1 7.1 %copy-start.4 = (bf16[384,768]{1,0:T(8,128)(2,1)S(1)}, bf16[384,768]{1,0:T(8,128)(2,1)}, u32[]{:S(2)}) copy-start(bf16[384,768]{1,0:T(8,128)(2,1)} %own_ref.6) | copy-start | bytes 1769476
  50.1 1.9 %copy-start.10 = (bf16[768,384]{1,0:T(8,128)(2,1)}, bf16[768,384]{1,0:T(8,128)(2,1)S(1)}, u32[]{:S(2)}) copy-start(bf16[768,384]{1,0:T(8,128)(2,1)S(1)} %collective-permute-done.other_ref) | copy-start | bytes 1769476
  52.0 36.4 %all-to-all-start.1 = ((bf16[8,64,768]{2,1,0:T(8,128)(2,1)}), bf16[8,64,768]{2,1,0:T(8,128)(2,1)S(1)}, u32[]{:S(2)}, u32[]{:S(2)}) async-start(bf16[8,64,768]{2,1,0:T(8,128)(2,1)} %bitcast.3), calls=%async_computation.1 | async-start | bytes 1572864 | tf_op jit(solution)/shard_map/all_to_all | solution.py:134
  57.2 28.0 %collective-permute-start.1 = (bf16[384,768]{1,0:T(8,128)(2,1)S(1)}, bf16[384,768]{1,0:T(8,128)(2,1)S(1)}, u32[]{:S(2)}, u32[]{:S(2)}) collective-permute-start(bf16[384,768]{1,0:T(8,128)(2,1)S(1)} %copy-done.4), channel_id=1, source_target_pairs={{0,64},{64,0},{128,192},{192,128},{256,320},{320,256},{384,448},{4... | collective-permute-start | bytes 1769480 | tf_op jit(solution)/shard_map/ppermute | solution.py:158
  86.7 0.9 copy-start
  87.6 0.8 copy-start.6
  109.5 13.5 %all-to-all-start.3 = ((bf16[8,64,768]{2,1,0:T(8,128)(2,1)}), bf16[8,64,768]{2,1,0:T(8,128)(2,1)S(1)}, u32[]{:S(2)}, u32[]{:S(2)}) async-start(bf16[8,64,768]{2,1,0:T(8,128)(2,1)} %broadcast_in_dim.19), calls=%async_computation.3 | async-start | bytes 1572864 | tf_op jit(solution)/shard_map/all_to_all | solution.py:134
  115.4 1.1 copy-start.5
  116.5 1.1 copy-start.7
  118.5 0.9 copy-start.2
  123.0 1.1 copy-start.9
  124.0 1.1 copy-start.11
  125.1 1.6 copy-start.3
  128.0 37.9 %all-to-all-start.4 = ((bf16[8,64,1536]{2,1,0:T(8,128)(2,1)}), bf16[8,64,1536]{2,1,0:T(8,128)(2,1)}, u32[]{:S(2)}, u32[]{:S(2)}) async-start(bf16[8,64,1536]{2,1,0:T(8,128)(2,1)} %bitcast.35), calls=%async_computation.4 | async-start | bytes 3145728 | tf_op jit(solution)/shard_map/all_to_all | solution.py:134
  133.3 6.5 %copy-start.1 = (bf16[512,768]{1,0:T(8,128)(2,1)S(1)}, bf16[512,768]{1,0:T(8,128)(2,1)}, u32[]{:S(2)}) copy-start(bf16[512,768]{1,0:T(8,128)(2,1)} %copy-done) | copy-start | bytes 2359300
  133.3 7.0 %collective-permute-start.5 = (bf16[512,768]{1,0:T(8,128)(2,1)}, bf16[512,768]{1,0:T(8,128)(2,1)S(1)}, u32[]{:S(2)}, u32[]{:S(2)}) collective-permute-start(bf16[512,768]{1,0:T(8,128)(2,1)} %copy-done), channel_id=1, source_target_pairs={{0,64},{64,0},{128,192},{192,128},{256,320},{320,256},{384,448},{4... | collective-permute-start | bytes 2359304 | tf_op jit(solution)/shard_map/ppermute | solution.py:158
  135.5 4.9 %collective-permute-start.4 = (bf16[512,384]{1,0:T(8,128)(2,1)S(1)}, bf16[512,384]{1,0:T(8,128)(2,1)S(1)}, u32[]{:S(2)}, u32[]{:S(2)}) collective-permute-start(bf16[512,384]{1,0:T(8,128)(2,1)S(1)} %slice.185), channel_id=1, source_target_pairs={{0,64},{64,0},{128,192},{192,128},{256,320},{320,256},{384,448},{4... | collective-permute-start | bytes 1179656 | tf_op jit(solution)/shard_map/ppermute | solution.py:158
  137.9 33.7 %collective-permute-start.2 = (bf16[512,768]{1,0:T(8,128)(2,1)S(1)}, bf16[512,768]{1,0:T(8,128)(2,1)S(1)}, u32[]{:S(2)}, u32[]{:S(2)}) collective-permute-start(bf16[512,768]{1,0:T(8,128)(2,1)S(1)} %bitcast.31), channel_id=1, source_target_pairs={{0,64},{64,0},{128,192},{192,128},{256,320},{320,256},{384,448},{4... | collective-permute-start | bytes 2359304 | tf_op jit(solution)/shard_map/ppermute | solution.py:158
  142.7 28.9 %collective-permute-start.3 = (bf16[512,384]{1,0:T(8,128)(2,1)}, bf16[512,384]{1,0:T(8,128)(2,1)}, u32[]{:S(2)}, u32[]{:S(2)}) collective-permute-start(bf16[512,384]{1,0:T(8,128)(2,1)} %slice.182), channel_id=1, source_target_pairs={{0,64},{64,0},{128,192},{192,128},{256,320},{320,256},{384,448},{4... | collective-permute-start | bytes 1179656 | tf_op jit(solution)/shard_map/ppermute | solution.py:158
  168.2 12.3 %all-to-all-start.5 = ((bf16[4,16,1536]{2,1,0:T(8,128)(2,1)}), bf16[4,16,1536]{2,1,0:T(8,128)(2,1)S(1)}, u32[]{:S(2)}, u32[]{:S(2)}) async-start(bf16[4,16,1536]{2,1,0:T(8,128)(2,1)} %bitcast.9), calls=%async_computation.5 | async-start | bytes 393216 | tf_op jit(solution)/shard_map/all_to_all | solution.py:134
  171.5 9.0 %copy-start.12 = (bf16[1,16,768]{2,1,0:T(8,128)(2,1)S(1)}, bf16[1,16,768]{2,1,0:T(8,128)(2,1)}, u32[]{:S(2)}) copy-start(bf16[1,16,768]{2,1,0:T(8,128)(2,1)} %tokens_ref.1) | copy-start | bytes 73732
  171.5 9.0 %copy-start.13 = (bf16[16,768]{1,0:T(8,128)(2,1)S(1)}, bf16[16,768]{1,0:T(8,128)(2,1)}, u32[]{:S(2)}) copy-start(bf16[16,768]{1,0:T(8,128)(2,1)} %get-tuple-element.15) | copy-start | bytes 73732

commit v13 on v9

--- a/solution.py
+++ b/solution.py
@@ -179,11 +179,13 @@
         blocks = lax.all_gather(line, "col", axis=0)
         return blocks, paired(blocks, line_rows, w_in, w_in_mate, False)
 
-    some_kept = jnp.sum(counts) > 0
-    tokens_blocks, hidden_terms = lax.cond(some_kept, forward_plain, forward, tokens_line)
+    in_grid = lax.axis_index("col") >= 0
+    tokens_blocks, hidden_terms = lax.cond(in_grid, forward_plain, forward, tokens_line)
     slope_terms = paired(scaled_blocks, line_rows, w_out, w_out_mate, True)
 
-    hidden = added_up(swapped(cut(hidden_terms, row_count), "row"))
+    hidden_pieces = swapped(cut(hidden_terms, row_count), "row")
+    hidden_pieces, slope_terms = lax.optimization_barrier((hidden_pieces, slope_terms))
+    hidden = added_up(hidden_pieces)
     active, slope = gelu_both(hidden)
     share = jnp.broadcast_to(active.astype(jnp.bfloat16)[None], (row_count, *active.shape))
     mixed = swapped(jnp.concatenate([share, cut(slope_terms, row_count)], axis=2), "row")
@@ -196,25 +198,26 @@
 
     def backward(share):
         shares = spread(share, "row", row_count)
+        w_out_grad = product(activated[:, :units], scaled_all, 0, 0) + product(
+            mate(activated[:, units:]), mate(scaled_all), 0, 0
+        )
+        return *backward_parts(shares), w_out_grad
+
+    def backward_plain(share):
+        shares = lax.all_gather(share, "row", axis=0)
+        full = product(mixed.reshape(rows_all, 4 * units), scaled_all, 0, 0)
+        return *backward_parts(shares), full[:units] + mate(full[units : 2 * units])
+
+    def backward_parts(shares):
         back_terms = joined(shares, w_in, w_in_mate, True)
         hidden_grad = shares.reshape(rows_all, -1)
         back_line = added_up(swapped(cut(back_terms, columns), "col")).astype(jnp.bfloat16)
-        w_out_grad = product(activated[:, :units], scaled_all, 0, 0) + product(
-            mate(activated[:, units:]), mate(scaled_all), 0, 0
-        )
         w_in_grad = product(tokens_all, hidden_grad[:, :units], 0, 0) + product(
             mate(tokens_all), mate(hidden_grad[:, units:]), 0, 0
         )
-        return back_line, w_in_grad, w_out_grad
-
-    def nothing(share):
-        return (
-            jnp.zeros((line_rows, width), jnp.bfloat16),
-            jnp.zeros((width, units), jnp.float32),
-            jnp.zeros((units, width), jnp.float32),
-        )
-
-    back_line, w_in_grad, w_out_grad = lax.cond(some_kept, backward, nothing, grad_share)
+        return back_line, w_in_grad
+
+    back_line, w_in_grad, w_out_grad = lax.cond(in_grid, backward, backward_plain, grad_share)
     ends = jnp.concatenate([cut(output_line, chips), cut(back_line, chips)], axis=1)
     finished = added_up(swapped(ends, "rep", same_core))
     block_output = (tokens_local.astype(jnp.float32) + finished[:rows_local]).astype(jnp.bfloat16)

time: 176 us -> 176 us (level); the launches traced: 175 us -> 173 us
  blocking collectives: 65.8 us -> 67.7 us
    all_to_all x4, waiting for transfers between devices: 25.4 us -> 22.3 us  [swapped(): lax.all_to_all(value, axis, 0, 0, axis_index_groups=groups, tiled=True)]
    ppermute x6, waiting for transfers between devices: 0.02 us -> 1.98 us  [body(): mate = lambda value: lax.ppermute(value, 'rep', to_mate)]
  transfers between devices with their start and end apart: 12 -> 12, of which waited for: 4 -> 5; matrix products, arithmetic and copies ran while one was open for 8% -> 7% of each run, Pallas kernels for 4% -> 5%
where the time goes in v13:
time: 176 us; the launch traced here: 173 us
  blocking collectives  67.7 us (38%)
  starting transfers between devices  38.7 us (22%)
  waiting for transfers between devices  24.3 us (14%)
  between operations  14.1 us (8%)
  Pallas kernels  12.6 us (7%)
  matrix products  6.61 us (4%)
  other arithmetic  4.79 us (3%)
  local copies, waits for them, and re-layouts  4.04 us (2%)
    all_to_all x2, blocking collectives, swapped(): lax.all_to_all(value, axis, 0, 0, axis_index_groups=groups, tiled=True)  36.6 us
    all_gather x1, blocking collectives, forward_plain(): blocks = lax.all_gather(line, 'col', axis=0)  31.1 us
    all_to_all x4, starting transfers between devices, swapped(): lax.all_to_all(value, axis, 0, 0, axis_index_groups=groups, tiled=True)  26.7 us
    all_to_all x4, waiting for transfers between devices, swapped(): lax.all_to_all(value, axis, 0, 0, axis_index_groups=groups, tiled=True)  22.3 us
    ppermute x6, starting transfers between devices, body(): mate = lambda value: lax.ppermute(value, 'rep', to_mate)  12 us
    dot_general x4, matrix products, product(): lax.dot_general(left, right, (((left_dim,), (right_dim,)), ((), ())), pre...  6.61 us
    pallas_call x2, Pallas kernels, paired(): pl.pallas_call(kernel, grid=(1,), in_specs=[pl.BlockSpec((count, rows, wi...  5.7 us
    pallas_call x2, Pallas kernels, joined(): pl.pallas_call(kernel, grid=(1,), in_specs=[pl.BlockSpec((count, rows, 2...  5.39 us
  transfers between devices with their start and end apart: 12, of which 5 were waited for; matrix products, arithmetic and copies ran while one was open for 7% of the time, Pallas kernels for 5%

profile of v13, /device:TPU:6, one launch (start us, length us, event | category | flops | bytes accessed | tf_op | source)
XLA Modules:
  0.0 173.0 jit_solution(5736665514926993660)
XLA Ops:
  7.2 1.5 shard_map.84
  8.6 10.3 %all-to-all-start.4 = ((bf16[4,32,768]{2,1,0:T(8,128)(2,1)}), bf16[4,32,768]{2,1,0:T(8,128)(2,1)S(1)}, u32[]{:S(2)}, u32[]{:S(2)}) async-start(bf16[4,32,768]{2,1,0:T(8,128)(2,1)} %get-tuple-element.86), calls=%async_computation.4 | async-start | bytes 393216 | tf_op jit(solution)/shard_map/all_to_all | solution.py:134
  18.9 1.9 %collective-permute-start.7 = (bf16[768,384]{1,0:T(8,128)(2,1)}, bf16[768,384]{1,0:T(8,128)(2,1)}, u32[]{:S(2)}, u32[]{:S(2)}) collective-permute-start(bf16[768,384]{1,0:T(8,128)(2,1)} %param.10), channel_id=1, source_target_pairs={{0,64},{64,0},{128,192},{192,128},{256,320},{320,256},{384,448},{4... | collective-permute-start | bytes 1769480 | tf_op jit(solution)/shard_map/ppermute | solution.py:158
  20.9 8.0 %all-to-all-done.4 = bf16[4,32,768]{2,1,0:T(8,128)(2,1)S(1)} async-done(((bf16[4,32,768]{2,1,0:T(8,128)(2,1)}), bf16[4,32,768]{2,1,0:T(8,128)(2,1)S(1)}, u32[]{:S(2)}, u32[]{:S(2)}) %all-to-all-start.4) | async-done | bytes 196640 | tf_op jit(solution)/shard_map/all_to_all | solution.py:134
  28.9 0.7 pad_maximum_fusion.2
  29.6 0.0 all-gather.4.cloned.1.call-update
  29.6 34.3 %conditional.4 = (bf16[512,768]{1,0:T(8,128)(2,1)}, bf16[512,768]{1,0:T(8,128)(2,1)}) conditional(s32[]{:T(128)} %convert_element_type.246, (bf16[4,32,768]{2,1,0:T(8,128)(2,1)S(1)}, bf16[768,384]{1,0:T(8,128)(2,1)}, bf16[768,384]{1,0:T(8,128)(2,1)}) %tuple.37, (bf16[4,32,768]{2,1,0:T(8,128)(2,1)S(1)}, bf16[768,384]{1,0:T(8,128)(2,1)}, ...), branch_computations={%region_0.0_spmd, %region_1.0_spmd} | conditional | flops 603979776 | bytes 9207852 | solution.py:183
  29.6 0.0 copy-start.3
  29.7 31.1 %all_gather.10.left_ref = bf16[8,64,768]{2,1,0:T(8,128)(2,1)} all-gather(bf16[1,64,768]{2,1,0:T(8,128)(2,1)S(1)} %bitcast.69), channel_id=1, replica_groups=mesh['rep'=8,'row'=8,'col'=8] {'col'}, dimensions={0}, use_global_device_ids=true | all-gather | bytes 884736 | tf_op jit(solution)/shard_map/cond/branch_1_fun/all_gather | solution.py:179
  60.8 3.2 %branch_1_fun.2 = bf16[512,768]{1,0:T(8,128)(2,1)} custom-call(bf16[8,64,768]{2,1,0:T(8,128)(2,1)} %all_gather.10.left_ref, bf16[768,384]{1,0:T(8,128)(2,1)S(1)} %copy-done.3, bf16[768,384]{1,0:T(8,128)(2,1)} %get-tuple-element.60.other_ref), custom_call_target="tpu_custom_call" | custom-call | flops 603979776 | bytes 4194304 | tf_op jit(solution)/shard_map/cond/branch_1_fun/pallas_call | solution.py:81
  63.9 5.1 %all-to-all-start.5 = ((bf16[8,64,768]{2,1,0:T(8,128)(2,1)}), bf16[8,64,768]{2,1,0:T(8,128)(2,1)S(1)}, u32[]{:S(2)}, u32[]{:S(2)}) async-start(bf16[8,64,768]{2,1,0:T(8,128)(2,1)} %bitcast.13), calls=%async_computation.5 | async-start | bytes 1572864 | tf_op jit(solution)/shard_map/all_to_all | solution.py:134
  69.1 1.9 %collective-permute-start.8 = (bf16[384,768]{1,0:T(8,128)(2,1)S(1)}, bf16[384,768]{1,0:T(8,128)(2,1)S(1)}, u32[]{:S(2)}, u32[]{:S(2)}) collective-permute-start(bf16[384,768]{1,0:T(8,128)(2,1)S(1)} %copy-done), channel_id=1, source_target_pairs={{0,64},{64,0},{128,192},{192,128},{256,320},{320,256},{384,448},{4... | collective-permute-start | bytes 1769480 | tf_op jit(solution)/shard_map/ppermute | solution.py:158
  71.0 2.0 %collective-permute-done.8.other_ref = bf16[384,768]{1,0:T(8,128)(2,1)S(1)} collective-permute-done((bf16[384,768]{1,0:T(8,128)(2,1)S(1)}, bf16[384,768]{1,0:T(8,128)(2,1)S(1)}, u32[]{:S(2)}, u32[]{:S(2)}) %collective-permute-start.8) | collective-permute-done | bytes 589856 | tf_op jit(solution)/shard_map/ppermute | solution.py:158
  73.0 2.5 %shard_map.85 = bf16[512,768]{1,0:T(8,128)(2,1)S(1)} custom-call(bf16[8,88,768]{2,1,0:T(8,128)(2,1)} %bitcast.59, bf16[384,768]{1,0:T(8,128)(2,1)S(1)} %copy-done, bf16[384,768]{1,0:T(8,128)(2,1)S(1)} %collective-permute-done.8.other_ref), custom_call_target="tpu_custom_call" | custom-call | flops 603979776 | bytes 4194304 | tf_op jit(solution)/shard_map/pallas_call | solution.py:81
  75.5 1.1 all-to-all-done.5
  76.6 0.2 fusion.21
  76.8 0.1 broadcast_in_dim.22
  76.9 0.1 pad_maximum_fusion
  77.0 23.6 %all_to_all.37.left_ref = bf16[8,64,1536]{2,1,0:T(8,128)(2,1)S(1)} all-to-all(bf16[8,64,1536]{2,1,0:T(8,128)(2,1)S(1)} %pad_maximum_fusion), channel_id=1, replica_groups=mesh['rep'=8,'row'=8,'col'=8] {'row'}, dimensions={0} | all-to-all | bytes 3145728 | tf_op jit(solution)/shard_map/all_to_all | solution.py:134
  100.6 1.9 %shard_map.86 = bf16[512,768]{1,0:T(8,128)(2,1)} custom-call(bf16[8,64,1536]{2,1,0:T(8,128)(2,1)S(1)} %all_to_all.37.left_ref, bf16[384,768]{1,0:T(8,128)(2,1)S(1)} %copy-done, bf16[384,768]{1,0:T(8,128)(2,1)S(1)} %collective-permute-done.8.other_ref), custom_call_target="tpu_custom_call" | custom-call | flops 603979776 | bytes 4194304 | tf_op jit(solution)/shard_map/pallas_call | solution.py:111
  102.5 0.0 reduce-scatter.2.cloned.1.call-update
  102.5 0.2 fusion.18
  102.7 0.8 copy-done.1
  103.5 47.3 %conditional.5 = (f32[768,384]{1,0:T(8,128)S(1)}, f32[384,768]{1,0:T(8,128)}, bf16[4,16,768]{2,1,0:T(8,128)(2,1)S(1)}) conditional(s32[]{:T(128)} %convert_element_type.246, (bf16[64,768]{1,0:T(8,128)(2,1)S(1)}, bf16[512,768]{1,0:T(8,128)(2,1)}, bf16[8,88,768]{2,1,0:T(8,128)(2,1)}, bf16[8,64,1536]{2,1,0:T(8,128)(2,1)S(1)}, ...), branch_computations={%region_3.0_spmd, %region_4.0_spmd} | conditional | flops 1813315584 | bytes 60129484
  103.5 0.9 broadcast_in_dim.10
  104.5 5.8 %all-to-all-start.2 = ((bf16[8,64,768]{2,1,0:T(8,128)(2,1)}), bf16[8,64,768]{2,1,0:T(8,128)(2,1)S(1)}, u32[]{:S(2)}, u32[]{:S(2)}) async-start(bf16[8,64,768]{2,1,0:T(8,128)(2,1)} %broadcast_in_dim.10), calls=%async_computation.2 | async-start | bytes 1572864 | tf_op jit(solution)/shard_map/cond/branch_1_fun/all_to_all | solution.py:134
  110.3 2.1 %slice.141 = bf16[8,64,768]{2,1,0:T(8,128)(2,1)} slice(bf16[8,88,768]{2,1,0:T(8,128)(2,1)} %get-tuple-element.70), slice={[0:8], [0:64], [0:768]} | slice | bytes 1572864 | tf_op jit(solution)/shard_map/slice | solution.py:197
  112.4 1.9 %collective-permute-start.6 = (bf16[512,768]{1,0:T(8,128)(2,1)}, bf16[512,768]{1,0:T(8,128)(2,1)}, u32[]{:S(2)}, u32[]{:S(2)}) collective-permute-start(bf16[512,768]{1,0:T(8,128)(2,1)} %bitcast.10), channel_id=1, source_target_pairs={{0,64},{64,0},{128,192},{192,128},{256,320},{320,256},{384,448},{4... | collective-permute-start | bytes 2359304 | tf_op jit(solution)/shard_map/cond/branch_1_fun/ppermute | solution.py:158
  114.3 4.7 %all-to-all-done.2.left_ref = bf16[8,64,768]{2,1,0:T(8,128)(2,1)S(1)} async-done(((bf16[8,64,768]{2,1,0:T(8,128)(2,1)}), bf16[8,64,768]{2,1,0:T(8,128)(2,1)S(1)}, u32[]{:S(2)}, u32[]{:S(2)}) %all-to-all-start.2) | async-done | bytes 786464 | tf_op jit(solution)/shard_map/cond/branch_1_fun/all_to_all | solution.py:134
  118.9 3.5 %branch_1_fun.3 = bf16[512,768]{1,0:T(8,128)(2,1)} custom-call(bf16[8,64,768]{2,1,0:T(8,128)(2,1)S(1)} %all-to-all-done.2.left_ref, bf16[768,384]{1,0:T(8,128)(2,1)S(1)} %get-tuple-element.71.own_ref, bf16[768,384]{1,0:T(8,128)(2,1)} %get-tuple-element.72.other_ref), custom_call_target="tpu_custom_call" | custom-call | flops 603979776 | bytes 4194304 | tf_op jit(solution)/shard_map/cond/branch_1_fun/pallas_call | solution.py:111
  122.4 5.4 %all-to-all-start.3 = ((bf16[8,64,768]{2,1,0:T(8,128)(2,1)}), bf16[8,64,768]{2,1,0:T(8,128)(2,1)}, u32[]{:S(2)}, u32[]{:S(2)}) async-start(bf16[8,64,768]{2,1,0:T(8,128)(2,1)} %bitcast.11), calls=%async_computation.3 | async-start | bytes 1572864 | tf_op jit(solution)/shard_map/cond/branch_1_fun/all_to_all | solution.py:134
  127.9 0.1 slice.139
  128.0 1.9 %collective-permute-start.5 = (bf16[512,384]{1,0:T(8,128)(2,1)S(1)}, bf16[512,384]{1,0:T(8,128)(2,1)S(1)}, u32[]{:S(2)}, u32[]{:S(2)}) collective-permute-start(bf16[512,384]{1,0:T(8,128)(2,1)S(1)} %slice.218), channel_id=1, source_target_pairs={{0,64},{64,0},{128,192},{192,128},{256,320},{320,256},{384,448},{4... | collective-permute-start | bytes 1179656 | tf_op jit(solution)/shard_map/cond/branch_1_fun/ppermute | solution.py:158
  129.9 2.4 %collective-permute-start.3 = (bf16[512,768]{1,0:T(8,128)(2,1)}, bf16[512,768]{1,0:T(8,128)(2,1)S(1)}, u32[]{:S(2)}, u32[]{:S(2)}) collective-permute-start(bf16[512,768]{1,0:T(8,128)(2,1)} %get-tuple-element.67), channel_id=1, source_target_pairs={{0,64},{64,0},{128,192},{192,128},{256,320},{320,256},{384,448},{4... | collective-permute-start | bytes 2359304 | tf_op jit(solution)/shard_map/cond/branch_1_fun/ppermute | solution.py:158
  132.4 1.6 fusion.3
  134.0 1.9 %collective-permute-start.4 = (bf16[512,384]{1,0:T(8,128)(2,1)S(1)}, bf16[512,384]{1,0:T(8,128)(2,1)S(1)}, u32[]{:S(2)}, u32[]{:S(2)}) collective-permute-start(bf16[512,384]{1,0:T(8,128)(2,1)S(1)} %slice.216), channel_id=1, source_target_pairs={{0,64},{64,0},{128,192},{192,128},{256,320},{320,256},{384,448},{4... | collective-permute-start | bytes 1179656 | tf_op jit(solution)/shard_map/cond/branch_1_fun/ppermute | solution.py:158
  136.0 2.6 %convolution_add_fusion.1 = f32[384,768]{1,0:T(8,128)} fusion(f32[384,768]{1,0:T(8,128)S(1)} %fusion.3, bf16[512,384]{1,0:T(8,128)(2,1)S(1)} %collective-permute-done.5, bf16[512,768]{1,0:T(8,128)(2,1)} %collective-permute-done.6), kind=kOutput, calls=%fused_computation.7 | convolution fusion | flops 302284800 | bytes 3538944 | tf_op jit(solution)/shard_map/cond/branch_1_fun/dot_general | solution.py:26
  138.6 1.7 %fusion.5 = f32[768,384]{1,0:T(8,128)S(1)} fusion(bf16[512,768]{1,0:T(8,128)(2,1)} %get-tuple-element.67, bf16[512,768]{1,0:T(8,128)(2,1)S(1)} %bitcast.56), kind=kOutput, calls=%fused_computation.11 | convolution fusion | flops 301989888 | bytes 2359296 | tf_op jit(solution)/shard_map/cond/branch_1_fun/dot_general | solution.py:26
  140.4 0.6 convolution_add_fusion.2
  141.0 8.5 %all-to-all-done.3 = bf16[8,64,768]{2,1,0:T(8,128)(2,1)} async-done(((bf16[8,64,768]{2,1,0:T(8,128)(2,1)}), bf16[8,64,768]{2,1,0:T(8,128)(2,1)}, u32[]{:S(2)}, u32[]{:S(2)}) %all-to-all-start.3) | async-done | bytes 786464 | tf_op jit(solution)/shard_map/cond/branch_1_fun/all_to_all | solution.py:134
  149.5 1.3 add_convert_fusion.1
  150.8 0.0 copy-start.4
  150.8 0.0 copy-start.7
  150.8 0.0 reduce-scatter.2.cloned.1.call-done
  150.8 1.0 pad_maximum_fusion.1
  151.9 13.0 %all_to_all.38 = bf16[4,32,768]{2,1,0:T(8,128)(2,1)S(1)} all-to-all(bf16[4,32,768]{2,1,0:T(8,128)(2,1)S(1)} %pad_maximum_fusion.1), channel_id=1, replica_groups={{0,128,256,384},{64,192,320,448},{1,129,257,385},{65,193,321,449},{2,13..., dimensions={0} | all-to-all | bytes 393216 | tf_op jit(solution)/shard_map/all_to_all | solution.py:134
  164.9 0.6 fusion.24
  165.5 0.6 fusion.25
  (22 shorter events, 0.2 us)
Async XLA Ops:
  8.6 20.2 %all-to-all-start.4 = ((bf16[4,32,768]{2,1,0:T(8,128)(2,1)}), bf16[4,32,768]{2,1,0:T(8,128)(2,1)S(1)}, u32[]{:S(2)}, u32[]{:S(2)}) async-start(bf16[4,32,768]{2,1,0:T(8,128)(2,1)} %get-tuple-element.86), calls=%async_computation.4 | async-start | bytes 393216 | tf_op jit(solution)/shard_map/all_to_all | solution.py:134
  18.9 54.0 %all-gather.4.cloned.1.call-start = ((), (), s32[]{:S(2)}) async-start(), calls=%async_computation.10 | async-start | bytes 1216512 | tf_op jit(solution)/shard_map/all_gather | solution.py:172
  18.9 10.7 %collective-permute-start.7 = (bf16[768,384]{1,0:T(8,128)(2,1)}, bf16[768,384]{1,0:T(8,128)(2,1)}, u32[]{:S(2)}, u32[]{:S(2)}) collective-permute-start(bf16[768,384]{1,0:T(8,128)(2,1)} %param.10), channel_id=1, source_target_pairs={{0,64},{64,0},{128,192},{192,128},{256,320},{320,256},{384,448},{4... | collective-permute-start | bytes 1769480 | tf_op jit(solution)/shard_map/ppermute | solution.py:158
  29.6 31.1 %copy-start.3 = (bf16[768,384]{1,0:T(8,128)(2,1)S(1)}, bf16[768,384]{1,0:T(8,128)(2,1)}, u32[]{:S(2)}) copy-start(bf16[768,384]{1,0:T(8,128)(2,1)} %get-tuple-element.59.own_ref) | copy-start | bytes 1769476 | tf_op jit(solution)/shard_map/cond
  63.9 5.1 %copy-start = (bf16[384,768]{1,0:T(8,128)(2,1)S(1)}, bf16[384,768]{1,0:T(8,128)(2,1)}, u32[]{:S(2)}) copy-start(bf16[384,768]{1,0:T(8,128)(2,1)} %own_ref.3) | copy-start | bytes 1769476
  63.9 12.7 %all-to-all-start.5 = ((bf16[8,64,768]{2,1,0:T(8,128)(2,1)}), bf16[8,64,768]{2,1,0:T(8,128)(2,1)S(1)}, u32[]{:S(2)}, u32[]{:S(2)}) async-start(bf16[8,64,768]{2,1,0:T(8,128)(2,1)} %bitcast.13), calls=%async_computation.5 | async-start | bytes 1572864 | tf_op jit(solution)/shard_map/all_to_all | solution.py:134
  69.1 81.8 %reduce-scatter.2.cloned.1.call-start = ((), (), s32[]{:S(2)}) async-start(), calls=%async_computation.9 | async-start | bytes 884736 | tf_op jit(solution)/shard_map/reduce_scatter | solution.py:195
  69.1 3.9 %collective-permute-start.8 = (bf16[384,768]{1,0:T(8,128)(2,1)S(1)}, bf16[384,768]{1,0:T(8,128)(2,1)S(1)}, u32[]{:S(2)}, u32[]{:S(2)}) collective-permute-start(bf16[384,768]{1,0:T(8,128)(2,1)S(1)} %copy-done), channel_id=1, source_target_pairs={{0,64},{64,0},{128,192},{192,128},{256,320},{320,256},{384,448},{4... | collective-permute-start | bytes 1769480 | tf_op jit(solution)/shard_map/ppermute | solution.py:158
  102.5 1.1 copy-start.1
  103.5 61.4 %copy-start.6 = (bf16[1,16,768]{2,1,0:T(8,128)(2,1)S(1)}, bf16[1,16,768]{2,1,0:T(8,128)(2,1)}, u32[]{:S(2)}) copy-start(bf16[1,16,768]{2,1,0:T(8,128)(2,1)} %tokens_ref.1) | copy-start | bytes 73732
  104.5 14.5 %all-to-all-start.2 = ((bf16[8,64,768]{2,1,0:T(8,128)(2,1)}), bf16[8,64,768]{2,1,0:T(8,128)(2,1)S(1)}, u32[]{:S(2)}, u32[]{:S(2)}) async-start(bf16[8,64,768]{2,1,0:T(8,128)(2,1)} %broadcast_in_dim.10), calls=%async_computation.2 | async-start | bytes 1572864 | tf_op jit(solution)/shard_map/cond/branch_1_fun/all_to_all | solution.py:134
  112.4 23.6 %collective-permute-start.6 = (bf16[512,768]{1,0:T(8,128)(2,1)}, bf16[512,768]{1,0:T(8,128)(2,1)}, u32[]{:S(2)}, u32[]{:S(2)}) collective-permute-start(bf16[512,768]{1,0:T(8,128)(2,1)} %bitcast.10), channel_id=1, source_target_pairs={{0,64},{64,0},{128,192},{192,128},{256,320},{320,256},{384,448},{4... | collective-permute-start | bytes 2359304 | tf_op jit(solution)/shard_map/cond/branch_1_fun/ppermute | solution.py:158
  122.4 27.0 %all-to-all-start.3 = ((bf16[8,64,768]{2,1,0:T(8,128)(2,1)}), bf16[8,64,768]{2,1,0:T(8,128)(2,1)}, u32[]{:S(2)}, u32[]{:S(2)}) async-start(bf16[8,64,768]{2,1,0:T(8,128)(2,1)} %bitcast.11), calls=%async_computation.3 | async-start | bytes 1572864 | tf_op jit(solution)/shard_map/cond/branch_1_fun/all_to_all | solution.py:134
  128.0 8.0 %collective-permute-start.5 = (bf16[512,384]{1,0:T(8,128)(2,1)S(1)}, bf16[512,384]{1,0:T(8,128)(2,1)S(1)}, u32[]{:S(2)}, u32[]{:S(2)}) collective-permute-start(bf16[512,384]{1,0:T(8,128)(2,1)S(1)} %slice.218), channel_id=1, source_target_pairs={{0,64},{64,0},{128,192},{192,128},{256,320},{320,256},{384,448},{4... | collective-permute-start | bytes 1179656 | tf_op jit(solution)/shard_map/cond/branch_1_fun/ppermute | solution.py:158
  129.9 10.4 %collective-permute-start.3 = (bf16[512,768]{1,0:T(8,128)(2,1)}, bf16[512,768]{1,0:T(8,128)(2,1)S(1)}, u32[]{:S(2)}, u32[]{:S(2)}) collective-permute-start(bf16[512,768]{1,0:T(8,128)(2,1)} %get-tuple-element.67), channel_id=1, source_target_pairs={{0,64},{64,0},{128,192},{192,128},{256,320},{320,256},{384,448},{4... | collective-permute-start | bytes 2359304 | tf_op jit(solution)/shard_map/cond/branch_1_fun/ppermute | solution.py:158
  134.0 6.3 %collective-permute-start.4 = (bf16[512,384]{1,0:T(8,128)(2,1)S(1)}, bf16[512,384]{1,0:T(8,128)(2,1)S(1)}, u32[]{:S(2)}, u32[]{:S(2)}) collective-permute-start(bf16[512,384]{1,0:T(8,128)(2,1)S(1)} %slice.216), channel_id=1, source_target_pairs={{0,64},{64,0},{128,192},{192,128},{256,320},{320,256},{384,448},{4... | collective-permute-start | bytes 1179656 | tf_op jit(solution)/shard_map/cond/branch_1_fun/ppermute | solution.py:158
  150.8 15.4 %copy-start.4 = (f32[768,384]{1,0:T(8,128)}, f32[768,384]{1,0:T(8,128)S(1)}, u32[]{:S(2)}) copy-start(f32[768,384]{1,0:T(8,128)S(1)} %get-tuple-element.84) | copy-start | bytes 3538948
  150.8 14.7 %copy-start.7 = (bf16[16,768]{1,0:T(8,128)(2,1)S(1)}, bf16[16,768]{1,0:T(8,128)(2,1)}, u32[]{:S(2)}) copy-start(bf16[16,768]{1,0:T(8,128)(2,1)} %get-tuple-element.92) | copy-start | bytes 73732
Sparse Core Ops, SparseCore 0:
  29.7 39.5 all-gather.3
  102.6 38.3 reduce-scatter.1

commit v14 on v13

--- a/solution.py
+++ b/solution.py
@@ -64,13 +64,13 @@
     )(counts, tokens, cotangent)
 
 
-def paired(blocks, rows, own, other, turned):
+def paired(blocks, rows, own, other, turned, parts):
     count, _, width = blocks.shape
     columns = own.shape[0] if turned else own.shape[1]
     step = count // 4
 
     def kernel(left_ref, own_ref, other_ref, out_ref):
-        for at in range(4):
+        for at in range(4 // parts):
             left = left_ref[at * step : (at + 1) * step].reshape(step * rows, width)
             for place, right_ref in enumerate((own_ref, other_ref)):
                 out_ref[
@@ -80,13 +80,13 @@
 
     return pl.pallas_call(
         kernel,
-        grid=(1,),
+        grid=(parts,),
         in_specs=[
-            pl.BlockSpec((count, rows, width), lambda i: (0, 0, 0)),
+            pl.BlockSpec((count // parts, rows, width), lambda i: (i, 0, 0)),
             pl.BlockSpec(own.shape, lambda i: (0, 0)),
             pl.BlockSpec(other.shape, lambda i: (0, 0)),
         ],
-        out_specs=pl.BlockSpec((count * rows, 2 * columns), lambda i: (0, 0)),
+        out_specs=pl.BlockSpec((count * rows // parts, 2 * columns), lambda i: (i, 0)),
         out_shape=jax.ShapeDtypeStruct((count * rows, 2 * columns), jnp.bfloat16),
         compiler_params=pltpu.CompilerParams(vmem_limit_bytes=VMEM),
         cost_estimate=pl.CostEstimate(
@@ -95,13 +95,13 @@
     )(blocks, own, other)
 
 
-def joined(blocks, own, other, turned):
+def joined(blocks, own, other, turned, parts):
     count, rows, _ = blocks.shape
     units, width = own.shape[::-1] if turned else own.shape
     step = count // 4
 
     def kernel(left_ref, own_ref, other_ref, out_ref):
-        for at in range(4):
+        for at in range(4 // parts):
             left = left_ref[at * step : (at + 1) * step].reshape(step * rows, 2 * units)
             dim = 1 if turned else 0
             total = product(left[:, :units], own_ref[...], 1, dim)
@@ -110,13 +110,13 @@
 
     return pl.pallas_call(
         kernel,
-        grid=(1,),
+        grid=(parts,),
         in_specs=[
-            pl.BlockSpec((count, rows, 2 * units), lambda i: (0, 0, 0)),
+            pl.BlockSpec((count // parts, rows, 2 * units), lambda i: (i, 0, 0)),
             pl.BlockSpec(own.shape, lambda i: (0, 0)),
             pl.BlockSpec(other.shape, lambda i: (0, 0)),
         ],
-        out_specs=pl.BlockSpec((count * rows, width), lambda i: (0, 0)),
+        out_specs=pl.BlockSpec((count * rows // parts, width), lambda i: (i, 0)),
         out_shape=jax.ShapeDtypeStruct((count * rows, width), jnp.bfloat16),
         compiler_params=pltpu.CompilerParams(vmem_limit_bytes=VMEM),
         cost_estimate=pl.CostEstimate(
@@ -173,15 +173,15 @@
 
     def forward(line):
         blocks = spread(line, "col", columns)
-        return blocks, paired(blocks, line_rows, w_in, w_in_mate, False)
+        return blocks, paired(blocks, line_rows, w_in, w_in_mate, False, 4)
 
     def forward_plain(line):
         blocks = lax.all_gather(line, "col", axis=0)
-        return blocks, paired(blocks, line_rows, w_in, w_in_mate, False)
+        return blocks, paired(blocks, line_rows, w_in, w_in_mate, False, 4)
 
     in_grid = lax.axis_index("col") >= 0
     tokens_blocks, hidden_terms = lax.cond(in_grid, forward_plain, forward, tokens_line)
-    slope_terms = paired(scaled_blocks, line_rows, w_out, w_out_mate, True)
+    slope_terms = paired(scaled_blocks, line_rows, w_out, w_out_mate, True, 1)
 
     hidden_pieces = swapped(cut(hidden_terms, row_count), "row")
     hidden_pieces, slope_terms = lax.optimization_barrier((hidden_pieces, slope_terms))
@@ -191,7 +191,7 @@
     mixed = swapped(jnp.concatenate([share, cut(slope_terms, row_count)], axis=2), "row")
     activated = mixed[:, :, : active.shape[1]].reshape(rows_all, -1)
     grad_share = (added_up(mixed[:, :, active.shape[1] :]) * slope).astype(jnp.bfloat16)
-    output_terms = joined(mixed, w_out, w_out_mate, False)
+    output_terms = joined(mixed, w_out, w_out_mate, False, 1)
     output_line = lax.psum_scatter(output_terms, "col", scatter_dimension=0, tiled=True)
     tokens_all = tokens_blocks.reshape(rows_all, width)
     scaled_all = scaled_blocks[:, :line_rows].reshape(rows_all, width)
@@ -209,7 +209,7 @@
         return *backward_parts(shares), full[:units] + mate(full[units : 2 * units])
 
     def backward_parts(shares):
-        back_terms = joined(shares, w_in, w_in_mate, True)
+        back_terms = joined(shares, w_in, w_in_mate, True, 4)
         hidden_grad = shares.reshape(rows_all, -1)
         back_line = added_up(swapped(cut(back_terms, columns), "col")).astype(jnp.bfloat16)
         w_in_grad = product(tokens_all, hidden_grad[:, :units], 0, 0) + product(

time: 176 us -> 177 us (level)
  transfers between devices with their start and end apart: 12 -> 12, of which waited for: 5 -> 5; matrix products, arithmetic and copies ran while one was open for 7% -> 7% of each run, Pallas kernels for 5% -> 6%
where the time goes in v14:
time: 177 us; the launch traced here: 174 us
  blocking collectives  67.3 us (38%)
  starting transfers between devices  38.7 us (22%)
  waiting for transfers between devices  24.2 us (14%)
  between operations  14.1 us (8%)
  Pallas kernels  14 us (8%)
  matrix products  6.61 us (4%)
  other arithmetic  4.79 us (3%)
  local copies, waits for them, and re-layouts  4.04 us (2%)
    all_to_all x2, blocking collectives, swapped(): lax.all_to_all(value, axis, 0, 0, axis_index_groups=groups, tiled=True)  36.2 us
    all_gather x1, blocking collectives, forward_plain(): blocks = lax.all_gather(line, 'col', axis=0)  31.1 us
    all_to_all x4, starting transfers between devices, swapped(): lax.all_to_all(value, axis, 0, 0, axis_index_groups=groups, tiled=True)  26.7 us
    all_to_all x4, waiting for transfers between devices, swapped(): lax.all_to_all(value, axis, 0, 0, axis_index_groups=groups, tiled=True)  22.1 us
    ppermute x6, starting transfers between devices, body(): mate = lambda value: lax.ppermute(value, 'rep', to_mate)  12 us
    pallas_call x2, Pallas kernels, paired(): pl.pallas_call(kernel, grid=(parts,), in_specs=[pl.BlockSpec((count // pa...  6.75 us
    dot_general x4, matrix products, product(): lax.dot_general(left, right, (((left_dim,), (right_dim,)), ((), ())), pre...  6.61 us
    pallas_call x2, Pallas kernels, joined(): pl.pallas_call(kernel, grid=(parts,), in_specs=[pl.BlockSpec((count // pa...  5.8 us
  transfers between devices with their start and end apart: 12, of which 5 were waited for; matrix products, arithmetic and copies ran while one was open for 7% of the time, Pallas kernels for 6%

profile of v14, /device:TPU:6, one launch (start us, length us, event | category | flops | bytes accessed | tf_op | source)
XLA Modules:
  0.0 173.9 jit_solution(9144444428080716946)
XLA Ops:
  7.2 1.5 shard_map.84
  8.6 10.3 %all-to-all-start.4 = ((bf16[4,32,768]{2,1,0:T(8,128)(2,1)}), bf16[4,32,768]{2,1,0:T(8,128)(2,1)S(1)}, u32[]{:S(2)}, u32[]{:S(2)}) async-start(bf16[4,32,768]{2,1,0:T(8,128)(2,1)} %get-tuple-element.86), calls=%async_computation.4 | async-start | bytes 393216 | tf_op jit(solution)/shard_map/all_to_all | solution.py:134
  18.9 1.9 %collective-permute-start.7 = (bf16[768,384]{1,0:T(8,128)(2,1)}, bf16[768,384]{1,0:T(8,128)(2,1)}, u32[]{:S(2)}, u32[]{:S(2)}) collective-permute-start(bf16[768,384]{1,0:T(8,128)(2,1)} %param.10), channel_id=1, source_target_pairs={{0,64},{64,0},{128,192},{192,128},{256,320},{320,256},{384,448},{4... | collective-permute-start | bytes 1769480 | tf_op jit(solution)/shard_map/ppermute | solution.py:158
  20.9 8.0 %all-to-all-done.4 = bf16[4,32,768]{2,1,0:T(8,128)(2,1)S(1)} async-done(((bf16[4,32,768]{2,1,0:T(8,128)(2,1)}), bf16[4,32,768]{2,1,0:T(8,128)(2,1)S(1)}, u32[]{:S(2)}, u32[]{:S(2)}) %all-to-all-start.4) | async-done | bytes 196640 | tf_op jit(solution)/shard_map/all_to_all | solution.py:134
  28.9 0.7 pad_maximum_fusion.2
  29.6 0.0 all-gather.4.cloned.1.call-update
  29.6 35.4 %conditional.4 = (bf16[512,768]{1,0:T(8,128)(2,1)}, bf16[512,768]{1,0:T(8,128)(2,1)}) conditional(s32[]{:T(128)} %convert_element_type.246, (bf16[4,32,768]{2,1,0:T(8,128)(2,1)S(1)}, bf16[768,384]{1,0:T(8,128)(2,1)}, bf16[768,384]{1,0:T(8,128)(2,1)}) %tuple.37, (bf16[4,32,768]{2,1,0:T(8,128)(2,1)S(1)}, bf16[768,384]{1,0:T(8,128)(2,1)}, ...), branch_computations={%region_0.0_spmd, %region_1.0_spmd} | conditional | flops 603979776 | bytes 9207852 | solution.py:183
  29.6 0.0 copy-start.3
  29.7 31.1 %all_gather.10.left_ref = bf16[8,64,768]{2,1,0:T(8,128)(2,1)} all-gather(bf16[1,64,768]{2,1,0:T(8,128)(2,1)S(1)} %bitcast.69), channel_id=1, replica_groups=mesh['rep'=8,'row'=8,'col'=8] {'col'}, dimensions={0}, use_global_device_ids=true | all-gather | bytes 884736 | tf_op jit(solution)/shard_map/cond/branch_1_fun/all_gather | solution.py:179
  60.8 4.2 %branch_1_fun.2 = bf16[512,768]{1,0:T(8,128)(2,1)} custom-call(bf16[8,64,768]{2,1,0:T(8,128)(2,1)} %all_gather.10.left_ref, bf16[768,384]{1,0:T(8,128)(2,1)S(1)} %copy-done.3, bf16[768,384]{1,0:T(8,128)(2,1)} %get-tuple-element.60.other_ref), custom_call_target="tpu_custom_call" | custom-call | flops 603979776 | bytes 4194304 | tf_op jit(solution)/shard_map/cond/branch_1_fun/pallas_call | solution.py:81
  65.0 5.1 %all-to-all-start.5 = ((bf16[8,64,768]{2,1,0:T(8,128)(2,1)}), bf16[8,64,768]{2,1,0:T(8,128)(2,1)S(1)}, u32[]{:S(2)}, u32[]{:S(2)}) async-start(bf16[8,64,768]{2,1,0:T(8,128)(2,1)} %bitcast.13), calls=%async_computation.5 | async-start | bytes 1572864 | tf_op jit(solution)/shard_map/all_to_all | solution.py:134
  70.1 1.9 %collective-permute-start.8 = (bf16[384,768]{1,0:T(8,128)(2,1)S(1)}, bf16[384,768]{1,0:T(8,128)(2,1)S(1)}, u32[]{:S(2)}, u32[]{:S(2)}) collective-permute-start(bf16[384,768]{1,0:T(8,128)(2,1)S(1)} %copy-done), channel_id=1, source_target_pairs={{0,64},{64,0},{128,192},{192,128},{256,320},{320,256},{384,448},{4... | collective-permute-start | bytes 1769480 | tf_op jit(solution)/shard_map/ppermute | solution.py:158
  72.0 2.0 %collective-permute-done.8.other_ref = bf16[384,768]{1,0:T(8,128)(2,1)S(1)} collective-permute-done((bf16[384,768]{1,0:T(8,128)(2,1)S(1)}, bf16[384,768]{1,0:T(8,128)(2,1)S(1)}, u32[]{:S(2)}, u32[]{:S(2)}) %collective-permute-start.8) | collective-permute-done | bytes 589856 | tf_op jit(solution)/shard_map/ppermute | solution.py:158
  74.0 2.5 %shard_map.85 = bf16[512,768]{1,0:T(8,128)(2,1)S(1)} custom-call(bf16[8,88,768]{2,1,0:T(8,128)(2,1)} %bitcast.59, bf16[384,768]{1,0:T(8,128)(2,1)S(1)} %copy-done, bf16[384,768]{1,0:T(8,128)(2,1)S(1)} %collective-permute-done.8.other_ref), custom_call_target="tpu_custom_call" | custom-call | flops 603979776 | bytes 4194304 | tf_op jit(solution)/shard_map/pallas_call | solution.py:81
  76.6 1.1 all-to-all-done.5
  77.7 0.2 fusion.21
  77.8 0.1 broadcast_in_dim.22
  77.9 0.1 pad_maximum_fusion
  78.0 23.6 %all_to_all.37.left_ref = bf16[8,64,1536]{2,1,0:T(8,128)(2,1)S(1)} all-to-all(bf16[8,64,1536]{2,1,0:T(8,128)(2,1)S(1)} %pad_maximum_fusion), channel_id=1, replica_groups=mesh['rep'=8,'row'=8,'col'=8] {'row'}, dimensions={0} | all-to-all | bytes 3145728 | tf_op jit(solution)/shard_map/all_to_all | solution.py:134
  101.6 1.9 %shard_map.86 = bf16[512,768]{1,0:T(8,128)(2,1)} custom-call(bf16[8,64,1536]{2,1,0:T(8,128)(2,1)S(1)} %all_to_all.37.left_ref, bf16[384,768]{1,0:T(8,128)(2,1)S(1)} %copy-done, bf16[384,768]{1,0:T(8,128)(2,1)S(1)} %collective-permute-done.8.other_ref), custom_call_target="tpu_custom_call" | custom-call | flops 603979776 | bytes 4194304 | tf_op jit(solution)/shard_map/pallas_call | solution.py:111
  103.5 0.0 reduce-scatter.2.cloned.1.call-update
  103.5 0.2 fusion.18
  103.8 0.8 copy-done.1
  104.6 47.6 %conditional.5 = (f32[768,384]{1,0:T(8,128)S(1)}, f32[384,768]{1,0:T(8,128)}, bf16[4,16,768]{2,1,0:T(8,128)(2,1)S(1)}) conditional(s32[]{:T(128)} %convert_element_type.246, (bf16[64,768]{1,0:T(8,128)(2,1)S(1)}, bf16[512,768]{1,0:T(8,128)(2,1)}, bf16[8,88,768]{2,1,0:T(8,128)(2,1)}, bf16[8,64,1536]{2,1,0:T(8,128)(2,1)S(1)}, ...), branch_computations={%region_3.0_spmd, %region_4.0_spmd} | conditional | flops 1813315584 | bytes 60129484
  104.6 0.9 broadcast_in_dim.10
  105.5 5.8 %all-to-all-start.2 = ((bf16[8,64,768]{2,1,0:T(8,128)(2,1)}), bf16[8,64,768]{2,1,0:T(8,128)(2,1)S(1)}, u32[]{:S(2)}, u32[]{:S(2)}) async-start(bf16[8,64,768]{2,1,0:T(8,128)(2,1)} %broadcast_in_dim.10), calls=%async_computation.2 | async-start | bytes 1572864 | tf_op jit(solution)/shard_map/cond/branch_1_fun/all_to_all | solution.py:134
  111.3 2.1 %slice.141 = bf16[8,64,768]{2,1,0:T(8,128)(2,1)} slice(bf16[8,88,768]{2,1,0:T(8,128)(2,1)} %get-tuple-element.70), slice={[0:8], [0:64], [0:768]} | slice | bytes 1572864 | tf_op jit(solution)/shard_map/slice | solution.py:197
  113.4 1.9 %collective-permute-start.6 = (bf16[512,768]{1,0:T(8,128)(2,1)}, bf16[512,768]{1,0:T(8,128)(2,1)}, u32[]{:S(2)}, u32[]{:S(2)}) collective-permute-start(bf16[512,768]{1,0:T(8,128)(2,1)} %bitcast.10), channel_id=1, source_target_pairs={{0,64},{64,0},{128,192},{192,128},{256,320},{320,256},{384,448},{4... | collective-permute-start | bytes 2359304 | tf_op jit(solution)/shard_map/cond/branch_1_fun/ppermute | solution.py:158
  115.3 4.7 %all-to-all-done.2.left_ref = bf16[8,64,768]{2,1,0:T(8,128)(2,1)S(1)} async-done(((bf16[8,64,768]{2,1,0:T(8,128)(2,1)}), bf16[8,64,768]{2,1,0:T(8,128)(2,1)S(1)}, u32[]{:S(2)}, u32[]{:S(2)}) %all-to-all-start.2) | async-done | bytes 786464 | tf_op jit(solution)/shard_map/cond/branch_1_fun/all_to_all | solution.py:134
  120.0 3.9 %branch_1_fun.3 = bf16[512,768]{1,0:T(8,128)(2,1)} custom-call(bf16[8,64,768]{2,1,0:T(8,128)(2,1)S(1)} %all-to-all-done.2.left_ref, bf16[768,384]{1,0:T(8,128)(2,1)S(1)} %get-tuple-element.71.own_ref, bf16[768,384]{1,0:T(8,128)(2,1)} %get-tuple-element.72.other_ref), custom_call_target="tpu_custom_call" | custom-call | flops 603979776 | bytes 4194304 | tf_op jit(solution)/shard_map/cond/branch_1_fun/pallas_call | solution.py:111
  123.9 5.5 %all-to-all-start.3 = ((bf16[8,64,768]{2,1,0:T(8,128)(2,1)}), bf16[8,64,768]{2,1,0:T(8,128)(2,1)}, u32[]{:S(2)}, u32[]{:S(2)}) async-start(bf16[8,64,768]{2,1,0:T(8,128)(2,1)} %bitcast.11), calls=%async_computation.3 | async-start | bytes 1572864 | tf_op jit(solution)/shard_map/cond/branch_1_fun/all_to_all | solution.py:134
  129.4 0.1 slice.139
  129.5 1.9 %collective-permute-start.5 = (bf16[512,384]{1,0:T(8,128)(2,1)S(1)}, bf16[512,384]{1,0:T(8,128)(2,1)S(1)}, u32[]{:S(2)}, u32[]{:S(2)}) collective-permute-start(bf16[512,384]{1,0:T(8,128)(2,1)S(1)} %slice.218), channel_id=1, source_target_pairs={{0,64},{64,0},{128,192},{192,128},{256,320},{320,256},{384,448},{4... | collective-permute-start | bytes 1179656 | tf_op jit(solution)/shard_map/cond/branch_1_fun/ppermute | solution.py:158
  131.4 2.4 %collective-permute-start.3 = (bf16[512,768]{1,0:T(8,128)(2,1)}, bf16[512,768]{1,0:T(8,128)(2,1)S(1)}, u32[]{:S(2)}, u32[]{:S(2)}) collective-permute-start(bf16[512,768]{1,0:T(8,128)(2,1)} %get-tuple-element.67), channel_id=1, source_target_pairs={{0,64},{64,0},{128,192},{192,128},{256,320},{320,256},{384,448},{4... | collective-permute-start | bytes 2359304 | tf_op jit(solution)/shard_map/cond/branch_1_fun/ppermute | solution.py:158
  133.8 1.6 fusion.3
  135.5 1.9 %collective-permute-start.4 = (bf16[512,384]{1,0:T(8,128)(2,1)S(1)}, bf16[512,384]{1,0:T(8,128)(2,1)S(1)}, u32[]{:S(2)}, u32[]{:S(2)}) collective-permute-start(bf16[512,384]{1,0:T(8,128)(2,1)S(1)} %slice.216), channel_id=1, source_target_pairs={{0,64},{64,0},{128,192},{192,128},{256,320},{320,256},{384,448},{4... | collective-permute-start | bytes 1179656 | tf_op jit(solution)/shard_map/cond/branch_1_fun/ppermute | solution.py:158
  137.5 2.6 %convolution_add_fusion.1 = f32[384,768]{1,0:T(8,128)} fusion(f32[384,768]{1,0:T(8,128)S(1)} %fusion.3, bf16[512,384]{1,0:T(8,128)(2,1)S(1)} %collective-permute-done.5, bf16[512,768]{1,0:T(8,128)(2,1)} %collective-permute-done.6), kind=kOutput, calls=%fused_computation.7 | convolution fusion | flops 302284800 | bytes 3538944 | tf_op jit(solution)/shard_map/cond/branch_1_fun/dot_general | solution.py:26
  140.1 1.7 fusion.5
  141.9 0.6 convolution_add_fusion.2
  142.5 8.3 %all-to-all-done.3 = bf16[8,64,768]{2,1,0:T(8,128)(2,1)} async-done(((bf16[8,64,768]{2,1,0:T(8,128)(2,1)}), bf16[8,64,768]{2,1,0:T(8,128)(2,1)}, u32[]{:S(2)}, u32[]{:S(2)}) %all-to-all-start.3) | async-done | bytes 786464 | tf_op jit(solution)/shard_map/cond/branch_1_fun/all_to_all | solution.py:134
  150.8 1.3 add_convert_fusion.1
  152.1 0.0 copy-start.4
  152.1 0.0 copy-start.7
  152.2 0.0 reduce-scatter.2.cloned.1.call-done
  152.2 1.0 pad_maximum_fusion.1
  153.2 12.6 %all_to_all.38 = bf16[4,32,768]{2,1,0:T(8,128)(2,1)S(1)} all-to-all(bf16[4,32,768]{2,1,0:T(8,128)(2,1)S(1)} %pad_maximum_fusion.1), channel_id=1, replica_groups={{0,128,256,384},{64,192,320,448},{1,129,257,385},{65,193,321,449},{2,13..., dimensions={0} | all-to-all | bytes 393216 | tf_op jit(solution)/shard_map/all_to_all | solution.py:134
  165.8 0.6 fusion.24
  166.4 0.6 fusion.25
  (22 shorter events, 0.2 us)
Async XLA Ops:
  8.6 20.2 %all-to-all-start.4 = ((bf16[4,32,768]{2,1,0:T(8,128)(2,1)}), bf16[4,32,768]{2,1,0:T(8,128)(2,1)S(1)}, u32[]{:S(2)}, u32[]{:S(2)}) async-start(bf16[4,32,768]{2,1,0:T(8,128)(2,1)} %get-tuple-element.86), calls=%async_computation.4 | async-start | bytes 393216 | tf_op jit(solution)/shard_map/all_to_all | solution.py:134
  18.9 55.1 %all-gather.4.cloned.1.call-start = ((), (), s32[]{:S(2)}) async-start(), calls=%async_computation.10 | async-start | bytes 1216512 | tf_op jit(solution)/shard_map/all_gather | solution.py:172
  18.9 10.7 %collective-permute-start.7 = (bf16[768,384]{1,0:T(8,128)(2,1)}, bf16[768,384]{1,0:T(8,128)(2,1)}, u32[]{:S(2)}, u32[]{:S(2)}) collective-permute-start(bf16[768,384]{1,0:T(8,128)(2,1)} %param.10), channel_id=1, source_target_pairs={{0,64},{64,0},{128,192},{192,128},{256,320},{320,256},{384,448},{4... | collective-permute-start | bytes 1769480 | tf_op jit(solution)/shard_map/ppermute | solution.py:158
  29.6 31.1 %copy-start.3 = (bf16[768,384]{1,0:T(8,128)(2,1)S(1)}, bf16[768,384]{1,0:T(8,128)(2,1)}, u32[]{:S(2)}) copy-start(bf16[768,384]{1,0:T(8,128)(2,1)} %get-tuple-element.59.own_ref) | copy-start | bytes 1769476 | tf_op jit(solution)/shard_map/cond
  65.0 5.1 %copy-start = (bf16[384,768]{1,0:T(8,128)(2,1)S(1)}, bf16[384,768]{1,0:T(8,128)(2,1)}, u32[]{:S(2)}) copy-start(bf16[384,768]{1,0:T(8,128)(2,1)} %own_ref.3) | copy-start | bytes 1769476
  65.0 12.7 %all-to-all-start.5 = ((bf16[8,64,768]{2,1,0:T(8,128)(2,1)}), bf16[8,64,768]{2,1,0:T(8,128)(2,1)S(1)}, u32[]{:S(2)}, u32[]{:S(2)}) async-start(bf16[8,64,768]{2,1,0:T(8,128)(2,1)} %bitcast.13), calls=%async_computation.5 | async-start | bytes 1572864 | tf_op jit(solution)/shard_map/all_to_all | solution.py:134
  70.1 82.1 %reduce-scatter.2.cloned.1.call-start = ((), (), s32[]{:S(2)}) async-start(), calls=%async_computation.9 | async-start | bytes 884736 | tf_op jit(solution)/shard_map/reduce_scatter | solution.py:195
  70.1 3.9 %collective-permute-start.8 = (bf16[384,768]{1,0:T(8,128)(2,1)S(1)}, bf16[384,768]{1,0:T(8,128)(2,1)S(1)}, u32[]{:S(2)}, u32[]{:S(2)}) collective-permute-start(bf16[384,768]{1,0:T(8,128)(2,1)S(1)} %copy-done), channel_id=1, source_target_pairs={{0,64},{64,0},{128,192},{192,128},{256,320},{320,256},{384,448},{4... | collective-permute-start | bytes 1769480 | tf_op jit(solution)/shard_map/ppermute | solution.py:158
  103.5 1.1 copy-start.1
  104.6 61.2 %copy-start.6 = (bf16[1,16,768]{2,1,0:T(8,128)(2,1)S(1)}, bf16[1,16,768]{2,1,0:T(8,128)(2,1)}, u32[]{:S(2)}) copy-start(bf16[1,16,768]{2,1,0:T(8,128)(2,1)} %tokens_ref.1) | copy-start | bytes 73732
  105.5 14.5 %all-to-all-start.2 = ((bf16[8,64,768]{2,1,0:T(8,128)(2,1)}), bf16[8,64,768]{2,1,0:T(8,128)(2,1)S(1)}, u32[]{:S(2)}, u32[]{:S(2)}) async-start(bf16[8,64,768]{2,1,0:T(8,128)(2,1)} %broadcast_in_dim.10), calls=%async_computation.2 | async-start | bytes 1572864 | tf_op jit(solution)/shard_map/cond/branch_1_fun/all_to_all | solution.py:134
  113.4 24.0 %collective-permute-start.6 = (bf16[512,768]{1,0:T(8,128)(2,1)}, bf16[512,768]{1,0:T(8,128)(2,1)}, u32[]{:S(2)}, u32[]{:S(2)}) collective-permute-start(bf16[512,768]{1,0:T(8,128)(2,1)} %bitcast.10), channel_id=1, source_target_pairs={{0,64},{64,0},{128,192},{192,128},{256,320},{320,256},{384,448},{4... | collective-permute-start | bytes 2359304 | tf_op jit(solution)/shard_map/cond/branch_1_fun/ppermute | solution.py:158
  123.9 26.9 %all-to-all-start.3 = ((bf16[8,64,768]{2,1,0:T(8,128)(2,1)}), bf16[8,64,768]{2,1,0:T(8,128)(2,1)}, u32[]{:S(2)}, u32[]{:S(2)}) async-start(bf16[8,64,768]{2,1,0:T(8,128)(2,1)} %bitcast.11), calls=%async_computation.3 | async-start | bytes 1572864 | tf_op jit(solution)/shard_map/cond/branch_1_fun/all_to_all | solution.py:134
  129.5 8.0 %collective-permute-start.5 = (bf16[512,384]{1,0:T(8,128)(2,1)S(1)}, bf16[512,384]{1,0:T(8,128)(2,1)S(1)}, u32[]{:S(2)}, u32[]{:S(2)}) collective-permute-start(bf16[512,384]{1,0:T(8,128)(2,1)S(1)} %slice.218), channel_id=1, source_target_pairs={{0,64},{64,0},{128,192},{192,128},{256,320},{320,256},{384,448},{4... | collective-permute-start | bytes 1179656 | tf_op jit(solution)/shard_map/cond/branch_1_fun/ppermute | solution.py:158
  131.4 10.4 %collective-permute-start.3 = (bf16[512,768]{1,0:T(8,128)(2,1)}, bf16[512,768]{1,0:T(8,128)(2,1)S(1)}, u32[]{:S(2)}, u32[]{:S(2)}) collective-permute-start(bf16[512,768]{1,0:T(8,128)(2,1)} %get-tuple-element.67), channel_id=1, source_target_pairs={{0,64},{64,0},{128,192},{192,128},{256,320},{320,256},{384,448},{4... | collective-permute-start | bytes 2359304 | tf_op jit(solution)/shard_map/cond/branch_1_fun/ppermute | solution.py:158
  135.5 6.3 %collective-permute-start.4 = (bf16[512,384]{1,0:T(8,128)(2,1)S(1)}, bf16[512,384]{1,0:T(8,128)(2,1)S(1)}, u32[]{:S(2)}, u32[]{:S(2)}) collective-permute-start(bf16[512,384]{1,0:T(8,128)(2,1)S(1)} %slice.216), channel_id=1, source_target_pairs={{0,64},{64,0},{128,192},{192,128},{256,320},{320,256},{384,448},{4... | collective-permute-start | bytes 1179656 | tf_op jit(solution)/shard_map/cond/branch_1_fun/ppermute | solution.py:158
  152.1 14.9 %copy-start.4 = (f32[768,384]{1,0:T(8,128)}, f32[768,384]{1,0:T(8,128)S(1)}, u32[]{:S(2)}) copy-start(f32[768,384]{1,0:T(8,128)S(1)} %get-tuple-element.84) | copy-start | bytes 3538948
  152.1 14.3 %copy-start.7 = (bf16[16,768]{1,0:T(8,128)(2,1)S(1)}, bf16[16,768]{1,0:T(8,128)(2,1)}, u32[]{:S(2)}) copy-start(bf16[16,768]{1,0:T(8,128)(2,1)} %get-tuple-element.92) | copy-start | bytes 73732
Sparse Core Ops, SparseCore 0:
  29.7 39.5 all-gather.3
  103.6 38.7 reduce-scatter.1

commit v15 on v13

--- a/solution.py
+++ b/solution.py
@@ -196,28 +196,31 @@
     tokens_all = tokens_blocks.reshape(rows_all, width)
     scaled_all = scaled_blocks[:, :line_rows].reshape(rows_all, width)
 
-    def backward(share):
-        shares = spread(share, "row", row_count)
+    shares = spread(grad_share, "row", row_count)
+
+    def backward(shares):
         w_out_grad = product(activated[:, :units], scaled_all, 0, 0) + product(
             mate(activated[:, units:]), mate(scaled_all), 0, 0
         )
-        return *backward_parts(shares), w_out_grad
-
-    def backward_plain(share):
-        shares = lax.all_gather(share, "row", axis=0)
+        back_terms = joined(shares, w_in, w_in_mate, True)
+        back_pieces = swapped(cut(back_terms, columns), "col")
+        return *backward_parts(shares, back_pieces), w_out_grad
+
+    def backward_plain(shares):
         full = product(mixed.reshape(rows_all, 4 * units), scaled_all, 0, 0)
-        return *backward_parts(shares), full[:units] + mate(full[units : 2 * units])
-
-    def backward_parts(shares):
         back_terms = joined(shares, w_in, w_in_mate, True)
+        back_pieces = swapped(cut(back_terms, columns), "col")
+        return *backward_parts(shares, back_pieces), full[:units] + mate(full[units : 2 * units])
+
+    def backward_parts(shares, back_pieces):
         hidden_grad = shares.reshape(rows_all, -1)
-        back_line = added_up(swapped(cut(back_terms, columns), "col")).astype(jnp.bfloat16)
+        back_line = added_up(back_pieces).astype(jnp.bfloat16)
         w_in_grad = product(tokens_all, hidden_grad[:, :units], 0, 0) + product(
             mate(tokens_all), mate(hidden_grad[:, units:]), 0, 0
         )
         return back_line, w_in_grad
 
-    back_line, w_in_grad, w_out_grad = lax.cond(in_grid, backward, backward_plain, grad_share)
+    back_line, w_in_grad, w_out_grad = lax.cond(in_grid, backward, backward_plain, shares)
     ends = jnp.concatenate([cut(output_line, chips), cut(back_line, chips)], axis=1)
     finished = added_up(swapped(ends, "rep", same_core))
     block_output = (tokens_local.astype(jnp.float32) + finished[:rows_local]).astype(jnp.bfloat16)

time: 176 us -> 177 us (level)
  blocking collectives: 67.7 us -> 82.7 us
  starting transfers between devices: 38.7 us -> 33.1 us
  waiting for transfers between devices: 24.3 us -> 20.6 us
  local copies, waits for them, and re-layouts: 4.04 us -> 1.23 us
    all_to_all x2 -> x3, blocking collectives: 36.6 us -> 51.6 us  [swapped(): lax.all_to_all(value, axis, 0, 0, axis_index_groups=groups, tiled=True)]
    all_to_all x4 -> x3, starting transfers between devices: 26.7 us -> 20.9 us  [swapped(): lax.all_to_all(value, axis, 0, 0, axis_index_groups=groups, tiled=True)]
    all_to_all x4 -> x3, waiting for transfers between devices: 22.3 us -> 18.6 us  [swapped(): lax.all_to_all(value, axis, 0, 0, axis_index_groups=groups, tiled=True)]
  transfers between devices with their start and end apart: 12 -> 11, of which waited for: 5 -> 4; matrix products, arithmetic and copies ran while one was open for 7% -> 5% of each run, Pallas kernels for 5% -> 5%
where the time goes in v15:
time: 177 us; the launch traced here: 175 us
  blocking collectives  82.7 us (47%)
  starting transfers between devices  33.1 us (19%)
  waiting for transfers between devices  20.6 us (12%)
  between operations  14.2 us (8%)
  Pallas kernels  12.6 us (7%)
  matrix products  6.63 us (4%)
  other arithmetic  3.58 us (2%)
    all_to_all x3, blocking collectives, swapped(): lax.all_to_all(value, axis, 0, 0, axis_index_groups=groups, tiled=True)  51.6 us
    all_gather x1, blocking collectives, forward_plain(): blocks = lax.all_gather(line, 'col', axis=0)  31.1 us
    all_to_all x3, starting transfers between devices, swapped(): lax.all_to_all(value, axis, 0, 0, axis_index_groups=groups, tiled=True)  20.9 us
    all_to_all x3, waiting for transfers between devices, swapped(): lax.all_to_all(value, axis, 0, 0, axis_index_groups=groups, tiled=True)  18.6 us
    ppermute x6, starting transfers between devices, body(): mate = lambda value: lax.ppermute(value, 'rep', to_mate)  12.2 us
    dot_general x4, matrix products, product(): lax.dot_general(left, right, (((left_dim,), (right_dim,)), ((), ())), pre...  6.63 us
    pallas_call x2, Pallas kernels, paired(): pl.pallas_call(kernel, grid=(1,), in_specs=[pl.BlockSpec((count, rows, wi...  5.7 us
    pallas_call x2, Pallas kernels, joined(): pl.pallas_call(kernel, grid=(1,), in_specs=[pl.BlockSpec((count, rows, 2...  5.44 us
  transfers between devices with their start and end apart: 11, of which 4 were waited for; matrix products, arithmetic and copies ran while one was open for 5% of the time, Pallas kernels for 5%

profile of v15, /device:TPU:6, one launch (start us, length us, event | category | flops | bytes accessed | tf_op | source)
XLA Modules:
  0.0 174.7 jit_solution(2269327312115727375)
XLA Ops:
  7.2 1.5 shard_map.84
  8.6 10.3 %all-to-all-start.3 = ((bf16[4,32,768]{2,1,0:T(8,128)(2,1)}), bf16[4,32,768]{2,1,0:T(8,128)(2,1)S(1)}, u32[]{:S(2)}, u32[]{:S(2)}) async-start(bf16[4,32,768]{2,1,0:T(8,128)(2,1)} %get-tuple-element.86), calls=%async_computation.3 | async-start | bytes 393216 | tf_op jit(solution)/shard_map/all_to_all | solution.py:134
  18.9 1.9 %collective-permute-start.7 = (bf16[768,384]{1,0:T(8,128)(2,1)}, bf16[768,384]{1,0:T(8,128)(2,1)}, u32[]{:S(2)}, u32[]{:S(2)}) collective-permute-start(bf16[768,384]{1,0:T(8,128)(2,1)} %param.10), channel_id=1, source_target_pairs={{0,64},{64,0},{128,192},{192,128},{256,320},{320,256},{384,448},{4... | collective-permute-start | bytes 1769480 | tf_op jit(solution)/shard_map/ppermute | solution.py:158
  20.9 8.0 %all-to-all-done.3 = bf16[4,32,768]{2,1,0:T(8,128)(2,1)S(1)} async-done(((bf16[4,32,768]{2,1,0:T(8,128)(2,1)}), bf16[4,32,768]{2,1,0:T(8,128)(2,1)S(1)}, u32[]{:S(2)}, u32[]{:S(2)}) %all-to-all-start.3) | async-done | bytes 196640 | tf_op jit(solution)/shard_map/all_to_all | solution.py:134
  28.9 0.7 pad_maximum_fusion.2
  29.6 0.0 all-gather.3.cloned.1.call-update
  29.6 0.0 collective-permute-done.7
  29.6 34.3 %conditional.4 = (bf16[512,768]{1,0:T(8,128)(2,1)}, bf16[512,768]{1,0:T(8,128)(2,1)}) conditional(s32[]{:T(128)} %convert_element_type.223, (bf16[4,32,768]{2,1,0:T(8,128)(2,1)S(1)}, bf16[768,384]{1,0:T(8,128)(2,1)}, bf16[768,384]{1,0:T(8,128)(2,1)}) %tuple.37, (bf16[4,32,768]{2,1,0:T(8,128)(2,1)S(1)}, bf16[768,384]{1,0:T(8,128)(2,1)}, ...), branch_computations={%region_0.0_spmd, %region_1.0_spmd} | conditional | flops 603979776 | bytes 9207852 | solution.py:183
  29.6 0.0 copy-start.3
  29.7 31.1 %all_gather.6.left_ref = bf16[8,64,768]{2,1,0:T(8,128)(2,1)} all-gather(bf16[1,64,768]{2,1,0:T(8,128)(2,1)S(1)} %bitcast.58), channel_id=1, replica_groups=mesh['rep'=8,'row'=8,'col'=8] {'col'}, dimensions={0}, use_global_device_ids=true | all-gather | bytes 884736 | tf_op jit(solution)/shard_map/cond/branch_1_fun/all_gather | solution.py:179
  60.8 3.2 %branch_1_fun.2 = bf16[512,768]{1,0:T(8,128)(2,1)} custom-call(bf16[8,64,768]{2,1,0:T(8,128)(2,1)} %all_gather.6.left_ref, bf16[768,384]{1,0:T(8,128)(2,1)S(1)} %copy-done.3, bf16[768,384]{1,0:T(8,128)(2,1)} %get-tuple-element.60.other_ref), custom_call_target="tpu_custom_call" | custom-call | flops 603979776 | bytes 4194304 | tf_op jit(solution)/shard_map/cond/branch_1_fun/pallas_call | solution.py:81
  63.9 5.1 %all-to-all-start.4 = ((bf16[8,64,768]{2,1,0:T(8,128)(2,1)}), bf16[8,64,768]{2,1,0:T(8,128)(2,1)S(1)}, u32[]{:S(2)}, u32[]{:S(2)}) async-start(bf16[8,64,768]{2,1,0:T(8,128)(2,1)} %bitcast.13), calls=%async_computation.4 | async-start | bytes 1572864 | tf_op jit(solution)/shard_map/all_to_all | solution.py:134
  69.1 1.9 %collective-permute-start.8 = (bf16[384,768]{1,0:T(8,128)(2,1)S(1)}, bf16[384,768]{1,0:T(8,128)(2,1)S(1)}, u32[]{:S(2)}, u32[]{:S(2)}) collective-permute-start(bf16[384,768]{1,0:T(8,128)(2,1)S(1)} %copy-done), channel_id=1, source_target_pairs={{0,64},{64,0},{128,192},{192,128},{256,320},{320,256},{384,448},{4... | collective-permute-start | bytes 1769480 | tf_op jit(solution)/shard_map/ppermute | solution.py:158
  71.0 2.0 %collective-permute-done.8.other_ref = bf16[384,768]{1,0:T(8,128)(2,1)S(1)} collective-permute-done((bf16[384,768]{1,0:T(8,128)(2,1)S(1)}, bf16[384,768]{1,0:T(8,128)(2,1)S(1)}, u32[]{:S(2)}, u32[]{:S(2)}) %collective-permute-start.8) | collective-permute-done | bytes 589856 | tf_op jit(solution)/shard_map/ppermute | solution.py:158
  73.0 2.5 %shard_map.85 = bf16[512,768]{1,0:T(8,128)(2,1)S(1)} custom-call(bf16[8,88,768]{2,1,0:T(8,128)(2,1)} %bitcast.48, bf16[384,768]{1,0:T(8,128)(2,1)S(1)} %copy-done, bf16[384,768]{1,0:T(8,128)(2,1)S(1)} %collective-permute-done.8.other_ref), custom_call_target="tpu_custom_call" | custom-call | flops 603979776 | bytes 4194304 | tf_op jit(solution)/shard_map/pallas_call | solution.py:81
  75.5 1.1 all-to-all-done.4
  76.6 0.2 fusion.14
  76.8 0.1 broadcast_in_dim.24
  76.9 0.1 pad_maximum_fusion
  77.0 23.6 %all_to_all.38.left_ref = bf16[8,64,1536]{2,1,0:T(8,128)(2,1)S(1)} all-to-all(bf16[8,64,1536]{2,1,0:T(8,128)(2,1)S(1)} %pad_maximum_fusion), channel_id=1, replica_groups=mesh['rep'=8,'row'=8,'col'=8] {'row'}, dimensions={0} | all-to-all | bytes 3145728 | tf_op jit(solution)/shard_map/all_to_all | solution.py:134
  100.6 1.9 %shard_map.86 = bf16[512,768]{1,0:T(8,128)(2,1)} custom-call(bf16[8,64,1536]{2,1,0:T(8,128)(2,1)S(1)} %all_to_all.38.left_ref, bf16[384,768]{1,0:T(8,128)(2,1)S(1)} %copy-done, bf16[384,768]{1,0:T(8,128)(2,1)S(1)} %collective-permute-done.8.other_ref), custom_call_target="tpu_custom_call" | custom-call | flops 603979776 | bytes 4194304 | tf_op jit(solution)/shard_map/pallas_call | solution.py:111
  102.5 0.0 reduce-scatter.2.cloned.1.call-update
  102.5 0.2 fusion.15
  102.8 0.0 copy-start.1
  102.8 0.1 broadcast_in_dim.26
  102.8 14.3 %all_to_all.39 = bf16[8,64,768]{2,1,0:T(8,128)(2,1)S(1)} all-to-all(bf16[8,64,768]{2,1,0:T(8,128)(2,1)S(1)} %broadcast_in_dim.26), channel_id=1, replica_groups=mesh['rep'=8,'row'=8,'col'=8] {'row'}, dimensions={0} | all-to-all | bytes 1572864 | tf_op jit(solution)/shard_map/all_to_all | solution.py:134
  117.1 34.7 %conditional.5 = (f32[768,384]{1,0:T(8,128)S(1)}, f32[384,768]{1,0:T(8,128)}, bf16[4,16,768]{2,1,0:T(8,128)(2,1)S(1)}) conditional(s32[]{:T(128)} %convert_element_type.223, (bf16[8,64,768]{2,1,0:T(8,128)(2,1)S(1)}, bf16[512,768]{1,0:T(8,128)(2,1)}, bf16[8,88,768]{2,1,0:T(8,128)(2,1)S(1)}, bf16[8,64,1536]{2,1,0:T(8,128)(2,1)S(1)}, ...), branch_computations={%region_3.0_spmd, %region_4.0_spmd} | conditional | flops 1813315584 | bytes 59244748
  117.1 0.9 slice.141
  118.0 1.9 %collective-permute-start.6 = (bf16[512,768]{1,0:T(8,128)(2,1)}, bf16[512,768]{1,0:T(8,128)(2,1)}, u32[]{:S(2)}, u32[]{:S(2)}) collective-permute-start(bf16[512,768]{1,0:T(8,128)(2,1)} %bitcast.10), channel_id=1, source_target_pairs={{0,64},{64,0},{128,192},{192,128},{256,320},{320,256},{384,448},{4... | collective-permute-start | bytes 2359304 | tf_op jit(solution)/shard_map/cond/branch_1_fun/ppermute | solution.py:158
  120.0 3.5 %branch_1_fun.3 = bf16[512,768]{1,0:T(8,128)(2,1)} custom-call(bf16[8,64,768]{2,1,0:T(8,128)(2,1)S(1)} %get-tuple-element.68.left_ref, bf16[768,384]{1,0:T(8,128)(2,1)S(1)} %get-tuple-element.71.own_ref, bf16[768,384]{1,0:T(8,128)(2,1)} %get-tuple-element.72.other_ref), custom_call_target="tpu_custom_call" | custom-call | flops 603979776 | bytes 4194304 | tf_op jit(solution)/shard_map/cond/branch_1_fun/pallas_call | solution.py:111
  123.5 5.5 %all-to-all-start.2 = ((bf16[8,64,768]{2,1,0:T(8,128)(2,1)}), bf16[8,64,768]{2,1,0:T(8,128)(2,1)S(1)}, u32[]{:S(2)}, u32[]{:S(2)}) async-start(bf16[8,64,768]{2,1,0:T(8,128)(2,1)} %bitcast.11), calls=%async_computation.2 | async-start | bytes 1572864 | tf_op jit(solution)/shard_map/cond/branch_1_fun/all_to_all | solution.py:134
  129.0 2.1 %collective-permute-start.4 = (bf16[512,384]{1,0:T(8,128)(2,1)S(1)}, bf16[512,384]{1,0:T(8,128)(2,1)S(1)}, u32[]{:S(2)}, u32[]{:S(2)}) collective-permute-start(bf16[512,384]{1,0:T(8,128)(2,1)S(1)} %slice.216), channel_id=1, source_target_pairs={{0,64},{64,0},{128,192},{192,128},{256,320},{320,256},{384,448},{4... | collective-permute-start | bytes 1179656 | tf_op jit(solution)/shard_map/cond/branch_1_fun/ppermute | solution.py:158
  131.1 0.1 slice.139
  131.3 2.2 %collective-permute-start.5 = (bf16[512,384]{1,0:T(8,128)(2,1)S(1)}, bf16[512,384]{1,0:T(8,128)(2,1)S(1)}, u32[]{:S(2)}, u32[]{:S(2)}) collective-permute-start(bf16[512,384]{1,0:T(8,128)(2,1)S(1)} %slice.218), channel_id=1, source_target_pairs={{0,64},{64,0},{128,192},{192,128},{256,320},{320,256},{384,448},{4... | collective-permute-start | bytes 1179656 | tf_op jit(solution)/shard_map/cond/branch_1_fun/ppermute | solution.py:158
  133.5 2.1 %collective-permute-start.3 = (bf16[512,768]{1,0:T(8,128)(2,1)}, bf16[512,768]{1,0:T(8,128)(2,1)S(1)}, u32[]{:S(2)}, u32[]{:S(2)}) collective-permute-start(bf16[512,768]{1,0:T(8,128)(2,1)} %get-tuple-element.67), channel_id=1, source_target_pairs={{0,64},{64,0},{128,192},{192,128},{256,320},{320,256},{384,448},{4... | collective-permute-start | bytes 2359304 | tf_op jit(solution)/shard_map/cond/branch_1_fun/ppermute | solution.py:158
  135.6 1.6 fusion.3
  137.2 1.7 fusion.5
  139.0 2.7 %convolution_add_fusion.1 = f32[384,768]{1,0:T(8,128)} fusion(f32[384,768]{1,0:T(8,128)S(1)} %fusion.3, bf16[512,384]{1,0:T(8,128)(2,1)S(1)} %collective-permute-done.5, bf16[512,768]{1,0:T(8,128)(2,1)} %collective-permute-done.6), kind=kOutput, calls=%fused_computation.7 | convolution fusion | flops 302284800 | bytes 3538944 | tf_op jit(solution)/shard_map/cond/branch_1_fun/dot_general | solution.py:26
  141.7 0.6 convolution_add_fusion.2
  142.3 9.4 %all-to-all-done.2 = bf16[8,64,768]{2,1,0:T(8,128)(2,1)S(1)} async-done(((bf16[8,64,768]{2,1,0:T(8,128)(2,1)}), bf16[8,64,768]{2,1,0:T(8,128)(2,1)S(1)}, u32[]{:S(2)}, u32[]{:S(2)}) %all-to-all-start.2) | async-done | bytes 786464 | tf_op jit(solution)/shard_map/cond/branch_1_fun/all_to_all | solution.py:134
  151.7 0.1 add_convert_fusion.1
  151.8 0.0 copy-start.5
  151.8 0.0 copy-start.8
  151.8 0.0 reduce-scatter.2.cloned.1.call-done
  151.9 1.0 pad_maximum_fusion.1
  152.9 13.7 %all_to_all.40 = bf16[4,32,768]{2,1,0:T(8,128)(2,1)S(1)} all-to-all(bf16[4,32,768]{2,1,0:T(8,128)(2,1)S(1)} %pad_maximum_fusion.1), channel_id=1, replica_groups={{0,128,256,384},{64,192,320,448},{1,129,257,385},{65,193,321,449},{2,13..., dimensions={0} | all-to-all | bytes 393216 | tf_op jit(solution)/shard_map/all_to_all | solution.py:134
  166.6 0.6 fusion.18
  167.2 0.6 fusion.19
  (23 shorter events, 0.2 us)
Async XLA Ops:
  8.6 20.2 %all-to-all-start.3 = ((bf16[4,32,768]{2,1,0:T(8,128)(2,1)}), bf16[4,32,768]{2,1,0:T(8,128)(2,1)S(1)}, u32[]{:S(2)}, u32[]{:S(2)}) async-start(bf16[4,32,768]{2,1,0:T(8,128)(2,1)} %get-tuple-element.86), calls=%async_computation.3 | async-start | bytes 393216 | tf_op jit(solution)/shard_map/all_to_all | solution.py:134
  18.9 54.0 %all-gather.3.cloned.1.call-start = ((), (), s32[]{:S(2)}) async-start(), calls=%async_computation.10 | async-start | bytes 1216512 | tf_op jit(solution)/shard_map/all_gather | solution.py:172
  18.9 10.7 %collective-permute-start.7 = (bf16[768,384]{1,0:T(8,128)(2,1)}, bf16[768,384]{1,0:T(8,128)(2,1)}, u32[]{:S(2)}, u32[]{:S(2)}) collective-permute-start(bf16[768,384]{1,0:T(8,128)(2,1)} %param.10), channel_id=1, source_target_pairs={{0,64},{64,0},{128,192},{192,128},{256,320},{320,256},{384,448},{4... | collective-permute-start | bytes 1769480 | tf_op jit(solution)/shard_map/ppermute | solution.py:158
  29.6 31.1 %copy-start.3 = (bf16[768,384]{1,0:T(8,128)(2,1)S(1)}, bf16[768,384]{1,0:T(8,128)(2,1)}, u32[]{:S(2)}) copy-start(bf16[768,384]{1,0:T(8,128)(2,1)} %get-tuple-element.59.own_ref) | copy-start | bytes 1769476 | tf_op jit(solution)/shard_map/cond
  63.9 5.1 %copy-start = (bf16[384,768]{1,0:T(8,128)(2,1)S(1)}, bf16[384,768]{1,0:T(8,128)(2,1)}, u32[]{:S(2)}) copy-start(bf16[384,768]{1,0:T(8,128)(2,1)} %own_ref.3) | copy-start | bytes 1769476
  63.9 12.7 %all-to-all-start.4 = ((bf16[8,64,768]{2,1,0:T(8,128)(2,1)}), bf16[8,64,768]{2,1,0:T(8,128)(2,1)S(1)}, u32[]{:S(2)}, u32[]{:S(2)}) async-start(bf16[8,64,768]{2,1,0:T(8,128)(2,1)} %bitcast.13), calls=%async_computation.4 | async-start | bytes 1572864 | tf_op jit(solution)/shard_map/all_to_all | solution.py:134
  69.1 82.8 %reduce-scatter.2.cloned.1.call-start = ((), (), s32[]{:S(2)}) async-start(), calls=%async_computation.9 | async-start | bytes 884736 | tf_op jit(solution)/shard_map/reduce_scatter | solution.py:195
  69.1 3.9 %collective-permute-start.8 = (bf16[384,768]{1,0:T(8,128)(2,1)S(1)}, bf16[384,768]{1,0:T(8,128)(2,1)S(1)}, u32[]{:S(2)}, u32[]{:S(2)}) collective-permute-start(bf16[384,768]{1,0:T(8,128)(2,1)S(1)} %copy-done), channel_id=1, source_target_pairs={{0,64},{64,0},{128,192},{192,128},{256,320},{320,256},{384,448},{4... | collective-permute-start | bytes 1769480 | tf_op jit(solution)/shard_map/ppermute | solution.py:158
  102.8 14.4 %copy-start.1 = (bf16[768,384]{1,0:T(8,128)(2,1)S(1)}, bf16[768,384]{1,0:T(8,128)(2,1)}, u32[]{:S(2)}) copy-start(bf16[768,384]{1,0:T(8,128)(2,1)} %param.10) | copy-start | bytes 1769476
  102.8 14.3 %copy-start.4 = (bf16[704,768]{1,0:T(8,128)(2,1)S(1)}, bf16[704,768]{1,0:T(8,128)(2,1)}, u32[]{:S(2)}) copy-start(bf16[704,768]{1,0:T(8,128)(2,1)} %all-gather.3.cloned.1.call-done) | copy-start | bytes 3244036
  117.1 49.5 %copy-start.7 = (bf16[1,16,768]{2,1,0:T(8,128)(2,1)S(1)}, bf16[1,16,768]{2,1,0:T(8,128)(2,1)}, u32[]{:S(2)}) copy-start(bf16[1,16,768]{2,1,0:T(8,128)(2,1)} %tokens_ref.1) | copy-start | bytes 73732
  118.0 20.9 %collective-permute-start.6 = (bf16[512,768]{1,0:T(8,128)(2,1)}, bf16[512,768]{1,0:T(8,128)(2,1)}, u32[]{:S(2)}, u32[]{:S(2)}) collective-permute-start(bf16[512,768]{1,0:T(8,128)(2,1)} %bitcast.10), channel_id=1, source_target_pairs={{0,64},{64,0},{128,192},{192,128},{256,320},{320,256},{384,448},{4... | collective-permute-start | bytes 2359304 | tf_op jit(solution)/shard_map/cond/branch_1_fun/ppermute | solution.py:158
  123.5 28.2 %all-to-all-start.2 = ((bf16[8,64,768]{2,1,0:T(8,128)(2,1)}), bf16[8,64,768]{2,1,0:T(8,128)(2,1)S(1)}, u32[]{:S(2)}, u32[]{:S(2)}) async-start(bf16[8,64,768]{2,1,0:T(8,128)(2,1)} %bitcast.11), calls=%async_computation.2 | async-start | bytes 1572864 | tf_op jit(solution)/shard_map/cond/branch_1_fun/all_to_all | solution.py:134
  129.0 12.6 %collective-permute-start.4 = (bf16[512,384]{1,0:T(8,128)(2,1)S(1)}, bf16[512,384]{1,0:T(8,128)(2,1)S(1)}, u32[]{:S(2)}, u32[]{:S(2)}) collective-permute-start(bf16[512,384]{1,0:T(8,128)(2,1)S(1)} %slice.216), channel_id=1, source_target_pairs={{0,64},{64,0},{128,192},{192,128},{256,320},{320,256},{384,448},{4... | collective-permute-start | bytes 1179656 | tf_op jit(solution)/shard_map/cond/branch_1_fun/ppermute | solution.py:158
  131.3 7.7 %collective-permute-start.5 = (bf16[512,384]{1,0:T(8,128)(2,1)S(1)}, bf16[512,384]{1,0:T(8,128)(2,1)S(1)}, u32[]{:S(2)}, u32[]{:S(2)}) collective-permute-start(bf16[512,384]{1,0:T(8,128)(2,1)S(1)} %slice.218), channel_id=1, source_target_pairs={{0,64},{64,0},{128,192},{192,128},{256,320},{320,256},{384,448},{4... | collective-permute-start | bytes 1179656 | tf_op jit(solution)/shard_map/cond/branch_1_fun/ppermute | solution.py:158
  133.5 8.2 %collective-permute-start.3 = (bf16[512,768]{1,0:T(8,128)(2,1)}, bf16[512,768]{1,0:T(8,128)(2,1)S(1)}, u32[]{:S(2)}, u32[]{:S(2)}) collective-permute-start(bf16[512,768]{1,0:T(8,128)(2,1)} %get-tuple-element.67), channel_id=1, source_target_pairs={{0,64},{64,0},{128,192},{192,128},{256,320},{320,256},{384,448},{4... | collective-permute-start | bytes 2359304 | tf_op jit(solution)/shard_map/cond/branch_1_fun/ppermute | solution.py:158
  151.8 16.1 %copy-start.5 = (f32[768,384]{1,0:T(8,128)}, f32[768,384]{1,0:T(8,128)S(1)}, u32[]{:S(2)}) copy-start(f32[768,384]{1,0:T(8,128)S(1)} %get-tuple-element.84) | copy-start | bytes 3538948
  151.8 15.4 %copy-start.8 = (bf16[16,768]{1,0:T(8,128)(2,1)S(1)}, bf16[16,768]{1,0:T(8,128)(2,1)}, u32[]{:S(2)}) copy-start(bf16[16,768]{1,0:T(8,128)(2,1)} %get-tuple-element.92) | copy-start | bytes 73732
Sparse Core Ops, SparseCore 0:
  29.7 39.5 all-gather.2
  102.6 37.7 reduce-scatter.1
